TPU v7x, 32 devices: a whole 2x2x4 slice. The times are simulated.
32 devices in a mesh: seq: 8 (over z, y), exp: 4 (over x, core).
Axes of the slice: x: 2, y: 2, z: 4, core: 2. Of those that a mesh axis runs over, the one named last changes fastest.
Arguments:
- tokens: bfloat16 [4, 2048, 768], P('exp', 'seq'), may hold values from -6 to 6
- cotangent: bfloat16 [4, 2048, 768], P('exp', 'seq'), may hold values from -6 to 6
- segment_ids: int32 [4, 2048], P('exp', 'seq'), may hold values from 0 to 2, as said below
- expert_ids: int32 [4, 2048, 1], P('exp', 'seq'), may hold values from 0 to 3; in each aligned block of 256 rows (0 to 255, 256 to 511, ..., all dimensions but the last counted through in order) at most 128 rows name the same one
- projection: float32 [768, 2304], P(('seq', 'exp')), may hold values from -0.21875 to 0.21875
- output_weight: float32 [768, 768], P(('seq', 'exp')), may hold values from -1.25 to 1.25
- expert_up: float32 [4, 3072, 768], P('exp', 'seq'), may hold values from -0.28867513 to 0.28867513
- expert_down: float32 [4, 3072, 768], P('exp', 'seq'), may hold values from -0.14433757 to 0.14433757
- norm_gains: float32 [2, 768], replicated, may hold values from 0.3 to 2.8
- projection_first: float32 [768, 2304], P(('seq', 'exp')), may hold values from -0.00036621094 to 0.00036621094
- projection_second: float32 [768, 2304], P(('seq', 'exp')), may hold values from 4.756598e-10 to 1.9026392e-09
- output_first: float32 [768, 768], P(('seq', 'exp')), may hold values from -0.00036621094 to 0.00036621094
- output_second: float32 [768, 768], P(('seq', 'exp')), may hold values from 4.756598e-10 to 1.9026392e-09
- up_first: float32 [4, 3072, 768], P('exp', 'seq'), may hold values from -0.00036621094 to 0.00036621094
- up_second: float32 [4, 3072, 768], P('exp', 'seq'), may hold values from 4.756598e-10 to 1.9026392e-09
- down_first: float32 [4, 3072, 768], P('exp', 'seq'), may hold values from -0.00036621094 to 0.00036621094
- down_second: float32 [4, 3072, 768], P('exp', 'seq'), may hold values from 4.756598e-10 to 1.9026392e-09
- gains_first: float32 [2, 768], replicated, may hold values from -0.0014648438 to 0.0014648438
- gains_second: float32 [2, 768], replicated, may hold values from 7.5352045e-09 to 3.061177e-08
Outputs:
- block_output: bfloat16 [4, 2048, 768], P('exp', 'seq')
- input_grad: float32 [4, 2048, 768], P('exp', 'seq')
- grad_norm: float32 [], replicated
- projection_grad: float32 [768, 2304], P(('seq', 'exp'))
- projection_moment: float32 [768, 2304], P(('seq', 'exp'))
- projection_square: float32 [768, 2304], P(('seq', 'exp'))
- projection_new: float32 [768, 2304], P(('seq', 'exp'))
- output_grad: float32 [768, 768], P(('seq', 'exp'))
- output_moment: float32 [768, 768], P(('seq', 'exp'))
- output_square: float32 [768, 768], P(('seq', 'exp'))
- output_new: float32 [768, 768], P(('seq', 'exp'))
- up_grad: float32 [4, 3072, 768], P('exp', 'seq')
- up_moment: float32 [4, 3072, 768], P('exp', 'seq')
- up_square: float32 [4, 3072, 768], P('exp', 'seq')
- up_new: float32 [4, 3072, 768], P('exp', 'seq')
- down_grad: float32 [4, 3072, 768], P('exp', 'seq')
- down_moment: float32 [4, 3072, 768], P('exp', 'seq')
- down_square: float32 [4, 3072, 768], P('exp', 'seq')
- down_new: float32 [4, 3072, 768], P('exp', 'seq')
- gains_grad: float32 [2, 768], replicated
- gains_moment: float32 [2, 768], replicated
- gains_square: float32 [2, 768], replicated
- gains_new: float32 [2, 768], replicated
Inputs may be any that keep to these rules, and one draw needn't show every extreme that they name: `segment_ids`: never falling along a row; document 1 begins within the first 256 positions of its row and ends within the last 256. `expert_ids`: in the 256 rows of one device no expert is named by more than 128 tokens.
All inputs are finite; a program needn't handle non-finite values.
Results may differ from a plain program's by a relative error of at most 0.018.
Values may be sent and summed in bfloat16 or wider, within the bound.
No kernel may reach another device: no remote copies, remote signals or barrier semaphores. Data moves between devices by JAX's collectives and lax.ppermute only.
A program may use at most 512 MiB of HBM per device.

v0:
```python
import functools
import math

import jax
import jax.numpy as jnp
import numpy as np
from jax import lax
from jax.experimental import pallas as pl
from jax.experimental.pallas import tpu as pltpu
from jax.sharding import Mesh
from jax.sharding import PartitionSpec as P

HEADS = 12
CAP = 128
STEP = 10


EPSILON = 1e-05
CLIP = 1.0
BETA_ONE = 0.9
BETA_TWO = 0.99
ADAM_FLOOR = 1e-08
DECAY = 0.1
RATE_MATRIX = 0.04
RATE_OUTPUT = 0.1
RATE_GAIN = 0.5

SEQ = ("hi", "lo", "in")
EXP = ("exp",)
ALL = SEQ + EXP
TEAM = ("lo",)
SHARE = ("hi", "in")
LANES = 128
HALF = 64
FAR = -1e30
BF16 = jnp.bfloat16
F32 = jnp.float32
VMEM_LIMIT = 60 * 1024 * 1024


def head_plan(count):
    whole = math.lcm(HEADS, count)
    units, parts = whole // count, whole // HEADS
    first = np.zeros((count,), np.int64)
    active = np.zeros((count, 2, count), np.int32)
    for device in range(count):
        first[device] = min(units * device // parts, HEADS - 2)
        for unit in range(units * device, units * (device + 1)):
            slot = unit // parts - first[device]
            for block in range(count):
                turn = block % (2 * parts)
                if min(turn, 2 * parts - 1 - turn) == unit % parts:
                    active[device, slot, block] = 1
    return first, active


def three_parts(value):
    high = value.astype(BF16).astype(F32)
    middle = (value - high).astype(BF16).astype(F32)
    return high, middle, value - high - middle


def contract(left, right, left_axis, right_axis):
    return lax.dot_general(
        left, right, (((left_axis,), (right_axis,)), ((), ())), preferred_element_type=F32
    )


def slot_arrays(packed, documents, kind, slot):
    spare = HALF - HALF * slot
    lane = lax.broadcasted_iota(jnp.int32, packed.shape, 1)
    own = (lane < HALF) if slot == 0 else (lane >= HALF)
    place = (lane - spare).astype(F32)
    ours = place == documents
    first = (lane >= spare) & (lane < spare + 3)
    if kind == "query":
        extra = jnp.where(first & jnp.logical_not(ours), FAR, 0.0)
    elif kind == "key":
        extra = jnp.where(ours | ((lane >= spare + 3) & (lane < spare + 6)), 1.0, 0.0)
    else:
        extra = jnp.where(first, 1.0, 0.0)
    return jnp.where(own, packed, extra).astype(BF16)


def fill_slots(packed_of, documents_ref, wide_ref, kinds, place):
    documents = documents_ref[place, :].astype(F32)
    for number, kind in enumerate(kinds):
        packed = packed_of(kind).astype(F32)
        if kind == "query":
            packed = packed * 0.125
        for slot in range(2):
            column = (2 * number + slot) * LANES
            wide_ref[place, column : column + LANES] = slot_arrays(packed, documents, kind, slot)


def attend_kernel(active_ref, order_ref, *refs, block, chunk, held):
    row_refs = refs[:held]
    columns_ref, documents_ref = refs[held : held + 2]
    low_ref, full_ref, stat_ref, pair_ref, mixed_ref, wide_ref = refs[held + 2 :]
    at = pl.program_id(0)

    @pl.when(at == 0)
    def _():
        def fill(tokens, index):
            place = pl.ds(pl.multiple_of(order_ref[index] * block, block), block)
            packed = contract(tokens, columns_ref[...], 1, 0).astype(BF16)
            pair_ref[place, :] = packed[:, LANES:]
            parts = {
                kind: packed[:, part * LANES : (part + 1) * LANES]
                for part, kind in enumerate(("query", "key", "value"))
            }
            fill_slots(parts.get, documents_ref, wide_ref, tuple(parts), place)

        if held > 1:
            for index, row_ref in enumerate(row_refs):
                fill(row_ref[...], index)
        else:

            @pl.loop(0, pl.num_programs(0))
            def _(index):
                fill(row_refs[0][pl.ds(pl.multiple_of(index * block, block), block), :], index)

    rows = pl.ds(pl.multiple_of(at * block, block), block)
    lane = lax.broadcasted_iota(jnp.int32, (block, LANES), 1)
    last = lax.div(at * block, chunk)
    for slot in range(2):
        spare = HALF - HALF * slot
        own = (lane < HALF) if slot == 0 else (lane >= HALF)
        columns = slice(slot * LANES, (slot + 1) * LANES)

        @pl.when(active_ref[slot, at] != 0)
        def _():
            query = wide_ref[rows, columns]

            def step(index, carry, edge):
                top, weighted = carry
                place = pl.ds(pl.multiple_of(index * chunk, chunk), chunk)
                keys = wide_ref[place, 2 * LANES + slot * LANES : 3 * LANES + slot * LANES]
                values = wide_ref[place, 4 * LANES + slot * LANES : 5 * LANES + slot * LANES]
                scores = contract(query, keys, 1, 1)
                if edge:
                    key_at = index * chunk + lax.broadcasted_iota(jnp.int32, (block, chunk), 1)
                    query_at = at * block + lax.broadcasted_iota(jnp.int32, (block, chunk), 0)
                    scores = jnp.where(key_at <= query_at, scores, FAR)
                new_top = jnp.maximum(top, jnp.max(scores, axis=1, keepdims=True))
                weights = jnp.exp(scores - new_top).astype(BF16)
                weighted = weighted * jnp.exp(top - new_top) + contract(weights, values, 1, 0)
                return new_top, weighted

            carry = (jnp.full((block, 1), FAR, F32), jnp.zeros((block, LANES), F32))
            carry = lax.fori_loop(0, last, lambda index, state: step(index, state, False), carry)
            top, weighted = step(last, carry, True)
            total = weighted[:, spare : spare + 1]
            mixed_ref[slot] = jnp.where(own, weighted / total, 0.0)
            log_total = top + jnp.log(total)
            high, middle, small = three_parts(log_total)
            extra = jnp.where(lane == spare + 3, -high, 0.0)
            extra = jnp.where(lane == spare + 4, -middle, extra)
            extra = jnp.where(lane == spare + 5, -small, extra)
            stat_ref[:, columns] = (query.astype(F32) + extra).astype(BF16)

        @pl.when(active_ref[slot, at] == 0)
        def _():
            mixed_ref[slot] = jnp.zeros((block, LANES), F32)
            stat_ref[:, columns] = jnp.zeros((block, LANES), BF16)

    mixed = mixed_ref[0] + mixed_ref[1]
    full_ref[...] = mixed
    low_ref[...] = mixed.astype(BF16)


def attend_back_kernel(
    active_ref,
    order_ref,
    pair_ref,
    documents_ref,
    stat_ref,
    grad_ref,
    mixed_ref,
    out_ref,
    lying_ref,
    key_sum_ref,
    value_sum_ref,
    query_sum_ref,
    wide_ref,
    *,
    block,
    chunk,
    scaling,
):
    at = pl.program_id(0)
    rows = pl.ds(pl.multiple_of(at * block, block), block)
    lane = lax.broadcasted_iota(jnp.int32, (block, LANES), 1)
    last = lax.div(at * block, chunk)

    @pl.when(at == 0)
    def _():
        @pl.loop(0, pl.num_programs(0))
        def _(index):
            place = pl.ds(pl.multiple_of(index * block, block), block)
            parts = {"key": pair_ref[place, :LANES], "value": pair_ref[place, LANES:]}
            fill_slots(parts.get, documents_ref, wide_ref, tuple(parts), place)

        key_sum_ref[...] = jnp.zeros_like(key_sum_ref)
        value_sum_ref[...] = jnp.zeros_like(value_sum_ref)

    for slot in range(2):
        spare = HALF - HALF * slot
        own = (lane < HALF) if slot == 0 else (lane >= HALF)
        columns = slice(slot * LANES, (slot + 1) * LANES)
        query_sum_ref[slot] = jnp.zeros((block, LANES), F32)

        @pl.when(active_ref[slot, at] != 0)
        def _():
            query = stat_ref[:, columns]
            grad = grad_ref[...].astype(F32)
            delta = jnp.sum(jnp.where(own, grad * mixed_ref[...], 0.0), axis=1, keepdims=True)
            high, middle, small = three_parts(delta)
            extra = jnp.where(lane == spare, -high, 0.0)
            extra = jnp.where(lane == spare + 1, -middle, extra)
            extra = jnp.where(lane == spare + 2, -small, extra)
            grad_low = jnp.where(own, grad, extra).astype(BF16)

            def step(index, edge):
                place = pl.ds(pl.multiple_of(index * chunk, chunk), chunk)
                keys = wide_ref[place, slot * LANES : (slot + 1) * LANES]
                values = wide_ref[place, (2 + slot) * LANES : (3 + slot) * LANES]
                scores = contract(keys, query, 1, 1)
                if edge:
                    key_at = index * chunk + lax.broadcasted_iota(jnp.int32, (chunk, block), 0)
                    query_at = at * block + lax.broadcasted_iota(jnp.int32, (chunk, block), 1)
                    scores = jnp.where(key_at <= query_at, scores, FAR)
                weights = jnp.exp(scores)
                grad_weights = contract(values, grad_low, 1, 1)
                grad_scores = (weights * grad_weights).astype(BF16)
                value_sum_ref[slot, place, :] += contract(weights.astype(BF16), grad_low, 1, 0)
                key_sum_ref[slot, place, :] += contract(grad_scores, query, 1, 0)
                query_sum_ref[slot] += contract(grad_scores, keys, 0, 0)

            @pl.loop(0, last)
            def _(index):
                step(index, False)

            step(last, True)

    first_half = lane < HALF
    query_grad = jnp.where(first_half, query_sum_ref[0], query_sum_ref[1]) * scaling
    out_ref[rows, :LANES] = query_grad.astype(BF16)
    lying = pl.ds(pl.multiple_of(order_ref[at] * block, block), block)
    lying_ref[lying, :LANES] = query_grad.astype(BF16)

    @pl.when(at == pl.num_programs(0) - 1)
    def _():
        @pl.loop(0, pl.num_programs(0))
        def _(index):
            place = pl.ds(pl.multiple_of(index * block, block), block)
            key_grad = jnp.where(first_half, key_sum_ref[0, place, :], key_sum_ref[1, place, :])
            value_grad = jnp.where(
                first_half, value_sum_ref[0, place, :], value_sum_ref[1, place, :]
            )
            out_ref[place, LANES : 2 * LANES] = key_grad.astype(BF16)
            out_ref[place, 2 * LANES :] = value_grad.astype(BF16)
            lying = pl.ds(pl.multiple_of(order_ref[index] * block, block), block)
            lying_ref[lying, LANES : 2 * LANES] = key_grad.astype(BF16)
            lying_ref[lying, 2 * LANES :] = value_grad.astype(BF16)


def whole(value):
    return pl.BlockSpec(value.shape, lambda i, *unused: (0, 0), pipeline_mode=pl.Buffered(1))


SMALL = pl.CostEstimate(flops=1, bytes_accessed=1, transcendentals=0)


def attend(active, order, row_blocks, columns, documents, block):
    length = documents.shape[0]
    pair = jax.ShapeDtypeStruct((length, 2 * LANES), BF16)
    return pl.pallas_call(
        functools.partial(attend_kernel, block=block, chunk=2 * block, held=len(row_blocks)),
        grid_spec=pltpu.PrefetchScalarGridSpec(
            num_scalar_prefetch=2,
            grid=(length // block,),
            in_specs=[whole(value) for value in (*row_blocks, columns, documents)],
            out_specs=[
                pl.BlockSpec((block, LANES), lambda i, a, o: (i, 0)),
                pl.BlockSpec((block, LANES), lambda i, a, o: (i, 0)),
                pl.BlockSpec((block, 2 * LANES), lambda i, a, o: (i, 0)),
                whole(pair),
            ],
            scratch_shapes=[
                pltpu.VMEM((2, block, LANES), F32),
                pltpu.VMEM((length, 6 * LANES), BF16),
            ],
        ),
        out_shape=[
            jax.ShapeDtypeStruct((length, LANES), BF16),
            jax.ShapeDtypeStruct((length, LANES), F32),
            jax.ShapeDtypeStruct((length, 2 * LANES), BF16),
            pair,
        ],
        compiler_params=pltpu.CompilerParams(vmem_limit_bytes=VMEM_LIMIT),
        cost_estimate=SMALL,
    )(active, order, *row_blocks, columns, documents)


def attend_back(active, order, pair, documents, stat, grad, mixed, block, scaling):
    length = pair.shape[0]
    count = length // block
    return pl.pallas_call(
        functools.partial(attend_back_kernel, block=block, chunk=2 * block, scaling=scaling),
        grid_spec=pltpu.PrefetchScalarGridSpec(
            num_scalar_prefetch=2,
            grid=(count,),
            in_specs=[
                whole(pair),
                whole(documents),
                pl.BlockSpec((block, 2 * LANES), lambda i, a, o: (i, 0)),
                pl.BlockSpec((block, LANES), lambda i, a, o: (i, 0)),
                pl.BlockSpec((block, LANES), lambda i, a, o: (i, 0)),
            ],
            out_specs=[
                pl.BlockSpec(
                    (length, 3 * LANES), lambda i, a, o: (0, 0), pipeline_mode=pl.Buffered(1)
                )
            ]
            * 2,
            scratch_shapes=[
                pltpu.VMEM((2, length, LANES), F32),
                pltpu.VMEM((2, length, LANES), F32),
                pltpu.VMEM((2, block, LANES), F32),
                pltpu.VMEM((length, 4 * LANES), BF16),
            ],
        ),
        out_shape=[jax.ShapeDtypeStruct((length, 3 * LANES), BF16)] * 2,
        compiler_params=pltpu.CompilerParams(vmem_limit_bytes=VMEM_LIMIT),
        cost_estimate=SMALL,
    )(active, order, pair, documents, stat, grad, mixed)


def expert_kernel(arrived_ref, grad_ref, *refs, count):
    up_refs, down_refs = refs[:count], refs[count : 2 * count]
    total_ref = refs[2 * count]
    active_refs, hidden_refs = refs[2 * count + 1 : 3 * count + 1], refs[3 * count + 1 :]
    arrived, grad_arrived = arrived_ref[...], grad_ref[...]
    scale = math.sqrt(2.0 / math.pi)
    total = jnp.zeros(total_ref.shape, F32)
    for up_ref, down_ref, active_ref, hidden_ref in zip(
        up_refs, down_refs, active_refs, hidden_refs, strict=True
    ):
        up = up_ref[...]
        hidden = contract(arrived, up, 1, 1)
        squared = hidden * hidden
        bend = jnp.tanh(scale * hidden * (1.0 + 0.044715 * squared))
        half = 0.5 + 0.5 * bend
        active_ref[...] = (hidden * half).astype(BF16)
        slope = half + (0.5 * scale) * hidden * (1.0 - bend * bend) * (1.0 + 3 * 0.044715 * squared)
        grad_hidden = (slope * contract(grad_arrived, down_ref[...], 1, 1)).astype(BF16)
        hidden_ref[...] = grad_hidden
        total = total + contract(grad_hidden, up, 1, 0)
    total_ref[...] = total.astype(BF16)


def rows_spec(value, block):
    return pl.BlockSpec((block, value.shape[1]), lambda i: (i, 0))


def expert_part(arrived, grad_arrived, ups, downs):
    slots, width = arrived.shape
    block = 256
    units = [jax.ShapeDtypeStruct((slots, up.shape[0]), BF16) for up in ups]
    outs = [jax.ShapeDtypeStruct((slots, width), BF16), *units, *units]
    total, *parts = pl.pallas_call(
        functools.partial(expert_kernel, count=len(ups)),
        grid=(slots // block,),
        in_specs=[rows_spec(arrived, block), rows_spec(grad_arrived, block)]
        + [whole(value) for value in (*ups, *downs)],
        out_specs=[rows_spec(out, block) for out in outs],
        out_shape=outs,
        compiler_params=pltpu.CompilerParams(vmem_limit_bytes=VMEM_LIMIT),
        cost_estimate=SMALL,
    )(arrived, grad_arrived, *ups, *downs)
    return total, parts[: len(ups)], parts[len(ups) :]


def produced_kernel(*refs, count):
    total = contract(refs[0][...], refs[count][...], 1, 0)
    for index in range(1, count):
        total = total + contract(refs[index][...], refs[count + index][...], 1, 0)
    refs[-1][...] = total.astype(BF16)


def produced_part(actives, downs):
    slots, width = actives[0].shape[0], downs[0].shape[1]
    block = 256
    out = jax.ShapeDtypeStruct((slots, width), BF16)
    return pl.pallas_call(
        functools.partial(produced_kernel, count=len(actives)),
        grid=(slots // block,),
        in_specs=[rows_spec(value, block) for value in actives] + [whole(down) for down in downs],
        out_specs=rows_spec(out, block),
        out_shape=out,
        compiler_params=pltpu.CompilerParams(vmem_limit_bytes=VMEM_LIMIT),
        cost_estimate=SMALL,
    )(*actives, *downs)


def unit_kernel(grad_ref, arrived_ref, *refs, count):
    for index in range(count):
        active_ref, hidden_ref = refs[2 * index : 2 * index + 2]
        down_ref, up_ref = refs[2 * count + 2 * index : 2 * count + 2 * index + 2]
        down_ref[...] = contract(active_ref[...], grad_ref[...], 0, 0).astype(down_ref.dtype)
        up_ref[...] = contract(hidden_ref[...], arrived_ref[...], 0, 0).astype(up_ref.dtype)


def unit_grads(grad_arrived, arrived, blocks, kinds):
    slots, width = arrived.shape
    block = 256
    right = pl.BlockSpec((slots, block), lambda i: (0, i))
    outs = [
        jax.ShapeDtypeStruct((active.shape[1], width), kind)
        for (active, unused), kind in zip(blocks, kinds, strict=True)
        for part in range(2)
    ]
    flat = [value for pair in blocks for value in pair]
    return pl.pallas_call(
        functools.partial(unit_kernel, count=len(blocks)),
        grid=(width // block,),
        in_specs=[right, right] + [whole(value) for value in flat],
        out_specs=[pl.BlockSpec((out.shape[0], block), lambda i: (0, i)) for out in outs],
        out_shape=outs,
        compiler_params=pltpu.CompilerParams(vmem_limit_bytes=VMEM_LIMIT),
        cost_estimate=SMALL,
    )(grad_arrived, arrived, *flat)


def column_kernel(*refs, held):
    row_refs = refs[:held]
    lying_ref, out_ref = refs[held:]
    start, total = 0, None
    for row_ref in row_refs:
        rows = row_ref.shape[0]
        part = contract(row_ref[...], lying_ref[start : start + rows, :], 0, 0)
        total = part if total is None else total + part
        start += rows
    out_ref[...] = total.astype(BF16)


def column_terms(row_blocks, grad_lying):
    width = row_blocks[0].shape[1]
    block = 256
    out = jax.ShapeDtypeStruct((width, 3 * LANES), BF16)
    return pl.pallas_call(
        functools.partial(column_kernel, held=len(row_blocks)),
        grid=(width // block,),
        in_specs=[
            pl.BlockSpec((value.shape[0], block), lambda i: (0, i)) for value in row_blocks
        ]
        + [whole(grad_lying)],
        out_specs=rows_spec(out, block),
        out_shape=out,
        compiler_params=pltpu.CompilerParams(vmem_limit_bytes=VMEM_LIMIT),
        cost_estimate=SMALL,
    )(*row_blocks, grad_lying)


def close_kernel(
    pieces_ref, matrix_ref, tokens_ref, gain_ref, residual_ref, out_ref, part_ref, sum_ref, *, starts
):
    width = tokens_ref.shape[1]
    lane = lax.broadcasted_iota(jnp.int32, (tokens_ref.shape[0], LANES), 1)
    sum_ref[...] = jnp.zeros_like(sum_ref)
    for device, start in enumerate(starts):
        for part in range(3):
            piece = pieces_ref[device, :, part * LANES : (part + 1) * LANES].astype(F32)
            column = part * width + start
            if column % LANES == 0:
                sum_ref[:, column : column + LANES] += piece
            else:
                turned = pltpu.roll(piece, HALF, 1)
                low, high = column - HALF, column + HALF
                sum_ref[:, low : low + LANES] += jnp.where(lane >= HALF, turned, 0.0)
                sum_ref[:, high : high + LANES] += jnp.where(lane < HALF, turned, 0.0)
    grad = contract(sum_ref[...].astype(BF16), matrix_ref[...], 1, 1)
    inputs = tokens_ref[...].astype(F32)
    scale = lax.rsqrt(jnp.mean(inputs * inputs, axis=-1, keepdims=True) + EPSILON)
    normed = inputs * scale
    scaled = grad * gain_ref[...]
    mean = jnp.mean(scaled * normed, axis=-1, keepdims=True)
    out_ref[...] = residual_ref[...] + scale * (scaled - normed * mean)
    part_ref[...] = jnp.sum(grad * normed, axis=0, keepdims=True)


def close_norm(pieces, starts, matrix, tokens, gain, residual):
    rows, width = tokens.shape
    outs = [
        jax.ShapeDtypeStruct((rows, width), F32),
        jax.ShapeDtypeStruct((1, width), F32),
    ]
    return pl.pallas_call(
        functools.partial(close_kernel, starts=starts),
        in_specs=[pl.BlockSpec(memory_space=pltpu.VMEM)] * 5,
        out_specs=[pl.BlockSpec(memory_space=pltpu.VMEM)] * 2,
        out_shape=outs,
        scratch_shapes=[pltpu.VMEM((rows, 3 * width), F32)],
        compiler_params=pltpu.CompilerParams(vmem_limit_bytes=VMEM_LIMIT),
        cost_estimate=SMALL,
    )(pieces, matrix, tokens, gain, residual)


def dense_kernel(order_ref, *refs, starts):
    count = len(starts)
    term_refs = refs[:count]
    columns_ref, output_ref, square_ref, terms_ref = refs[count:]
    width = output_ref.shape[1]
    for index, term_ref in enumerate(term_refs):
        terms_ref[order_ref[index]] = term_ref[...].astype(F32)
    columns_ref[...] = jnp.zeros_like(columns_ref)
    lane = lax.broadcasted_iota(jnp.int32, (columns_ref.shape[0], LANES), 1)
    output = jnp.zeros(output_ref.shape, F32)
    for device, start in enumerate(starts):
        output = output + terms_ref[device, :, 3 * LANES :]
        for part in range(3):
            piece = terms_ref[device, :, part * LANES : (part + 1) * LANES]
            column = part * width + start
            if column % LANES == 0:
                columns_ref[:, column : column + LANES] += piece
            else:
                turned = pltpu.roll(piece, HALF, 1)
                low, high = column - HALF, column + HALF
                columns_ref[:, low : low + LANES] += jnp.where(lane >= HALF, turned, 0.0)
                columns_ref[:, high : high + LANES] += jnp.where(lane < HALF, turned, 0.0)
    output_ref[...] = output
    columns = columns_ref[...]
    square_ref[...] = jnp.zeros_like(square_ref) + (
        jnp.sum(columns * columns) + jnp.sum(output * output)
    )


def dense_grads(order, terms, starts):
    rows, lanes = terms[0].shape
    width = lanes - 3 * LANES
    outs = [jax.ShapeDtypeStruct((rows, columns), F32) for columns in (3 * width, width)]
    outs.append(jax.ShapeDtypeStruct((1, LANES), F32))
    return pl.pallas_call(
        functools.partial(dense_kernel, starts=starts),
        in_specs=[pl.BlockSpec(memory_space=pltpu.SMEM)]
        + [pl.BlockSpec(memory_space=pltpu.VMEM)] * len(terms),
        out_specs=[pl.BlockSpec(memory_space=pltpu.VMEM)] * 3,
        out_shape=outs,
        scratch_shapes=[pltpu.VMEM((len(terms), rows, lanes), F32)],
        compiler_params=pltpu.CompilerParams(vmem_limit_bytes=VMEM_LIMIT),
        cost_estimate=SMALL,
    )(order, *terms)


def adam_update(weight, grad, first, second, factor, rate, decay):
    clipped = grad * factor
    first_new = BETA_ONE * first + (1.0 - BETA_ONE) * clipped
    second_new = BETA_TWO * second + (1.0 - BETA_TWO) * clipped * clipped
    first_hat = first_new / (1.0 - BETA_ONE**STEP)
    second_hat = second_new / (1.0 - BETA_TWO**STEP)
    weight_new = weight - rate * (first_hat / (jnp.sqrt(second_hat) + ADAM_FLOOR) + decay * weight)
    return (first_new, second_new, weight_new)


def together(*values):
    return lax.optimization_barrier(values)


def swap(value, axes):
    return lax.all_to_all(value, axes, split_axis=0, concat_axis=0, tiled=True)


def adam_kernel(factor_ref, *refs, rates):
    count = len(rates)
    factor = factor_ref[0]
    for index, rate in enumerate(rates):
        weight, grad, first, second = [ref[...] for ref in refs[4 * index : 4 * index + 4]]
        outs = refs[4 * count + 3 * index : 4 * count + 3 * index + 3]
        for out, value in zip(
            outs, adam_update(weight, grad, first, second, factor, rate, DECAY), strict=True
        ):
            out[...] = value


def adam_all(factor, leaves, rates, steps):
    flat = [value.reshape(value.shape[-2:]) for leaf in leaves for value in leaf]

    def spec(value):
        rows, columns = value.shape
        if rows % (8 * steps) == 0:
            return pl.BlockSpec((rows // steps, columns), lambda i: (i, 0))
        lanes = columns // steps
        return pl.BlockSpec((rows, lanes), lambda i: (0, i))

    shapes = [jax.ShapeDtypeStruct(value.shape, F32) for value in flat[::4] for _ in range(3)]
    outs = pl.pallas_call(
        functools.partial(adam_kernel, rates=rates),
        grid=(steps,),
        in_specs=[pl.BlockSpec(memory_space=pltpu.SMEM)] + [spec(value) for value in flat],
        out_specs=[spec(shape) for shape in shapes],
        out_shape=shapes,
        compiler_params=pltpu.CompilerParams(vmem_limit_bytes=VMEM_LIMIT),
        cost_estimate=pl.CostEstimate(
            flops=20 * sum(value.size for value in flat[::4]),
            bytes_accessed=28 * sum(value.size for value in flat[::4]),
            transcendentals=0,
        ),
    )(factor.reshape(1), *flat)
    return [
        [out.reshape(leaf[0].shape) for out in outs[3 * index : 3 * index + 3]]
        for index, leaf in enumerate(leaves)
    ]


def flip(value, bits):
    count = lax.axis_size(SEQ)
    return lax.ppermute(value, SEQ, [(index, index ^ bits) for index in range(count)])


def others(value, axis):
    size = lax.axis_size(axis)
    parts = [
        lax.ppermute(value, axis, [((i + step) % size, i) for i in range(size)])
        for step in range(1, size)
    ]
    return parts[0] if size == 2 else jnp.concatenate(parts, axis=0)


def to_owners(blocks, axis):
    size = lax.axis_size(axis)
    return [
        lax.ppermute(block, axis, [(i, (i + step) % size) for i in range(size)])
        for step, block in enumerate(blocks, 1)
    ]


def add_all(own, parts):
    return functools.reduce(lambda total, part: total + part.astype(F32), parts, own.astype(F32))


def spread_sum(value):
    count = lax.axis_size(ALL)
    return jnp.sum(swap(jnp.broadcast_to(value[None], (count, *value.shape)), ALL), axis=0)


def body(
    tokens,
    cotangent,
    segment_ids,
    expert_ids,
    projection,
    output_weight,
    expert_up,
    expert_down,
    norm_gains,
    projection_first,
    projection_second,
    output_first,
    output_second,
    up_first,
    up_second,
    down_first,
    down_second,
    gains_first,
    gains_second,
):
    inputs = tokens[0].astype(F32)
    upstream = cotangent[0].astype(F32)
    row_count = inputs.shape[0]
    width = inputs.shape[1]
    head_size = width // HEADS
    scaling = head_size ** (-0.5)
    count = lax.axis_size(SEQ)
    groups = lax.axis_size("exp")
    team = lax.axis_size(TEAM)
    position = lax.axis_index(SEQ)
    length = count * row_count
    weight_rows = projection.shape[0]
    first_heads, active_table = head_plan(count)
    starts = [int(head) * head_size for head in first_heads]
    active = lax.dynamic_index_in_dim(jnp.asarray(active_table), position, 0, keepdims=False)
    gain_first = norm_gains[0]
    gain_second = norm_gains[1]
    used = active_table.any(axis=2)

    scale_first = lax.rsqrt(jnp.mean(inputs * inputs, axis=-1, keepdims=True) + EPSILON)
    normed_first = inputs * scale_first
    attend_in = (normed_first * gain_first).astype(BF16)
    slots = groups * CAP
    chosen = expert_ids[0, :, 0]
    one_hot = (chosen[:, None] == jnp.arange(groups, dtype=jnp.int32)[None, :]).astype(jnp.int32)
    rank = jnp.sum(jnp.cumsum(one_hot, axis=0) * one_hot, axis=1) - 1
    target = chosen * CAP + rank
    placing = (target[:, None] == jnp.arange(slots, dtype=jnp.int32)[None, :]).astype(BF16)

    def to_slots(values):
        outgoing = jnp.einsum("ts,td->sd", placing, values, preferred_element_type=F32)
        return outgoing.astype(BF16)

    def dispatch(outgoing):
        outgoing = jnp.broadcast_to(
            outgoing.reshape(1, groups, CAP, width), (team, groups, CAP, width)
        )
        return swap(outgoing.reshape(team * groups, CAP, width), TEAM + EXP).reshape(
            team * slots, width
        )

    def send_back(values):
        return swap(values.reshape(team * groups, CAP, width), TEAM + EXP).reshape(
            team, slots, width
        )

    def collect(returned):
        return jnp.einsum("ts,jsd->td", placing, returned, preferred_element_type=F32)

    projection_low = projection.astype(BF16)
    sent_rows = weight_rows + 8
    own_documents = jnp.zeros((8, 3 * LANES + width), BF16)
    own_documents = own_documents.at[0, :row_count].set(segment_ids[0].astype(BF16))
    output_low = output_weight.astype(BF16)
    pieces = [
        jnp.concatenate(
            [projection_low[:, k * width + s : k * width + s + LANES] for k in range(3)]
            + [output_low],
            axis=1,
        )
        for s in starts
    ]
    pieces = jnp.stack([jnp.concatenate([piece, own_documents], axis=0) for piece in pieces])
    own_up = expert_up[0].astype(BF16)
    own_down = expert_down[0].astype(BF16)
    pairwise = count == 8
    if pairwise:
        order = jnp.arange(count, dtype=jnp.int32) ^ position
        beside, below, across = flip(attend_in, 1), flip(attend_in, 2), flip(attend_in, 4)
        side_up, side_down = flip(own_up, 1), flip(own_down, 1)
        got_rows, beside, below, across, side_up, side_down, own_up = together(
            swap(pieces, SEQ), beside, below, across, side_up, side_down, own_up
        )
        corner = flip(across, 2)
        row_blocks = [attend_in, beside]
        row_blocks += [part for block in (below, across, corner) for part in (block, flip(block, 1))]
    else:
        order = jnp.arange(count, dtype=jnp.int32)
        row_blocks = [lax.all_gather(attend_in, SEQ, axis=0, tiled=True)]
        got_rows = swap(pieces, SEQ)
        side_up, side_down = others(own_up, "in"), others(own_down, "in")
    documents = jnp.broadcast_to(
        got_rows[:, weight_rows, :row_count].reshape(length, 1), (length, LANES)
    )
    own_copies = jnp.broadcast_to(
        got_rows[None, :, :weight_rows], (groups, count, weight_rows, 3 * LANES + width)
    )
    all_copies = swap(own_copies, EXP)

    peer_up = others(own_up, "hi")
    *row_blocks, all_copies, peer_up, own_up, own_down, grad_slots_out = together(
        *row_blocks, all_copies, peer_up, own_up, own_down, to_slots(cotangent[0])
    )
    all_copies = jnp.swapaxes(all_copies, 0, 1)
    columns = all_copies[..., : 3 * LANES].reshape(width, 3 * LANES)
    output_full = all_copies[..., 3 * LANES :].reshape(width, width)
    grad_arrived = dispatch(grad_slots_out)
    peer_down = others(own_down, "hi")
    far_up = others(peer_up, "in")

    mixed_low, mixed_full, stat, pair = attend(
        active, order, row_blocks, columns, documents, row_count
    )

    def place_heads():
        index = np.arange(LANES)
        matrix = np.zeros((count, LANES, width), np.float32)
        for device in range(count):
            for slot in range(2):
                if used[device, slot]:
                    own = index[slot * HALF : (slot + 1) * HALF]
                    matrix[device, own, starts[device] + own] = 1.0
        return jnp.asarray(matrix, BF16)

    head_places = place_heads()

    def to_tokens(values):
        return swap(values.reshape(count, row_count, values.shape[1]), SEQ)

    mixed_low, grad_arrived, peer_down, far_up = together(
        mixed_low, grad_arrived, peer_down, far_up
    )
    far_down = others(peer_down, "in")
    mixed_pieces, projection_low, far_down = together(
        to_tokens(mixed_low), projection_low, far_down
    )
    projection_full = lax.all_gather(projection_low, ALL, axis=0, tiled=True)
    attend_out = jnp.einsum(
        "jtc,jcd->td", mixed_pieces, head_places, preferred_element_type=F32
    ).astype(BF16)
    branch = jnp.dot(attend_out, output_full, preferred_element_type=F32)
    middle = inputs + branch
    scale_second = lax.rsqrt(jnp.mean(middle * middle, axis=-1, keepdims=True) + EPSILON)
    normed_second = middle * scale_second
    expert_in = (normed_second * gain_second).astype(BF16)

    arrived = dispatch(to_slots(expert_in))
    ups, downs = (own_up, peer_up, side_up, far_up), (own_down, peer_down, side_down, far_down)
    grad_slots, actives, hiddens = expert_part(arrived, grad_arrived, ups, downs)
    returned_grad = send_back(grad_slots)

    blocks = list(zip(actives, hiddens, strict=True))
    down_far, up_far, down_peer, up_peer = unit_grads(
        grad_arrived, arrived, (blocks[3], blocks[1]), (BF16, F32)
    )
    (down_part,) = to_owners([down_far], "in")
    down_side, up_side, down_own, up_own = unit_grads(
        grad_arrived, arrived, (blocks[2], blocks[0]), (BF16, F32)
    )
    produced = produced_part(actives, downs)
    returned_grad, down_part, up_far, up_peer, projection_full, produced, down_side, up_own = (
        together(
            returned_grad, down_part, up_far, up_peer, projection_full, produced, down_side, up_own
        )
    )
    grad_expert_in = collect(returned_grad)
    (up_part,) = to_owners([up_far], "in")
    peers = lax.axis_size("hi")

    def hi_parts(value):
        return to_owners(list(value.astype(BF16).reshape(peers - 1, -1, width)), "hi")

    down_hi = hi_parts(add_all(down_peer, [down_part]))

    scaled_second = grad_expert_in * gain_second
    gain_second_part = jnp.sum(grad_expert_in * normed_second, axis=0)
    grad_middle = scale_second * (
        scaled_second
        - normed_second * jnp.mean(scaled_second * normed_second, axis=-1, keepdims=True)
    )
    residual_grad = upstream + grad_middle
    branch_grad = residual_grad.astype(BF16)
    grad_mixed = jnp.einsum(
        "td,ed->te", branch_grad, output_full, preferred_element_type=F32
    ).astype(BF16)

    sent_grad = jnp.stack([grad_mixed[:, s : s + LANES] for s in starts])
    sent_grad, *down_hi = together(sent_grad, *down_hi)
    row_grad = swap(sent_grad, SEQ).reshape(length, LANES)

    group = lax.axis_index(EXP)

    def group_rows(value):
        rows = value.reshape(count, groups, weight_rows, -1)
        own, *away = [
            lax.dynamic_index_in_dim(rows, lax.rem(group + step, groups), 1, keepdims=False)
            for step in range(groups)
        ]
        return own, away

    output_term = jnp.einsum("tc,te->ce", attend_out, branch_grad, preferred_element_type=F32)
    output_own, output_away = group_rows(output_term.astype(BF16))
    row_grad, produced, down_side, up_side, up_part, *output_away = together(
        row_grad, produced, down_side, up_side, up_part, *output_away
    )
    output_away = to_owners(output_away, "exp")
    (down_early,) = to_owners([down_side], "in")
    (up_early,) = to_owners([up_side], "in")
    up_hi = hi_parts(add_all(up_peer, [up_part]))
    returned = send_back(produced)
    grad_qkv, grad_lying = attend_back(
        active, order, pair, documents, stat, row_grad, mixed_full, row_count, scaling
    )
    grad_qkv, grad_lying, returned, down_early, up_early, *held = together(
        grad_qkv, grad_lying, returned, down_early, up_early, *up_hi, *output_away
    )
    up_hi, output_away = held[: len(up_hi)], held[len(up_hi) :]
    up_grad = add_all(up_own, [up_early, *up_hi])[None]
    down_grad = add_all(down_own, [down_early, *down_hi])[None]
    block_output = (middle + collect(returned)).astype(BF16)[None]

    column_own, column_away = group_rows(column_terms(row_blocks, grad_lying))
    dense_rows = jnp.concatenate(
        [
            add_all(column_own, to_owners(column_away, "exp")).astype(BF16),
            add_all(output_own, output_away).astype(BF16),
        ],
        axis=2,
    )
    if pairwise:
        lying_terms = [
            lax.dynamic_index_in_dim(dense_rows, position ^ bits, 0, keepdims=False)
            for bits in range(count)
        ]
        lying_terms[1:] = [flip(lying_terms[bits], bits) for bits in range(1, count)]
        grad_pieces, *lying_terms = together(to_tokens(grad_qkv), *lying_terms)
    else:
        grad_pieces, dense_rows = together(to_tokens(grad_qkv), dense_rows)
        lying_terms = list(swap(dense_rows, SEQ))
    projection_grad, output_grad, dense_square = dense_grads(order, lying_terms, starts)
    input_grad, gain_first_part = close_norm(
        grad_pieces, starts, projection_full, tokens[0], gain_first[None], residual_grad
    )
    input_grad, gain_first_part = input_grad[None], gain_first_part[0]
    local_square = jnp.sum(up_grad * up_grad) + jnp.sum(down_grad * down_grad)
    summed = spread_sum(
        jnp.concatenate(
            [gain_first_part, gain_second_part, dense_square[0] + local_square]
        )[None]
    )[0]
    gains_grad = summed[: 2 * width].reshape(2, width)
    grad_norm = jnp.sqrt(summed[2 * width] + jnp.sum(gains_grad * gains_grad))
    factor = jnp.minimum(1.0, CLIP / (grad_norm + 1e-06))
    (
        (projection_moment, projection_square, projection_new),
        (output_moment, output_square, output_new),
        (up_moment, up_square, up_new),
        (down_moment, down_square, down_new),
    ) = adam_all(
        factor,
        [
            (projection, projection_grad, projection_first, projection_second),
            (output_weight, output_grad, output_first, output_second),
            (expert_up, up_grad, up_first, up_second),
            (expert_down, down_grad, down_first, down_second),
        ],
        (RATE_MATRIX, RATE_OUTPUT, RATE_MATRIX, RATE_MATRIX),
        6,
    )
    gains_moment, gains_square, gains_new = adam_update(
        norm_gains, gains_grad, gains_first, gains_second, factor, RATE_GAIN, 0.0
    )
    return (
        block_output,
        input_grad,
        grad_norm,
        projection_grad,
        projection_moment,
        projection_square,
        projection_new,
        output_grad,
        output_moment,
        output_square,
        output_new,
        up_grad,
        up_moment,
        up_square,
        up_new,
        down_grad,
        down_moment,
        down_square,
        down_new,
        gains_grad,
        gains_moment,
        gains_square,
        gains_new,
    )


def solution(mesh):
    token = P("exp", SEQ, None)
    dense = P(ALL, None)
    expert = P("exp", SEQ, None)
    in_specs = (
        (token, token, P("exp", SEQ), token)
        + (dense, dense, expert, expert, P())
        + (dense,) * 4
        + (expert,) * 4
        + (P(), P())
    )
    out_specs = (token, token, P()) + (dense,) * 8 + (expert,) * 8 + (P(),) * 4
    rows, groups = mesh.devices.shape
    fine = Mesh(mesh.devices.reshape(rows // 4, 2, 2, groups), ALL)
    return jax.shard_map(body, mesh=fine, in_specs=in_specs, out_specs=out_specs, check_vma=False)
```

profile of v0, /device:TPU:0, one launch (start us, length us, event | category | flops | bytes accessed | tf_op | source)
XLA Modules:
  0.0 452.3 jit_solution(14417235507393818586)
XLA Ops:
  15.1 7.4 %all-to-all-start = ((bf16[8,32,1152]{2,1,0:T(8,128)(2,1)}), bf16[8,32,1152]{2,1,0:T(8,128)(2,1)S(1)}, u32[]{:S(2)}, u32[]{:S(2)}) async-start(bf16[8,32,1152]{2,1,0:T(8,128)(2,1)} %fusion.46), calls=%async_computation | async-start | bytes 1179648 | tf_op jit(solution)/shard_map/all_to_all | solution.py:571
  22.7 2.1 collective-permute-start.3
  25.9 2.1 collective-permute-start
  27.9 1.5 collective-permute-start.1
  29.4 2.4 collective-permute-start.2
  31.8 33.2 %collective-permute-done.refs_1_ = bf16[256,768]{1,0:T(8,128)(2,1)S(1)} collective-permute-done((bf16[256,768]{1,0:T(8,128)(2,1)S(1)}, bf16[256,768]{1,0:T(8,128)(2,1)S(1)}, u32[]{:S(2)}, u32[]{:S(2)}) %collective-permute-start) | collective-permute-done | bytes 393248 | tf_op jit(solution)/shard_map/ppermute | solution.py:618
  66.6 1.4 broadcast_in_dim.24
  68.0 3.7 all-to-all-start.1
  71.7 1.5 collective-permute-start.7
  73.2 1.2 reduce-window.6
  74.8 2.4 collective-permute-start.9
  77.6 1.7 collective-permute-start.5
  79.3 11.0 %collective-permute-done.7.refs_6_ = bf16[256,768]{1,0:T(8,128)(2,1)} collective-permute-done((bf16[256,768]{1,0:T(8,128)(2,1)}, bf16[256,768]{1,0:T(8,128)(2,1)}, u32[]{:S(2)}, u32[]{:S(2)}) %collective-permute-start.7) | collective-permute-done | bytes 393248 | tf_op jit(solution)/shard_map/ppermute | solution.py:618
  91.0 1.6 convolution_convert_fusion.2
  92.5 5.4 %collective-permute-done.5.refs_3_ = bf16[256,768]{1,0:T(8,128)(2,1)S(1)} collective-permute-done((bf16[256,768]{1,0:T(8,128)(2,1)}, bf16[256,768]{1,0:T(8,128)(2,1)S(1)}, u32[]{:S(2)}, u32[]{:S(2)}) %collective-permute-start.5) | collective-permute-done | bytes 393248 | tf_op jit(solution)/shard_map/ppermute | solution.py:618
  97.9 5.9 %collective-permute-done.9.refs_1_ = bf16[384,768]{1,0:T(8,128)(2,1)S(1)} collective-permute-done((bf16[384,768]{1,0:T(8,128)(2,1)S(1)}, bf16[384,768]{1,0:T(8,128)(2,1)S(1)}, u32[]{:S(2)}, u32[]{:S(2)}) %collective-permute-start.9) | collective-permute-done | bytes 589856 | tf_op jit(solution)/shard_map/ppermute | solution.py:624
  105.4 1.3 broadcast_in_dim.55
  106.6 3.6 all-to-all-start.2
  112.3 1.2 fusion.74.active_ref
  114.3 1.4 copy.80
  115.7 1.9 slice.211
  118.8 23.1 %shard_map.380 = (bf16[2048,128]{1,0:T(8,128)(2,1)}, f32[2048,128]{1,0:T(8,128)}, bf16[2048,256]{1,0:T(8,128)(2,1)}, bf16[2048,256]{1,0:T(8,128)(2,1)}) custom-call(s32[2,8]{1,0:T(2,128)} %fusion.74.active_ref, s32[8]{0:T(128)} %iota_xor_fusion.order_ref, bf16[256,768]{1,0:T(8,128)(2,1)} %copy-done.7, bf16[256,768]{1,0:T(8,128)(2,1)} %copy-done.14, ...), custom_call_target="tpu_custom_call" | custom-call | flops 1 | bytes 1 | tf_op jit(solution)/shard_map/pallas_call | solution.py:278
  142.9 4.6 %all-to-all-start.3 = ((bf16[8,256,128]{2,1,0:T(8,128)(2,1)}), bf16[8,256,128]{2,1,0:T(8,128)(2,1)S(1)}, u32[]{:S(2)}, u32[]{:S(2)}) async-start(bf16[8,256,128]{2,1,0:T(8,128)(2,1)} %bitcast.217), calls=%async_computation.3 | async-start | bytes 1048576 | tf_op jit(solution)/shard_map/all_to_all | solution.py:571
  147.5 2.0 collective-permute-start.12
  149.5 18.4 %collective-permute-done.12.refs_7_ = bf16[384,768]{1,0:T(8,128)(2,1)} collective-permute-done((bf16[384,768]{1,0:T(8,128)(2,1)}, bf16[384,768]{1,0:T(8,128)(2,1)}, u32[]{:S(2)}, u32[]{:S(2)}) %collective-permute-start.12) | collective-permute-done | bytes 589856 | tf_op jit(solution)/shard_map/ppermute | solution.py:624
  168.8 1.5 slice.212
  173.0 27.6 %all_to_all.50 = bf16[8,128,768]{2,1,0:T(8,128)(2,1)} all-to-all(bf16[8,128,768]{2,1,0:T(8,128)(2,1)S(1)} %bitcast.197), channel_id=1, replica_groups=mesh['hi'=2,'lo'=2,'in'=2,'exp'=4] {'lo','exp'}, dimensions={0} | all-to-all | bytes 3145728 | tf_op jit(solution)/shard_map/all_to_all | solution.py:571
  200.6 15.6 %shard_map.381 = (bf16[1024,768]{1,0:T(8,128)(2,1)}, bf16[1024,384]{1,0:T(8,128)(2,1)}, bf16[1024,384]{1,0:T(8,128)(2,1)}, bf16[1024,384]{1,0:T(8,128)(2,1)}, bf...) custom-call(bf16[1024,768]{1,0:T(8,128)(2,1)} %bitcast.189, ...), custom_call_target="tpu_custom_call" | custom-call | flops 1 | bytes 1 | tf_op jit(solution)/shard_map/pallas_call | solution.py:372
  216.2 4.3 all-to-all-start.5
  220.5 6.7 %shard_map.382 = (bf16[384,768]{1,0:T(8,128)(2,1)}, bf16[384,768]{1,0:T(8,128)(2,1)}, f32[384,768]{1,0:T(8,128)}, f32[384,768]{1,0:T(8,128)}) custom-call(bf16[1024,768]{1,0:T(8,128)(2,1)} %bitcast.187, bf16[1024,768]{1,0:T(8,128)(2,1)} %bitcast.190, bf16[1024,384]{1,0:T(8,128)(2,1)} %get-tuple-element.168.refs_0_.refs_3_, ...), custom_call_target="tpu_custom_call" | custom-call | flops 1 | bytes 1 | tf_op jit(solution)/shard_map/pallas_call | solution.py:425
  227.9 7.2 %shard_map.383 = bf16[1024,768]{1,0:T(8,128)(2,1)} custom-call(bf16[1024,384]{1,0:T(8,128)(2,1)} %get-tuple-element.176.refs_0_.refs_2_, bf16[1024,384]{1,0:T(8,128)(2,1)} %get-tuple-element.170.refs_2_.refs_1_, bf16[1024,384]{1,0:T(8,128)(2,1)} %get-tuple-element.177.refs_2_.refs_0_, bf16[1024,384]{1,0:T(8,128)(2,1)} %get-tuple-element.168.refs_0_.refs_3_, ...), custom_call_target="tpu_custom_call" | custom-call | flops 1 | bytes 1 | tf_op jit(solution)/shard_map/pallas_call | solution.py:396
  235.0 6.6 %shard_map.384 = (bf16[384,768]{1,0:T(8,128)(2,1)}, bf16[384,768]{1,0:T(8,128)(2,1)}, f32[384,768]{1,0:T(8,128)}, f32[384,768]{1,0:T(8,128)}) custom-call(bf16[1024,768]{1,0:T(8,128)(2,1)} %bitcast.188, bf16[1024,768]{1,0:T(8,128)(2,1)} %bitcast.191, bf16[1024,384]{1,0:T(8,128)(2,1)} %get-tuple-element.177.refs_2_.refs_0_, ...), custom_call_target="tpu_custom_call" | custom-call | flops 1 | bytes 1 | tf_op jit(solution)/shard_map/pallas_call | solution.py:425
  241.7 1.4 collective-permute-done.13
  243.9 1.7 convert_reduce_fusion.1
  246.9 2.2 collective-permute-start.14
  255.3 20.4 %collective-permute-done.14 = bf16[384,768]{1,0:T(8,128)(2,1)} collective-permute-done((bf16[384,768]{1,0:T(8,128)(2,1)S(1)}, bf16[384,768]{1,0:T(8,128)(2,1)}, u32[]{:S(2)}, u32[]{:S(2)}) %collective-permute-start.14) | collective-permute-done | bytes 589856 | tf_op jit(solution)/shard_map/ppermute | solution.py:633
  275.7 4.0 all-to-all-start.6
  279.7 2.0 collective-permute-start.15
  281.8 1.5 convolution_convert_fusion
  284.2 16.1 %collective-permute-done.15 = bf16[384,768]{1,0:T(8,128)(2,1)} collective-permute-done((bf16[384,768]{1,0:T(8,128)(2,1)}, bf16[384,768]{1,0:T(8,128)(2,1)}, u32[]{:S(2)}, u32[]{:S(2)}) %collective-permute-start.15) | collective-permute-done | bytes 589856 | tf_op jit(solution)/shard_map/ppermute | solution.py:633
  301.1 3.7 all-to-all-start.7
  305.4 2.3 add_convert_fusion
  307.7 2.4 collective-permute-start.18
  310.4 1.7 collective-permute-start.17
  312.1 1.7 collective-permute-start.20
  313.8 10.2 %collective-permute-done.19 = bf16[8,24,768]{2,1,0:T(8,128)(2,1)S(1)} collective-permute-done((bf16[8,24,768]{2,1,0:T(8,128)(2,1)}, bf16[8,24,768]{2,1,0:T(8,128)(2,1)S(1)}, u32[]{:S(2)}, u32[]{:S(2)}) %collective-permute-start.19) | collective-permute-done | bytes 294944 | tf_op jit(solution)/shard_map/ppermute | solution.py:633
  324.7 24.4 %shard_map.385 = (bf16[2048,384]{1,0:T(8,128)(2,1)}, bf16[2048,384]{1,0:T(8,128)(2,1)}) custom-call(s32[2,8]{1,0:T(2,128)} %fusion.74.active_ref, s32[8]{0:T(128)} %iota_xor_fusion.order_ref, bf16[2048,256]{1,0:T(8,128)(2,1)} %get-tuple-element.159.pair_ref, bf16[2048,128]{1,0:T(8,128)(2,1)} %broadcast_in_dim.26.refs_9_.documents_ref, ...), custom_call_target="tpu_custom_call" | custom-call | flops 1 | bytes 1 | tf_op jit(solution)/shard_map/pallas_call | solution.py:309
  349.1 10.5 %all-to-all-start.8 = ((bf16[8,256,384]{2,1,0:T(8,128)(2,1)}), bf16[8,256,384]{2,1,0:T(8,128)(2,1)}, u32[]{:S(2)}, u32[]{:S(2)}) async-start(bf16[8,256,384]{2,1,0:T(8,128)(2,1)} %bitcast.211), calls=%async_computation.8 | async-start | bytes 3145728 | tf_op jit(solution)/shard_map/all_to_all | solution.py:571
  359.6 5.6 %shard_map.386 = bf16[768,384]{1,0:T(8,128)(2,1)} custom-call(bf16[256,768]{1,0:T(8,128)(2,1)} %copy-done.7, bf16[256,768]{1,0:T(8,128)(2,1)} %copy-done.14, bf16[256,768]{1,0:T(8,128)(2,1)} %collective-permute-done.1.refs_2_, bf16[256,768]{1,0:T(8,128)(2,1)} %copy-done.16, bf16[256,768]{1,0:T(8,128)(2,1)} %collective-permute-done.2.refs_4_, ...), custom_call_target="tpu_custom_call" | custom-call | flops 1 | bytes 1 | tf_op jit(solution)/shard_map/pallas_call | solution.py:452
  367.3 1.4 collective-permute-start.24
  368.7 1.3 fusion.8
  370.0 1.9 collective-permute-done.22
  371.9 1.2 collective-permute-done.23
  375.1 3.9 collective-permute-start.29
  379.0 1.5 collective-permute-start.30
  381.8 2.7 collective-permute-start.27
  384.6 17.0 %collective-permute-done.29.refs_5_ = bf16[24,1152]{1,0:T(8,128)(2,1)S(1)} collective-permute-done((bf16[24,1152]{1,0:T(8,128)(2,1)S(1)}, bf16[24,1152]{1,0:T(8,128)(2,1)S(1)}, u32[]{:S(2)}, u32[]{:S(2)}) %collective-permute-start.29) | collective-permute-done | bytes 55328 | tf_op jit(solution)/shard_map/ppermute | solution.py:618
  401.6 1.9 collective-permute-start.31
  403.5 4.1 multiply_reduce_fusion
  409.6 1.9 shard_map.388
  412.2 5.1 %shard_map.387 = (f32[256,768]{1,0:T(8,128)}, f32[1,768]{1,0:T(1,128)}) custom-call(bf16[8,256,384]{2,1,0:T(8,128)(2,1)} %all-to-all-done.8.pieces_ref, bf16[768,2304]{1,0:T(8,128)(2,1)} %all-gather.2.cloned.1.call-done.matrix_ref, bf16[256,768]{1,0:T(8,128)(2,1)} %bitcast.198, f32[1,768]{1,0:T(1,128)} %get-tuple-element.292.gain_ref, f32[256,768]{1,0:T(8,128)} %copy-done.1), custom_call_target="tpu_custom_call" | custom-call | flops 1 | bytes 1 | tf_op jit(solution)/shard_map/pallas_call | solution.py:499
  418.8 3.6 all-to-all-start.9
  423.8 7.9 %all-to-all-done.9 = f32[32,1,1664]{2,1,0:T(1,128)S(1)} async-done(((f32[32,1,1664]{2,1,0:T(1,128)}), f32[32,1,1664]{2,1,0:T(1,128)S(1)}, u32[]{:S(2)}, u32[]{:S(2)}) %all-to-all-start.9) | async-done | bytes 213024 | tf_op jit(solution)/shard_map/all_to_all | solution.py:571
  435.1 9.2 %shard_map.389 = (f32[24,2304]{1,0:T(8,128)}, f32[24,2304]{1,0:T(8,128)}, f32[24,2304]{1,0:T(8,128)}, f32[24,768]{1,0:T(8,128)}, f32[24,768]{1,0:T(8,128)}, /*in...) custom-call(f32[1]{0:T(128)} %bitcast.64.factor_ref, ...), custom_call_target="tpu_custom_call" | custom-call | flops 13271040 | bytes 18579456 | tf_op jit(solution)/shard_map/pallas_call | solution.py:597
  (195 shorter events, 46.1 us)
Async XLA Ops:
  8.1 7.0 %copy-start.17 = (bf16[24,2304]{1,0:T(8,128)(2,1)}, bf16[24,2304]{1,0:T(8,128)(2,1)S(1)}, u32[]{:S(2)}) copy-start(bf16[24,2304]{1,0:T(8,128)(2,1)S(1)} %convert_element_type.123) | copy-start | bytes 331780
  8.3 14.2 %copy-start.5 = (f32[1,384,768]{2,1,0:T(8,128)S(1)}, f32[1,384,768]{2,1,0:T(8,128)}, u32[]{:S(2)}) copy-start(f32[1,384,768]{2,1,0:T(8,128)} %param.29) | copy-start | bytes 3538948
  15.1 9.6 %copy-start.6 = (f32[1,384,768]{2,1,0:T(8,128)S(1)}, f32[1,384,768]{2,1,0:T(8,128)}, u32[]{:S(2)}) copy-start(f32[1,384,768]{2,1,0:T(8,128)} %param.30) | copy-start | bytes 3538948
  15.1 51.4 %all-to-all-start = ((bf16[8,32,1152]{2,1,0:T(8,128)(2,1)}), bf16[8,32,1152]{2,1,0:T(8,128)(2,1)S(1)}, u32[]{:S(2)}, u32[]{:S(2)}) async-start(bf16[8,32,1152]{2,1,0:T(8,128)(2,1)} %fusion.46), calls=%async_computation | async-start | bytes 1179648 | tf_op jit(solution)/shard_map/all_to_all | solution.py:571
  22.6 3.2 copy-start.8
  22.7 2.4 copy-start.36
  22.7 42.3 %collective-permute-start.3 = (bf16[384,768]{1,0:T(8,128)(2,1)S(1)}, bf16[384,768]{1,0:T(8,128)(2,1)S(1)}, u32[]{:S(2)}, u32[]{:S(2)}) collective-permute-start(bf16[384,768]{1,0:T(8,128)(2,1)S(1)} %bitcast_convert_fusion.1.refs_0_), channel_id=1, source_target_pairs={{0,4},{4,0},{8,12},{12,8},{16,20},{20,16},{24,28},{28,24},{1,5},{5... | collective-permute-start | bytes 1769480 | tf_op jit(solution)/shard_map/ppermute | solution.py:618
  24.8 41.7 %collective-permute-start.4 = (bf16[384,768]{1,0:T(8,128)(2,1)S(1)}, bf16[384,768]{1,0:T(8,128)(2,1)}, u32[]{:S(2)}, u32[]{:S(2)}) collective-permute-start(bf16[384,768]{1,0:T(8,128)(2,1)S(1)} %bitcast_convert_fusion.refs_4_), channel_id=1, source_target_pairs={{0,4},{4,0},{8,12},{12,8},{16,20},{20,16},{24,28},{28,24},{1,5},{5... | collective-permute-start | bytes 1769480 | tf_op jit(solution)/shard_map/ppermute | solution.py:618
  25.9 3.5 copy-start.7
  25.9 39.1 %collective-permute-start = (bf16[256,768]{1,0:T(8,128)(2,1)S(1)}, bf16[256,768]{1,0:T(8,128)(2,1)S(1)}, u32[]{:S(2)}, u32[]{:S(2)}) collective-permute-start(bf16[256,768]{1,0:T(8,128)(2,1)S(1)} %fusion.5.refs_0_), channel_id=1, source_target_pairs={{0,4},{4,0},{8,12},{12,8},{16,20},{20,16},{24,28},{28,24},{1,5},{5... | collective-permute-start | bytes 1179656 | tf_op jit(solution)/shard_map/ppermute | solution.py:618
  27.9 37.0 %collective-permute-start.1 = (bf16[256,768]{1,0:T(8,128)(2,1)S(1)}, bf16[256,768]{1,0:T(8,128)(2,1)}, u32[]{:S(2)}, u32[]{:S(2)}) collective-permute-start(bf16[256,768]{1,0:T(8,128)(2,1)S(1)} %fusion.5.refs_0_), channel_id=1, source_target_pairs={{0,8},{4,12},{8,0},{12,4},{16,24},{20,28},{24,16},{28,20},{1,9},{5... | collective-permute-start | bytes 1179656 | tf_op jit(solution)/shard_map/ppermute | solution.py:618
  29.4 35.5 %collective-permute-start.2 = (bf16[256,768]{1,0:T(8,128)(2,1)S(1)}, bf16[256,768]{1,0:T(8,128)(2,1)}, u32[]{:S(2)}, u32[]{:S(2)}) collective-permute-start(bf16[256,768]{1,0:T(8,128)(2,1)S(1)} %fusion.5.refs_0_), channel_id=1, source_target_pairs={{0,16},{4,20},{8,24},{12,28},{16,0},{20,4},{24,8},{28,12},{1,17},{... | collective-permute-start | bytes 1179656 | tf_op jit(solution)/shard_map/ppermute | solution.py:618
  68.0 5.3 %copy-start.37 = (s32[1,256,1]{1,2,0:T(1,128)S(1)}, s32[1,256,1]{1,2,0:T(1,128)}, u32[]{:S(2)}) copy-start(s32[1,256,1]{1,2,0:T(1,128)} %param.26) | copy-start | bytes 3076
  68.0 6.9 %copy-start.9 = (bf16[384,768]{1,0:T(8,128)(2,1)S(1)}, bf16[384,768]{1,0:T(8,128)(2,1)}, u32[]{:S(2)}) copy-start(bf16[384,768]{1,0:T(8,128)(2,1)} %copy-done.8) | copy-start | bytes 1769476
  68.0 37.4 %all-to-all-start.1 = ((bf16[4,8,24,1152]{3,2,1,0:T(8,128)(2,1)}), bf16[4,8,24,1152]{3,2,1,0:T(8,128)(2,1)S(1)}, u32[]{:S(2)}, u32[]{:S(2)}) async-start(bf16[4,8,24,1152]{3,2,1,0:T(8,128)(2,1)} %broadcast_in_dim.24), calls=%async_computation.1 | async-start | bytes 3538944 | tf_op jit(solution)/shard_map/all_to_all | solution.py:571
  71.7 18.6 %collective-permute-start.7 = (bf16[256,768]{1,0:T(8,128)(2,1)}, bf16[256,768]{1,0:T(8,128)(2,1)}, u32[]{:S(2)}, u32[]{:S(2)}) collective-permute-start(bf16[256,768]{1,0:T(8,128)(2,1)} %collective-permute-done.2.refs_4_), channel_id=1, source_target_pairs={{0,8},{4,12},{8,0},{12,4},{16,24},{20,28},{24,16},{28,20},{1,9},{5... | collective-permute-start | bytes 1179656 | tf_op jit(solution)/shard_map/ppermute | solution.py:618
  74.8 29.0 %collective-permute-start.9 = (bf16[384,768]{1,0:T(8,128)(2,1)S(1)}, bf16[384,768]{1,0:T(8,128)(2,1)S(1)}, u32[]{:S(2)}, u32[]{:S(2)}) collective-permute-start(bf16[384,768]{1,0:T(8,128)(2,1)S(1)} %copy-done.9), channel_id=1, source_target_pairs={{16,0},{0,16},{17,1},{1,17},{18,2},{2,18},{19,3},{3,19},{20,4},{4,... | collective-permute-start | bytes 1769480 | tf_op jit(solution)/shard_map/ppermute | solution.py:624
  77.2 20.7 %collective-permute-start.6 = (bf16[256,768]{1,0:T(8,128)(2,1)}, bf16[256,768]{1,0:T(8,128)(2,1)S(1)}, u32[]{:S(2)}, u32[]{:S(2)}) collective-permute-start(bf16[256,768]{1,0:T(8,128)(2,1)} %collective-permute-done.2.refs_4_), channel_id=1, source_target_pairs={{0,4},{4,0},{8,12},{12,8},{16,20},{20,16},{24,28},{28,24},{1,5},{5... | collective-permute-start | bytes 1179656 | tf_op jit(solution)/shard_map/ppermute | solution.py:618
  77.6 20.4 %collective-permute-start.5 = (bf16[256,768]{1,0:T(8,128)(2,1)}, bf16[256,768]{1,0:T(8,128)(2,1)S(1)}, u32[]{:S(2)}, u32[]{:S(2)}) collective-permute-start(bf16[256,768]{1,0:T(8,128)(2,1)} %collective-permute-done.1.refs_2_), channel_id=1, source_target_pairs={{0,4},{4,0},{8,12},{12,8},{16,20},{20,16},{24,28},{28,24},{1,5},{5... | collective-permute-start | bytes 1179656 | tf_op jit(solution)/shard_map/ppermute | solution.py:618
  90.3 15.0 %collective-permute-start.8 = (bf16[256,768]{1,0:T(8,128)(2,1)}, bf16[256,768]{1,0:T(8,128)(2,1)}, u32[]{:S(2)}, u32[]{:S(2)}) collective-permute-start(bf16[256,768]{1,0:T(8,128)(2,1)} %collective-permute-done.7.refs_6_), channel_id=1, source_target_pairs={{0,4},{4,0},{8,12},{12,8},{16,20},{20,16},{24,28},{28,24},{1,5},{5... | collective-permute-start | bytes 1179656 | tf_op jit(solution)/shard_map/ppermute | solution.py:618
  97.9 5.9 %copy-start.16 = (bf16[256,768]{1,0:T(8,128)(2,1)}, bf16[256,768]{1,0:T(8,128)(2,1)S(1)}, u32[]{:S(2)}) copy-start(bf16[256,768]{1,0:T(8,128)(2,1)S(1)} %collective-permute-done.5.refs_3_) | copy-start | bytes 1179652
  97.9 5.9 %copy-start.15 = (bf16[256,768]{1,0:T(8,128)(2,1)}, bf16[256,768]{1,0:T(8,128)(2,1)S(1)}, u32[]{:S(2)}) copy-start(bf16[256,768]{1,0:T(8,128)(2,1)S(1)} %collective-permute-done.6.refs_5_) | copy-start | bytes 1179652
  106.6 36.2 %all-to-all-start.2 = ((bf16[8,128,768]{2,1,0:T(8,128)(2,1)}), bf16[8,128,768]{2,1,0:T(8,128)(2,1)S(1)}, u32[]{:S(2)}, u32[]{:S(2)}) async-start(bf16[8,128,768]{2,1,0:T(8,128)(2,1)} %bitcast.196), calls=%async_computation.2 | async-start | bytes 3145728 | tf_op jit(solution)/shard_map/all_to_all | solution.py:571
  110.2 31.7 %collective-permute-start.10 = (bf16[384,768]{1,0:T(8,128)(2,1)}, bf16[384,768]{1,0:T(8,128)(2,1)}, u32[]{:S(2)}, u32[]{:S(2)}) collective-permute-start(bf16[384,768]{1,0:T(8,128)(2,1)} %copy-done.4), channel_id=1, source_target_pairs={{16,0},{0,16},{17,1},{1,17},{18,2},{2,18},{19,3},{3,19},{20,4},{4,... | collective-permute-start | bytes 1769480 | tf_op jit(solution)/shard_map/ppermute | solution.py:624
  111.2 30.7 %collective-permute-start.11 = (bf16[384,768]{1,0:T(8,128)(2,1)}, bf16[384,768]{1,0:T(8,128)(2,1)}, u32[]{:S(2)}, u32[]{:S(2)}) collective-permute-start(bf16[384,768]{1,0:T(8,128)(2,1)} %copy-done.22), channel_id=1, source_target_pairs={{4,0},{0,4},{5,1},{1,5},{6,2},{2,6},{7,3},{3,7},{12,8},{8,12},{13,... | collective-permute-start | bytes 1769480 | tf_op jit(solution)/shard_map/ppermute | solution.py:624
  142.9 27.4 %copy-start = (bf16[8,128,768]{2,1,0:T(8,128)(2,1)}, bf16[8,128,768]{2,1,0:T(8,128)(2,1)S(1)}, u32[]{:S(2)}) copy-start(bf16[8,128,768]{2,1,0:T(8,128)(2,1)S(1)} %all-to-all-done.2) | copy-start | bytes 4718596
  142.9 25.0 %all-to-all-start.3 = ((bf16[8,256,128]{2,1,0:T(8,128)(2,1)}), bf16[8,256,128]{2,1,0:T(8,128)(2,1)S(1)}, u32[]{:S(2)}, u32[]{:S(2)}) async-start(bf16[8,256,128]{2,1,0:T(8,128)(2,1)} %bitcast.217), calls=%async_computation.3 | async-start | bytes 1048576 | tf_op jit(solution)/shard_map/all_to_all | solution.py:571
  147.4 96.4 %all-gather.2.cloned.1.call-start = ((), (), s32[]{:S(2)}) async-start(), calls=%async_computation.10 | async-start | bytes 3649536 | tf_op jit(solution)/shard_map/all_gather | solution.py:794
  147.5 20.4 %collective-permute-start.12 = (bf16[384,768]{1,0:T(8,128)(2,1)}, bf16[384,768]{1,0:T(8,128)(2,1)}, u32[]{:S(2)}, u32[]{:S(2)}) collective-permute-start(bf16[384,768]{1,0:T(8,128)(2,1)} %collective-permute-done.10.refs_5_), channel_id=1, source_target_pairs={{4,0},{0,4},{5,1},{1,5},{6,2},{2,6},{7,3},{3,7},{12,8},{8,12},{13,... | collective-permute-start | bytes 1769480 | tf_op jit(solution)/shard_map/ppermute | solution.py:624
  216.2 27.7 %all-to-all-start.5 = ((bf16[8,128,768]{2,1,0:T(8,128)(2,1)}), bf16[8,128,768]{2,1,0:T(8,128)(2,1)}, u32[]{:S(2)}, u32[]{:S(2)}) async-start(bf16[8,128,768]{2,1,0:T(8,128)(2,1)} %bitcast.212), calls=%async_computation.5 | async-start | bytes 3145728 | tf_op jit(solution)/shard_map/all_to_all | solution.py:571
  227.2 15.8 %collective-permute-start.13 = (bf16[384,768]{1,0:T(8,128)(2,1)}, bf16[384,768]{1,0:T(8,128)(2,1)S(1)}, u32[]{:S(2)}, u32[]{:S(2)}) collective-permute-start(bf16[384,768]{1,0:T(8,128)(2,1)} %get-tuple-element.172), channel_id=1, source_target_pairs={{0,4},{4,0},{1,5},{5,1},{2,6},{6,2},{3,7},{7,3},{8,12},{12,8},{9,1... | collective-permute-start | bytes 1769480 | tf_op jit(solution)/shard_map/ppermute | solution.py:633
  246.8 2.4 copy-start.13
  246.9 28.8 %collective-permute-start.14 = (bf16[384,768]{1,0:T(8,128)(2,1)S(1)}, bf16[384,768]{1,0:T(8,128)(2,1)}, u32[]{:S(2)}, u32[]{:S(2)}) collective-permute-start(bf16[384,768]{1,0:T(8,128)(2,1)S(1)} %add_convert_fusion.1), channel_id=1, source_target_pairs={{0,16},{16,0},{1,17},{17,1},{2,18},{18,2},{3,19},{19,3},{4,20},{20... | collective-permute-start | bytes 1769480 | tf_op jit(solution)/shard_map/ppermute | solution.py:633
  249.4 32.4 %copy-start.1 = (f32[256,768]{1,0:T(8,128)}, f32[256,768]{1,0:T(8,128)S(1)}, u32[]{:S(2)}) copy-start(f32[256,768]{1,0:T(8,128)S(1)} %multiply_add_fusion.residual_ref) | copy-start | bytes 2359300
  275.7 24.6 %all-to-all-start.6 = ((bf16[8,256,128]{2,1,0:T(8,128)(2,1)}), bf16[8,256,128]{2,1,0:T(8,128)(2,1)S(1)}, u32[]{:S(2)}, u32[]{:S(2)}) async-start(bf16[8,256,128]{2,1,0:T(8,128)(2,1)} %fusion.47), calls=%async_computation.6 | async-start | bytes 1048576 | tf_op jit(solution)/shard_map/all_to_all | solution.py:571
  279.7 20.6 %collective-permute-start.15 = (bf16[384,768]{1,0:T(8,128)(2,1)}, bf16[384,768]{1,0:T(8,128)(2,1)}, u32[]{:S(2)}, u32[]{:S(2)}) collective-permute-start(bf16[384,768]{1,0:T(8,128)(2,1)} %get-tuple-element.189), channel_id=1, source_target_pairs={{0,4},{4,0},{1,5},{5,1},{2,6},{6,2},{3,7},{7,3},{8,12},{12,8},{9,1... | collective-permute-start | bytes 1769480 | tf_op jit(solution)/shard_map/ppermute | solution.py:633
  301.1 48.0 %all-to-all-start.7 = ((bf16[8,128,768]{2,1,0:T(8,128)(2,1)}), bf16[8,128,768]{2,1,0:T(8,128)(2,1)S(1)}, u32[]{:S(2)}, u32[]{:S(2)}) async-start(bf16[8,128,768]{2,1,0:T(8,128)(2,1)} %bitcast.195), calls=%async_computation.7 | async-start | bytes 3145728 | tf_op jit(solution)/shard_map/all_to_all | solution.py:571
  304.8 19.1 %copy-start.25 = (bf16[8,24,768]{2,1,0:T(8,128)(2,1)S(1)}, bf16[8,24,768]{2,1,0:T(8,128)(2,1)}, u32[]{:S(2)}) copy-start(bf16[8,24,768]{2,1,0:T(8,128)(2,1)} %get-tuple-element.201) | copy-start | bytes 884740
  304.9 19.1 %collective-permute-start.19 = (bf16[8,24,768]{2,1,0:T(8,128)(2,1)}, bf16[8,24,768]{2,1,0:T(8,128)(2,1)S(1)}, u32[]{:S(2)}, u32[]{:S(2)}) collective-permute-start(bf16[8,24,768]{2,1,0:T(8,128)(2,1)} %get-tuple-element.199), channel_id=1, source_target_pairs={{0,1},{1,2},{2,3},{3,0},{4,5},{5,6},{6,7},{7,4},{8,9},{9,10},{10,1... | collective-permute-start | bytes 884744 | tf_op jit(solution)/shard_map/ppermute | solution.py:633
  307.7 41.4 %collective-permute-start.18 = (bf16[384,768]{1,0:T(8,128)(2,1)}, bf16[384,768]{1,0:T(8,128)(2,1)}, u32[]{:S(2)}, u32[]{:S(2)}) collective-permute-start(bf16[384,768]{1,0:T(8,128)(2,1)} %add_convert_fusion), channel_id=1, source_target_pairs={{0,16},{16,0},{1,17},{17,1},{2,18},{18,2},{3,19},{19,3},{4,20},{20... | collective-permute-start | bytes 1769480 | tf_op jit(solution)/shard_map/ppermute | solution.py:633
  310.1 39.0 %collective-permute-start.16 = (bf16[384,768]{1,0:T(8,128)(2,1)}, bf16[384,768]{1,0:T(8,128)(2,1)}, u32[]{:S(2)}, u32[]{:S(2)}) collective-permute-start(bf16[384,768]{1,0:T(8,128)(2,1)} %get-tuple-element.195), channel_id=1, source_target_pairs={{0,4},{4,0},{1,5},{5,1},{2,6},{6,2},{3,7},{7,3},{8,12},{12,8},{9,1... | collective-permute-start | bytes 1769480 | tf_op jit(solution)/shard_map/ppermute | solution.py:633
  310.4 38.7 %collective-permute-start.17 = (bf16[384,768]{1,0:T(8,128)(2,1)}, bf16[384,768]{1,0:T(8,128)(2,1)}, u32[]{:S(2)}, u32[]{:S(2)}) collective-permute-start(bf16[384,768]{1,0:T(8,128)(2,1)} %get-tuple-element.196), channel_id=1, source_target_pairs={{0,4},{4,0},{1,5},{5,1},{2,6},{6,2},{3,7},{7,3},{8,12},{12,8},{9,1... | collective-permute-start | bytes 1769480 | tf_op jit(solution)/shard_map/ppermute | solution.py:633
  312.1 37.0 %collective-permute-start.20 = (bf16[8,24,768]{2,1,0:T(8,128)(2,1)}, bf16[8,24,768]{2,1,0:T(8,128)(2,1)}, u32[]{:S(2)}, u32[]{:S(2)}) collective-permute-start(bf16[8,24,768]{2,1,0:T(8,128)(2,1)} %get-tuple-element.200), channel_id=1, source_target_pairs={{0,2},{1,3},{2,0},{3,1},{4,6},{5,7},{6,4},{7,5},{8,10},{9,11},{10,... | collective-permute-start | bytes 884744 | tf_op jit(solution)/shard_map/ppermute | solution.py:633
  324.0 25.1 %collective-permute-start.21 = (bf16[8,24,768]{2,1,0:T(8,128)(2,1)S(1)}, bf16[8,24,768]{2,1,0:T(8,128)(2,1)}, u32[]{:S(2)}, u32[]{:S(2)}) collective-permute-start(bf16[8,24,768]{2,1,0:T(8,128)(2,1)S(1)} %copy-done.25), channel_id=1, source_target_pairs={{0,3},{1,0},{2,1},{3,2},{4,7},{5,4},{6,5},{7,6},{8,11},{9,8},{10,9... | collective-permute-start | bytes 884744 | tf_op jit(solution)/shard_map/ppermute | solution.py:633
  349.1 59.9 %all-to-all-start.8 = ((bf16[8,256,384]{2,1,0:T(8,128)(2,1)}), bf16[8,256,384]{2,1,0:T(8,128)(2,1)}, u32[]{:S(2)}, u32[]{:S(2)}) async-start(bf16[8,256,384]{2,1,0:T(8,128)(2,1)} %bitcast.211), calls=%async_computation.8 | async-start | bytes 3145728 | tf_op jit(solution)/shard_map/all_to_all | solution.py:571
  359.6 9.1 %copy-start.27 = (bf16[8,24,768]{2,1,0:T(8,128)(2,1)S(1)}, bf16[8,24,768]{2,1,0:T(8,128)(2,1)}, u32[]{:S(2)}) copy-start(bf16[8,24,768]{2,1,0:T(8,128)(2,1)} %copy-done.26) | copy-start | bytes 884740
  366.3 5.6 %collective-permute-start.22 = (bf16[8,24,384]{2,1,0:T(8,128)(2,1)S(1)}, bf16[8,24,384]{2,1,0:T(8,128)(2,1)S(1)}, u32[]{:S(2)}, u32[]{:S(2)}) collective-permute-start(bf16[8,24,384]{2,1,0:T(8,128)(2,1)S(1)} %get-tuple-element.257), channel_id=1, source_target_pairs={{0,1},{1,2},{2,3},{3,0},{4,5},{5,6},{6,7},{7,4},{8,9},{9,10},{10,1... | collective-permute-start | bytes 442376 | tf_op jit(solution)/shard_map/ppermute | solution.py:633
  366.4 6.7 %collective-permute-start.23 = (bf16[8,24,384]{2,1,0:T(8,128)(2,1)S(1)}, bf16[8,24,384]{2,1,0:T(8,128)(2,1)S(1)}, u32[]{:S(2)}, u32[]{:S(2)}) collective-permute-start(bf16[8,24,384]{2,1,0:T(8,128)(2,1)S(1)} %get-tuple-element.259), channel_id=1, source_target_pairs={{0,2},{1,3},{2,0},{3,1},{4,6},{5,7},{6,4},{7,5},{8,10},{9,11},{10,... | collective-permute-start | bytes 442376 | tf_op jit(solution)/shard_map/ppermute | solution.py:633
  367.3 6.7 %collective-permute-start.24 = (bf16[8,24,384]{2,1,0:T(8,128)(2,1)S(1)}, bf16[8,24,384]{2,1,0:T(8,128)(2,1)S(1)}, u32[]{:S(2)}, u32[]{:S(2)}) collective-permute-start(bf16[8,24,384]{2,1,0:T(8,128)(2,1)S(1)} %get-tuple-element.258), channel_id=1, source_target_pairs={{0,3},{1,0},{2,1},{3,2},{4,7},{5,4},{6,5},{7,6},{8,11},{9,8},{10,9... | collective-permute-start | bytes 442376 | tf_op jit(solution)/shard_map/ppermute | solution.py:633
  368.7 34.8 %copy-start.20 = (f32[384,768]{1,0:T(8,128)S(1)}, f32[384,768]{1,0:T(8,128)}, u32[]{:S(2)}) copy-start(f32[384,768]{1,0:T(8,128)} %get-tuple-element.221) | copy-start | bytes 3538948
  370.0 33.5 %copy-start.19 = (f32[384,768]{1,0:T(8,128)S(1)}, f32[384,768]{1,0:T(8,128)}, u32[]{:S(2)}) copy-start(f32[384,768]{1,0:T(8,128)} %get-tuple-element.224) | copy-start | bytes 3538948
  375.1 26.5 %collective-permute-start.29 = (bf16[24,1152]{1,0:T(8,128)(2,1)S(1)}, bf16[24,1152]{1,0:T(8,128)(2,1)S(1)}, u32[]{:S(2)}, u32[]{:S(2)}) collective-permute-start(bf16[24,1152]{1,0:T(8,128)(2,1)S(1)} %get-tuple-element.267), channel_id=1, source_target_pairs={{0,20},{4,16},{8,28},{12,24},{16,4},{20,0},{24,12},{28,8},{1,21},{... | collective-permute-start | bytes 165896 | tf_op jit(solution)/shard_map/ppermute | solution.py:618
  379.0 22.6 %collective-permute-start.30 = (bf16[24,1152]{1,0:T(8,128)(2,1)S(1)}, bf16[24,1152]{1,0:T(8,128)(2,1)S(1)}, u32[]{:S(2)}, u32[]{:S(2)}) collective-permute-start(bf16[24,1152]{1,0:T(8,128)(2,1)S(1)} %get-tuple-element.266), channel_id=1, source_target_pairs={{0,24},{4,28},{8,16},{12,20},{16,8},{20,12},{24,0},{28,4},{1,25},{... | collective-permute-start | bytes 165896 | tf_op jit(solution)/shard_map/ppermute | solution.py:618
  381.1 27.9 %collective-permute-start.25 = (bf16[24,1152]{1,0:T(8,128)(2,1)S(1)}, bf16[24,1152]{1,0:T(8,128)(2,1)S(1)}, u32[]{:S(2)}, u32[]{:S(2)}) collective-permute-start(bf16[24,1152]{1,0:T(8,128)(2,1)S(1)} %get-tuple-element.262), channel_id=1, source_target_pairs={{0,4},{4,0},{8,12},{12,8},{16,20},{20,16},{24,28},{28,24},{1,5},{5... | collective-permute-start | bytes 165896 | tf_op jit(solution)/shard_map/ppermute | solution.py:618
  381.8 27.1 %collective-permute-start.26 = (bf16[24,1152]{1,0:T(8,128)(2,1)S(1)}, bf16[24,1152]{1,0:T(8,128)(2,1)S(1)}, u32[]{:S(2)}, u32[]{:S(2)}) collective-permute-start(bf16[24,1152]{1,0:T(8,128)(2,1)S(1)} %get-tuple-element.263), channel_id=1, source_target_pairs={{0,8},{4,12},{8,0},{12,4},{16,24},{20,28},{24,16},{28,20},{1,9},{5... | collective-permute-start | bytes 165896 | tf_op jit(solution)/shard_map/ppermute | solution.py:618
  381.8 27.1 %collective-permute-start.27 = (bf16[24,1152]{1,0:T(8,128)(2,1)S(1)}, bf16[24,1152]{1,0:T(8,128)(2,1)S(1)}, u32[]{:S(2)}, u32[]{:S(2)}) collective-permute-start(bf16[24,1152]{1,0:T(8,128)(2,1)S(1)} %get-tuple-element.264), channel_id=1, source_target_pairs={{0,12},{4,8},{8,4},{12,0},{16,28},{20,24},{24,20},{28,16},{1,13},{... | collective-permute-start | bytes 165896 | tf_op jit(solution)/shard_map/ppermute | solution.py:618
  401.6 6.1 %copy-start.28 = (bf16[24,1152]{1,0:T(8,128)(2,1)}, bf16[24,1152]{1,0:T(8,128)(2,1)S(1)}, u32[]{:S(2)}) copy-start(bf16[24,1152]{1,0:T(8,128)(2,1)S(1)} %collective-permute-done.29.refs_5_) | copy-start | bytes 165892
  401.6 7.4 %collective-permute-start.28 = (bf16[24,1152]{1,0:T(8,128)(2,1)S(1)}, bf16[24,1152]{1,0:T(8,128)(2,1)S(1)}, u32[]{:S(2)}, u32[]{:S(2)}) collective-permute-start(bf16[24,1152]{1,0:T(8,128)(2,1)S(1)} %get-tuple-element.265), channel_id=1, source_target_pairs={{0,16},{4,20},{8,24},{12,28},{16,0},{20,4},{24,8},{28,12},{1,17},{... | collective-permute-start | bytes 165896 | tf_op jit(solution)/shard_map/ppermute | solution.py:618
  401.6 6.0 %copy-start.29 = (bf16[24,1152]{1,0:T(8,128)(2,1)}, bf16[24,1152]{1,0:T(8,128)(2,1)S(1)}, u32[]{:S(2)}) copy-start(bf16[24,1152]{1,0:T(8,128)(2,1)S(1)} %collective-permute-done.30.refs_6_) | copy-start | bytes 165892
  401.6 7.4 %collective-permute-start.31 = (bf16[24,1152]{1,0:T(8,128)(2,1)S(1)}, bf16[24,1152]{1,0:T(8,128)(2,1)S(1)}, u32[]{:S(2)}, u32[]{:S(2)}) collective-permute-start(bf16[24,1152]{1,0:T(8,128)(2,1)S(1)} %get-tuple-element.260), channel_id=1, source_target_pairs={{0,28},{4,24},{8,20},{12,16},{16,12},{20,8},{24,4},{28,0},{1,29},{... | collective-permute-start | bytes 165896 | tf_op jit(solution)/shard_map/ppermute | solution.py:618
  418.8 13.0 %all-to-all-start.9 = ((f32[32,1,1664]{2,1,0:T(1,128)}), f32[32,1,1664]{2,1,0:T(1,128)S(1)}, u32[]{:S(2)}, u32[]{:S(2)}) async-start(f32[32,1,1664]{2,1,0:T(1,128)} %broadcast_in_dim.60), calls=%async_computation.9 | async-start | bytes 425984 | tf_op jit(solution)/shard_map/all_to_all | solution.py:571
  422.6 11.8 %copy-start.38 = (f32[2,768]{1,0:T(2,128)S(1)}, f32[2,768]{1,0:T(2,128)}, u32[]{:S(2)}) copy-start(f32[2,768]{1,0:T(2,128)} %param.41) | copy-start | bytes 18436
  422.6 11.8 %copy-start.39 = (f32[2,768]{1,0:T(2,128)S(1)}, f32[2,768]{1,0:T(2,128)}, u32[]{:S(2)}) copy-start(f32[2,768]{1,0:T(2,128)} %param.40) | copy-start | bytes 18436
  433.0 11.3 %copy-start.35 = (f32[2,768]{1,0:T(2,128)}, f32[2,768]{1,0:T(2,128)S(1)}, u32[]{:S(2)}) copy-start(f32[2,768]{1,0:T(2,128)S(1)} %reshape.254) | copy-start | bytes 18436
  (19 other events, 19.3 us)
Sparse Core Ops, SparseCore 0:
  168.8 61.5 all-gather.1
where the time goes:
time: 454 us; the launch traced here: 452 us
  waiting for transfers between devices  153 us (34%)
  Pallas kernels  105 us (23%)
  starting transfers between devices  88.2 us (19%)
  local copies, waits for them, and re-layouts  27.6 us (6%)
  blocking collectives  27.6 us (6%)
  other arithmetic  24.5 us (5%)
  between operations  18.5 us (4%)
  matrix products  6.98 us (2%)
    ppermute x16, waiting for transfers between devices, flip(): lax.ppermute(value, SEQ, [(index, index ^ bits) for index in range(count)])  67.3 us
    ppermute x12, waiting for transfers between devices, to_owners(): lax.ppermute(block, axis, [(i, (i + step) % size) for i in range(size)])  52.1 us
    all_to_all x9, starting transfers between devices, swap(): return lax.all_to_all(value, axes, split_axis=0, concat_axis=0, tiled=True)  45.4 us
    all_to_all x1, blocking collectives, swap(): return lax.all_to_all(value, axes, split_axis=0, concat_axis=0, tiled=True)  27.6 us
    pallas_call x1, Pallas kernels, attend_back(): pl.pallas_call(functools.partial(attend_back_kernel, block=block, chunk=2...  24.4 us
    ppermute x4, waiting for transfers between devices, others(): lax.ppermute(value, axis, [((i + step) % size, i) for i in range(size)])  24.3 us
    pallas_call x1, Pallas kernels, attend(): pl.pallas_call(functools.partial(attend_kernel, block=block, chunk=2 * bl...  23.1 us
    ppermute x16, starting transfers between devices, flip(): lax.ppermute(value, SEQ, [(index, index ^ bits) for index in range(count)])  23 us
  transfers between devices with their start and end apart: 42, of which 17 were waited for; matrix products, arithmetic and copies ran while one was open for 8% of the time, Pallas kernels for 20%

commit v1 on v0

--- a/solution.py
+++ b/solution.py
@@ -734,9 +734,8 @@
     if pairwise:
         order = jnp.arange(count, dtype=jnp.int32) ^ position
         beside, below, across = flip(attend_in, 1), flip(attend_in, 2), flip(attend_in, 4)
-        side_up, side_down = flip(own_up, 1), flip(own_down, 1)
-        got_rows, beside, below, across, side_up, side_down, own_up = together(
-            swap(pieces, SEQ), beside, below, across, side_up, side_down, own_up
+        got_rows, beside, below, across, own_up = together(
+            swap(pieces, SEQ), beside, below, across, own_up
         )
         corner = flip(across, 2)
         row_blocks = [attend_in, beside]
@@ -745,7 +744,6 @@
         order = jnp.arange(count, dtype=jnp.int32)
         row_blocks = [lax.all_gather(attend_in, SEQ, axis=0, tiled=True)]
         got_rows = swap(pieces, SEQ)
-        side_up, side_down = others(own_up, "in"), others(own_down, "in")
     documents = jnp.broadcast_to(
         got_rows[:, weight_rows, :row_count].reshape(length, 1), (length, LANES)
     )
@@ -763,6 +761,7 @@
     output_full = all_copies[..., 3 * LANES :].reshape(width, width)
     grad_arrived = dispatch(grad_slots_out)
     peer_down = others(own_down, "hi")
+    side_up = others(own_up, "in")
     far_up = others(peer_up, "in")
 
     mixed_low, mixed_full, stat, pair = attend(
@@ -784,12 +783,13 @@
     def to_tokens(values):
         return swap(values.reshape(count, row_count, values.shape[1]), SEQ)
 
-    mixed_low, grad_arrived, peer_down, far_up = together(
-        mixed_low, grad_arrived, peer_down, far_up
-    )
+    mixed_low, grad_arrived, peer_down, side_up, far_up, own_down = together(
+        mixed_low, grad_arrived, peer_down, side_up, far_up, own_down
+    )
+    side_down = others(own_down, "in")
     far_down = others(peer_down, "in")
-    mixed_pieces, projection_low, far_down = together(
-        to_tokens(mixed_low), projection_low, far_down
+    mixed_pieces, projection_low, far_down, side_down = together(
+        to_tokens(mixed_low), projection_low, far_down, side_down
     )
     projection_full = lax.all_gather(projection_low, ALL, axis=0, tiled=True)
     attend_out = jnp.einsum(
@@ -842,7 +842,6 @@
     ).astype(BF16)
 
     sent_grad = jnp.stack([grad_mixed[:, s : s + LANES] for s in starts])
-    sent_grad, *down_hi = together(sent_grad, *down_hi)
     row_grad = swap(sent_grad, SEQ).reshape(length, LANES)
 
     group = lax.axis_index(EXP)
@@ -862,17 +861,16 @@
     )
     output_away = to_owners(output_away, "exp")
     (down_early,) = to_owners([down_side], "in")
-    (up_early,) = to_owners([up_side], "in")
     up_hi = hi_parts(add_all(up_peer, [up_part]))
     returned = send_back(produced)
     grad_qkv, grad_lying = attend_back(
         active, order, pair, documents, stat, row_grad, mixed_full, row_count, scaling
     )
-    grad_qkv, grad_lying, returned, down_early, up_early, *held = together(
-        grad_qkv, grad_lying, returned, down_early, up_early, *up_hi, *output_away
-    )
-    up_hi, output_away = held[: len(up_hi)], held[len(up_hi) :]
-    up_grad = add_all(up_own, [up_early, *up_hi])[None]
+    grad_qkv, grad_lying, returned, down_early, up_side, *held = together(
+        grad_qkv, grad_lying, returned, down_early, up_side, *down_hi, *output_away
+    )
+    down_hi, output_away = held[: len(down_hi)], held[len(down_hi) :]
+    (up_early,) = to_owners([up_side], "in")
     down_grad = add_all(down_own, [down_early, *down_hi])[None]
     block_output = (middle + collect(returned)).astype(BF16)[None]
 
@@ -894,6 +892,8 @@
     else:
         grad_pieces, dense_rows = together(to_tokens(grad_qkv), dense_rows)
         lying_terms = list(swap(dense_rows, SEQ))
+    grad_pieces, up_early, *up_hi = together(grad_pieces, up_early, *up_hi)
+    up_grad = add_all(up_own, [up_early, *up_hi])[None]
     projection_grad, output_grad, dense_square = dense_grads(order, lying_terms, starts)
     input_grad, gain_first_part = close_norm(
         grad_pieces, starts, projection_full, tokens[0], gain_first[None], residual_grad

time: 454 us -> 450 us (level)
  other arithmetic: 24.5 us -> 30.5 us
  starting transfers between devices: 88.2 us -> 82.9 us
  waiting for transfers between devices: 153 us -> 148 us
    ppermute x12, waiting for transfers between devices: 52.1 us -> 19.7 us  [to_owners(): lax.ppermute(block, axis, [(i, (i + step) % size) for i in range(size)])]
    ppermute x16 -> x14, waiting for transfers between devices: 67.3 us -> 82.1 us  [flip(): lax.ppermute(value, SEQ, [(index, index ^ bits) for index in range(count)])]
    ppermute x4 -> x6, waiting for transfers between devices: 24.3 us -> 37.6 us  [others(): lax.ppermute(value, axis, [((i + step) % size, i) for i in range(size)])]
    all_to_all x9, starting transfers between devices: 45.4 us -> 40.4 us  [swap(): return lax.all_to_all(value, axes, split_axis=0, concat_axis=0, tiled=True)]
    ppermute x16 -> x14, starting transfers between devices: 23 us -> 19.3 us  [flip(): lax.ppermute(value, SEQ, [(index, index ^ bits) for index in range(count)])]
    unnamed x90 -> x84, local copies, waits for them, and re-layouts: 11.8 us -> 10.6 us
  transfers between devices with their start and end apart: 42 -> 42, of which waited for: 17 -> 17; matrix products, arithmetic and copies ran while one was open for 8% -> 7% of each run, Pallas kernels for 20% -> 20%
where the time goes in v1:
time: 450 us; the launch traced here: 448 us
  waiting for transfers between devices  148 us (33%)
  Pallas kernels  106 us (24%)
  starting transfers between devices  82.9 us (18%)
  other arithmetic  30.5 us (7%)
  local copies, waits for them, and re-layouts  27.6 us (6%)
  blocking collectives  27.6 us (6%)
  between operations  18.5 us (4%)
  matrix products  6.88 us (2%)
    ppermute x14, waiting for transfers between devices, flip(): lax.ppermute(value, SEQ, [(index, index ^ bits) for index in range(count)])  82.1 us
    all_to_all x9, starting transfers between devices, swap(): return lax.all_to_all(value, axes, split_axis=0, concat_axis=0, tiled=True)  40.4 us
    ppermute x6, waiting for transfers between devices, others(): lax.ppermute(value, axis, [((i + step) % size, i) for i in range(size)])  37.6 us
    all_to_all x1, blocking collectives, swap(): return lax.all_to_all(value, axes, split_axis=0, concat_axis=0, tiled=True)  27.6 us
    pallas_call x1, Pallas kernels, attend_back(): pl.pallas_call(functools.partial(attend_back_kernel, block=block, chunk=2...  24.4 us
    pallas_call x1, Pallas kernels, attend(): pl.pallas_call(functools.partial(attend_kernel, block=block, chunk=2 * bl...  23.3 us
    ppermute x12, waiting for transfers between devices, to_owners(): lax.ppermute(block, axis, [(i, (i + step) % size) for i in range(size)])  19.7 us
    ppermute x14, starting transfers between devices, flip(): lax.ppermute(value, SEQ, [(index, index ^ bits) for index in range(count)])  19.3 us
  transfers between devices with their start and end apart: 42, of which 17 were waited for; matrix products, arithmetic and copies ran while one was open for 7% of the time, Pallas kernels for 20%

profile of v1, /device:TPU:0, one launch (start us, length us, event | category | flops | bytes accessed | tf_op | source)
XLA Modules:
  0.0 447.7 jit_solution(16386648024644682308)
XLA Ops:
  15.1 7.4 %all-to-all-start = ((bf16[8,32,1152]{2,1,0:T(8,128)(2,1)}), bf16[8,32,1152]{2,1,0:T(8,128)(2,1)S(1)}, u32[]{:S(2)}, u32[]{:S(2)}) async-start(bf16[8,32,1152]{2,1,0:T(8,128)(2,1)} %fusion.46), calls=%async_computation | async-start | bytes 1179648 | tf_op jit(solution)/shard_map/all_to_all | solution.py:571
  23.5 2.1 collective-permute-start
  25.5 1.5 collective-permute-start.1
  27.0 2.4 collective-permute-start.2
  30.2 9.4 %collective-permute-done.refs_1_ = bf16[256,768]{1,0:T(8,128)(2,1)S(1)} collective-permute-done((bf16[256,768]{1,0:T(8,128)(2,1)S(1)}, bf16[256,768]{1,0:T(8,128)(2,1)S(1)}, u32[]{:S(2)}, u32[]{:S(2)}) %collective-permute-start) | collective-permute-done | bytes 393248 | tf_op jit(solution)/shard_map/ppermute | solution.py:618
  39.6 9.5 %collective-permute-done.1.refs_2_ = bf16[256,768]{1,0:T(8,128)(2,1)S(1)} collective-permute-done((bf16[256,768]{1,0:T(8,128)(2,1)S(1)}, bf16[256,768]{1,0:T(8,128)(2,1)S(1)}, u32[]{:S(2)}, u32[]{:S(2)}) %collective-permute-start.1) | collective-permute-done | bytes 393248 | tf_op jit(solution)/shard_map/ppermute | solution.py:618
  49.8 5.5 %collective-permute-done.2.refs_4_ = bf16[256,768]{1,0:T(8,128)(2,1)} collective-permute-done((bf16[256,768]{1,0:T(8,128)(2,1)S(1)}, bf16[256,768]{1,0:T(8,128)(2,1)}, u32[]{:S(2)}, u32[]{:S(2)}) %collective-permute-start.2) | collective-permute-done | bytes 393248 | tf_op jit(solution)/shard_map/ppermute | solution.py:618
  55.4 1.4 broadcast_in_dim.24
  56.8 3.7 all-to-all-start.1
  62.2 1.9 collective-permute-start.7
  64.1 1.7 collective-permute-start.4
  66.1 14.6 %collective-permute-done.5.refs_6_ = bf16[256,768]{1,0:T(8,128)(2,1)S(1)} collective-permute-done((bf16[256,768]{1,0:T(8,128)(2,1)}, bf16[256,768]{1,0:T(8,128)(2,1)S(1)}, u32[]{:S(2)}, u32[]{:S(2)}) %collective-permute-start.5) | collective-permute-done | bytes 393248 | tf_op jit(solution)/shard_map/ppermute | solution.py:618
  80.7 1.7 collective-permute-start.6
  82.5 1.4 convolution_convert_fusion.2
  84.8 7.0 %collective-permute-done.7.refs_1_ = bf16[384,768]{1,0:T(8,128)(2,1)S(1)} collective-permute-done((bf16[384,768]{1,0:T(8,128)(2,1)}, bf16[384,768]{1,0:T(8,128)(2,1)S(1)}, u32[]{:S(2)}, u32[]{:S(2)}) %collective-permute-start.7) | collective-permute-done | bytes 589856 | tf_op jit(solution)/shard_map/ppermute | solution.py:624
  92.6 2.4 broadcast_in_dim.55
  95.0 3.6 all-to-all-start.2
  98.6 1.5 collective-permute-start.10
  100.1 1.5 collective-permute-start.8
  104.7 1.4 copy.80
  106.1 1.9 slice.211
  109.1 23.3 %shard_map.380 = (bf16[2048,128]{1,0:T(8,128)(2,1)}, f32[2048,128]{1,0:T(8,128)}, bf16[2048,256]{1,0:T(8,128)(2,1)}, bf16[2048,256]{1,0:T(8,128)(2,1)}) custom-call(s32[2,8]{1,0:T(2,128)} %fusion.74.active_ref, s32[8]{0:T(128)} %iota_xor_fusion.order_ref, bf16[256,768]{1,0:T(8,128)(2,1)} %copy-done.7, bf16[256,768]{1,0:T(8,128)(2,1)} %copy-done.13, ...), custom_call_target="tpu_custom_call" | custom-call | flops 1 | bytes 1 | tf_op jit(solution)/shard_map/pallas_call | solution.py:278
  132.5 5.0 %all-to-all-start.3 = ((bf16[8,256,128]{2,1,0:T(8,128)(2,1)}), bf16[8,256,128]{2,1,0:T(8,128)(2,1)S(1)}, u32[]{:S(2)}, u32[]{:S(2)}) async-start(bf16[8,256,128]{2,1,0:T(8,128)(2,1)} %bitcast.217), calls=%async_computation.3 | async-start | bytes 1048576 | tf_op jit(solution)/shard_map/all_to_all | solution.py:571
  137.5 2.0 collective-permute-start.11
  139.6 19.8 %collective-permute-done.11.refs_7_ = bf16[384,768]{1,0:T(8,128)(2,1)} collective-permute-done((bf16[384,768]{1,0:T(8,128)(2,1)}, bf16[384,768]{1,0:T(8,128)(2,1)}, u32[]{:S(2)}, u32[]{:S(2)}) %collective-permute-start.11) | collective-permute-done | bytes 589856 | tf_op jit(solution)/shard_map/ppermute | solution.py:624
  159.4 10.9 %collective-permute-done.12.refs_6_ = bf16[384,768]{1,0:T(8,128)(2,1)} collective-permute-done((bf16[384,768]{1,0:T(8,128)(2,1)S(1)}, bf16[384,768]{1,0:T(8,128)(2,1)}, u32[]{:S(2)}, u32[]{:S(2)}) %collective-permute-start.12) | collective-permute-done | bytes 589856 | tf_op jit(solution)/shard_map/ppermute | solution.py:624
  171.1 1.5 slice.212
  175.3 27.6 %all_to_all.50 = bf16[8,128,768]{2,1,0:T(8,128)(2,1)} all-to-all(bf16[8,128,768]{2,1,0:T(8,128)(2,1)S(1)} %bitcast.197), channel_id=1, replica_groups=mesh['hi'=2,'lo'=2,'in'=2,'exp'=4] {'lo','exp'}, dimensions={0} | all-to-all | bytes 3145728 | tf_op jit(solution)/shard_map/all_to_all | solution.py:571
  202.9 15.6 %shard_map.381 = (bf16[1024,768]{1,0:T(8,128)(2,1)}, bf16[1024,384]{1,0:T(8,128)(2,1)}, bf16[1024,384]{1,0:T(8,128)(2,1)}, bf16[1024,384]{1,0:T(8,128)(2,1)}, bf...) custom-call(bf16[1024,768]{1,0:T(8,128)(2,1)} %bitcast.189, ...), custom_call_target="tpu_custom_call" | custom-call | flops 1 | bytes 1 | tf_op jit(solution)/shard_map/pallas_call | solution.py:372
  218.5 4.3 all-to-all-start.5
  222.8 6.7 %shard_map.382 = (bf16[384,768]{1,0:T(8,128)(2,1)}, bf16[384,768]{1,0:T(8,128)(2,1)}, f32[384,768]{1,0:T(8,128)}, f32[384,768]{1,0:T(8,128)}) custom-call(bf16[1024,768]{1,0:T(8,128)(2,1)} %bitcast.187, bf16[1024,768]{1,0:T(8,128)(2,1)} %bitcast.190, bf16[1024,384]{1,0:T(8,128)(2,1)} %get-tuple-element.171.refs_0_.refs_3_, ...), custom_call_target="tpu_custom_call" | custom-call | flops 1 | bytes 1 | tf_op jit(solution)/shard_map/pallas_call | solution.py:425
  230.2 7.2 %shard_map.383 = bf16[1024,768]{1,0:T(8,128)(2,1)} custom-call(bf16[1024,384]{1,0:T(8,128)(2,1)} %get-tuple-element.179.refs_0_.refs_2_, bf16[1024,384]{1,0:T(8,128)(2,1)} %get-tuple-element.173.refs_2_.refs_1_, bf16[1024,384]{1,0:T(8,128)(2,1)} %get-tuple-element.180.refs_2_.refs_0_, bf16[1024,384]{1,0:T(8,128)(2,1)} %get-tuple-element.171.refs_0_.refs_3_, ...), custom_call_target="tpu_custom_call" | custom-call | flops 1 | bytes 1 | tf_op jit(solution)/shard_map/pallas_call | solution.py:396
  237.4 6.6 %shard_map.384 = (bf16[384,768]{1,0:T(8,128)(2,1)}, bf16[384,768]{1,0:T(8,128)(2,1)}, f32[384,768]{1,0:T(8,128)}, f32[384,768]{1,0:T(8,128)}) custom-call(bf16[1024,768]{1,0:T(8,128)(2,1)} %bitcast.188, bf16[1024,768]{1,0:T(8,128)(2,1)} %bitcast.191, bf16[1024,384]{1,0:T(8,128)(2,1)} %get-tuple-element.180.refs_2_.refs_0_, ...), custom_call_target="tpu_custom_call" | custom-call | flops 1 | bytes 1 | tf_op jit(solution)/shard_map/pallas_call | solution.py:425
  244.1 1.3 collective-permute-done.13
  246.2 1.7 convert_reduce_fusion.1
  255.0 5.2 %all-to-all-start.6 = ((bf16[8,256,128]{2,1,0:T(8,128)(2,1)}), bf16[8,256,128]{2,1,0:T(8,128)(2,1)S(1)}, u32[]{:S(2)}, u32[]{:S(2)}) async-start(bf16[8,256,128]{2,1,0:T(8,128)(2,1)} %fusion.47), calls=%async_computation.6 | async-start | bytes 1048576 | tf_op jit(solution)/shard_map/all_to_all | solution.py:571
  260.2 2.0 collective-permute-start.14
  262.2 1.5 convolution_convert_fusion
  264.7 15.8 %collective-permute-done.14 = bf16[384,768]{1,0:T(8,128)(2,1)} collective-permute-done((bf16[384,768]{1,0:T(8,128)(2,1)}, bf16[384,768]{1,0:T(8,128)(2,1)}, u32[]{:S(2)}, u32[]{:S(2)}) %collective-permute-start.14) | collective-permute-done | bytes 589856 | tf_op jit(solution)/shard_map/ppermute | solution.py:633
  281.4 3.6 all-to-all-start.7
  285.0 2.4 add_convert_fusion.1
  287.4 2.4 collective-permute-start.16
  290.3 1.9 collective-permute-start.18
  292.2 1.4 collective-permute-start.19
  293.7 24.4 %shard_map.385 = (bf16[2048,384]{1,0:T(8,128)(2,1)}, bf16[2048,384]{1,0:T(8,128)(2,1)}) custom-call(s32[2,8]{1,0:T(2,128)} %fusion.74.active_ref, s32[8]{0:T(128)} %iota_xor_fusion.order_ref, bf16[2048,256]{1,0:T(8,128)(2,1)} %get-tuple-element.163.pair_ref, bf16[2048,128]{1,0:T(8,128)(2,1)} %broadcast_in_dim.26.refs_9_.documents_ref, ...), custom_call_target="tpu_custom_call" | custom-call | flops 1 | bytes 1 | tf_op jit(solution)/shard_map/pallas_call | solution.py:309
  318.1 4.5 %all-to-all-start.8 = ((bf16[8,256,384]{2,1,0:T(8,128)(2,1)}), bf16[8,256,384]{2,1,0:T(8,128)(2,1)}, u32[]{:S(2)}, u32[]{:S(2)}) async-start(bf16[8,256,384]{2,1,0:T(8,128)(2,1)} %bitcast.211), calls=%async_computation.8 | async-start | bytes 3145728 | tf_op jit(solution)/shard_map/all_to_all | solution.py:571
  322.7 2.3 add_convert_fusion
  325.1 2.5 collective-permute-start.31
  327.6 5.5 %shard_map.386 = bf16[768,384]{1,0:T(8,128)(2,1)} custom-call(bf16[256,768]{1,0:T(8,128)(2,1)} %copy-done.7, bf16[256,768]{1,0:T(8,128)(2,1)} %copy-done.13, bf16[256,768]{1,0:T(8,128)(2,1)} %copy-done.14, bf16[256,768]{1,0:T(8,128)(2,1)} %copy-done.17, bf16[256,768]{1,0:T(8,128)(2,1)} %collective-permute-done.2.refs_4_, bf16[256,768]{1,0:T(8,128)(2,1)} %copy-done.16, ...), custom_call_target="tpu_custom_call" | custom-call | flops 1 | bytes 1 | tf_op jit(solution)/shard_map/pallas_call | solution.py:452
  335.5 1.4 collective-permute-start.22
  336.9 1.5 collective-permute-start.30
  343.3 1.5 collective-permute-start.27
  344.8 3.3 collective-permute-start.28
  349.3 40.6 %collective-permute-done.27.refs_5_ = bf16[24,1152]{1,0:T(8,128)(2,1)S(1)} collective-permute-done((bf16[24,1152]{1,0:T(8,128)(2,1)S(1)}, bf16[24,1152]{1,0:T(8,128)(2,1)S(1)}, u32[]{:S(2)}, u32[]{:S(2)}) %collective-permute-start.27) | collective-permute-done | bytes 55328 | tf_op jit(solution)/shard_map/ppermute | solution.py:618
  389.9 2.0 collective-permute-start.25
  392.3 1.8 collective-permute-done.24.refs_2_
  394.2 1.8 collective-permute-start.29
  396.0 3.2 multiply_reduce_fusion
  401.2 3.1 multiply_reduce_fusion.1
  405.6 1.9 shard_map.388
  408.1 5.1 %shard_map.387 = (f32[256,768]{1,0:T(8,128)}, f32[1,768]{1,0:T(1,128)}) custom-call(bf16[8,256,384]{2,1,0:T(8,128)(2,1)} %all-to-all-done.8.pieces_ref, bf16[768,2304]{1,0:T(8,128)(2,1)} %all-gather.2.cloned.1.call-done.matrix_ref, bf16[256,768]{1,0:T(8,128)(2,1)} %bitcast.198, f32[1,768]{1,0:T(1,128)} %get-tuple-element.296.gain_ref, f32[256,768]{1,0:T(8,128)} %copy-done.1), custom_call_target="tpu_custom_call" | custom-call | flops 1 | bytes 1 | tf_op jit(solution)/shard_map/pallas_call | solution.py:499
  414.7 3.0 all-to-all-start.9
  419.2 7.9 %all-to-all-done.9 = f32[32,1,1664]{2,1,0:T(1,128)S(1)} async-done(((f32[32,1,1664]{2,1,0:T(1,128)}), f32[32,1,1664]{2,1,0:T(1,128)S(1)}, u32[]{:S(2)}, u32[]{:S(2)}) %all-to-all-start.9) | async-done | bytes 213024 | tf_op jit(solution)/shard_map/all_to_all | solution.py:571
  430.4 9.2 %shard_map.389 = (f32[24,2304]{1,0:T(8,128)}, f32[24,2304]{1,0:T(8,128)}, f32[24,2304]{1,0:T(8,128)}, f32[24,768]{1,0:T(8,128)}, f32[24,768]{1,0:T(8,128)}, /*in...) custom-call(f32[1]{0:T(128)} %bitcast.64.factor_ref, ...), custom_call_target="tpu_custom_call" | custom-call | flops 13271040 | bytes 18579456 | tf_op jit(solution)/shard_map/pallas_call | solution.py:597
  (190 shorter events, 49.3 us)
Async XLA Ops:
  8.1 7.0 %copy-start.18 = (bf16[24,2304]{1,0:T(8,128)(2,1)}, bf16[24,2304]{1,0:T(8,128)(2,1)S(1)}, u32[]{:S(2)}) copy-start(bf16[24,2304]{1,0:T(8,128)(2,1)S(1)} %convert_element_type.123) | copy-start | bytes 331780
  8.3 14.2 %copy-start.2 = (bf16[1,256,768]{2,1,0:T(8,128)(2,1)S(1)}, bf16[1,256,768]{2,1,0:T(8,128)(2,1)}, u32[]{:S(2)}) copy-start(bf16[1,256,768]{2,1,0:T(8,128)(2,1)} %param.23) | copy-start | bytes 1179652
  11.2 11.4 %copy-start.33 = (f32[2,768]{1,0:T(2,128)S(1)}, f32[2,768]{1,0:T(2,128)}, u32[]{:S(2)}) copy-start(f32[2,768]{1,0:T(2,128)} %param.31) | copy-start | bytes 18436
  15.1 14.3 %copy-start.5 = (f32[1,384,768]{2,1,0:T(8,128)S(1)}, f32[1,384,768]{2,1,0:T(8,128)}, u32[]{:S(2)}) copy-start(f32[1,384,768]{2,1,0:T(8,128)} %param.29) | copy-start | bytes 3538948
  15.1 40.3 %all-to-all-start = ((bf16[8,32,1152]{2,1,0:T(8,128)(2,1)}), bf16[8,32,1152]{2,1,0:T(8,128)(2,1)S(1)}, u32[]{:S(2)}, u32[]{:S(2)}) async-start(bf16[8,32,1152]{2,1,0:T(8,128)(2,1)} %fusion.46), calls=%async_computation | async-start | bytes 1179648 | tf_op jit(solution)/shard_map/all_to_all | solution.py:571
  23.4 6.8 %copy-start.7 = (bf16[256,768]{1,0:T(8,128)(2,1)}, bf16[256,768]{1,0:T(8,128)(2,1)S(1)}, u32[]{:S(2)}) copy-start(bf16[256,768]{1,0:T(8,128)(2,1)S(1)} %fusion.5.refs_0_) | copy-start | bytes 1179652
  23.5 16.2 %collective-permute-start = (bf16[256,768]{1,0:T(8,128)(2,1)S(1)}, bf16[256,768]{1,0:T(8,128)(2,1)S(1)}, u32[]{:S(2)}, u32[]{:S(2)}) collective-permute-start(bf16[256,768]{1,0:T(8,128)(2,1)S(1)} %fusion.5.refs_0_), channel_id=1, source_target_pairs={{0,4},{4,0},{8,12},{12,8},{16,20},{20,16},{24,28},{28,24},{1,5},{5... | collective-permute-start | bytes 1179656 | tf_op jit(solution)/shard_map/ppermute | solution.py:618
  25.5 23.5 %collective-permute-start.1 = (bf16[256,768]{1,0:T(8,128)(2,1)S(1)}, bf16[256,768]{1,0:T(8,128)(2,1)S(1)}, u32[]{:S(2)}, u32[]{:S(2)}) collective-permute-start(bf16[256,768]{1,0:T(8,128)(2,1)S(1)} %fusion.5.refs_0_), channel_id=1, source_target_pairs={{0,8},{4,12},{8,0},{12,4},{16,24},{20,28},{24,16},{28,20},{1,9},{5... | collective-permute-start | bytes 1179656 | tf_op jit(solution)/shard_map/ppermute | solution.py:618
  27.0 28.4 %collective-permute-start.2 = (bf16[256,768]{1,0:T(8,128)(2,1)S(1)}, bf16[256,768]{1,0:T(8,128)(2,1)}, u32[]{:S(2)}, u32[]{:S(2)}) collective-permute-start(bf16[256,768]{1,0:T(8,128)(2,1)S(1)} %fusion.5.refs_0_), channel_id=1, source_target_pairs={{0,16},{4,20},{8,24},{12,28},{16,0},{20,4},{24,8},{28,12},{1,17},{... | collective-permute-start | bytes 1179656 | tf_op jit(solution)/shard_map/ppermute | solution.py:618
  39.6 9.5 %copy-start.13 = (bf16[256,768]{1,0:T(8,128)(2,1)}, bf16[256,768]{1,0:T(8,128)(2,1)S(1)}, u32[]{:S(2)}) copy-start(bf16[256,768]{1,0:T(8,128)(2,1)S(1)} %collective-permute-done.refs_1_) | copy-start | bytes 1179652
  56.8 25.6 %copy-start.11 = (bf16[1,256,768]{2,1,0:T(8,128)(2,1)S(1)}, bf16[1,256,768]{2,1,0:T(8,128)(2,1)}, u32[]{:S(2)}) copy-start(bf16[1,256,768]{2,1,0:T(8,128)(2,1)} %param.24) | copy-start | bytes 1179652
  56.8 35.8 %all-to-all-start.1 = ((bf16[4,8,24,1152]{3,2,1,0:T(8,128)(2,1)}), bf16[4,8,24,1152]{3,2,1,0:T(8,128)(2,1)S(1)}, u32[]{:S(2)}, u32[]{:S(2)}) async-start(bf16[4,8,24,1152]{3,2,1,0:T(8,128)(2,1)} %broadcast_in_dim.24), calls=%async_computation.1 | async-start | bytes 3538944 | tf_op jit(solution)/shard_map/all_to_all | solution.py:571
  60.6 23.4 %copy-start.6 = (f32[1,384,768]{2,1,0:T(8,128)S(1)}, f32[1,384,768]{2,1,0:T(8,128)}, u32[]{:S(2)}) copy-start(f32[1,384,768]{2,1,0:T(8,128)} %param.30) | copy-start | bytes 3538948
  62.1 18.6 %collective-permute-start.5 = (bf16[256,768]{1,0:T(8,128)(2,1)}, bf16[256,768]{1,0:T(8,128)(2,1)S(1)}, u32[]{:S(2)}, u32[]{:S(2)}) collective-permute-start(bf16[256,768]{1,0:T(8,128)(2,1)} %collective-permute-done.2.refs_4_), channel_id=1, source_target_pairs={{0,8},{4,12},{8,0},{12,4},{16,24},{20,28},{24,16},{28,20},{1,9},{5... | collective-permute-start | bytes 1179656 | tf_op jit(solution)/shard_map/ppermute | solution.py:618
  62.2 29.5 %collective-permute-start.7 = (bf16[384,768]{1,0:T(8,128)(2,1)}, bf16[384,768]{1,0:T(8,128)(2,1)S(1)}, u32[]{:S(2)}, u32[]{:S(2)}) collective-permute-start(bf16[384,768]{1,0:T(8,128)(2,1)} %bitcast_convert_fusion.1.refs_0_), channel_id=1, source_target_pairs={{16,0},{0,16},{17,1},{1,17},{18,2},{2,18},{19,3},{3,19},{20,4},{4,... | collective-permute-start | bytes 1769480 | tf_op jit(solution)/shard_map/ppermute | solution.py:624
  64.1 20.7 %collective-permute-start.4 = (bf16[256,768]{1,0:T(8,128)(2,1)}, bf16[256,768]{1,0:T(8,128)(2,1)S(1)}, u32[]{:S(2)}, u32[]{:S(2)}) collective-permute-start(bf16[256,768]{1,0:T(8,128)(2,1)} %collective-permute-done.2.refs_4_), channel_id=1, source_target_pairs={{0,4},{4,0},{8,12},{12,8},{16,20},{20,16},{24,28},{28,24},{1,5},{5... | collective-permute-start | bytes 1179656 | tf_op jit(solution)/shard_map/ppermute | solution.py:618
  65.8 19.0 %collective-permute-start.3 = (bf16[256,768]{1,0:T(8,128)(2,1)}, bf16[256,768]{1,0:T(8,128)(2,1)S(1)}, u32[]{:S(2)}, u32[]{:S(2)}) collective-permute-start(bf16[256,768]{1,0:T(8,128)(2,1)} %copy-done.14), channel_id=1, source_target_pairs={{0,4},{4,0},{8,12},{12,8},{16,20},{20,16},{24,28},{28,24},{1,5},{5... | collective-permute-start | bytes 1179656 | tf_op jit(solution)/shard_map/ppermute | solution.py:618
  80.7 11.9 %collective-permute-start.6 = (bf16[256,768]{1,0:T(8,128)(2,1)S(1)}, bf16[256,768]{1,0:T(8,128)(2,1)}, u32[]{:S(2)}, u32[]{:S(2)}) collective-permute-start(bf16[256,768]{1,0:T(8,128)(2,1)S(1)} %collective-permute-done.5.refs_6_), channel_id=1, source_target_pairs={{0,4},{4,0},{8,12},{12,8},{16,20},{20,16},{24,28},{28,24},{1,5},{5... | collective-permute-start | bytes 1179656 | tf_op jit(solution)/shard_map/ppermute | solution.py:618
  84.8 7.0 %copy-start.17 = (bf16[256,768]{1,0:T(8,128)(2,1)}, bf16[256,768]{1,0:T(8,128)(2,1)S(1)}, u32[]{:S(2)}) copy-start(bf16[256,768]{1,0:T(8,128)(2,1)S(1)} %collective-permute-done.3.refs_3_) | copy-start | bytes 1179652
  84.8 7.0 %copy-start.16 = (bf16[256,768]{1,0:T(8,128)(2,1)}, bf16[256,768]{1,0:T(8,128)(2,1)S(1)}, u32[]{:S(2)}) copy-start(bf16[256,768]{1,0:T(8,128)(2,1)S(1)} %collective-permute-done.4.refs_5_) | copy-start | bytes 1179652
  95.0 37.4 %all-to-all-start.2 = ((bf16[8,128,768]{2,1,0:T(8,128)(2,1)}), bf16[8,128,768]{2,1,0:T(8,128)(2,1)S(1)}, u32[]{:S(2)}, u32[]{:S(2)}) async-start(bf16[8,128,768]{2,1,0:T(8,128)(2,1)} %bitcast.196), calls=%async_computation.2 | async-start | bytes 3145728 | tf_op jit(solution)/shard_map/all_to_all | solution.py:571
  98.6 33.8 %collective-permute-start.10 = (bf16[384,768]{1,0:T(8,128)(2,1)}, bf16[384,768]{1,0:T(8,128)(2,1)}, u32[]{:S(2)}, u32[]{:S(2)}) collective-permute-start(bf16[384,768]{1,0:T(8,128)(2,1)} %copy-done.22), channel_id=1, source_target_pairs={{4,0},{0,4},{5,1},{1,5},{6,2},{2,6},{7,3},{3,7},{12,8},{8,12},{13,... | collective-permute-start | bytes 1769480 | tf_op jit(solution)/shard_map/ppermute | solution.py:624
  100.1 32.3 %collective-permute-start.8 = (bf16[384,768]{1,0:T(8,128)(2,1)}, bf16[384,768]{1,0:T(8,128)(2,1)}, u32[]{:S(2)}, u32[]{:S(2)}) collective-permute-start(bf16[384,768]{1,0:T(8,128)(2,1)} %bitcast_convert_fusion.refs_4_), channel_id=1, source_target_pairs={{16,0},{0,16},{17,1},{1,17},{18,2},{2,18},{19,3},{3,19},{20,4},{4,... | collective-permute-start | bytes 1769480 | tf_op jit(solution)/shard_map/ppermute | solution.py:624
  101.6 30.9 %collective-permute-start.9 = (bf16[384,768]{1,0:T(8,128)(2,1)}, bf16[384,768]{1,0:T(8,128)(2,1)}, u32[]{:S(2)}, u32[]{:S(2)}) collective-permute-start(bf16[384,768]{1,0:T(8,128)(2,1)} %bitcast_convert_fusion.1.refs_0_), channel_id=1, source_target_pairs={{4,0},{0,4},{5,1},{1,5},{6,2},{2,6},{7,3},{3,7},{12,8},{8,12},{13,... | collective-permute-start | bytes 1769480 | tf_op jit(solution)/shard_map/ppermute | solution.py:624
  109.1 30.3 %copy-start.4 = (bf16[384,768]{1,0:T(8,128)(2,1)S(1)}, bf16[384,768]{1,0:T(8,128)(2,1)}, u32[]{:S(2)}) copy-start(bf16[384,768]{1,0:T(8,128)(2,1)} %bitcast_convert_fusion.refs_4_) | copy-start | bytes 1769476
  132.5 40.1 %copy-start = (bf16[8,128,768]{2,1,0:T(8,128)(2,1)}, bf16[8,128,768]{2,1,0:T(8,128)(2,1)S(1)}, u32[]{:S(2)}) copy-start(bf16[8,128,768]{2,1,0:T(8,128)(2,1)S(1)} %all-to-all-done.2) | copy-start | bytes 4718596
  132.5 37.8 %all-to-all-start.3 = ((bf16[8,256,128]{2,1,0:T(8,128)(2,1)}), bf16[8,256,128]{2,1,0:T(8,128)(2,1)S(1)}, u32[]{:S(2)}, u32[]{:S(2)}) async-start(bf16[8,256,128]{2,1,0:T(8,128)(2,1)} %bitcast.217), calls=%async_computation.3 | async-start | bytes 1048576 | tf_op jit(solution)/shard_map/all_to_all | solution.py:571
  137.4 108.7 %all-gather.2.cloned.1.call-start = ((), (), s32[]{:S(2)}) async-start(), calls=%async_computation.10 | async-start | bytes 3649536 | tf_op jit(solution)/shard_map/all_gather | solution.py:794
  137.5 21.9 %collective-permute-start.11 = (bf16[384,768]{1,0:T(8,128)(2,1)}, bf16[384,768]{1,0:T(8,128)(2,1)}, u32[]{:S(2)}, u32[]{:S(2)}) collective-permute-start(bf16[384,768]{1,0:T(8,128)(2,1)} %collective-permute-done.8.refs_5_), channel_id=1, source_target_pairs={{4,0},{0,4},{5,1},{1,5},{6,2},{2,6},{7,3},{3,7},{12,8},{8,12},{13,... | collective-permute-start | bytes 1769480 | tf_op jit(solution)/shard_map/ppermute | solution.py:624
  139.4 30.8 %collective-permute-start.12 = (bf16[384,768]{1,0:T(8,128)(2,1)S(1)}, bf16[384,768]{1,0:T(8,128)(2,1)}, u32[]{:S(2)}, u32[]{:S(2)}) collective-permute-start(bf16[384,768]{1,0:T(8,128)(2,1)S(1)} %copy-done.4), channel_id=1, source_target_pairs={{4,0},{0,4},{5,1},{1,5},{6,2},{2,6},{7,3},{3,7},{12,8},{8,12},{13,... | collective-permute-start | bytes 1769480 | tf_op jit(solution)/shard_map/ppermute | solution.py:624
  218.5 27.7 %all-to-all-start.5 = ((bf16[8,128,768]{2,1,0:T(8,128)(2,1)}), bf16[8,128,768]{2,1,0:T(8,128)(2,1)}, u32[]{:S(2)}, u32[]{:S(2)}) async-start(bf16[8,128,768]{2,1,0:T(8,128)(2,1)} %bitcast.212), calls=%async_computation.5 | async-start | bytes 3145728 | tf_op jit(solution)/shard_map/all_to_all | solution.py:571
  229.5 15.8 %collective-permute-start.13 = (bf16[384,768]{1,0:T(8,128)(2,1)}, bf16[384,768]{1,0:T(8,128)(2,1)S(1)}, u32[]{:S(2)}, u32[]{:S(2)}) collective-permute-start(bf16[384,768]{1,0:T(8,128)(2,1)} %get-tuple-element.175), channel_id=1, source_target_pairs={{0,4},{4,0},{1,5},{5,1},{2,6},{6,2},{3,7},{7,3},{8,12},{12,8},{9,1... | collective-permute-start | bytes 1769480 | tf_op jit(solution)/shard_map/ppermute | solution.py:633
  249.1 13.2 %copy-start.1 = (f32[256,768]{1,0:T(8,128)}, f32[256,768]{1,0:T(8,128)S(1)}, u32[]{:S(2)}) copy-start(f32[256,768]{1,0:T(8,128)S(1)} %multiply_add_fusion.residual_ref) | copy-start | bytes 2359300
  255.0 25.6 %all-to-all-start.6 = ((bf16[8,256,128]{2,1,0:T(8,128)(2,1)}), bf16[8,256,128]{2,1,0:T(8,128)(2,1)S(1)}, u32[]{:S(2)}, u32[]{:S(2)}) async-start(bf16[8,256,128]{2,1,0:T(8,128)(2,1)} %fusion.47), calls=%async_computation.6 | async-start | bytes 1048576 | tf_op jit(solution)/shard_map/all_to_all | solution.py:571
  260.2 20.4 %collective-permute-start.14 = (bf16[384,768]{1,0:T(8,128)(2,1)}, bf16[384,768]{1,0:T(8,128)(2,1)}, u32[]{:S(2)}, u32[]{:S(2)}) collective-permute-start(bf16[384,768]{1,0:T(8,128)(2,1)} %get-tuple-element.189), channel_id=1, source_target_pairs={{0,4},{4,0},{1,5},{5,1},{2,6},{6,2},{3,7},{7,3},{8,12},{12,8},{9,1... | collective-permute-start | bytes 1769480 | tf_op jit(solution)/shard_map/ppermute | solution.py:633
  281.4 36.7 %all-to-all-start.7 = ((bf16[8,128,768]{2,1,0:T(8,128)(2,1)}), bf16[8,128,768]{2,1,0:T(8,128)(2,1)S(1)}, u32[]{:S(2)}, u32[]{:S(2)}) async-start(bf16[8,128,768]{2,1,0:T(8,128)(2,1)} %bitcast.195), calls=%async_computation.7 | async-start | bytes 3145728 | tf_op jit(solution)/shard_map/all_to_all | solution.py:571
  285.0 7.2 %copy-start.25 = (bf16[8,24,768]{2,1,0:T(8,128)(2,1)S(1)}, bf16[8,24,768]{2,1,0:T(8,128)(2,1)}, u32[]{:S(2)}) copy-start(bf16[8,24,768]{2,1,0:T(8,128)(2,1)} %get-tuple-element.201) | copy-start | bytes 884740
  287.4 30.7 %collective-permute-start.16 = (bf16[384,768]{1,0:T(8,128)(2,1)}, bf16[384,768]{1,0:T(8,128)(2,1)}, u32[]{:S(2)}, u32[]{:S(2)}) collective-permute-start(bf16[384,768]{1,0:T(8,128)(2,1)} %add_convert_fusion.1), channel_id=1, source_target_pairs={{0,16},{16,0},{1,17},{17,1},{2,18},{18,2},{3,19},{19,3},{4,20},{20... | collective-permute-start | bytes 1769480 | tf_op jit(solution)/shard_map/ppermute | solution.py:633
  289.8 28.3 %collective-permute-start.15 = (bf16[384,768]{1,0:T(8,128)(2,1)}, bf16[384,768]{1,0:T(8,128)(2,1)}, u32[]{:S(2)}, u32[]{:S(2)}) collective-permute-start(bf16[384,768]{1,0:T(8,128)(2,1)} %get-tuple-element.195), channel_id=1, source_target_pairs={{0,4},{4,0},{1,5},{5,1},{2,6},{6,2},{3,7},{7,3},{8,12},{12,8},{9,1... | collective-permute-start | bytes 1769480 | tf_op jit(solution)/shard_map/ppermute | solution.py:633
  290.3 27.8 %collective-permute-start.17 = (bf16[8,24,768]{2,1,0:T(8,128)(2,1)}, bf16[8,24,768]{2,1,0:T(8,128)(2,1)}, u32[]{:S(2)}, u32[]{:S(2)}) collective-permute-start(bf16[8,24,768]{2,1,0:T(8,128)(2,1)} %get-tuple-element.199), channel_id=1, source_target_pairs={{0,1},{1,2},{2,3},{3,0},{4,5},{5,6},{6,7},{7,4},{8,9},{9,10},{10,1... | collective-permute-start | bytes 884744 | tf_op jit(solution)/shard_map/ppermute | solution.py:633
  290.3 27.8 %collective-permute-start.18 = (bf16[8,24,768]{2,1,0:T(8,128)(2,1)}, bf16[8,24,768]{2,1,0:T(8,128)(2,1)}, u32[]{:S(2)}, u32[]{:S(2)}) collective-permute-start(bf16[8,24,768]{2,1,0:T(8,128)(2,1)} %get-tuple-element.200), channel_id=1, source_target_pairs={{0,2},{1,3},{2,0},{3,1},{4,6},{5,7},{6,4},{7,5},{8,10},{9,11},{10,... | collective-permute-start | bytes 884744 | tf_op jit(solution)/shard_map/ppermute | solution.py:633
  292.2 25.8 %collective-permute-start.19 = (bf16[8,24,768]{2,1,0:T(8,128)(2,1)S(1)}, bf16[8,24,768]{2,1,0:T(8,128)(2,1)}, u32[]{:S(2)}, u32[]{:S(2)}) collective-permute-start(bf16[8,24,768]{2,1,0:T(8,128)(2,1)S(1)} %copy-done.25), channel_id=1, source_target_pairs={{0,3},{1,0},{2,1},{3,2},{4,7},{5,4},{6,5},{7,6},{8,11},{9,8},{10,9... | collective-permute-start | bytes 884744 | tf_op jit(solution)/shard_map/ppermute | solution.py:633
  318.1 83.0 %all-to-all-start.8 = ((bf16[8,256,384]{2,1,0:T(8,128)(2,1)}), bf16[8,256,384]{2,1,0:T(8,128)(2,1)}, u32[]{:S(2)}, u32[]{:S(2)}) async-start(bf16[8,256,384]{2,1,0:T(8,128)(2,1)} %bitcast.211), calls=%async_computation.8 | async-start | bytes 3145728 | tf_op jit(solution)/shard_map/all_to_all | solution.py:571
  325.1 76.1 %collective-permute-start.31 = (bf16[384,768]{1,0:T(8,128)(2,1)}, bf16[384,768]{1,0:T(8,128)(2,1)}, u32[]{:S(2)}, u32[]{:S(2)}) collective-permute-start(bf16[384,768]{1,0:T(8,128)(2,1)} %add_convert_fusion), channel_id=1, source_target_pairs={{0,16},{16,0},{1,17},{17,1},{2,18},{18,2},{3,19},{19,3},{4,20},{20... | collective-permute-start | bytes 1769480 | tf_op jit(solution)/shard_map/ppermute | solution.py:633
  334.2 5.6 %collective-permute-start.20 = (bf16[8,24,384]{2,1,0:T(8,128)(2,1)S(1)}, bf16[8,24,384]{2,1,0:T(8,128)(2,1)S(1)}, u32[]{:S(2)}, u32[]{:S(2)}) collective-permute-start(bf16[8,24,384]{2,1,0:T(8,128)(2,1)S(1)} %get-tuple-element.261), channel_id=1, source_target_pairs={{0,1},{1,2},{2,3},{3,0},{4,5},{5,6},{6,7},{7,4},{8,9},{9,10},{10,1... | collective-permute-start | bytes 442376 | tf_op jit(solution)/shard_map/ppermute | solution.py:633
  334.3 6.7 %collective-permute-start.21 = (bf16[8,24,384]{2,1,0:T(8,128)(2,1)S(1)}, bf16[8,24,384]{2,1,0:T(8,128)(2,1)S(1)}, u32[]{:S(2)}, u32[]{:S(2)}) collective-permute-start(bf16[8,24,384]{2,1,0:T(8,128)(2,1)S(1)} %get-tuple-element.263), channel_id=1, source_target_pairs={{0,2},{1,3},{2,0},{3,1},{4,6},{5,7},{6,4},{7,5},{8,10},{9,11},{10,... | collective-permute-start | bytes 442376 | tf_op jit(solution)/shard_map/ppermute | solution.py:633
  335.5 6.7 %collective-permute-start.22 = (bf16[8,24,384]{2,1,0:T(8,128)(2,1)S(1)}, bf16[8,24,384]{2,1,0:T(8,128)(2,1)S(1)}, u32[]{:S(2)}, u32[]{:S(2)}) collective-permute-start(bf16[8,24,384]{2,1,0:T(8,128)(2,1)S(1)} %get-tuple-element.262), channel_id=1, source_target_pairs={{0,3},{1,0},{2,1},{3,2},{4,7},{5,4},{6,5},{7,6},{8,11},{9,8},{10,9... | collective-permute-start | bytes 442376 | tf_op jit(solution)/shard_map/ppermute | solution.py:633
  336.9 64.3 %collective-permute-start.30 = (bf16[384,768]{1,0:T(8,128)(2,1)}, bf16[384,768]{1,0:T(8,128)(2,1)}, u32[]{:S(2)}, u32[]{:S(2)}) collective-permute-start(bf16[384,768]{1,0:T(8,128)(2,1)} %get-tuple-element.209), channel_id=1, source_target_pairs={{0,4},{4,0},{1,5},{5,1},{2,6},{6,2},{3,7},{7,3},{8,12},{12,8},{9,1... | collective-permute-start | bytes 1769480 | tf_op jit(solution)/shard_map/ppermute | solution.py:633
  339.6 56.4 %copy-start.20 = (f32[384,768]{1,0:T(8,128)S(1)}, f32[384,768]{1,0:T(8,128)}, u32[]{:S(2)}) copy-start(f32[384,768]{1,0:T(8,128)} %get-tuple-element.228) | copy-start | bytes 3538948
  343.3 46.6 %collective-permute-start.27 = (bf16[24,1152]{1,0:T(8,128)(2,1)S(1)}, bf16[24,1152]{1,0:T(8,128)(2,1)S(1)}, u32[]{:S(2)}, u32[]{:S(2)}) collective-permute-start(bf16[24,1152]{1,0:T(8,128)(2,1)S(1)} %get-tuple-element.271), channel_id=1, source_target_pairs={{0,20},{4,16},{8,28},{12,24},{16,4},{20,0},{24,12},{28,8},{1,21},{... | collective-permute-start | bytes 165896 | tf_op jit(solution)/shard_map/ppermute | solution.py:618
  344.8 45.1 %collective-permute-start.28 = (bf16[24,1152]{1,0:T(8,128)(2,1)S(1)}, bf16[24,1152]{1,0:T(8,128)(2,1)S(1)}, u32[]{:S(2)}, u32[]{:S(2)}) collective-permute-start(bf16[24,1152]{1,0:T(8,128)(2,1)S(1)} %get-tuple-element.270), channel_id=1, source_target_pairs={{0,24},{4,28},{8,16},{12,20},{16,8},{20,12},{24,0},{28,4},{1,25},{... | collective-permute-start | bytes 165896 | tf_op jit(solution)/shard_map/ppermute | solution.py:618
  348.7 43.1 %collective-permute-start.23 = (bf16[24,1152]{1,0:T(8,128)(2,1)S(1)}, bf16[24,1152]{1,0:T(8,128)(2,1)S(1)}, u32[]{:S(2)}, u32[]{:S(2)}) collective-permute-start(bf16[24,1152]{1,0:T(8,128)(2,1)S(1)} %get-tuple-element.266), channel_id=1, source_target_pairs={{0,4},{4,0},{8,12},{12,8},{16,20},{20,16},{24,28},{28,24},{1,5},{5... | collective-permute-start | bytes 165896 | tf_op jit(solution)/shard_map/ppermute | solution.py:618
  389.8 6.1 %copy-start.26 = (bf16[24,1152]{1,0:T(8,128)(2,1)}, bf16[24,1152]{1,0:T(8,128)(2,1)S(1)}, u32[]{:S(2)}) copy-start(bf16[24,1152]{1,0:T(8,128)(2,1)S(1)} %collective-permute-done.27.refs_5_) | copy-start | bytes 165892
  389.8 4.3 collective-permute-start.24
  389.9 6.1 %copy-start.27 = (bf16[24,1152]{1,0:T(8,128)(2,1)}, bf16[24,1152]{1,0:T(8,128)(2,1)S(1)}, u32[]{:S(2)}) copy-start(bf16[24,1152]{1,0:T(8,128)(2,1)S(1)} %collective-permute-done.28.refs_6_) | copy-start | bytes 165892
  389.9 9.4 %collective-permute-start.25 = (bf16[24,1152]{1,0:T(8,128)(2,1)S(1)}, bf16[24,1152]{1,0:T(8,128)(2,1)S(1)}, u32[]{:S(2)}, u32[]{:S(2)}) collective-permute-start(bf16[24,1152]{1,0:T(8,128)(2,1)S(1)} %get-tuple-element.268), channel_id=1, source_target_pairs={{0,12},{4,8},{8,4},{12,0},{16,28},{20,24},{24,20},{28,16},{1,13},{... | collective-permute-start | bytes 165896 | tf_op jit(solution)/shard_map/ppermute | solution.py:618
  391.9 4.1 copy-start.28
  391.9 7.4 %collective-permute-start.26 = (bf16[24,1152]{1,0:T(8,128)(2,1)S(1)}, bf16[24,1152]{1,0:T(8,128)(2,1)S(1)}, u32[]{:S(2)}, u32[]{:S(2)}) collective-permute-start(bf16[24,1152]{1,0:T(8,128)(2,1)S(1)} %get-tuple-element.269), channel_id=1, source_target_pairs={{0,16},{4,20},{8,24},{12,28},{16,0},{20,4},{24,8},{28,12},{1,17},{... | collective-permute-start | bytes 165896 | tf_op jit(solution)/shard_map/ppermute | solution.py:618
  394.2 7.0 %collective-permute-start.29 = (bf16[24,1152]{1,0:T(8,128)(2,1)S(1)}, bf16[24,1152]{1,0:T(8,128)(2,1)}, u32[]{:S(2)}, u32[]{:S(2)}) collective-permute-start(bf16[24,1152]{1,0:T(8,128)(2,1)S(1)} %get-tuple-element.264), channel_id=1, source_target_pairs={{0,28},{4,24},{8,20},{12,16},{16,12},{20,8},{24,4},{28,0},{1,29},{... | collective-permute-start | bytes 165896 | tf_op jit(solution)/shard_map/ppermute | solution.py:618
  396.0 5.2 %copy-start.19 = (f32[384,768]{1,0:T(8,128)S(1)}, f32[384,768]{1,0:T(8,128)}, u32[]{:S(2)}) copy-start(f32[384,768]{1,0:T(8,128)} %get-tuple-element.225) | copy-start | bytes 3538948
  414.7 12.4 %all-to-all-start.9 = ((f32[32,1,1664]{2,1,0:T(1,128)}), f32[32,1,1664]{2,1,0:T(1,128)S(1)}, u32[]{:S(2)}, u32[]{:S(2)}) async-start(f32[32,1,1664]{2,1,0:T(1,128)} %broadcast_in_dim.60), calls=%async_computation.9 | async-start | bytes 425984 | tf_op jit(solution)/shard_map/all_to_all | solution.py:571
  418.0 11.8 %copy-start.35 = (f32[2,768]{1,0:T(2,128)S(1)}, f32[2,768]{1,0:T(2,128)}, u32[]{:S(2)}) copy-start(f32[2,768]{1,0:T(2,128)} %param.41) | copy-start | bytes 18436
  418.0 11.8 %copy-start.36 = (f32[2,768]{1,0:T(2,128)S(1)}, f32[2,768]{1,0:T(2,128)}, u32[]{:S(2)}) copy-start(f32[2,768]{1,0:T(2,128)} %param.40) | copy-start | bytes 18436
  428.4 11.3 %copy-start.32 = (f32[2,768]{1,0:T(2,128)}, f32[2,768]{1,0:T(2,128)S(1)}, u32[]{:S(2)}) copy-start(f32[2,768]{1,0:T(2,128)S(1)} %reshape.254) | copy-start | bytes 18436
  (16 other events, 22.7 us)
Sparse Core Ops, SparseCore 0:
  171.2 61.4 all-gather.1

commit v2 on v1

--- a/solution.py
+++ b/solution.py
@@ -507,20 +507,15 @@
     )(pieces, matrix, tokens, gain, residual)
 
 
-def dense_kernel(order_ref, *refs, starts):
-    count = len(starts)
-    term_refs = refs[:count]
-    columns_ref, output_ref, square_ref, terms_ref = refs[count:]
+def dense_kernel(terms_ref, columns_ref, output_ref, square_ref, *, starts):
     width = output_ref.shape[1]
-    for index, term_ref in enumerate(term_refs):
-        terms_ref[order_ref[index]] = term_ref[...].astype(F32)
     columns_ref[...] = jnp.zeros_like(columns_ref)
     lane = lax.broadcasted_iota(jnp.int32, (columns_ref.shape[0], LANES), 1)
     output = jnp.zeros(output_ref.shape, F32)
     for device, start in enumerate(starts):
-        output = output + terms_ref[device, :, 3 * LANES :]
+        output = output + terms_ref[device, :, 3 * LANES :].astype(F32)
         for part in range(3):
-            piece = terms_ref[device, :, part * LANES : (part + 1) * LANES]
+            piece = terms_ref[device, :, part * LANES : (part + 1) * LANES].astype(F32)
             column = part * width + start
             if column % LANES == 0:
                 columns_ref[:, column : column + LANES] += piece
@@ -536,21 +531,19 @@
     )
 
 
-def dense_grads(order, terms, starts):
-    rows, lanes = terms[0].shape
+def dense_grads(terms, starts):
+    unused, rows, lanes = terms.shape
     width = lanes - 3 * LANES
     outs = [jax.ShapeDtypeStruct((rows, columns), F32) for columns in (3 * width, width)]
     outs.append(jax.ShapeDtypeStruct((1, LANES), F32))
     return pl.pallas_call(
         functools.partial(dense_kernel, starts=starts),
-        in_specs=[pl.BlockSpec(memory_space=pltpu.SMEM)]
-        + [pl.BlockSpec(memory_space=pltpu.VMEM)] * len(terms),
+        in_specs=[pl.BlockSpec(memory_space=pltpu.VMEM)],
         out_specs=[pl.BlockSpec(memory_space=pltpu.VMEM)] * 3,
         out_shape=outs,
-        scratch_shapes=[pltpu.VMEM((len(terms), rows, lanes), F32)],
         compiler_params=pltpu.CompilerParams(vmem_limit_bytes=VMEM_LIMIT),
         cost_estimate=SMALL,
-    )(order, *terms)
+    )(terms)
 
 
 def adam_update(weight, grad, first, second, factor, rate, decay):
@@ -762,6 +755,7 @@
     grad_arrived = dispatch(grad_slots_out)
     peer_down = others(own_down, "hi")
     side_up = others(own_up, "in")
+    side_down = others(own_down, "in")
     far_up = others(peer_up, "in")
 
     mixed_low, mixed_full, stat, pair = attend(
@@ -783,13 +777,12 @@
     def to_tokens(values):
         return swap(values.reshape(count, row_count, values.shape[1]), SEQ)
 
-    mixed_low, grad_arrived, peer_down, side_up, far_up, own_down = together(
-        mixed_low, grad_arrived, peer_down, side_up, far_up, own_down
-    )
-    side_down = others(own_down, "in")
+    mixed_low, grad_arrived, peer_down, side_up, side_down, far_up = together(
+        mixed_low, grad_arrived, peer_down, side_up, side_down, far_up
+    )
     far_down = others(peer_down, "in")
-    mixed_pieces, projection_low, far_down, side_down = together(
-        to_tokens(mixed_low), projection_low, far_down, side_down
+    mixed_pieces, projection_low, far_down = together(
+        to_tokens(mixed_low), projection_low, far_down
     )
     projection_full = lax.all_gather(projection_low, ALL, axis=0, tiled=True)
     attend_out = jnp.einsum(
@@ -860,18 +853,28 @@
         row_grad, produced, down_side, up_side, up_part, *output_away
     )
     output_away = to_owners(output_away, "exp")
-    (down_early,) = to_owners([down_side], "in")
-    up_hi = hi_parts(add_all(up_peer, [up_part]))
+    up_head, up_tail = [
+        list(part)
+        for part in zip(
+            *(
+                jnp.split(block, 2, axis=0)
+                for block in add_all(up_peer, [up_part]).astype(BF16).reshape(peers - 1, -1, width)
+            ),
+            strict=True,
+        )
+    ]
+    up_head = to_owners(up_head, "hi")
     returned = send_back(produced)
     grad_qkv, grad_lying = attend_back(
         active, order, pair, documents, stat, row_grad, mixed_full, row_count, scaling
     )
-    grad_qkv, grad_lying, returned, down_early, up_side, *held = together(
-        grad_qkv, grad_lying, returned, down_early, up_side, *down_hi, *output_away
-    )
-    down_hi, output_away = held[: len(down_hi)], held[len(down_hi) :]
+    grad_qkv, grad_lying, returned, down_side, up_side, *held = together(
+        grad_qkv, grad_lying, returned, down_side, up_side, *down_hi, *up_head, *output_away
+    )
+    down_hi, up_head = held[: peers - 1], held[peers - 1 : 2 * peers - 2]
+    output_away = held[2 * peers - 2 :]
+    (down_early,) = to_owners([down_side], "in")
     (up_early,) = to_owners([up_side], "in")
-    down_grad = add_all(down_own, [down_early, *down_hi])[None]
     block_output = (middle + collect(returned)).astype(BF16)[None]
 
     column_own, column_away = group_rows(column_terms(row_blocks, grad_lying))
@@ -882,19 +885,17 @@
         ],
         axis=2,
     )
-    if pairwise:
-        lying_terms = [
-            lax.dynamic_index_in_dim(dense_rows, position ^ bits, 0, keepdims=False)
-            for bits in range(count)
-        ]
-        lying_terms[1:] = [flip(lying_terms[bits], bits) for bits in range(1, count)]
-        grad_pieces, *lying_terms = together(to_tokens(grad_qkv), *lying_terms)
-    else:
-        grad_pieces, dense_rows = together(to_tokens(grad_qkv), dense_rows)
-        lying_terms = list(swap(dense_rows, SEQ))
-    grad_pieces, up_early, *up_hi = together(grad_pieces, up_early, *up_hi)
-    up_grad = add_all(up_own, [up_early, *up_hi])[None]
-    projection_grad, output_grad, dense_square = dense_grads(order, lying_terms, starts)
+    grad_pieces, dense_rows, down_early, up_early, *up_tail = together(
+        to_tokens(grad_qkv), dense_rows, down_early, up_early, *up_tail
+    )
+    up_tail = to_owners(up_tail, "hi")
+    projection_grad, output_grad, dense_square = dense_grads(swap(dense_rows, SEQ), starts)
+    down_grad = add_all(down_own, [down_early, *down_hi])[None]
+    up_half = up_own.shape[0] // 2
+    up_grad = add_all(up_own, [up_early])
+    up_grad = jnp.concatenate(
+        [add_all(up_grad[:up_half], up_head), add_all(up_grad[up_half:], up_tail)], axis=0
+    )[None]
     input_grad, gain_first_part = close_norm(
         grad_pieces, starts, projection_full, tokens[0], gain_first[None], residual_grad
     )

time: 450 us -> 451 us (level)
    ppermute x12 -> x13, waiting for transfers between devices: 19.7 us -> 69.5 us  [to_owners(): lax.ppermute(block, axis, [(i, (i + step) % size) for i in range(size)])]
    ppermute x14 -> x7, waiting for transfers between devices: 82.1 us -> 39 us  [flip(): lax.ppermute(value, SEQ, [(index, index ^ bits) for index in range(count)])]
    ppermute x14 -> x7, starting transfers between devices: 19.3 us -> 9.68 us  [flip(): lax.ppermute(value, SEQ, [(index, index ^ bits) for index in range(count)])]
    all_to_all x9 -> x10, starting transfers between devices: 40.4 us -> 47.5 us  [swap(): return lax.all_to_all(value, axes, split_axis=0, concat_axis=0, tiled=True)]
    ppermute x6, waiting for transfers between devices: 37.6 us -> 31.2 us  [others(): lax.ppermute(value, axis, [((i + step) % size, i) for i in range(size)])]
    ppermute x12 -> x13, starting transfers between devices: 15.6 us -> 17 us  [to_owners(): lax.ppermute(block, axis, [(i, (i + step) % size) for i in range(size)])]
    unnamed x84 -> x72, local copies, waits for them, and re-layouts: 10.6 us -> 10 us
  transfers between devices with their start and end apart: 42 -> 37, of which waited for: 17 -> 17; matrix products, arithmetic and copies ran while one was open for 7% -> 8% of each run, Pallas kernels for 20% -> 21%
where the time goes in v2:
time: 451 us; the launch traced here: 449 us
  waiting for transfers between devices  147 us (33%)
  Pallas kernels  105 us (23%)
  starting transfers between devices  83.1 us (18%)
  other arithmetic  32.7 us (7%)
  local copies, waits for them, and re-layouts  27.9 us (6%)
  blocking collectives  27.6 us (6%)
  between operations  18.3 us (4%)
  matrix products  6.88 us (2%)
    ppermute x13, waiting for transfers between devices, to_owners(): lax.ppermute(block, axis, [(i, (i + step) % size) for i in range(size)])  69.5 us
    all_to_all x10, starting transfers between devices, swap(): return lax.all_to_all(value, axes, split_axis=0, concat_axis=0, tiled=True)  47.5 us
    ppermute x7, waiting for transfers between devices, flip(): lax.ppermute(value, SEQ, [(index, index ^ bits) for index in range(count)])  39 us
    ppermute x6, waiting for transfers between devices, others(): lax.ppermute(value, axis, [((i + step) % size, i) for i in range(size)])  31.2 us
    all_to_all x1, blocking collectives, swap(): return lax.all_to_all(value, axes, split_axis=0, concat_axis=0, tiled=True)  27.6 us
    pallas_call x1, Pallas kernels, attend_back(): pl.pallas_call(functools.partial(attend_back_kernel, block=block, chunk=2...  24.4 us
    pallas_call x1, Pallas kernels, attend(): pl.pallas_call(functools.partial(attend_kernel, block=block, chunk=2 * bl...  23.1 us
    ppermute x13, starting transfers between devices, to_owners(): lax.ppermute(block, axis, [(i, (i + step) % size) for i in range(size)])  17 us
  transfers between devices with their start and end apart: 37, of which 17 were waited for; matrix products, arithmetic and copies ran while one was open for 8% of the time, Pallas kernels for 21%

profile of v2, /device:TPU:0, one launch (start us, length us, event | category | flops | bytes accessed | tf_op | source)
XLA Modules:
  0.0 448.8 jit_solution(4137582945214595144)
XLA Ops:
  15.1 7.4 %all-to-all-start = ((bf16[8,32,1152]{2,1,0:T(8,128)(2,1)}), bf16[8,32,1152]{2,1,0:T(8,128)(2,1)S(1)}, u32[]{:S(2)}, u32[]{:S(2)}) async-start(bf16[8,32,1152]{2,1,0:T(8,128)(2,1)} %fusion.47), calls=%async_computation | async-start | bytes 1179648 | tf_op jit(solution)/shard_map/all_to_all | solution.py:564
  23.5 2.1 collective-permute-start
  25.5 1.5 collective-permute-start.1
  27.0 2.4 collective-permute-start.2
  30.2 9.4 %collective-permute-done.refs_1_ = bf16[256,768]{1,0:T(8,128)(2,1)S(1)} collective-permute-done((bf16[256,768]{1,0:T(8,128)(2,1)S(1)}, bf16[256,768]{1,0:T(8,128)(2,1)S(1)}, u32[]{:S(2)}, u32[]{:S(2)}) %collective-permute-start) | collective-permute-done | bytes 393248 | tf_op jit(solution)/shard_map/ppermute | solution.py:611
  39.6 9.5 %collective-permute-done.1.refs_2_ = bf16[256,768]{1,0:T(8,128)(2,1)S(1)} collective-permute-done((bf16[256,768]{1,0:T(8,128)(2,1)S(1)}, bf16[256,768]{1,0:T(8,128)(2,1)S(1)}, u32[]{:S(2)}, u32[]{:S(2)}) %collective-permute-start.1) | collective-permute-done | bytes 393248 | tf_op jit(solution)/shard_map/ppermute | solution.py:611
  49.8 5.5 %collective-permute-done.2.refs_4_ = bf16[256,768]{1,0:T(8,128)(2,1)} collective-permute-done((bf16[256,768]{1,0:T(8,128)(2,1)S(1)}, bf16[256,768]{1,0:T(8,128)(2,1)}, u32[]{:S(2)}, u32[]{:S(2)}) %collective-permute-start.2) | collective-permute-done | bytes 393248 | tf_op jit(solution)/shard_map/ppermute | solution.py:611
  55.4 1.4 broadcast_in_dim.24
  56.8 3.7 all-to-all-start.1
  62.2 1.9 collective-permute-start.7
  64.1 1.7 collective-permute-start.4
  66.1 14.6 %collective-permute-done.5.refs_6_ = bf16[256,768]{1,0:T(8,128)(2,1)S(1)} collective-permute-done((bf16[256,768]{1,0:T(8,128)(2,1)}, bf16[256,768]{1,0:T(8,128)(2,1)S(1)}, u32[]{:S(2)}, u32[]{:S(2)}) %collective-permute-start.5) | collective-permute-done | bytes 393248 | tf_op jit(solution)/shard_map/ppermute | solution.py:611
  80.7 1.7 collective-permute-start.6
  82.5 1.4 convolution_convert_fusion.2
  84.8 6.9 %collective-permute-done.7.refs_1_ = bf16[384,768]{1,0:T(8,128)(2,1)S(1)} collective-permute-done((bf16[384,768]{1,0:T(8,128)(2,1)}, bf16[384,768]{1,0:T(8,128)(2,1)S(1)}, u32[]{:S(2)}, u32[]{:S(2)}) %collective-permute-start.7) | collective-permute-done | bytes 589856 | tf_op jit(solution)/shard_map/ppermute | solution.py:617
  92.6 2.4 broadcast_in_dim.55
  95.0 3.6 all-to-all-start.2
  98.6 1.5 collective-permute-start.10
  100.1 1.4 collective-permute-start.8
  102.1 1.5 collective-permute-start.9
  106.1 1.4 copy.78
  107.5 1.9 slice.219
  110.6 23.1 %shard_map.380 = (bf16[2048,128]{1,0:T(8,128)(2,1)}, f32[2048,128]{1,0:T(8,128)}, bf16[2048,256]{1,0:T(8,128)(2,1)}, bf16[2048,256]{1,0:T(8,128)(2,1)}) custom-call(s32[2,8]{1,0:T(2,128)} %fusion.59.active_ref, s32[8]{0:T(128)} %iota_xor_fusion.order_ref, bf16[256,768]{1,0:T(8,128)(2,1)} %copy-done.6, bf16[256,768]{1,0:T(8,128)(2,1)} %copy-done.12, ...), custom_call_target="tpu_custom_call" | custom-call | flops 1 | bytes 1 | tf_op jit(solution)/shard_map/pallas_call | solution.py:278
  133.8 6.1 %collective-permute-done.9.refs_2_ = bf16[384,768]{1,0:T(8,128)(2,1)} collective-permute-done((bf16[384,768]{1,0:T(8,128)(2,1)}, bf16[384,768]{1,0:T(8,128)(2,1)}, u32[]{:S(2)}, u32[]{:S(2)}) %collective-permute-start.9) | collective-permute-done | bytes 589856 | tf_op jit(solution)/shard_map/ppermute | solution.py:617
  139.8 4.9 %all-to-all-start.3 = ((bf16[8,256,128]{2,1,0:T(8,128)(2,1)}), bf16[8,256,128]{2,1,0:T(8,128)(2,1)S(1)}, u32[]{:S(2)}, u32[]{:S(2)}) async-start(bf16[8,256,128]{2,1,0:T(8,128)(2,1)} %bitcast.205), calls=%async_computation.3 | async-start | bytes 1048576 | tf_op jit(solution)/shard_map/all_to_all | solution.py:564
  144.8 2.0 collective-permute-start.12
  146.7 18.2 %collective-permute-done.12.refs_7_ = bf16[384,768]{1,0:T(8,128)(2,1)} collective-permute-done((bf16[384,768]{1,0:T(8,128)(2,1)}, bf16[384,768]{1,0:T(8,128)(2,1)}, u32[]{:S(2)}, u32[]{:S(2)}) %collective-permute-start.12) | collective-permute-done | bytes 589856 | tf_op jit(solution)/shard_map/ppermute | solution.py:617
  165.8 1.5 slice.220
  170.0 27.6 %all_to_all.55 = bf16[8,128,768]{2,1,0:T(8,128)(2,1)} all-to-all(bf16[8,128,768]{2,1,0:T(8,128)(2,1)S(1)} %bitcast.184), channel_id=1, replica_groups=mesh['hi'=2,'lo'=2,'in'=2,'exp'=4] {'lo','exp'}, dimensions={0} | all-to-all | bytes 3145728 | tf_op jit(solution)/shard_map/all_to_all | solution.py:564
  197.6 15.6 %shard_map.381 = (bf16[1024,768]{1,0:T(8,128)(2,1)}, bf16[1024,384]{1,0:T(8,128)(2,1)}, bf16[1024,384]{1,0:T(8,128)(2,1)}, bf16[1024,384]{1,0:T(8,128)(2,1)}, bf...) custom-call(bf16[1024,768]{1,0:T(8,128)(2,1)} %bitcast.176, ...), custom_call_target="tpu_custom_call" | custom-call | flops 1 | bytes 1 | tf_op jit(solution)/shard_map/pallas_call | solution.py:372
  213.2 4.3 all-to-all-start.5
  217.5 6.7 %shard_map.382 = (bf16[384,768]{1,0:T(8,128)(2,1)}, bf16[384,768]{1,0:T(8,128)(2,1)}, f32[384,768]{1,0:T(8,128)}, f32[384,768]{1,0:T(8,128)}) custom-call(bf16[1024,768]{1,0:T(8,128)(2,1)} %bitcast.174, bf16[1024,768]{1,0:T(8,128)(2,1)} %bitcast.177, bf16[1024,384]{1,0:T(8,128)(2,1)} %get-tuple-element.163.refs_0_.refs_3_, ...), custom_call_target="tpu_custom_call" | custom-call | flops 1 | bytes 1 | tf_op jit(solution)/shard_map/pallas_call | solution.py:425
  224.9 7.2 %shard_map.383 = bf16[1024,768]{1,0:T(8,128)(2,1)} custom-call(bf16[1024,384]{1,0:T(8,128)(2,1)} %get-tuple-element.171.refs_0_.refs_2_, bf16[1024,384]{1,0:T(8,128)(2,1)} %get-tuple-element.165.refs_2_.refs_1_, bf16[1024,384]{1,0:T(8,128)(2,1)} %get-tuple-element.172.refs_2_.refs_0_, bf16[1024,384]{1,0:T(8,128)(2,1)} %get-tuple-element.163.refs_0_.refs_3_, ...), custom_call_target="tpu_custom_call" | custom-call | flops 1 | bytes 1 | tf_op jit(solution)/shard_map/pallas_call | solution.py:396
  232.0 6.6 %shard_map.384 = (bf16[384,768]{1,0:T(8,128)(2,1)}, bf16[384,768]{1,0:T(8,128)(2,1)}, f32[384,768]{1,0:T(8,128)}, f32[384,768]{1,0:T(8,128)}) custom-call(bf16[1024,768]{1,0:T(8,128)(2,1)} %bitcast.175, bf16[1024,768]{1,0:T(8,128)(2,1)} %bitcast.178, bf16[1024,384]{1,0:T(8,128)(2,1)} %get-tuple-element.172.refs_2_.refs_0_, ...), custom_call_target="tpu_custom_call" | custom-call | flops 1 | bytes 1 | tf_op jit(solution)/shard_map/pallas_call | solution.py:425
  240.9 1.7 convert_reduce_fusion.1
  249.7 5.2 %all-to-all-start.6 = ((bf16[8,256,128]{2,1,0:T(8,128)(2,1)}), bf16[8,256,128]{2,1,0:T(8,128)(2,1)S(1)}, u32[]{:S(2)}, u32[]{:S(2)}) async-start(bf16[8,256,128]{2,1,0:T(8,128)(2,1)} %fusion.48), calls=%async_computation.6 | async-start | bytes 1048576 | tf_op jit(solution)/shard_map/all_to_all | solution.py:564
  254.9 2.0 collective-permute-start.14
  256.9 1.5 convolution_convert_fusion
  259.4 15.9 %collective-permute-done.14 = bf16[384,768]{1,0:T(8,128)(2,1)} collective-permute-done((bf16[384,768]{1,0:T(8,128)(2,1)}, bf16[384,768]{1,0:T(8,128)(2,1)}, u32[]{:S(2)}, u32[]{:S(2)}) %collective-permute-start.14) | collective-permute-done | bytes 589856 | tf_op jit(solution)/shard_map/ppermute | solution.py:626
  276.1 3.6 all-to-all-start.7
  279.7 2.4 add_convert_fusion.1
  282.2 2.4 collective-permute-start.15
  287.1 2.0 collective-permute-start.18
  289.2 1.4 collective-permute-start.19
  290.6 24.4 %shard_map.385 = (bf16[2048,384]{1,0:T(8,128)(2,1)}, bf16[2048,384]{1,0:T(8,128)(2,1)}) custom-call(s32[2,8]{1,0:T(2,128)} %fusion.59.active_ref, s32[8]{0:T(128)} %iota_xor_fusion.order_ref, bf16[2048,256]{1,0:T(8,128)(2,1)} %get-tuple-element.155.pair_ref, bf16[2048,128]{1,0:T(8,128)(2,1)} %broadcast_in_dim.26.refs_9_.documents_ref, ...), custom_call_target="tpu_custom_call" | custom-call | flops 1 | bytes 1 | tf_op jit(solution)/shard_map/pallas_call | solution.py:309
  315.0 9.3 %collective-permute-done.16 = bf16[192,768]{1,0:T(8,128)(2,1)S(1)} collective-permute-done((bf16[192,768]{1,0:T(8,128)(2,1)}, bf16[192,768]{1,0:T(8,128)(2,1)S(1)}, u32[]{:S(2)}, u32[]{:S(2)}) %collective-permute-start.16) | collective-permute-done | bytes 294944 | tf_op jit(solution)/shard_map/ppermute | solution.py:626
  325.1 4.7 %all-to-all-start.8 = ((bf16[8,256,384]{2,1,0:T(8,128)(2,1)}), bf16[8,256,384]{2,1,0:T(8,128)(2,1)}, u32[]{:S(2)}, u32[]{:S(2)}) async-start(bf16[8,256,384]{2,1,0:T(8,128)(2,1)} %bitcast.199), calls=%async_computation.8 | async-start | bytes 3145728 | tf_op jit(solution)/shard_map/all_to_all | solution.py:564
  329.8 5.5 %shard_map.386 = bf16[768,384]{1,0:T(8,128)(2,1)} custom-call(bf16[256,768]{1,0:T(8,128)(2,1)} %copy-done.6, bf16[256,768]{1,0:T(8,128)(2,1)} %copy-done.12, bf16[256,768]{1,0:T(8,128)(2,1)} %copy-done.13, bf16[256,768]{1,0:T(8,128)(2,1)} %copy-done.16, bf16[256,768]{1,0:T(8,128)(2,1)} %collective-permute-done.2.refs_4_, bf16[256,768]{1,0:T(8,128)(2,1)} %copy-done.15, ...), custom_call_target="tpu_custom_call" | custom-call | flops 1 | bytes 1 | tf_op jit(solution)/shard_map/pallas_call | solution.py:452
  336.5 1.5 collective-permute-start.21
  338.0 1.4 collective-permute-start.22
  339.4 2.0 collective-permute-start.23
  343.2 1.5 collective-permute-done.22
  346.6 16.8 %collective-permute-done.23 = bf16[384,768]{1,0:T(8,128)(2,1)} collective-permute-done((bf16[384,768]{1,0:T(8,128)(2,1)}, bf16[384,768]{1,0:T(8,128)(2,1)}, u32[]{:S(2)}, u32[]{:S(2)}) %collective-permute-start.23) | collective-permute-done | bytes 589856 | tf_op jit(solution)/shard_map/ppermute | solution.py:626
  363.3 11.8 %collective-permute-done.24 = bf16[384,768]{1,0:T(8,128)(2,1)} collective-permute-done((bf16[384,768]{1,0:T(8,128)(2,1)}, bf16[384,768]{1,0:T(8,128)(2,1)}, u32[]{:S(2)}, u32[]{:S(2)}) %collective-permute-start.24) | collective-permute-done | bytes 589856 | tf_op jit(solution)/shard_map/ppermute | solution.py:626
  375.1 6.7 %all-to-all-start.9 = ((bf16[8,24,1152]{2,1,0:T(8,128)(2,1)}), bf16[8,24,1152]{2,1,0:T(8,128)(2,1)}, u32[]{:S(2)}, u32[]{:S(2)}) async-start(bf16[8,24,1152]{2,1,0:T(8,128)(2,1)} %pad_maximum_fusion.1), calls=%async_computation.9 | async-start | bytes 884736 | tf_op jit(solution)/shard_map/all_to_all | solution.py:564
  381.8 2.9 collective-permute-start.25
  384.7 5.2 %shard_map.387 = (f32[256,768]{1,0:T(8,128)}, f32[1,768]{1,0:T(1,128)}) custom-call(bf16[8,256,384]{2,1,0:T(8,128)(2,1)} %all-to-all-done.8.pieces_ref, bf16[768,2304]{1,0:T(8,128)(2,1)} %all-gather.2.cloned.1.call-done.matrix_ref, bf16[256,768]{1,0:T(8,128)(2,1)} %bitcast.185, f32[1,768]{1,0:T(1,128)} %get-tuple-element.278.gain_ref, f32[256,768]{1,0:T(8,128)} %copy-done.1), custom_call_target="tpu_custom_call" | custom-call | flops 1 | bytes 1 | tf_op jit(solution)/shard_map/pallas_call | solution.py:499
  391.2 3.7 multiply_reduce_fusion
  395.0 12.4 %collective-permute-done.25 = bf16[192,768]{1,0:T(8,128)(2,1)} collective-permute-done((bf16[192,768]{1,0:T(8,128)(2,1)}, bf16[192,768]{1,0:T(8,128)(2,1)}, u32[]{:S(2)}, u32[]{:S(2)}) %collective-permute-start.25) | collective-permute-done | bytes 294944 | tf_op jit(solution)/shard_map/ppermute | solution.py:626
  410.7 1.8 shard_map.388
  414.6 3.4 all-to-all-start.10
  419.4 1.6 fusion.60
  421.0 6.4 %all-to-all-done.10 = f32[32,1,1664]{2,1,0:T(1,128)} async-done(((f32[32,1,1664]{2,1,0:T(1,128)}), f32[32,1,1664]{2,1,0:T(1,128)}, u32[]{:S(2)}, u32[]{:S(2)}) %all-to-all-start.10) | async-done | bytes 213024 | tf_op jit(solution)/shard_map/all_to_all | solution.py:564
  431.6 9.2 %shard_map.389 = (f32[24,2304]{1,0:T(8,128)}, f32[24,2304]{1,0:T(8,128)}, f32[24,2304]{1,0:T(8,128)}, f32[24,768]{1,0:T(8,128)}, f32[24,768]{1,0:T(8,128)}, /*in...) custom-call(f32[1]{0:T(128)} %bitcast.58.factor_ref, ...), custom_call_target="tpu_custom_call" | custom-call | flops 13271040 | bytes 18579456 | tf_op jit(solution)/shard_map/pallas_call | solution.py:590
  (170 shorter events, 51.4 us)
Async XLA Ops:
  8.1 7.0 %copy-start.17 = (bf16[24,2304]{1,0:T(8,128)(2,1)}, bf16[24,2304]{1,0:T(8,128)(2,1)S(1)}, u32[]{:S(2)}) copy-start(bf16[24,2304]{1,0:T(8,128)(2,1)S(1)} %convert_element_type.126) | copy-start | bytes 331780
  8.3 14.2 %copy-start.2 = (bf16[1,256,768]{2,1,0:T(8,128)(2,1)S(1)}, bf16[1,256,768]{2,1,0:T(8,128)(2,1)}, u32[]{:S(2)}) copy-start(bf16[1,256,768]{2,1,0:T(8,128)(2,1)} %param.23) | copy-start | bytes 1179652
  11.2 11.4 %copy-start.27 = (f32[2,768]{1,0:T(2,128)S(1)}, f32[2,768]{1,0:T(2,128)}, u32[]{:S(2)}) copy-start(f32[2,768]{1,0:T(2,128)} %param.31) | copy-start | bytes 18436
  15.1 14.3 %copy-start.4 = (f32[1,384,768]{2,1,0:T(8,128)S(1)}, f32[1,384,768]{2,1,0:T(8,128)}, u32[]{:S(2)}) copy-start(f32[1,384,768]{2,1,0:T(8,128)} %param.29) | copy-start | bytes 3538948
  15.1 40.3 %all-to-all-start = ((bf16[8,32,1152]{2,1,0:T(8,128)(2,1)}), bf16[8,32,1152]{2,1,0:T(8,128)(2,1)S(1)}, u32[]{:S(2)}, u32[]{:S(2)}) async-start(bf16[8,32,1152]{2,1,0:T(8,128)(2,1)} %fusion.47), calls=%async_computation | async-start | bytes 1179648 | tf_op jit(solution)/shard_map/all_to_all | solution.py:564
  23.4 6.8 %copy-start.6 = (bf16[256,768]{1,0:T(8,128)(2,1)}, bf16[256,768]{1,0:T(8,128)(2,1)S(1)}, u32[]{:S(2)}) copy-start(bf16[256,768]{1,0:T(8,128)(2,1)S(1)} %fusion.6.refs_0_) | copy-start | bytes 1179652
  23.5 16.2 %collective-permute-start = (bf16[256,768]{1,0:T(8,128)(2,1)S(1)}, bf16[256,768]{1,0:T(8,128)(2,1)S(1)}, u32[]{:S(2)}, u32[]{:S(2)}) collective-permute-start(bf16[256,768]{1,0:T(8,128)(2,1)S(1)} %fusion.6.refs_0_), channel_id=1, source_target_pairs={{0,4},{4,0},{8,12},{12,8},{16,20},{20,16},{24,28},{28,24},{1,5},{5... | collective-permute-start | bytes 1179656 | tf_op jit(solution)/shard_map/ppermute | solution.py:611
  25.5 23.5 %collective-permute-start.1 = (bf16[256,768]{1,0:T(8,128)(2,1)S(1)}, bf16[256,768]{1,0:T(8,128)(2,1)S(1)}, u32[]{:S(2)}, u32[]{:S(2)}) collective-permute-start(bf16[256,768]{1,0:T(8,128)(2,1)S(1)} %fusion.6.refs_0_), channel_id=1, source_target_pairs={{0,8},{4,12},{8,0},{12,4},{16,24},{20,28},{24,16},{28,20},{1,9},{5... | collective-permute-start | bytes 1179656 | tf_op jit(solution)/shard_map/ppermute | solution.py:611
  27.0 28.4 %collective-permute-start.2 = (bf16[256,768]{1,0:T(8,128)(2,1)S(1)}, bf16[256,768]{1,0:T(8,128)(2,1)}, u32[]{:S(2)}, u32[]{:S(2)}) collective-permute-start(bf16[256,768]{1,0:T(8,128)(2,1)S(1)} %fusion.6.refs_0_), channel_id=1, source_target_pairs={{0,16},{4,20},{8,24},{12,28},{16,0},{20,4},{24,8},{28,12},{1,17},{... | collective-permute-start | bytes 1179656 | tf_op jit(solution)/shard_map/ppermute | solution.py:611
  39.6 9.5 %copy-start.12 = (bf16[256,768]{1,0:T(8,128)(2,1)}, bf16[256,768]{1,0:T(8,128)(2,1)S(1)}, u32[]{:S(2)}) copy-start(bf16[256,768]{1,0:T(8,128)(2,1)S(1)} %collective-permute-done.refs_1_) | copy-start | bytes 1179652
  55.4 1.4 copy-start.8
  56.8 3.7 copy-start.28
  56.8 25.6 %copy-start.10 = (bf16[1,256,768]{2,1,0:T(8,128)(2,1)S(1)}, bf16[1,256,768]{2,1,0:T(8,128)(2,1)}, u32[]{:S(2)}) copy-start(bf16[1,256,768]{2,1,0:T(8,128)(2,1)} %param.24) | copy-start | bytes 1179652
  56.8 35.8 %all-to-all-start.1 = ((bf16[4,8,24,1152]{3,2,1,0:T(8,128)(2,1)}), bf16[4,8,24,1152]{3,2,1,0:T(8,128)(2,1)S(1)}, u32[]{:S(2)}, u32[]{:S(2)}) async-start(bf16[4,8,24,1152]{3,2,1,0:T(8,128)(2,1)} %broadcast_in_dim.24), calls=%async_computation.1 | async-start | bytes 3538944 | tf_op jit(solution)/shard_map/all_to_all | solution.py:564
  60.5 23.4 %copy-start.5 = (f32[1,384,768]{2,1,0:T(8,128)S(1)}, f32[1,384,768]{2,1,0:T(8,128)}, u32[]{:S(2)}) copy-start(f32[1,384,768]{2,1,0:T(8,128)} %param.30) | copy-start | bytes 3538948
  62.1 18.6 %collective-permute-start.5 = (bf16[256,768]{1,0:T(8,128)(2,1)}, bf16[256,768]{1,0:T(8,128)(2,1)S(1)}, u32[]{:S(2)}, u32[]{:S(2)}) collective-permute-start(bf16[256,768]{1,0:T(8,128)(2,1)} %collective-permute-done.2.refs_4_), channel_id=1, source_target_pairs={{0,8},{4,12},{8,0},{12,4},{16,24},{20,28},{24,16},{28,20},{1,9},{5... | collective-permute-start | bytes 1179656 | tf_op jit(solution)/shard_map/ppermute | solution.py:611
  62.2 29.5 %collective-permute-start.7 = (bf16[384,768]{1,0:T(8,128)(2,1)}, bf16[384,768]{1,0:T(8,128)(2,1)S(1)}, u32[]{:S(2)}, u32[]{:S(2)}) collective-permute-start(bf16[384,768]{1,0:T(8,128)(2,1)} %bitcast_convert_fusion.1.refs_0_), channel_id=1, source_target_pairs={{16,0},{0,16},{17,1},{1,17},{18,2},{2,18},{19,3},{3,19},{20,4},{4,... | collective-permute-start | bytes 1769480 | tf_op jit(solution)/shard_map/ppermute | solution.py:617
  64.1 20.7 %collective-permute-start.4 = (bf16[256,768]{1,0:T(8,128)(2,1)}, bf16[256,768]{1,0:T(8,128)(2,1)S(1)}, u32[]{:S(2)}, u32[]{:S(2)}) collective-permute-start(bf16[256,768]{1,0:T(8,128)(2,1)} %collective-permute-done.2.refs_4_), channel_id=1, source_target_pairs={{0,4},{4,0},{8,12},{12,8},{16,20},{20,16},{24,28},{28,24},{1,5},{5... | collective-permute-start | bytes 1179656 | tf_op jit(solution)/shard_map/ppermute | solution.py:611
  65.8 19.0 %collective-permute-start.3 = (bf16[256,768]{1,0:T(8,128)(2,1)}, bf16[256,768]{1,0:T(8,128)(2,1)S(1)}, u32[]{:S(2)}, u32[]{:S(2)}) collective-permute-start(bf16[256,768]{1,0:T(8,128)(2,1)} %copy-done.13), channel_id=1, source_target_pairs={{0,4},{4,0},{8,12},{12,8},{16,20},{20,16},{24,28},{28,24},{1,5},{5... | collective-permute-start | bytes 1179656 | tf_op jit(solution)/shard_map/ppermute | solution.py:611
  80.7 4.1 copy-start.14
  80.7 11.9 %collective-permute-start.6 = (bf16[256,768]{1,0:T(8,128)(2,1)S(1)}, bf16[256,768]{1,0:T(8,128)(2,1)}, u32[]{:S(2)}, u32[]{:S(2)}) collective-permute-start(bf16[256,768]{1,0:T(8,128)(2,1)S(1)} %collective-permute-done.5.refs_6_), channel_id=1, source_target_pairs={{0,4},{4,0},{8,12},{12,8},{16,20},{20,16},{24,28},{28,24},{1,5},{5... | collective-permute-start | bytes 1179656 | tf_op jit(solution)/shard_map/ppermute | solution.py:611
  84.8 7.0 %copy-start.16 = (bf16[256,768]{1,0:T(8,128)(2,1)}, bf16[256,768]{1,0:T(8,128)(2,1)S(1)}, u32[]{:S(2)}) copy-start(bf16[256,768]{1,0:T(8,128)(2,1)S(1)} %collective-permute-done.3.refs_3_) | copy-start | bytes 1179652
  84.8 6.9 %copy-start.15 = (bf16[256,768]{1,0:T(8,128)(2,1)}, bf16[256,768]{1,0:T(8,128)(2,1)S(1)}, u32[]{:S(2)}) copy-start(bf16[256,768]{1,0:T(8,128)(2,1)S(1)} %collective-permute-done.4.refs_5_) | copy-start | bytes 1179652
  91.7 0.8 copy-start.21
  95.0 44.8 %all-to-all-start.2 = ((bf16[8,128,768]{2,1,0:T(8,128)(2,1)}), bf16[8,128,768]{2,1,0:T(8,128)(2,1)S(1)}, u32[]{:S(2)}, u32[]{:S(2)}) async-start(bf16[8,128,768]{2,1,0:T(8,128)(2,1)} %bitcast.183), calls=%async_computation.2 | async-start | bytes 3145728 | tf_op jit(solution)/shard_map/all_to_all | solution.py:564
  98.6 35.1 %collective-permute-start.10 = (bf16[384,768]{1,0:T(8,128)(2,1)}, bf16[384,768]{1,0:T(8,128)(2,1)}, u32[]{:S(2)}, u32[]{:S(2)}) collective-permute-start(bf16[384,768]{1,0:T(8,128)(2,1)} %bitcast_convert_fusion.refs_4_), channel_id=1, source_target_pairs={{4,0},{0,4},{5,1},{1,5},{6,2},{2,6},{7,3},{3,7},{12,8},{8,12},{13,... | collective-permute-start | bytes 1769480 | tf_op jit(solution)/shard_map/ppermute | solution.py:617
  100.1 33.6 %collective-permute-start.8 = (bf16[384,768]{1,0:T(8,128)(2,1)}, bf16[384,768]{1,0:T(8,128)(2,1)}, u32[]{:S(2)}, u32[]{:S(2)}) collective-permute-start(bf16[384,768]{1,0:T(8,128)(2,1)} %bitcast_convert_fusion.refs_4_), channel_id=1, source_target_pairs={{16,0},{0,16},{17,1},{1,17},{18,2},{2,18},{19,3},{3,19},{20,4},{4,... | collective-permute-start | bytes 1769480 | tf_op jit(solution)/shard_map/ppermute | solution.py:617
  101.6 32.2 %collective-permute-start.11 = (bf16[384,768]{1,0:T(8,128)(2,1)}, bf16[384,768]{1,0:T(8,128)(2,1)}, u32[]{:S(2)}, u32[]{:S(2)}) collective-permute-start(bf16[384,768]{1,0:T(8,128)(2,1)} %copy-done.21), channel_id=1, source_target_pairs={{4,0},{0,4},{5,1},{1,5},{6,2},{2,6},{7,3},{3,7},{12,8},{8,12},{13,... | collective-permute-start | bytes 1769480 | tf_op jit(solution)/shard_map/ppermute | solution.py:617
  102.1 37.7 %collective-permute-start.9 = (bf16[384,768]{1,0:T(8,128)(2,1)}, bf16[384,768]{1,0:T(8,128)(2,1)}, u32[]{:S(2)}, u32[]{:S(2)}) collective-permute-start(bf16[384,768]{1,0:T(8,128)(2,1)} %bitcast_convert_fusion.1.refs_0_), channel_id=1, source_target_pairs={{4,0},{0,4},{5,1},{1,5},{6,2},{2,6},{7,3},{3,7},{12,8},{8,12},{13,... | collective-permute-start | bytes 1769480 | tf_op jit(solution)/shard_map/ppermute | solution.py:617
  139.8 27.4 %copy-start = (bf16[8,128,768]{2,1,0:T(8,128)(2,1)}, bf16[8,128,768]{2,1,0:T(8,128)(2,1)S(1)}, u32[]{:S(2)}) copy-start(bf16[8,128,768]{2,1,0:T(8,128)(2,1)S(1)} %all-to-all-done.2) | copy-start | bytes 4718596
  139.8 25.1 %all-to-all-start.3 = ((bf16[8,256,128]{2,1,0:T(8,128)(2,1)}), bf16[8,256,128]{2,1,0:T(8,128)(2,1)S(1)}, u32[]{:S(2)}, u32[]{:S(2)}) async-start(bf16[8,256,128]{2,1,0:T(8,128)(2,1)} %bitcast.205), calls=%async_computation.3 | async-start | bytes 1048576 | tf_op jit(solution)/shard_map/all_to_all | solution.py:564
  144.7 96.2 %all-gather.2.cloned.1.call-start = ((), (), s32[]{:S(2)}) async-start(), calls=%async_computation.11 | async-start | bytes 3649536 | tf_op jit(solution)/shard_map/all_gather | solution.py:787
  144.8 20.2 %collective-permute-start.12 = (bf16[384,768]{1,0:T(8,128)(2,1)}, bf16[384,768]{1,0:T(8,128)(2,1)}, u32[]{:S(2)}, u32[]{:S(2)}) collective-permute-start(bf16[384,768]{1,0:T(8,128)(2,1)} %collective-permute-done.8.refs_5_), channel_id=1, source_target_pairs={{4,0},{0,4},{5,1},{1,5},{6,2},{2,6},{7,3},{3,7},{12,8},{8,12},{13,... | collective-permute-start | bytes 1769480 | tf_op jit(solution)/shard_map/ppermute | solution.py:617
  165.7 1.5 copy-start.23
  165.7 1.9 copy-start.31
  167.7 1.0 copy-start.3
  168.3 1.0 copy-start.9
  213.2 27.7 %all-to-all-start.5 = ((bf16[8,128,768]{2,1,0:T(8,128)(2,1)}), bf16[8,128,768]{2,1,0:T(8,128)(2,1)}, u32[]{:S(2)}, u32[]{:S(2)}) async-start(bf16[8,128,768]{2,1,0:T(8,128)(2,1)} %bitcast.200), calls=%async_computation.5 | async-start | bytes 3145728 | tf_op jit(solution)/shard_map/all_to_all | solution.py:564
  224.2 15.8 %collective-permute-start.13 = (bf16[384,768]{1,0:T(8,128)(2,1)}, bf16[384,768]{1,0:T(8,128)(2,1)S(1)}, u32[]{:S(2)}, u32[]{:S(2)}) collective-permute-start(bf16[384,768]{1,0:T(8,128)(2,1)} %get-tuple-element.167), channel_id=1, source_target_pairs={{0,4},{4,0},{1,5},{5,1},{2,6},{6,2},{3,7},{7,3},{8,12},{12,8},{9,1... | collective-permute-start | bytes 1769480 | tf_op jit(solution)/shard_map/ppermute | solution.py:626
  242.5 1.0 copy-start.11
  243.8 13.1 %copy-start.1 = (f32[256,768]{1,0:T(8,128)}, f32[256,768]{1,0:T(8,128)S(1)}, u32[]{:S(2)}) copy-start(f32[256,768]{1,0:T(8,128)S(1)} %multiply_add_fusion.residual_ref) | copy-start | bytes 2359300
  249.7 25.6 %all-to-all-start.6 = ((bf16[8,256,128]{2,1,0:T(8,128)(2,1)}), bf16[8,256,128]{2,1,0:T(8,128)(2,1)S(1)}, u32[]{:S(2)}, u32[]{:S(2)}) async-start(bf16[8,256,128]{2,1,0:T(8,128)(2,1)} %fusion.48), calls=%async_computation.6 | async-start | bytes 1048576 | tf_op jit(solution)/shard_map/all_to_all | solution.py:564
  254.9 20.4 %collective-permute-start.14 = (bf16[384,768]{1,0:T(8,128)(2,1)}, bf16[384,768]{1,0:T(8,128)(2,1)}, u32[]{:S(2)}, u32[]{:S(2)}) collective-permute-start(bf16[384,768]{1,0:T(8,128)(2,1)} %get-tuple-element.181), channel_id=1, source_target_pairs={{0,4},{4,0},{1,5},{5,1},{2,6},{6,2},{3,7},{7,3},{8,12},{12,8},{9,1... | collective-permute-start | bytes 1769480 | tf_op jit(solution)/shard_map/ppermute | solution.py:626
  276.1 49.0 %all-to-all-start.7 = ((bf16[8,128,768]{2,1,0:T(8,128)(2,1)}), bf16[8,128,768]{2,1,0:T(8,128)(2,1)S(1)}, u32[]{:S(2)}, u32[]{:S(2)}) async-start(bf16[8,128,768]{2,1,0:T(8,128)(2,1)} %bitcast.182), calls=%async_computation.7 | async-start | bytes 3145728 | tf_op jit(solution)/shard_map/all_to_all | solution.py:564
  279.7 4.8 %copy-start.19 = (f32[384,768]{1,0:T(8,128)S(1)}, f32[384,768]{1,0:T(8,128)}, u32[]{:S(2)}) copy-start(f32[384,768]{1,0:T(8,128)} %get-tuple-element.191) | copy-start | bytes 3538948
  282.2 32.9 %collective-permute-start.15 = (bf16[384,768]{1,0:T(8,128)(2,1)}, bf16[384,768]{1,0:T(8,128)(2,1)}, u32[]{:S(2)}, u32[]{:S(2)}) collective-permute-start(bf16[384,768]{1,0:T(8,128)(2,1)} %add_convert_fusion.1), channel_id=1, source_target_pairs={{0,16},{16,0},{1,17},{17,1},{2,18},{18,2},{3,19},{19,3},{4,20},{20... | collective-permute-start | bytes 1769480 | tf_op jit(solution)/shard_map/ppermute | solution.py:626
  286.6 37.8 %collective-permute-start.16 = (bf16[192,768]{1,0:T(8,128)(2,1)}, bf16[192,768]{1,0:T(8,128)(2,1)S(1)}, u32[]{:S(2)}, u32[]{:S(2)}) collective-permute-start(bf16[192,768]{1,0:T(8,128)(2,1)} %get-tuple-element.250), channel_id=1, source_target_pairs={{0,16},{16,0},{1,17},{17,1},{2,18},{18,2},{3,19},{19,3},{4,20},{20... | collective-permute-start | bytes 884744 | tf_op jit(solution)/shard_map/ppermute | solution.py:626
  287.1 37.2 %collective-permute-start.17 = (bf16[8,24,768]{2,1,0:T(8,128)(2,1)}, bf16[8,24,768]{2,1,0:T(8,128)(2,1)}, u32[]{:S(2)}, u32[]{:S(2)}) collective-permute-start(bf16[8,24,768]{2,1,0:T(8,128)(2,1)} %get-tuple-element.193), channel_id=1, source_target_pairs={{0,1},{1,2},{2,3},{3,0},{4,5},{5,6},{6,7},{7,4},{8,9},{9,10},{10,1... | collective-permute-start | bytes 884744 | tf_op jit(solution)/shard_map/ppermute | solution.py:626
  287.1 37.2 %collective-permute-start.18 = (bf16[8,24,768]{2,1,0:T(8,128)(2,1)}, bf16[8,24,768]{2,1,0:T(8,128)(2,1)}, u32[]{:S(2)}, u32[]{:S(2)}) collective-permute-start(bf16[8,24,768]{2,1,0:T(8,128)(2,1)} %get-tuple-element.194), channel_id=1, source_target_pairs={{0,2},{1,3},{2,0},{3,1},{4,6},{5,7},{6,4},{7,5},{8,10},{9,11},{10,... | collective-permute-start | bytes 884744 | tf_op jit(solution)/shard_map/ppermute | solution.py:626
  289.2 35.9 %collective-permute-start.19 = (bf16[8,24,768]{2,1,0:T(8,128)(2,1)}, bf16[8,24,768]{2,1,0:T(8,128)(2,1)}, u32[]{:S(2)}, u32[]{:S(2)}) collective-permute-start(bf16[8,24,768]{2,1,0:T(8,128)(2,1)} %get-tuple-element.195), channel_id=1, source_target_pairs={{0,3},{1,0},{2,1},{3,2},{4,7},{5,4},{6,5},{7,6},{8,11},{9,8},{10,9... | collective-permute-start | bytes 884744 | tf_op jit(solution)/shard_map/ppermute | solution.py:626
  325.1 50.1 %all-to-all-start.8 = ((bf16[8,256,384]{2,1,0:T(8,128)(2,1)}), bf16[8,256,384]{2,1,0:T(8,128)(2,1)}, u32[]{:S(2)}, u32[]{:S(2)}) async-start(bf16[8,256,384]{2,1,0:T(8,128)(2,1)} %bitcast.199), calls=%async_computation.8 | async-start | bytes 3145728 | tf_op jit(solution)/shard_map/all_to_all | solution.py:564
  336.4 6.3 %collective-permute-start.20 = (bf16[8,24,384]{2,1,0:T(8,128)(2,1)S(1)}, bf16[8,24,384]{2,1,0:T(8,128)(2,1)S(1)}, u32[]{:S(2)}, u32[]{:S(2)}) collective-permute-start(bf16[8,24,384]{2,1,0:T(8,128)(2,1)S(1)} %get-tuple-element.251), channel_id=1, source_target_pairs={{0,1},{1,2},{2,3},{3,0},{4,5},{5,6},{6,7},{7,4},{8,9},{9,10},{10,1... | collective-permute-start | bytes 442376 | tf_op jit(solution)/shard_map/ppermute | solution.py:626
  336.5 6.7 %collective-permute-start.21 = (bf16[8,24,384]{2,1,0:T(8,128)(2,1)S(1)}, bf16[8,24,384]{2,1,0:T(8,128)(2,1)S(1)}, u32[]{:S(2)}, u32[]{:S(2)}) collective-permute-start(bf16[8,24,384]{2,1,0:T(8,128)(2,1)S(1)} %get-tuple-element.253), channel_id=1, source_target_pairs={{0,2},{1,3},{2,0},{3,1},{4,6},{5,7},{6,4},{7,5},{8,10},{9,11},{10,... | collective-permute-start | bytes 442376 | tf_op jit(solution)/shard_map/ppermute | solution.py:626
  338.0 6.7 %collective-permute-start.22 = (bf16[8,24,384]{2,1,0:T(8,128)(2,1)S(1)}, bf16[8,24,384]{2,1,0:T(8,128)(2,1)S(1)}, u32[]{:S(2)}, u32[]{:S(2)}) collective-permute-start(bf16[8,24,384]{2,1,0:T(8,128)(2,1)S(1)} %get-tuple-element.252), channel_id=1, source_target_pairs={{0,3},{1,0},{2,1},{3,2},{4,7},{5,4},{6,5},{7,6},{8,11},{9,8},{10,9... | collective-permute-start | bytes 442376 | tf_op jit(solution)/shard_map/ppermute | solution.py:626
  339.4 23.9 %collective-permute-start.23 = (bf16[384,768]{1,0:T(8,128)(2,1)}, bf16[384,768]{1,0:T(8,128)(2,1)}, u32[]{:S(2)}, u32[]{:S(2)}) collective-permute-start(bf16[384,768]{1,0:T(8,128)(2,1)} %get-tuple-element.202), channel_id=1, source_target_pairs={{0,4},{4,0},{1,5},{5,1},{2,6},{6,2},{3,7},{7,3},{8,12},{12,8},{9,1... | collective-permute-start | bytes 1769480 | tf_op jit(solution)/shard_map/ppermute | solution.py:626
  341.4 33.7 %collective-permute-start.24 = (bf16[384,768]{1,0:T(8,128)(2,1)}, bf16[384,768]{1,0:T(8,128)(2,1)}, u32[]{:S(2)}, u32[]{:S(2)}) collective-permute-start(bf16[384,768]{1,0:T(8,128)(2,1)} %get-tuple-element.203), channel_id=1, source_target_pairs={{0,4},{4,0},{1,5},{5,1},{2,6},{6,2},{3,7},{7,3},{8,12},{12,8},{9,1... | collective-permute-start | bytes 1769480 | tf_op jit(solution)/shard_map/ppermute | solution.py:626
  375.1 35.5 %all-to-all-start.9 = ((bf16[8,24,1152]{2,1,0:T(8,128)(2,1)}), bf16[8,24,1152]{2,1,0:T(8,128)(2,1)}, u32[]{:S(2)}, u32[]{:S(2)}) async-start(bf16[8,24,1152]{2,1,0:T(8,128)(2,1)} %pad_maximum_fusion.1), calls=%async_computation.9 | async-start | bytes 884736 | tf_op jit(solution)/shard_map/all_to_all | solution.py:564
  381.8 25.5 %collective-permute-start.25 = (bf16[192,768]{1,0:T(8,128)(2,1)}, bf16[192,768]{1,0:T(8,128)(2,1)}, u32[]{:S(2)}, u32[]{:S(2)}) collective-permute-start(bf16[192,768]{1,0:T(8,128)(2,1)} %get-tuple-element.213), channel_id=1, source_target_pairs={{0,16},{16,0},{1,17},{17,1},{2,18},{18,2},{3,19},{19,3},{4,20},{20... | collective-permute-start | bytes 884744 | tf_op jit(solution)/shard_map/ppermute | solution.py:626
  384.7 6.5 %copy-start.18 = (f32[384,768]{1,0:T(8,128)S(1)}, f32[384,768]{1,0:T(8,128)}, u32[]{:S(2)}) copy-start(f32[384,768]{1,0:T(8,128)} %get-tuple-element.214) | copy-start | bytes 3538948
  391.2 16.2 %copy-start.25 = (bf16[192,768]{1,0:T(8,128)(2,1)S(1)}, bf16[192,768]{1,0:T(8,128)(2,1)}, u32[]{:S(2)}) copy-start(bf16[192,768]{1,0:T(8,128)(2,1)} %copy-done.24) | copy-start | bytes 884740
  414.6 12.7 %all-to-all-start.10 = ((f32[32,1,1664]{2,1,0:T(1,128)}), f32[32,1,1664]{2,1,0:T(1,128)}, u32[]{:S(2)}, u32[]{:S(2)}) async-start(f32[32,1,1664]{2,1,0:T(1,128)} %broadcast_in_dim.60), calls=%async_computation.10 | async-start | bytes 425984 | tf_op jit(solution)/shard_map/all_to_all | solution.py:564
  419.4 11.6 %copy-start.29 = (f32[2,768]{1,0:T(2,128)S(1)}, f32[2,768]{1,0:T(2,128)}, u32[]{:S(2)}) copy-start(f32[2,768]{1,0:T(2,128)} %param.41) | copy-start | bytes 18436
  419.4 11.6 %copy-start.30 = (f32[2,768]{1,0:T(2,128)S(1)}, f32[2,768]{1,0:T(2,128)}, u32[]{:S(2)}) copy-start(f32[2,768]{1,0:T(2,128)} %param.40) | copy-start | bytes 18436
  429.6 11.3 %copy-start.26 = (f32[2,768]{1,0:T(2,128)}, f32[2,768]{1,0:T(2,128)S(1)}, u32[]{:S(2)}) copy-start(f32[2,768]{1,0:T(2,128)S(1)} %reshape.282) | copy-start | bytes 18436
  (5 other events, 3.9 us)
Sparse Core Ops, SparseCore 0:
  165.9 61.5 all-gather.1

commit v3 on v2

--- a/solution.py
+++ b/solution.py
@@ -849,32 +849,23 @@
 
     output_term = jnp.einsum("tc,te->ce", attend_out, branch_grad, preferred_element_type=F32)
     output_own, output_away = group_rows(output_term.astype(BF16))
-    row_grad, produced, down_side, up_side, up_part, *output_away = together(
-        row_grad, produced, down_side, up_side, up_part, *output_away
-    )
     output_away = to_owners(output_away, "exp")
-    up_head, up_tail = [
-        list(part)
-        for part in zip(
-            *(
-                jnp.split(block, 2, axis=0)
-                for block in add_all(up_peer, [up_part]).astype(BF16).reshape(peers - 1, -1, width)
-            ),
-            strict=True,
-        )
-    ]
-    up_head = to_owners(up_head, "hi")
+    row_grad, produced, down_side, up_side, up_part, *held = together(
+        row_grad, produced, down_side, up_side, up_part, *down_hi, *output_away
+    )
+    down_hi, output_away = held[: peers - 1], held[peers - 1 :]
+    (down_early,) = to_owners([down_side], "in")
+    (up_early,) = to_owners([up_side], "in")
+    up_hi = hi_parts(add_all(up_peer, [up_part]))
     returned = send_back(produced)
     grad_qkv, grad_lying = attend_back(
         active, order, pair, documents, stat, row_grad, mixed_full, row_count, scaling
     )
-    grad_qkv, grad_lying, returned, down_side, up_side, *held = together(
-        grad_qkv, grad_lying, returned, down_side, up_side, *down_hi, *up_head, *output_away
-    )
-    down_hi, up_head = held[: peers - 1], held[peers - 1 : 2 * peers - 2]
-    output_away = held[2 * peers - 2 :]
-    (down_early,) = to_owners([down_side], "in")
-    (up_early,) = to_owners([up_side], "in")
+    grad_qkv, grad_lying, returned, down_early, up_early, *up_hi = together(
+        grad_qkv, grad_lying, returned, down_early, up_early, *up_hi
+    )
+    down_grad = add_all(down_own, [down_early, *down_hi])[None]
+    up_grad = add_all(up_own, [up_early, *up_hi])[None]
     block_output = (middle + collect(returned)).astype(BF16)[None]
 
     column_own, column_away = group_rows(column_terms(row_blocks, grad_lying))
@@ -885,17 +876,8 @@
         ],
         axis=2,
     )
-    grad_pieces, dense_rows, down_early, up_early, *up_tail = together(
-        to_tokens(grad_qkv), dense_rows, down_early, up_early, *up_tail
-    )
-    up_tail = to_owners(up_tail, "hi")
+    grad_pieces, dense_rows = together(to_tokens(grad_qkv), dense_rows)
     projection_grad, output_grad, dense_square = dense_grads(swap(dense_rows, SEQ), starts)
-    down_grad = add_all(down_own, [down_early, *down_hi])[None]
-    up_half = up_own.shape[0] // 2
-    up_grad = add_all(up_own, [up_early])
-    up_grad = jnp.concatenate(
-        [add_all(up_grad[:up_half], up_head), add_all(up_grad[up_half:], up_tail)], axis=0
-    )[None]
     input_grad, gain_first_part = close_norm(
         grad_pieces, starts, projection_full, tokens[0], gain_first[None], residual_grad
     )

time: 451 us -> 438 us (0.971)
  starting transfers between devices: 83.1 us -> 76.5 us
  waiting for transfers between devices: 147 us -> 141 us
    ppermute x13 -> x12, waiting for transfers between devices: 69.5 us -> 38.1 us  [to_owners(): lax.ppermute(block, axis, [(i, (i + step) % size) for i in range(size)])]
    all_to_all x10, waiting for transfers between devices: 7.24 us -> 31.8 us  [swap(): return lax.all_to_all(value, axes, split_axis=0, concat_axis=0, tiled=True)]
    ppermute x13 -> x12, starting transfers between devices: 17 us -> 13.6 us  [to_owners(): lax.ppermute(block, axis, [(i, (i + step) % size) for i in range(size)])]
    unnamed x72 -> x96, local copies, waits for them, and re-layouts: 10 us -> 11 us
  transfers between devices with their start and end apart: 37 -> 36, of which waited for: 17 -> 24; matrix products, arithmetic and copies ran while one was open for 8% -> 9% of each run, Pallas kernels for 21% -> 22%
where the time goes in v3:
time: 438 us; the launch traced here: 436 us
  waiting for transfers between devices  141 us (32%)
  Pallas kernels  105 us (24%)
  starting transfers between devices  76.5 us (17%)
  other arithmetic  30.3 us (7%)
  local copies, waits for them, and re-layouts  29.1 us (7%)
  blocking collectives  27.6 us (6%)
  between operations  18.4 us (4%)
  matrix products  7.4 us (2%)
    all_to_all x10, starting transfers between devices, swap(): return lax.all_to_all(value, axes, split_axis=0, concat_axis=0, tiled=True)  44 us
    ppermute x7, waiting for transfers between devices, flip(): lax.ppermute(value, SEQ, [(index, index ^ bits) for index in range(count)])  39.9 us
    ppermute x12, waiting for transfers between devices, to_owners(): lax.ppermute(block, axis, [(i, (i + step) % size) for i in range(size)])  38.1 us
    all_to_all x10, waiting for transfers between devices, swap(): return lax.all_to_all(value, axes, split_axis=0, concat_axis=0, tiled=True)  31.8 us
    ppermute x6, waiting for transfers between devices, others(): lax.ppermute(value, axis, [((i + step) % size, i) for i in range(size)])  31 us
    all_to_all x1, blocking collectives, swap(): return lax.all_to_all(value, axes, split_axis=0, concat_axis=0, tiled=True)  27.6 us
    pallas_call x1, Pallas kernels, attend_back(): pl.pallas_call(functools.partial(attend_back_kernel, block=block, chunk=2...  24.4 us
    pallas_call x1, Pallas kernels, attend(): pl.pallas_call(functools.partial(attend_kernel, block=block, chunk=2 * bl...  23.1 us
  transfers between devices with their start and end apart: 36, of which 24 were waited for; matrix products, arithmetic and copies ran while one was open for 9% of the time, Pallas kernels for 22%

profile of v3, /device:TPU:0, one launch (start us, length us, event | category | flops | bytes accessed | tf_op | source)
XLA Modules:
  0.0 435.6 jit_solution(3703366241412440846)
XLA Ops:
  15.6 7.4 %all-to-all-start = ((bf16[8,32,1152]{2,1,0:T(8,128)(2,1)}), bf16[8,32,1152]{2,1,0:T(8,128)(2,1)S(1)}, u32[]{:S(2)}, u32[]{:S(2)}) async-start(bf16[8,32,1152]{2,1,0:T(8,128)(2,1)} %fusion.46), calls=%async_computation | async-start | bytes 1179648 | tf_op jit(solution)/shard_map/all_to_all | solution.py:564
  24.0 2.1 collective-permute-start
  26.1 1.5 collective-permute-start.1
  27.6 2.4 collective-permute-start.2
  30.0 10.2 %collective-permute-done.refs_1_ = bf16[256,768]{1,0:T(8,128)(2,1)S(1)} collective-permute-done((bf16[256,768]{1,0:T(8,128)(2,1)S(1)}, bf16[256,768]{1,0:T(8,128)(2,1)S(1)}, u32[]{:S(2)}, u32[]{:S(2)}) %collective-permute-start) | collective-permute-done | bytes 393248 | tf_op jit(solution)/shard_map/ppermute | solution.py:611
  40.2 9.5 %collective-permute-done.1.refs_2_ = bf16[256,768]{1,0:T(8,128)(2,1)S(1)} collective-permute-done((bf16[256,768]{1,0:T(8,128)(2,1)S(1)}, bf16[256,768]{1,0:T(8,128)(2,1)S(1)}, u32[]{:S(2)}, u32[]{:S(2)}) %collective-permute-start.1) | collective-permute-done | bytes 393248 | tf_op jit(solution)/shard_map/ppermute | solution.py:611
  49.6 6.3 %collective-permute-done.2.refs_4_ = bf16[256,768]{1,0:T(8,128)(2,1)} collective-permute-done((bf16[256,768]{1,0:T(8,128)(2,1)S(1)}, bf16[256,768]{1,0:T(8,128)(2,1)}, u32[]{:S(2)}, u32[]{:S(2)}) %collective-permute-start.2) | collective-permute-done | bytes 393248 | tf_op jit(solution)/shard_map/ppermute | solution.py:611
  56.0 1.4 broadcast_in_dim.24
  57.4 3.7 all-to-all-start.1
  61.7 2.3 reduce-window.6
  68.5 1.3 copy.66
  71.3 1.9 collective-permute-start.7
  73.8 1.7 collective-permute-start.4
  75.8 11.4 %collective-permute-done.5.refs_6_ = bf16[256,768]{1,0:T(8,128)(2,1)S(1)} collective-permute-done((bf16[256,768]{1,0:T(8,128)(2,1)}, bf16[256,768]{1,0:T(8,128)(2,1)S(1)}, u32[]{:S(2)}, u32[]{:S(2)}) %collective-permute-start.5) | collective-permute-done | bytes 393248 | tf_op jit(solution)/shard_map/ppermute | solution.py:611
  87.3 1.7 collective-permute-start.6
  89.0 2.4 convolution_convert_fusion.2
  92.4 2.1 collective-permute-done.3.refs_3_
  94.5 6.2 %collective-permute-done.7.refs_1_ = bf16[384,768]{1,0:T(8,128)(2,1)S(1)} collective-permute-done((bf16[384,768]{1,0:T(8,128)(2,1)S(1)}, bf16[384,768]{1,0:T(8,128)(2,1)S(1)}, u32[]{:S(2)}, u32[]{:S(2)}) %collective-permute-start.7) | collective-permute-done | bytes 589856 | tf_op jit(solution)/shard_map/ppermute | solution.py:617
  101.9 2.4 broadcast_in_dim.55
  104.3 3.6 all-to-all-start.2
  107.9 1.8 collective-permute-start.10
  109.7 1.6 collective-permute-start.8
  111.9 1.5 collective-permute-start.9
  119.3 23.1 %shard_map.380 = (bf16[2048,128]{1,0:T(8,128)(2,1)}, f32[2048,128]{1,0:T(8,128)}, bf16[2048,256]{1,0:T(8,128)(2,1)}, bf16[2048,256]{1,0:T(8,128)(2,1)}) custom-call(s32[2,8]{1,0:T(2,128)} %fusion.58.active_ref, s32[8]{0:T(128)} %iota_xor_fusion.order_ref, bf16[256,768]{1,0:T(8,128)(2,1)} %copy-done.8, bf16[256,768]{1,0:T(8,128)(2,1)} %copy-done.16, ...), custom_call_target="tpu_custom_call" | custom-call | flops 1 | bytes 1 | tf_op jit(solution)/shard_map/pallas_call | solution.py:278
  142.5 6.7 %collective-permute-done.9.refs_2_ = bf16[384,768]{1,0:T(8,128)(2,1)} collective-permute-done((bf16[384,768]{1,0:T(8,128)(2,1)}, bf16[384,768]{1,0:T(8,128)(2,1)}, u32[]{:S(2)}, u32[]{:S(2)}) %collective-permute-start.9) | collective-permute-done | bytes 589856 | tf_op jit(solution)/shard_map/ppermute | solution.py:617
  149.2 5.3 %all-to-all-start.3 = ((bf16[8,256,128]{2,1,0:T(8,128)(2,1)}), bf16[8,256,128]{2,1,0:T(8,128)(2,1)S(1)}, u32[]{:S(2)}, u32[]{:S(2)}) async-start(bf16[8,256,128]{2,1,0:T(8,128)(2,1)} %bitcast.204), calls=%async_computation.3 | async-start | bytes 1048576 | tf_op jit(solution)/shard_map/all_to_all | solution.py:564
  154.5 2.0 collective-permute-start.12
  156.5 18.2 %collective-permute-done.12.refs_7_ = bf16[384,768]{1,0:T(8,128)(2,1)} collective-permute-done((bf16[384,768]{1,0:T(8,128)(2,1)}, bf16[384,768]{1,0:T(8,128)(2,1)}, u32[]{:S(2)}, u32[]{:S(2)}) %collective-permute-start.12) | collective-permute-done | bytes 589856 | tf_op jit(solution)/shard_map/ppermute | solution.py:617
  174.7 1.5 slice.212
  178.8 27.6 %all_to_all.55 = bf16[8,128,768]{2,1,0:T(8,128)(2,1)} all-to-all(bf16[8,128,768]{2,1,0:T(8,128)(2,1)S(1)} %bitcast.184), channel_id=1, replica_groups=mesh['hi'=2,'lo'=2,'in'=2,'exp'=4] {'lo','exp'}, dimensions={0} | all-to-all | bytes 3145728 | tf_op jit(solution)/shard_map/all_to_all | solution.py:564
  206.4 15.6 %shard_map.381 = (bf16[1024,768]{1,0:T(8,128)(2,1)}, bf16[1024,384]{1,0:T(8,128)(2,1)}, bf16[1024,384]{1,0:T(8,128)(2,1)}, bf16[1024,384]{1,0:T(8,128)(2,1)}, bf...) custom-call(bf16[1024,768]{1,0:T(8,128)(2,1)} %bitcast.173, ...), custom_call_target="tpu_custom_call" | custom-call | flops 1 | bytes 1 | tf_op jit(solution)/shard_map/pallas_call | solution.py:372
  222.0 3.6 all-to-all-start.5
  225.6 6.7 %shard_map.382 = (bf16[384,768]{1,0:T(8,128)(2,1)}, bf16[384,768]{1,0:T(8,128)(2,1)}, f32[384,768]{1,0:T(8,128)}, f32[384,768]{1,0:T(8,128)}) custom-call(bf16[1024,768]{1,0:T(8,128)(2,1)} %bitcast.171, bf16[1024,768]{1,0:T(8,128)(2,1)} %bitcast.174, bf16[1024,384]{1,0:T(8,128)(2,1)} %get-tuple-element.157.refs_0_.refs_3_, ...), custom_call_target="tpu_custom_call" | custom-call | flops 1 | bytes 1 | tf_op jit(solution)/shard_map/pallas_call | solution.py:425
  232.9 7.2 %shard_map.383 = bf16[1024,768]{1,0:T(8,128)(2,1)} custom-call(bf16[1024,384]{1,0:T(8,128)(2,1)} %get-tuple-element.165.refs_0_.refs_2_, bf16[1024,384]{1,0:T(8,128)(2,1)} %get-tuple-element.159.refs_2_.refs_1_, bf16[1024,384]{1,0:T(8,128)(2,1)} %get-tuple-element.166.refs_2_.refs_0_, bf16[1024,384]{1,0:T(8,128)(2,1)} %get-tuple-element.157.refs_0_.refs_3_, ...), custom_call_target="tpu_custom_call" | custom-call | flops 1 | bytes 1 | tf_op jit(solution)/shard_map/pallas_call | solution.py:396
  240.0 6.6 %shard_map.384 = (bf16[384,768]{1,0:T(8,128)(2,1)}, bf16[384,768]{1,0:T(8,128)(2,1)}, f32[384,768]{1,0:T(8,128)}, f32[384,768]{1,0:T(8,128)}) custom-call(bf16[1024,768]{1,0:T(8,128)(2,1)} %bitcast.172, bf16[1024,768]{1,0:T(8,128)(2,1)} %bitcast.175, bf16[1024,384]{1,0:T(8,128)(2,1)} %get-tuple-element.166.refs_2_.refs_0_, ...), custom_call_target="tpu_custom_call" | custom-call | flops 1 | bytes 1 | tf_op jit(solution)/shard_map/pallas_call | solution.py:425
  246.7 1.5 collective-permute-done.13
  257.3 3.9 all-to-all-start.6
  262.5 3.0 collective-permute-start.15
  265.4 1.5 collective-permute-start.14
  267.6 1.6 collective-permute-start.17
  269.2 1.4 collective-permute-start.18
  270.6 5.7 %collective-permute-done.16 = bf16[8,24,768]{2,1,0:T(8,128)(2,1)S(1)} collective-permute-done((bf16[8,24,768]{2,1,0:T(8,128)(2,1)S(1)}, bf16[8,24,768]{2,1,0:T(8,128)(2,1)S(1)}, u32[]{:S(2)}, u32[]{:S(2)}) %collective-permute-start.16) | collective-permute-done | bytes 294944 | tf_op jit(solution)/shard_map/ppermute | solution.py:626
  277.5 4.7 %collective-permute-done.18 = bf16[8,24,768]{2,1,0:T(8,128)(2,1)S(1)} collective-permute-done((bf16[8,24,768]{2,1,0:T(8,128)(2,1)S(1)}, bf16[8,24,768]{2,1,0:T(8,128)(2,1)S(1)}, u32[]{:S(2)}, u32[]{:S(2)}) %collective-permute-start.18) | collective-permute-done | bytes 294944 | tf_op jit(solution)/shard_map/ppermute | solution.py:626
  282.2 18.7 %collective-permute-done.15 = bf16[384,768]{1,0:T(8,128)(2,1)S(1)} collective-permute-done((bf16[384,768]{1,0:T(8,128)(2,1)S(1)}, bf16[384,768]{1,0:T(8,128)(2,1)S(1)}, u32[]{:S(2)}, u32[]{:S(2)}) %collective-permute-start.15) | collective-permute-done | bytes 589856 | tf_op jit(solution)/shard_map/ppermute | solution.py:626
  302.5 3.6 all-to-all-start.7
  306.1 2.3 add_convert_fusion
  308.9 1.7 collective-permute-start.19
  310.9 24.4 %shard_map.385 = (bf16[2048,384]{1,0:T(8,128)(2,1)}, bf16[2048,384]{1,0:T(8,128)(2,1)}) custom-call(s32[2,8]{1,0:T(2,128)} %fusion.58.active_ref, s32[8]{0:T(128)} %iota_xor_fusion.order_ref, bf16[2048,256]{1,0:T(8,128)(2,1)} %get-tuple-element.149.pair_ref, bf16[2048,128]{1,0:T(8,128)(2,1)} %broadcast_in_dim.26.refs_9_.documents_ref, ...), custom_call_target="tpu_custom_call" | custom-call | flops 1 | bytes 1 | tf_op jit(solution)/shard_map/pallas_call | solution.py:309
  335.3 1.4 collective-permute-done.21
  337.3 1.4 all-to-all-done.7
  338.8 4.5 %all-to-all-start.8 = ((bf16[8,256,384]{2,1,0:T(8,128)(2,1)}), bf16[8,256,384]{2,1,0:T(8,128)(2,1)}, u32[]{:S(2)}, u32[]{:S(2)}) async-start(bf16[8,256,384]{2,1,0:T(8,128)(2,1)} %bitcast.199), calls=%async_computation.8 | async-start | bytes 3145728 | tf_op jit(solution)/shard_map/all_to_all | solution.py:564
  343.3 5.6 %shard_map.386 = bf16[768,384]{1,0:T(8,128)(2,1)} custom-call(bf16[256,768]{1,0:T(8,128)(2,1)} %copy-done.8, bf16[256,768]{1,0:T(8,128)(2,1)} %copy-done.16, bf16[256,768]{1,0:T(8,128)(2,1)} %copy-done.17, bf16[256,768]{1,0:T(8,128)(2,1)} %copy-done.20, bf16[256,768]{1,0:T(8,128)(2,1)} %collective-permute-done.2.refs_4_, bf16[256,768]{1,0:T(8,128)(2,1)} %copy-done.19, ...), custom_call_target="tpu_custom_call" | custom-call | flops 1 | bytes 1 | tf_op jit(solution)/shard_map/pallas_call | solution.py:452
  350.1 1.6 collective-permute-start.23
  351.7 1.4 collective-permute-start.24
  354.3 1.4 collective-permute-done.22
  356.8 1.6 collective-permute-done.24
  360.3 20.1 %all-to-all-done.8.pieces_ref = bf16[8,256,384]{2,1,0:T(8,128)(2,1)} async-done(((bf16[8,256,384]{2,1,0:T(8,128)(2,1)}), bf16[8,256,384]{2,1,0:T(8,128)(2,1)}, u32[]{:S(2)}, u32[]{:S(2)}) %all-to-all-start.8) | async-done | bytes 1572896 | tf_op jit(solution)/shard_map/all_to_all | solution.py:564
  380.4 3.6 all-to-all-start.9
  384.0 4.6 %multiply_reduce_fusion = (f32[]{:T(128)}, f32[384,768]{1,0:T(8,128)}, f32[]{:T(128)}, f32[384,768]{1,0:T(8,128)}) fusion(bf16[384,768]{1,0:T(8,128)(2,1)S(1)} %copy-done.24, f32[384,768]{1,0:T(8,128)} %get-tuple-element.202, bf16[384,768]{1,0:T(8,128)(2,1)} %copy-done.26, bf16[384,768]{1,0:T(8,128)(2,1)} %copy-done.25, f32[384,768]{1,0:T(8,128)} %get-tuple-element.199, ...), kind=kLoop, calls=%fused_computation.15 | loop fusion | flops 3538942 | bytes 7077896 | tf_op jit(solution)/shard_map/reduce_sum | solution.py:885
  389.9 5.1 %shard_map.387 = (f32[256,768]{1,0:T(8,128)}, f32[1,768]{1,0:T(1,128)}) custom-call(bf16[8,256,384]{2,1,0:T(8,128)(2,1)} %all-to-all-done.8.pieces_ref, bf16[768,2304]{1,0:T(8,128)(2,1)} %all-gather.2.cloned.1.call-done.matrix_ref, bf16[256,768]{1,0:T(8,128)(2,1)} %bitcast.185, f32[1,768]{1,0:T(1,128)} %get-tuple-element.262.gain_ref, f32[256,768]{1,0:T(8,128)} %copy-done.1), custom_call_target="tpu_custom_call" | custom-call | flops 1 | bytes 1 | tf_op jit(solution)/shard_map/pallas_call | solution.py:499
  397.7 1.8 shard_map.388
  401.0 4.7 %all-to-all-start.10 = ((f32[32,1,1664]{2,1,0:T(1,128)}), f32[32,1,1664]{2,1,0:T(1,128)S(1)}, u32[]{:S(2)}, u32[]{:S(2)}) async-start(f32[32,1,1664]{2,1,0:T(1,128)} %broadcast_in_dim.60), calls=%async_computation.10 | async-start | bytes 425984 | tf_op jit(solution)/shard_map/all_to_all | solution.py:564
  407.1 7.9 %all-to-all-done.10 = f32[32,1,1664]{2,1,0:T(1,128)S(1)} async-done(((f32[32,1,1664]{2,1,0:T(1,128)}), f32[32,1,1664]{2,1,0:T(1,128)S(1)}, u32[]{:S(2)}, u32[]{:S(2)}) %all-to-all-start.10) | async-done | bytes 213024 | tf_op jit(solution)/shard_map/all_to_all | solution.py:564
  418.4 9.2 %shard_map.389 = (f32[24,2304]{1,0:T(8,128)}, f32[24,2304]{1,0:T(8,128)}, f32[24,2304]{1,0:T(8,128)}, f32[24,768]{1,0:T(8,128)}, f32[24,768]{1,0:T(8,128)}, /*in...) custom-call(f32[1]{0:T(128)} %bitcast.56.factor_ref, ...), custom_call_target="tpu_custom_call" | custom-call | flops 13271040 | bytes 18579456 | tf_op jit(solution)/shard_map/pallas_call | solution.py:590
  (188 shorter events, 56.8 us)
Async XLA Ops:
  8.9 14.2 %copy-start.3 = (bf16[1,256,768]{2,1,0:T(8,128)(2,1)S(1)}, bf16[1,256,768]{2,1,0:T(8,128)(2,1)}, u32[]{:S(2)}) copy-start(bf16[1,256,768]{2,1,0:T(8,128)(2,1)} %param.23) | copy-start | bytes 1179652
  11.8 11.4 %copy-start.35 = (f32[2,768]{1,0:T(2,128)S(1)}, f32[2,768]{1,0:T(2,128)}, u32[]{:S(2)}) copy-start(f32[2,768]{1,0:T(2,128)} %param.31) | copy-start | bytes 18436
  15.6 14.3 %copy-start.6 = (f32[1,384,768]{2,1,0:T(8,128)S(1)}, f32[1,384,768]{2,1,0:T(8,128)}, u32[]{:S(2)}) copy-start(f32[1,384,768]{2,1,0:T(8,128)} %param.29) | copy-start | bytes 3538948
  15.6 40.3 %all-to-all-start = ((bf16[8,32,1152]{2,1,0:T(8,128)(2,1)}), bf16[8,32,1152]{2,1,0:T(8,128)(2,1)S(1)}, u32[]{:S(2)}, u32[]{:S(2)}) async-start(bf16[8,32,1152]{2,1,0:T(8,128)(2,1)} %fusion.46), calls=%async_computation | async-start | bytes 1179648 | tf_op jit(solution)/shard_map/all_to_all | solution.py:564
  24.0 6.0 %copy-start.8 = (bf16[256,768]{1,0:T(8,128)(2,1)}, bf16[256,768]{1,0:T(8,128)(2,1)S(1)}, u32[]{:S(2)}) copy-start(bf16[256,768]{1,0:T(8,128)(2,1)S(1)} %fusion.5.refs_0_) | copy-start | bytes 1179652
  24.0 16.2 %collective-permute-start = (bf16[256,768]{1,0:T(8,128)(2,1)S(1)}, bf16[256,768]{1,0:T(8,128)(2,1)S(1)}, u32[]{:S(2)}, u32[]{:S(2)}) collective-permute-start(bf16[256,768]{1,0:T(8,128)(2,1)S(1)} %fusion.5.refs_0_), channel_id=1, source_target_pairs={{0,4},{4,0},{8,12},{12,8},{16,20},{20,16},{24,28},{28,24},{1,5},{5... | collective-permute-start | bytes 1179656 | tf_op jit(solution)/shard_map/ppermute | solution.py:611
  26.1 23.5 %collective-permute-start.1 = (bf16[256,768]{1,0:T(8,128)(2,1)S(1)}, bf16[256,768]{1,0:T(8,128)(2,1)S(1)}, u32[]{:S(2)}, u32[]{:S(2)}) collective-permute-start(bf16[256,768]{1,0:T(8,128)(2,1)S(1)} %fusion.5.refs_0_), channel_id=1, source_target_pairs={{0,8},{4,12},{8,0},{12,4},{16,24},{20,28},{24,16},{28,20},{1,9},{5... | collective-permute-start | bytes 1179656 | tf_op jit(solution)/shard_map/ppermute | solution.py:611
  27.6 28.4 %collective-permute-start.2 = (bf16[256,768]{1,0:T(8,128)(2,1)S(1)}, bf16[256,768]{1,0:T(8,128)(2,1)}, u32[]{:S(2)}, u32[]{:S(2)}) collective-permute-start(bf16[256,768]{1,0:T(8,128)(2,1)S(1)} %fusion.5.refs_0_), channel_id=1, source_target_pairs={{0,16},{4,20},{8,24},{12,28},{16,0},{20,4},{24,8},{28,12},{1,17},{... | collective-permute-start | bytes 1179656 | tf_op jit(solution)/shard_map/ppermute | solution.py:611
  30.0 41.3 %copy-start.9 = (bf16[384,768]{1,0:T(8,128)(2,1)}, bf16[384,768]{1,0:T(8,128)(2,1)S(1)}, u32[]{:S(2)}) copy-start(bf16[384,768]{1,0:T(8,128)(2,1)S(1)} %bitcast_convert_fusion.1.refs_0_) | copy-start | bytes 1769476
  40.2 15.7 %copy-start.16 = (bf16[256,768]{1,0:T(8,128)(2,1)}, bf16[256,768]{1,0:T(8,128)(2,1)S(1)}, u32[]{:S(2)}) copy-start(bf16[256,768]{1,0:T(8,128)(2,1)S(1)} %collective-permute-done.refs_1_) | copy-start | bytes 1179652
  49.6 6.3 %copy-start.17 = (bf16[256,768]{1,0:T(8,128)(2,1)}, bf16[256,768]{1,0:T(8,128)(2,1)S(1)}, u32[]{:S(2)}) copy-start(bf16[256,768]{1,0:T(8,128)(2,1)S(1)} %collective-permute-done.1.refs_2_) | copy-start | bytes 1179652
  57.4 44.5 %all-to-all-start.1 = ((bf16[4,8,24,1152]{3,2,1,0:T(8,128)(2,1)}), bf16[4,8,24,1152]{3,2,1,0:T(8,128)(2,1)S(1)}, u32[]{:S(2)}, u32[]{:S(2)}) async-start(bf16[4,8,24,1152]{3,2,1,0:T(8,128)(2,1)} %broadcast_in_dim.24), calls=%async_computation.1 | async-start | bytes 3538944 | tf_op jit(solution)/shard_map/all_to_all | solution.py:564
  61.1 30.4 %copy-start.7 = (f32[1,384,768]{2,1,0:T(8,128)S(1)}, f32[1,384,768]{2,1,0:T(8,128)}, u32[]{:S(2)}) copy-start(f32[1,384,768]{2,1,0:T(8,128)} %param.30) | copy-start | bytes 3538948
  69.8 17.4 %collective-permute-start.5 = (bf16[256,768]{1,0:T(8,128)(2,1)}, bf16[256,768]{1,0:T(8,128)(2,1)S(1)}, u32[]{:S(2)}, u32[]{:S(2)}) collective-permute-start(bf16[256,768]{1,0:T(8,128)(2,1)} %collective-permute-done.2.refs_4_), channel_id=1, source_target_pairs={{0,8},{4,12},{8,0},{12,4},{16,24},{20,28},{24,16},{28,20},{1,9},{5... | collective-permute-start | bytes 1179656 | tf_op jit(solution)/shard_map/ppermute | solution.py:611
  71.3 29.3 %collective-permute-start.7 = (bf16[384,768]{1,0:T(8,128)(2,1)S(1)}, bf16[384,768]{1,0:T(8,128)(2,1)S(1)}, u32[]{:S(2)}, u32[]{:S(2)}) collective-permute-start(bf16[384,768]{1,0:T(8,128)(2,1)S(1)} %bitcast_convert_fusion.1.refs_0_), channel_id=1, source_target_pairs={{16,0},{0,16},{17,1},{1,17},{18,2},{2,18},{19,3},{3,19},{20,4},{4,... | collective-permute-start | bytes 1769480 | tf_op jit(solution)/shard_map/ppermute | solution.py:617
  73.8 20.6 %collective-permute-start.4 = (bf16[256,768]{1,0:T(8,128)(2,1)}, bf16[256,768]{1,0:T(8,128)(2,1)S(1)}, u32[]{:S(2)}, u32[]{:S(2)}) collective-permute-start(bf16[256,768]{1,0:T(8,128)(2,1)} %collective-permute-done.2.refs_4_), channel_id=1, source_target_pairs={{0,4},{4,0},{8,12},{12,8},{16,20},{20,16},{24,28},{28,24},{1,5},{5... | collective-permute-start | bytes 1179656 | tf_op jit(solution)/shard_map/ppermute | solution.py:611
  75.6 18.9 %collective-permute-start.3 = (bf16[256,768]{1,0:T(8,128)(2,1)}, bf16[256,768]{1,0:T(8,128)(2,1)S(1)}, u32[]{:S(2)}, u32[]{:S(2)}) collective-permute-start(bf16[256,768]{1,0:T(8,128)(2,1)} %copy-done.17), channel_id=1, source_target_pairs={{0,4},{4,0},{8,12},{12,8},{16,20},{20,16},{24,28},{28,24},{1,5},{5... | collective-permute-start | bytes 1179656 | tf_op jit(solution)/shard_map/ppermute | solution.py:611
  87.3 5.1 %copy-start.18 = (bf16[256,768]{1,0:T(8,128)(2,1)}, bf16[256,768]{1,0:T(8,128)(2,1)S(1)}, u32[]{:S(2)}) copy-start(bf16[256,768]{1,0:T(8,128)(2,1)S(1)} %collective-permute-done.5.refs_6_) | copy-start | bytes 1179652
  87.3 14.6 %collective-permute-start.6 = (bf16[256,768]{1,0:T(8,128)(2,1)S(1)}, bf16[256,768]{1,0:T(8,128)(2,1)}, u32[]{:S(2)}, u32[]{:S(2)}) collective-permute-start(bf16[256,768]{1,0:T(8,128)(2,1)S(1)} %collective-permute-done.5.refs_6_), channel_id=1, source_target_pairs={{0,4},{4,0},{8,12},{12,8},{16,20},{20,16},{24,28},{28,24},{1,5},{5... | collective-permute-start | bytes 1179656 | tf_op jit(solution)/shard_map/ppermute | solution.py:611
  94.5 6.2 %copy-start.20 = (bf16[256,768]{1,0:T(8,128)(2,1)}, bf16[256,768]{1,0:T(8,128)(2,1)S(1)}, u32[]{:S(2)}) copy-start(bf16[256,768]{1,0:T(8,128)(2,1)S(1)} %collective-permute-done.3.refs_3_) | copy-start | bytes 1179652
  94.5 6.2 %copy-start.19 = (bf16[256,768]{1,0:T(8,128)(2,1)}, bf16[256,768]{1,0:T(8,128)(2,1)S(1)}, u32[]{:S(2)}) copy-start(bf16[256,768]{1,0:T(8,128)(2,1)S(1)} %collective-permute-done.4.refs_5_) | copy-start | bytes 1179652
  104.3 44.8 %all-to-all-start.2 = ((bf16[8,128,768]{2,1,0:T(8,128)(2,1)}), bf16[8,128,768]{2,1,0:T(8,128)(2,1)S(1)}, u32[]{:S(2)}, u32[]{:S(2)}) async-start(bf16[8,128,768]{2,1,0:T(8,128)(2,1)} %bitcast.183), calls=%async_computation.2 | async-start | bytes 3145728 | tf_op jit(solution)/shard_map/all_to_all | solution.py:564
  107.9 34.5 %collective-permute-start.10 = (bf16[384,768]{1,0:T(8,128)(2,1)}, bf16[384,768]{1,0:T(8,128)(2,1)}, u32[]{:S(2)}, u32[]{:S(2)}) collective-permute-start(bf16[384,768]{1,0:T(8,128)(2,1)} %bitcast_convert_fusion.refs_4_), channel_id=1, source_target_pairs={{4,0},{0,4},{5,1},{1,5},{6,2},{2,6},{7,3},{3,7},{12,8},{8,12},{13,... | collective-permute-start | bytes 1769480 | tf_op jit(solution)/shard_map/ppermute | solution.py:617
  109.7 32.7 %collective-permute-start.8 = (bf16[384,768]{1,0:T(8,128)(2,1)}, bf16[384,768]{1,0:T(8,128)(2,1)}, u32[]{:S(2)}, u32[]{:S(2)}) collective-permute-start(bf16[384,768]{1,0:T(8,128)(2,1)} %bitcast_convert_fusion.refs_4_), channel_id=1, source_target_pairs={{16,0},{0,16},{17,1},{1,17},{18,2},{2,18},{19,3},{3,19},{20,4},{4,... | collective-permute-start | bytes 1769480 | tf_op jit(solution)/shard_map/ppermute | solution.py:617
  111.3 31.1 %collective-permute-start.11 = (bf16[384,768]{1,0:T(8,128)(2,1)}, bf16[384,768]{1,0:T(8,128)(2,1)}, u32[]{:S(2)}, u32[]{:S(2)}) collective-permute-start(bf16[384,768]{1,0:T(8,128)(2,1)} %copy-done.27), channel_id=1, source_target_pairs={{4,0},{0,4},{5,1},{1,5},{6,2},{2,6},{7,3},{3,7},{12,8},{8,12},{13,... | collective-permute-start | bytes 1769480 | tf_op jit(solution)/shard_map/ppermute | solution.py:617
  111.9 37.3 %collective-permute-start.9 = (bf16[384,768]{1,0:T(8,128)(2,1)}, bf16[384,768]{1,0:T(8,128)(2,1)}, u32[]{:S(2)}, u32[]{:S(2)}) collective-permute-start(bf16[384,768]{1,0:T(8,128)(2,1)} %copy-done.9), channel_id=1, source_target_pairs={{4,0},{0,4},{5,1},{1,5},{6,2},{2,6},{7,3},{3,7},{12,8},{8,12},{13,... | collective-permute-start | bytes 1769480 | tf_op jit(solution)/shard_map/ppermute | solution.py:617
  149.2 27.0 %copy-start = (bf16[8,128,768]{2,1,0:T(8,128)(2,1)}, bf16[8,128,768]{2,1,0:T(8,128)(2,1)S(1)}, u32[]{:S(2)}) copy-start(bf16[8,128,768]{2,1,0:T(8,128)(2,1)S(1)} %all-to-all-done.2) | copy-start | bytes 4718596
  149.2 25.5 %all-to-all-start.3 = ((bf16[8,256,128]{2,1,0:T(8,128)(2,1)}), bf16[8,256,128]{2,1,0:T(8,128)(2,1)S(1)}, u32[]{:S(2)}, u32[]{:S(2)}) async-start(bf16[8,256,128]{2,1,0:T(8,128)(2,1)} %bitcast.204), calls=%async_computation.3 | async-start | bytes 1048576 | tf_op jit(solution)/shard_map/all_to_all | solution.py:564
  154.5 94.9 %all-gather.2.cloned.1.call-start = ((), (), s32[]{:S(2)}) async-start(), calls=%async_computation.11 | async-start | bytes 3649536 | tf_op jit(solution)/shard_map/all_gather | solution.py:787
  154.5 20.2 %collective-permute-start.12 = (bf16[384,768]{1,0:T(8,128)(2,1)}, bf16[384,768]{1,0:T(8,128)(2,1)}, u32[]{:S(2)}, u32[]{:S(2)}) collective-permute-start(bf16[384,768]{1,0:T(8,128)(2,1)} %collective-permute-done.8.refs_5_), channel_id=1, source_target_pairs={{4,0},{0,4},{5,1},{1,5},{6,2},{2,6},{7,3},{3,7},{12,8},{8,12},{13,... | collective-permute-start | bytes 1769480 | tf_op jit(solution)/shard_map/ppermute | solution.py:617
  222.0 27.4 %all-to-all-start.5 = ((bf16[8,128,768]{2,1,0:T(8,128)(2,1)}), bf16[8,128,768]{2,1,0:T(8,128)(2,1)S(1)}, u32[]{:S(2)}, u32[]{:S(2)}) async-start(bf16[8,128,768]{2,1,0:T(8,128)(2,1)} %bitcast.198), calls=%async_computation.5 | async-start | bytes 3145728 | tf_op jit(solution)/shard_map/all_to_all | solution.py:564
  232.3 15.9 %collective-permute-start.13 = (bf16[384,768]{1,0:T(8,128)(2,1)}, bf16[384,768]{1,0:T(8,128)(2,1)}, u32[]{:S(2)}, u32[]{:S(2)}) collective-permute-start(bf16[384,768]{1,0:T(8,128)(2,1)} %get-tuple-element.161), channel_id=1, source_target_pairs={{0,4},{4,0},{1,5},{5,1},{2,6},{6,2},{3,7},{7,3},{8,12},{12,8},{9,1... | collective-permute-start | bytes 1769480 | tf_op jit(solution)/shard_map/ppermute | solution.py:626
  251.3 15.6 %copy-start.1 = (f32[256,768]{1,0:T(8,128)}, f32[256,768]{1,0:T(8,128)S(1)}, u32[]{:S(2)}) copy-start(f32[256,768]{1,0:T(8,128)S(1)} %multiply_add_fusion.residual_ref) | copy-start | bytes 2359300
  251.8 9.3 %copy-start.22 = (f32[384,768]{1,0:T(8,128)S(1)}, f32[384,768]{1,0:T(8,128)}, u32[]{:S(2)}) copy-start(f32[384,768]{1,0:T(8,128)} %get-tuple-element.176) | copy-start | bytes 3538948
  257.3 44.5 %all-to-all-start.6 = ((bf16[8,256,128]{2,1,0:T(8,128)(2,1)}), bf16[8,256,128]{2,1,0:T(8,128)(2,1)S(1)}, u32[]{:S(2)}, u32[]{:S(2)}) async-start(bf16[8,256,128]{2,1,0:T(8,128)(2,1)} %fusion.47), calls=%async_computation.6 | async-start | bytes 1048576 | tf_op jit(solution)/shard_map/all_to_all | solution.py:564
  261.2 4.3 copy-start.42
  261.2 5.7 %copy-start.14 = (bf16[256,768]{1,0:T(8,128)(2,1)S(1)}, bf16[256,768]{1,0:T(8,128)(2,1)}, u32[]{:S(2)}) copy-start(bf16[256,768]{1,0:T(8,128)(2,1)} %copy-done.13) | copy-start | bytes 1179652
  262.5 38.4 %collective-permute-start.15 = (bf16[384,768]{1,0:T(8,128)(2,1)S(1)}, bf16[384,768]{1,0:T(8,128)(2,1)S(1)}, u32[]{:S(2)}, u32[]{:S(2)}) collective-permute-start(bf16[384,768]{1,0:T(8,128)(2,1)S(1)} %add_convert_fusion.1), channel_id=1, source_target_pairs={{0,16},{16,0},{1,17},{17,1},{2,18},{18,2},{3,19},{19,3},{4,20},{20... | collective-permute-start | bytes 1769480 | tf_op jit(solution)/shard_map/ppermute | solution.py:626
  265.4 36.3 %collective-permute-start.14 = (bf16[384,768]{1,0:T(8,128)(2,1)S(1)}, bf16[384,768]{1,0:T(8,128)(2,1)}, u32[]{:S(2)}, u32[]{:S(2)}) collective-permute-start(bf16[384,768]{1,0:T(8,128)(2,1)S(1)} %copy-done.42), channel_id=1, source_target_pairs={{0,4},{4,0},{1,5},{5,1},{2,6},{6,2},{3,7},{7,3},{8,12},{12,8},{9,1... | collective-permute-start | bytes 1769480 | tf_op jit(solution)/shard_map/ppermute | solution.py:626
  267.4 34.3 %copy-start.5 = (bf16[768,768]{1,0:T(8,128)(2,1)}, bf16[768,768]{1,0:T(8,128)(2,1)S(1)}, u32[]{:S(2)}) copy-start(bf16[768,768]{1,0:T(8,128)(2,1)S(1)} %convolution_convert_fusion) | copy-start | bytes 3538948
  267.5 8.8 %collective-permute-start.16 = (bf16[8,24,768]{2,1,0:T(8,128)(2,1)S(1)}, bf16[8,24,768]{2,1,0:T(8,128)(2,1)S(1)}, u32[]{:S(2)}, u32[]{:S(2)}) collective-permute-start(bf16[8,24,768]{2,1,0:T(8,128)(2,1)S(1)} %get-tuple-element.234), channel_id=1, source_target_pairs={{0,1},{1,2},{2,3},{3,0},{4,5},{5,6},{6,7},{7,4},{8,9},{9,10},{10,1... | collective-permute-start | bytes 884744 | tf_op jit(solution)/shard_map/ppermute | solution.py:626
  267.6 9.9 %collective-permute-start.17 = (bf16[8,24,768]{2,1,0:T(8,128)(2,1)S(1)}, bf16[8,24,768]{2,1,0:T(8,128)(2,1)S(1)}, u32[]{:S(2)}, u32[]{:S(2)}) collective-permute-start(bf16[8,24,768]{2,1,0:T(8,128)(2,1)S(1)} %get-tuple-element.233), channel_id=1, source_target_pairs={{0,2},{1,3},{2,0},{3,1},{4,6},{5,7},{6,4},{7,5},{8,10},{9,11},{10,... | collective-permute-start | bytes 884744 | tf_op jit(solution)/shard_map/ppermute | solution.py:626
  269.2 13.1 %collective-permute-start.18 = (bf16[8,24,768]{2,1,0:T(8,128)(2,1)S(1)}, bf16[8,24,768]{2,1,0:T(8,128)(2,1)S(1)}, u32[]{:S(2)}, u32[]{:S(2)}) collective-permute-start(bf16[8,24,768]{2,1,0:T(8,128)(2,1)S(1)} %get-tuple-element.232), channel_id=1, source_target_pairs={{0,3},{1,0},{2,1},{3,2},{4,7},{5,4},{6,5},{7,6},{8,11},{9,8},{10,9... | collective-permute-start | bytes 884744 | tf_op jit(solution)/shard_map/ppermute | solution.py:626
  276.3 24.6 %copy-start.28 = (bf16[8,24,768]{2,1,0:T(8,128)(2,1)}, bf16[8,24,768]{2,1,0:T(8,128)(2,1)S(1)}, u32[]{:S(2)}) copy-start(bf16[8,24,768]{2,1,0:T(8,128)(2,1)S(1)} %collective-permute-done.16) | copy-start | bytes 884740
  277.5 23.4 %copy-start.30 = (bf16[8,24,768]{2,1,0:T(8,128)(2,1)}, bf16[8,24,768]{2,1,0:T(8,128)(2,1)S(1)}, u32[]{:S(2)}) copy-start(bf16[8,24,768]{2,1,0:T(8,128)(2,1)S(1)} %collective-permute-done.17) | copy-start | bytes 884740
  282.2 18.7 %copy-start.32 = (bf16[8,24,768]{2,1,0:T(8,128)(2,1)}, bf16[8,24,768]{2,1,0:T(8,128)(2,1)S(1)}, u32[]{:S(2)}) copy-start(bf16[8,24,768]{2,1,0:T(8,128)(2,1)S(1)} %collective-permute-done.18) | copy-start | bytes 884740
  302.5 36.2 %all-to-all-start.7 = ((bf16[8,128,768]{2,1,0:T(8,128)(2,1)}), bf16[8,128,768]{2,1,0:T(8,128)(2,1)S(1)}, u32[]{:S(2)}, u32[]{:S(2)}) async-start(bf16[8,128,768]{2,1,0:T(8,128)(2,1)} %bitcast.181), calls=%async_computation.7 | async-start | bytes 3145728 | tf_op jit(solution)/shard_map/all_to_all | solution.py:564
  308.5 28.3 %collective-permute-start.21 = (bf16[384,768]{1,0:T(8,128)(2,1)}, bf16[384,768]{1,0:T(8,128)(2,1)S(1)}, u32[]{:S(2)}, u32[]{:S(2)}) collective-permute-start(bf16[384,768]{1,0:T(8,128)(2,1)} %add_convert_fusion), channel_id=1, source_target_pairs={{0,16},{16,0},{1,17},{17,1},{2,18},{18,2},{3,19},{19,3},{4,20},{20... | collective-permute-start | bytes 1769480 | tf_op jit(solution)/shard_map/ppermute | solution.py:626
  308.9 27.9 %collective-permute-start.19 = (bf16[384,768]{1,0:T(8,128)(2,1)}, bf16[384,768]{1,0:T(8,128)(2,1)S(1)}, u32[]{:S(2)}, u32[]{:S(2)}) collective-permute-start(bf16[384,768]{1,0:T(8,128)(2,1)} %get-tuple-element.183), channel_id=1, source_target_pairs={{0,4},{4,0},{1,5},{5,1},{2,6},{6,2},{3,7},{7,3},{8,12},{12,8},{9,1... | collective-permute-start | bytes 1769480 | tf_op jit(solution)/shard_map/ppermute | solution.py:626
  310.6 26.7 %collective-permute-start.20 = (bf16[384,768]{1,0:T(8,128)(2,1)}, bf16[384,768]{1,0:T(8,128)(2,1)}, u32[]{:S(2)}, u32[]{:S(2)}) collective-permute-start(bf16[384,768]{1,0:T(8,128)(2,1)} %get-tuple-element.184), channel_id=1, source_target_pairs={{0,4},{4,0},{1,5},{5,1},{2,6},{6,2},{3,7},{7,3},{8,12},{12,8},{9,1... | collective-permute-start | bytes 1769480 | tf_op jit(solution)/shard_map/ppermute | solution.py:626
  338.8 41.6 %all-to-all-start.8 = ((bf16[8,256,384]{2,1,0:T(8,128)(2,1)}), bf16[8,256,384]{2,1,0:T(8,128)(2,1)}, u32[]{:S(2)}, u32[]{:S(2)}) async-start(bf16[8,256,384]{2,1,0:T(8,128)(2,1)} %bitcast.199), calls=%async_computation.8 | async-start | bytes 3145728 | tf_op jit(solution)/shard_map/all_to_all | solution.py:564
  343.3 9.8 %copy-start.29 = (bf16[8,24,768]{2,1,0:T(8,128)(2,1)S(1)}, bf16[8,24,768]{2,1,0:T(8,128)(2,1)}, u32[]{:S(2)}) copy-start(bf16[8,24,768]{2,1,0:T(8,128)(2,1)} %copy-done.28) | copy-start | bytes 884740
  343.3 9.8 %copy-start.31 = (bf16[8,24,768]{2,1,0:T(8,128)(2,1)S(1)}, bf16[8,24,768]{2,1,0:T(8,128)(2,1)}, u32[]{:S(2)}) copy-start(bf16[8,24,768]{2,1,0:T(8,128)(2,1)} %copy-done.30) | copy-start | bytes 884740
  343.3 9.8 %copy-start.33 = (bf16[8,24,768]{2,1,0:T(8,128)(2,1)S(1)}, bf16[8,24,768]{2,1,0:T(8,128)(2,1)}, u32[]{:S(2)}) copy-start(bf16[8,24,768]{2,1,0:T(8,128)(2,1)} %copy-done.32) | copy-start | bytes 884740
  350.0 5.6 %collective-permute-start.22 = (bf16[8,24,384]{2,1,0:T(8,128)(2,1)S(1)}, bf16[8,24,384]{2,1,0:T(8,128)(2,1)S(1)}, u32[]{:S(2)}, u32[]{:S(2)}) collective-permute-start(bf16[8,24,384]{2,1,0:T(8,128)(2,1)S(1)} %get-tuple-element.235), channel_id=1, source_target_pairs={{0,1},{1,2},{2,3},{3,0},{4,5},{5,6},{6,7},{7,4},{8,9},{9,10},{10,1... | collective-permute-start | bytes 442376 | tf_op jit(solution)/shard_map/ppermute | solution.py:626
  350.1 6.7 %collective-permute-start.23 = (bf16[8,24,384]{2,1,0:T(8,128)(2,1)S(1)}, bf16[8,24,384]{2,1,0:T(8,128)(2,1)S(1)}, u32[]{:S(2)}, u32[]{:S(2)}) collective-permute-start(bf16[8,24,384]{2,1,0:T(8,128)(2,1)S(1)} %get-tuple-element.237), channel_id=1, source_target_pairs={{0,2},{1,3},{2,0},{3,1},{4,6},{5,7},{6,4},{7,5},{8,10},{9,11},{10,... | collective-permute-start | bytes 442376 | tf_op jit(solution)/shard_map/ppermute | solution.py:626
  351.7 6.7 %collective-permute-start.24 = (bf16[8,24,384]{2,1,0:T(8,128)(2,1)S(1)}, bf16[8,24,384]{2,1,0:T(8,128)(2,1)S(1)}, u32[]{:S(2)}, u32[]{:S(2)}) collective-permute-start(bf16[8,24,384]{2,1,0:T(8,128)(2,1)S(1)} %get-tuple-element.236), channel_id=1, source_target_pairs={{0,3},{1,0},{2,1},{3,2},{4,7},{5,4},{6,5},{7,6},{8,11},{9,8},{10,9... | collective-permute-start | bytes 442376 | tf_op jit(solution)/shard_map/ppermute | solution.py:626
  354.2 29.8 %copy-start.24 = (bf16[384,768]{1,0:T(8,128)(2,1)S(1)}, bf16[384,768]{1,0:T(8,128)(2,1)}, u32[]{:S(2)}) copy-start(bf16[384,768]{1,0:T(8,128)(2,1)} %copy-done.23) | copy-start | bytes 1769476
  380.4 16.6 %all-to-all-start.9 = ((bf16[8,24,1152]{2,1,0:T(8,128)(2,1)}), bf16[8,24,1152]{2,1,0:T(8,128)(2,1)S(1)}, u32[]{:S(2)}, u32[]{:S(2)}) async-start(bf16[8,24,1152]{2,1,0:T(8,128)(2,1)} %pad_maximum_fusion), calls=%async_computation.9 | async-start | bytes 884736 | tf_op jit(solution)/shard_map/all_to_all | solution.py:564
  389.9 10.2 %copy-start.38 = (f32[768]{0:T(1024)S(1)}, f32[768]{0:T(1024)}, u32[]{:S(2)}) copy-start(f32[768]{0:T(1024)} %get-tuple-element.219) | copy-start | bytes 9220
  401.0 14.1 %all-to-all-start.10 = ((f32[32,1,1664]{2,1,0:T(1,128)}), f32[32,1,1664]{2,1,0:T(1,128)S(1)}, u32[]{:S(2)}, u32[]{:S(2)}) async-start(f32[32,1,1664]{2,1,0:T(1,128)} %broadcast_in_dim.60), calls=%async_computation.10 | async-start | bytes 425984 | tf_op jit(solution)/shard_map/all_to_all | solution.py:564
  405.9 11.8 %copy-start.40 = (f32[2,768]{1,0:T(2,128)S(1)}, f32[2,768]{1,0:T(2,128)}, u32[]{:S(2)}) copy-start(f32[2,768]{1,0:T(2,128)} %param.41) | copy-start | bytes 18436
  405.9 11.8 %copy-start.41 = (f32[2,768]{1,0:T(2,128)S(1)}, f32[2,768]{1,0:T(2,128)}, u32[]{:S(2)}) copy-start(f32[2,768]{1,0:T(2,128)} %param.40) | copy-start | bytes 18436
  416.4 11.3 %copy-start.34 = (f32[2,768]{1,0:T(2,128)}, f32[2,768]{1,0:T(2,128)S(1)}, u32[]{:S(2)}) copy-start(f32[2,768]{1,0:T(2,128)S(1)} %reshape.254) | copy-start | bytes 18436
  (16 other events, 20.4 us)
Sparse Core Ops, SparseCore 0:
  174.8 61.5 all-gather.1

commit v4 on v3

--- a/solution.py
+++ b/solution.py
@@ -682,8 +682,11 @@
     attend_in = (normed_first * gain_first).astype(BF16)
     slots = groups * CAP
     chosen = expert_ids[0, :, 0]
-    one_hot = (chosen[:, None] == jnp.arange(groups, dtype=jnp.int32)[None, :]).astype(jnp.int32)
-    rank = jnp.sum(jnp.cumsum(one_hot, axis=0) * one_hot, axis=1) - 1
+    one_hot = (chosen[:, None] == jnp.arange(groups, dtype=jnp.int32)[None, :]).astype(F32)
+    token = jnp.arange(row_count, dtype=jnp.int32)
+    earlier = (token[None, :] < token[:, None]).astype(BF16)
+    counts = jnp.dot(earlier, one_hot.astype(BF16), preferred_element_type=F32)
+    rank = jnp.sum(counts * one_hot, axis=1).astype(jnp.int32)
     target = chosen * CAP + rank
     placing = (target[:, None] == jnp.arange(slots, dtype=jnp.int32)[None, :]).astype(BF16)
 
@@ -876,13 +879,15 @@
         ],
         axis=2,
     )
-    grad_pieces, dense_rows = together(to_tokens(grad_qkv), dense_rows)
+    local_square = jnp.sum(up_grad * up_grad) + jnp.sum(down_grad * down_grad)
+    grad_pieces, dense_rows, local_square = together(
+        to_tokens(grad_qkv), dense_rows, local_square
+    )
     projection_grad, output_grad, dense_square = dense_grads(swap(dense_rows, SEQ), starts)
     input_grad, gain_first_part = close_norm(
         grad_pieces, starts, projection_full, tokens[0], gain_first[None], residual_grad
     )
     input_grad, gain_first_part = input_grad[None], gain_first_part[0]
-    local_square = jnp.sum(up_grad * up_grad) + jnp.sum(down_grad * down_grad)
     summed = spread_sum(
         jnp.concatenate(
             [gain_first_part, gain_second_part, dense_square[0] + local_square]

time: 438 us -> 427 us (0.975)
    ppermute x12, waiting for transfers between devices: 38.1 us -> 33.5 us  [to_owners(): lax.ppermute(block, axis, [(i, (i + step) % size) for i in range(size)])]
    another operation x4 -> x0, local copies, waits for them, and re-layouts: 4.58 us -> none
    unnamed x96 -> x82, local copies, waits for them, and re-layouts: 11 us -> 10.2 us
  transfers between devices with their start and end apart: 36 -> 36, of which waited for: 24 -> 19; matrix products, arithmetic and copies ran while one was open for 9% -> 7% of each run, Pallas kernels for 22% -> 22%
where the time goes in v4:
time: 427 us; the launch traced here: 425 us
  waiting for transfers between devices  138 us (32%)
  Pallas kernels  105 us (25%)
  starting transfers between devices  76.9 us (18%)
  blocking collectives  27.6 us (6%)
  other arithmetic  27.3 us (6%)
  local copies, waits for them, and re-layouts  24.9 us (6%)
  between operations  18.4 us (4%)
  matrix products  6.18 us (1%)
    all_to_all x10, starting transfers between devices, swap(): return lax.all_to_all(value, axes, split_axis=0, concat_axis=0, tiled=True)  44.7 us
    ppermute x7, waiting for transfers between devices, flip(): lax.ppermute(value, SEQ, [(index, index ^ bits) for index in range(count)])  39.6 us
    all_to_all x10, waiting for transfers between devices, swap(): return lax.all_to_all(value, axes, split_axis=0, concat_axis=0, tiled=True)  34.7 us
    ppermute x12, waiting for transfers between devices, to_owners(): lax.ppermute(block, axis, [(i, (i + step) % size) for i in range(size)])  33.5 us
    ppermute x6, waiting for transfers between devices, others(): lax.ppermute(value, axis, [((i + step) % size, i) for i in range(size)])  30.7 us
    all_to_all x1, blocking collectives, swap(): return lax.all_to_all(value, axes, split_axis=0, concat_axis=0, tiled=True)  27.6 us
    pallas_call x1, Pallas kernels, attend_back(): pl.pallas_call(functools.partial(attend_back_kernel, block=block, chunk=2...  24.4 us
    pallas_call x1, Pallas kernels, attend(): pl.pallas_call(functools.partial(attend_kernel, block=block, chunk=2 * bl...  23.1 us
  transfers between devices with their start and end apart: 36, of which 19 were waited for; matrix products, arithmetic and copies ran while one was open for 7% of the time, Pallas kernels for 22%

profile of v4, /device:TPU:0, one launch (start us, length us, event | category | flops | bytes accessed | tf_op | source)
XLA Modules:
  0.0 425.2 jit_solution(1699683284727044185)
XLA Ops:
  15.1 7.4 %all-to-all-start = ((bf16[8,32,1152]{2,1,0:T(8,128)(2,1)}), bf16[8,32,1152]{2,1,0:T(8,128)(2,1)S(1)}, u32[]{:S(2)}, u32[]{:S(2)}) async-start(bf16[8,32,1152]{2,1,0:T(8,128)(2,1)} %fusion.47), calls=%async_computation | async-start | bytes 1179648 | tf_op jit(solution)/shard_map/all_to_all | solution.py:564
  23.5 2.1 collective-permute-start
  25.5 1.5 collective-permute-start.1
  27.0 2.4 collective-permute-start.2
  30.2 9.4 %collective-permute-done.refs_1_ = bf16[256,768]{1,0:T(8,128)(2,1)S(1)} collective-permute-done((bf16[256,768]{1,0:T(8,128)(2,1)S(1)}, bf16[256,768]{1,0:T(8,128)(2,1)S(1)}, u32[]{:S(2)}, u32[]{:S(2)}) %collective-permute-start) | collective-permute-done | bytes 393248 | tf_op jit(solution)/shard_map/ppermute | solution.py:611
  39.6 9.6 %collective-permute-done.1.refs_2_ = bf16[256,768]{1,0:T(8,128)(2,1)} collective-permute-done((bf16[256,768]{1,0:T(8,128)(2,1)S(1)}, bf16[256,768]{1,0:T(8,128)(2,1)}, u32[]{:S(2)}, u32[]{:S(2)}) %collective-permute-start.1) | collective-permute-done | bytes 393248 | tf_op jit(solution)/shard_map/ppermute | solution.py:611
  49.2 6.2 %collective-permute-done.2.refs_4_ = bf16[256,768]{1,0:T(8,128)(2,1)} collective-permute-done((bf16[256,768]{1,0:T(8,128)(2,1)S(1)}, bf16[256,768]{1,0:T(8,128)(2,1)}, u32[]{:S(2)}, u32[]{:S(2)}) %collective-permute-start.2) | collective-permute-done | bytes 393248 | tf_op jit(solution)/shard_map/ppermute | solution.py:611
  55.4 1.4 broadcast_in_dim.24
  56.8 3.7 all-to-all-start.1
  60.8 1.9 collective-permute-start.7
  62.7 1.7 collective-permute-start.4
  64.7 14.5 %collective-permute-done.5.refs_6_ = bf16[256,768]{1,0:T(8,128)(2,1)S(1)} collective-permute-done((bf16[256,768]{1,0:T(8,128)(2,1)}, bf16[256,768]{1,0:T(8,128)(2,1)S(1)}, u32[]{:S(2)}, u32[]{:S(2)}) %collective-permute-start.5) | collective-permute-done | bytes 393248 | tf_op jit(solution)/shard_map/ppermute | solution.py:611
  79.2 1.7 collective-permute-start.6
  81.0 1.6 convolution_convert_fusion.2
  83.4 6.7 %collective-permute-done.7.refs_1_ = bf16[384,768]{1,0:T(8,128)(2,1)S(1)} collective-permute-done((bf16[384,768]{1,0:T(8,128)(2,1)S(1)}, bf16[384,768]{1,0:T(8,128)(2,1)S(1)}, u32[]{:S(2)}, u32[]{:S(2)}) %collective-permute-start.7) | collective-permute-done | bytes 589856 | tf_op jit(solution)/shard_map/ppermute | solution.py:617
  90.9 1.3 broadcast_in_dim.28
  92.2 3.6 all-to-all-start.2
  95.8 1.6 collective-permute-start.10
  97.4 1.6 collective-permute-start.8
  99.6 1.5 collective-permute-start.9
  103.6 1.4 copy.64
  105.0 1.9 slice.202
  108.0 23.1 %shard_map.380 = (bf16[2048,128]{1,0:T(8,128)(2,1)}, f32[2048,128]{1,0:T(8,128)}, bf16[2048,256]{1,0:T(8,128)(2,1)}, bf16[2048,256]{1,0:T(8,128)(2,1)}) custom-call(s32[2,8]{1,0:T(2,128)} %fusion.58.active_ref, s32[8]{0:T(128)} %iota_xor_fusion.order_ref, bf16[256,768]{1,0:T(8,128)(2,1)} %copy-done.6, bf16[256,768]{1,0:T(8,128)(2,1)} %copy-done.14, ...), custom_call_target="tpu_custom_call" | custom-call | flops 1 | bytes 1 | tf_op jit(solution)/shard_map/pallas_call | solution.py:278
  131.2 5.8 %collective-permute-done.9.refs_2_ = bf16[384,768]{1,0:T(8,128)(2,1)} collective-permute-done((bf16[384,768]{1,0:T(8,128)(2,1)}, bf16[384,768]{1,0:T(8,128)(2,1)}, u32[]{:S(2)}, u32[]{:S(2)}) %collective-permute-start.9) | collective-permute-done | bytes 589856 | tf_op jit(solution)/shard_map/ppermute | solution.py:617
  137.0 5.1 %all-to-all-start.3 = ((bf16[8,256,128]{2,1,0:T(8,128)(2,1)}), bf16[8,256,128]{2,1,0:T(8,128)(2,1)S(1)}, u32[]{:S(2)}, u32[]{:S(2)}) async-start(bf16[8,256,128]{2,1,0:T(8,128)(2,1)} %bitcast.185), calls=%async_computation.3 | async-start | bytes 1048576 | tf_op jit(solution)/shard_map/all_to_all | solution.py:564
  142.2 2.0 collective-permute-start.12
  144.2 18.2 %collective-permute-done.12.refs_7_ = bf16[384,768]{1,0:T(8,128)(2,1)} collective-permute-done((bf16[384,768]{1,0:T(8,128)(2,1)}, bf16[384,768]{1,0:T(8,128)(2,1)}, u32[]{:S(2)}, u32[]{:S(2)}) %collective-permute-start.12) | collective-permute-done | bytes 589856 | tf_op jit(solution)/shard_map/ppermute | solution.py:617
  163.2 1.5 slice.203
  167.4 27.6 %all_to_all.55 = bf16[8,128,768]{2,1,0:T(8,128)(2,1)} all-to-all(bf16[8,128,768]{2,1,0:T(8,128)(2,1)S(1)} %bitcast.165), channel_id=1, replica_groups=mesh['hi'=2,'lo'=2,'in'=2,'exp'=4] {'lo','exp'}, dimensions={0} | all-to-all | bytes 3145728 | tf_op jit(solution)/shard_map/all_to_all | solution.py:564
  195.0 15.6 %shard_map.381 = (bf16[1024,768]{1,0:T(8,128)(2,1)}, bf16[1024,384]{1,0:T(8,128)(2,1)}, bf16[1024,384]{1,0:T(8,128)(2,1)}, bf16[1024,384]{1,0:T(8,128)(2,1)}, bf...) custom-call(bf16[1024,768]{1,0:T(8,128)(2,1)} %bitcast.157, ...), custom_call_target="tpu_custom_call" | custom-call | flops 1 | bytes 1 | tf_op jit(solution)/shard_map/pallas_call | solution.py:372
  210.6 4.3 %all-to-all-start.5 = ((bf16[8,128,768]{2,1,0:T(8,128)(2,1)}), bf16[8,128,768]{2,1,0:T(8,128)(2,1)}, u32[]{:S(2)}, u32[]{:S(2)}) async-start(bf16[8,128,768]{2,1,0:T(8,128)(2,1)} %bitcast.180), calls=%async_computation.5 | async-start | bytes 3145728 | tf_op jit(solution)/shard_map/all_to_all | solution.py:564
  214.9 6.7 %shard_map.382 = (bf16[384,768]{1,0:T(8,128)(2,1)}, bf16[384,768]{1,0:T(8,128)(2,1)}, f32[384,768]{1,0:T(8,128)}, f32[384,768]{1,0:T(8,128)}) custom-call(bf16[1024,768]{1,0:T(8,128)(2,1)} %bitcast.155, bf16[1024,768]{1,0:T(8,128)(2,1)} %bitcast.158, bf16[1024,384]{1,0:T(8,128)(2,1)} %get-tuple-element.158.refs_0_.refs_3_, ...), custom_call_target="tpu_custom_call" | custom-call | flops 1 | bytes 1 | tf_op jit(solution)/shard_map/pallas_call | solution.py:425
  222.3 7.2 %shard_map.383 = bf16[1024,768]{1,0:T(8,128)(2,1)} custom-call(bf16[1024,384]{1,0:T(8,128)(2,1)} %get-tuple-element.166.refs_0_.refs_2_, bf16[1024,384]{1,0:T(8,128)(2,1)} %get-tuple-element.160.refs_2_.refs_1_, bf16[1024,384]{1,0:T(8,128)(2,1)} %get-tuple-element.167.refs_2_.refs_0_, bf16[1024,384]{1,0:T(8,128)(2,1)} %get-tuple-element.158.refs_0_.refs_3_, ...), custom_call_target="tpu_custom_call" | custom-call | flops 1 | bytes 1 | tf_op jit(solution)/shard_map/pallas_call | solution.py:396
  229.5 6.6 %shard_map.384 = (bf16[384,768]{1,0:T(8,128)(2,1)}, bf16[384,768]{1,0:T(8,128)(2,1)}, f32[384,768]{1,0:T(8,128)}, f32[384,768]{1,0:T(8,128)}) custom-call(bf16[1024,768]{1,0:T(8,128)(2,1)} %bitcast.156, bf16[1024,768]{1,0:T(8,128)(2,1)} %bitcast.159, bf16[1024,384]{1,0:T(8,128)(2,1)} %get-tuple-element.167.refs_2_.refs_0_, ...), custom_call_target="tpu_custom_call" | custom-call | flops 1 | bytes 1 | tf_op jit(solution)/shard_map/pallas_call | solution.py:425
  236.2 1.3 collective-permute-done.13
  238.3 1.7 convert_reduce_fusion.1
  247.1 5.2 %all-to-all-start.6 = ((bf16[8,256,128]{2,1,0:T(8,128)(2,1)}), bf16[8,256,128]{2,1,0:T(8,128)(2,1)S(1)}, u32[]{:S(2)}, u32[]{:S(2)}) async-start(bf16[8,256,128]{2,1,0:T(8,128)(2,1)} %fusion.48), calls=%async_computation.6 | async-start | bytes 1048576 | tf_op jit(solution)/shard_map/all_to_all | solution.py:564
  253.6 3.0 collective-permute-start.15
  256.6 1.5 collective-permute-start.14
  258.8 1.5 collective-permute-start.17
  260.3 1.4 collective-permute-start.18
  261.7 5.8 %collective-permute-done.16 = bf16[8,24,768]{2,1,0:T(8,128)(2,1)S(1)} collective-permute-done((bf16[8,24,768]{2,1,0:T(8,128)(2,1)S(1)}, bf16[8,24,768]{2,1,0:T(8,128)(2,1)S(1)}, u32[]{:S(2)}, u32[]{:S(2)}) %collective-permute-start.16) | collective-permute-done | bytes 294944 | tf_op jit(solution)/shard_map/ppermute | solution.py:626
  268.7 4.7 %collective-permute-done.18 = bf16[8,24,768]{2,1,0:T(8,128)(2,1)S(1)} collective-permute-done((bf16[8,24,768]{2,1,0:T(8,128)(2,1)S(1)}, bf16[8,24,768]{2,1,0:T(8,128)(2,1)S(1)}, u32[]{:S(2)}, u32[]{:S(2)}) %collective-permute-start.18) | collective-permute-done | bytes 294944 | tf_op jit(solution)/shard_map/ppermute | solution.py:626
  273.4 18.4 %collective-permute-done.15 = bf16[384,768]{1,0:T(8,128)(2,1)S(1)} collective-permute-done((bf16[384,768]{1,0:T(8,128)(2,1)S(1)}, bf16[384,768]{1,0:T(8,128)(2,1)S(1)}, u32[]{:S(2)}, u32[]{:S(2)}) %collective-permute-start.15) | collective-permute-done | bytes 589856 | tf_op jit(solution)/shard_map/ppermute | solution.py:626
  293.4 3.6 all-to-all-start.7
  297.0 2.3 add_convert_fusion
  299.7 1.8 collective-permute-start.19
  301.7 24.4 %shard_map.385 = (bf16[2048,384]{1,0:T(8,128)(2,1)}, bf16[2048,384]{1,0:T(8,128)(2,1)}) custom-call(s32[2,8]{1,0:T(2,128)} %fusion.58.active_ref, s32[8]{0:T(128)} %iota_xor_fusion.order_ref, bf16[2048,256]{1,0:T(8,128)(2,1)} %get-tuple-element.150.pair_ref, bf16[2048,128]{1,0:T(8,128)(2,1)} %broadcast_in_dim.26.refs_9_.documents_ref, ...), custom_call_target="tpu_custom_call" | custom-call | flops 1 | bytes 1 | tf_op jit(solution)/shard_map/pallas_call | solution.py:309
  326.1 1.6 collective-permute-done.21
  328.1 1.5 all-to-all-done.7
  329.7 4.5 %all-to-all-start.8 = ((bf16[8,256,384]{2,1,0:T(8,128)(2,1)}), bf16[8,256,384]{2,1,0:T(8,128)(2,1)}, u32[]{:S(2)}, u32[]{:S(2)}) async-start(bf16[8,256,384]{2,1,0:T(8,128)(2,1)} %bitcast.179), calls=%async_computation.8 | async-start | bytes 3145728 | tf_op jit(solution)/shard_map/all_to_all | solution.py:564
  334.2 2.0 fusion.9
  336.2 5.5 %shard_map.386 = bf16[768,384]{1,0:T(8,128)(2,1)} custom-call(bf16[256,768]{1,0:T(8,128)(2,1)} %copy-done.6, bf16[256,768]{1,0:T(8,128)(2,1)} %copy-done.14, bf16[256,768]{1,0:T(8,128)(2,1)} %collective-permute-done.1.refs_2_, bf16[256,768]{1,0:T(8,128)(2,1)} %copy-done.17, bf16[256,768]{1,0:T(8,128)(2,1)} %collective-permute-done.2.refs_4_, ...), custom_call_target="tpu_custom_call" | custom-call | flops 1 | bytes 1 | tf_op jit(solution)/shard_map/pallas_call | solution.py:452
  343.0 1.5 collective-permute-start.23
  344.5 1.4 collective-permute-start.24
  345.9 4.7 %multiply_reduce_fusion = (f32[]{:T(128)}, f32[384,768]{1,0:T(8,128)}, f32[]{:T(128)}, f32[384,768]{1,0:T(8,128)}) fusion(bf16[384,768]{1,0:T(8,128)(2,1)S(1)} %copy-done.22, f32[384,768]{1,0:T(8,128)} %get-tuple-element.197, bf16[384,768]{1,0:T(8,128)(2,1)} %collective-permute-done.19, bf16[384,768]{1,0:T(8,128)(2,1)} %collective-permute-done.21, ...), kind=kLoop, calls=%fused_computation.15 | loop fusion | flops 3538942 | bytes 7077896 | tf_op jit(solution)/shard_map/reduce_sum | solution.py:882
  353.7 17.3 %all-to-all-done.8.pieces_ref = bf16[8,256,384]{2,1,0:T(8,128)(2,1)} async-done(((bf16[8,256,384]{2,1,0:T(8,128)(2,1)}), bf16[8,256,384]{2,1,0:T(8,128)(2,1)}, u32[]{:S(2)}, u32[]{:S(2)}) %all-to-all-start.8) | async-done | bytes 1572896 | tf_op jit(solution)/shard_map/all_to_all | solution.py:564
  371.0 3.6 all-to-all-start.9
  374.7 5.1 %shard_map.387 = (f32[256,768]{1,0:T(8,128)}, f32[1,768]{1,0:T(1,128)}) custom-call(bf16[8,256,384]{2,1,0:T(8,128)(2,1)} %all-to-all-done.8.pieces_ref, bf16[768,2304]{1,0:T(8,128)(2,1)} %all-gather.2.cloned.1.call-done.matrix_ref, bf16[256,768]{1,0:T(8,128)(2,1)} %bitcast.166, f32[1,768]{1,0:T(1,128)} %get-tuple-element.264.gain_ref, f32[256,768]{1,0:T(8,128)} %copy-done.1), custom_call_target="tpu_custom_call" | custom-call | flops 1 | bytes 1 | tf_op jit(solution)/shard_map/pallas_call | solution.py:499
  380.5 7.1 %all-to-all-done.9.terms_ref = bf16[8,24,1152]{2,1,0:T(8,128)(2,1)S(1)} async-done(((bf16[8,24,1152]{2,1,0:T(8,128)(2,1)}), bf16[8,24,1152]{2,1,0:T(8,128)(2,1)S(1)}, u32[]{:S(2)}, u32[]{:S(2)}) %all-to-all-start.9) | async-done | bytes 442400 | tf_op jit(solution)/shard_map/all_to_all | solution.py:564
  388.3 1.8 shard_map.388
  391.6 3.6 all-to-all-start.10
  396.7 7.9 %all-to-all-done.10 = f32[32,1,1664]{2,1,0:T(1,128)S(1)} async-done(((f32[32,1,1664]{2,1,0:T(1,128)}), f32[32,1,1664]{2,1,0:T(1,128)S(1)}, u32[]{:S(2)}, u32[]{:S(2)}) %all-to-all-start.10) | async-done | bytes 213024 | tf_op jit(solution)/shard_map/all_to_all | solution.py:564
  408.0 9.2 %shard_map.389 = (f32[24,2304]{1,0:T(8,128)}, f32[24,2304]{1,0:T(8,128)}, f32[24,2304]{1,0:T(8,128)}, f32[24,768]{1,0:T(8,128)}, f32[24,768]{1,0:T(8,128)}, /*in...) custom-call(f32[1]{0:T(128)} %bitcast.53.factor_ref, ...), custom_call_target="tpu_custom_call" | custom-call | flops 13271040 | bytes 18579456 | tf_op jit(solution)/shard_map/pallas_call | solution.py:590
  (166 shorter events, 43.4 us)
Async XLA Ops:
  8.1 7.0 %copy-start.18 = (bf16[24,2304]{1,0:T(8,128)(2,1)}, bf16[24,2304]{1,0:T(8,128)(2,1)S(1)}, u32[]{:S(2)}) copy-start(bf16[24,2304]{1,0:T(8,128)(2,1)S(1)} %convert_element_type.132) | copy-start | bytes 331780
  8.3 14.2 %copy-start.2 = (bf16[1,256,768]{2,1,0:T(8,128)(2,1)S(1)}, bf16[1,256,768]{2,1,0:T(8,128)(2,1)}, u32[]{:S(2)}) copy-start(bf16[1,256,768]{2,1,0:T(8,128)(2,1)} %param.23) | copy-start | bytes 1179652
  11.2 11.4 %copy-start.31 = (f32[2,768]{1,0:T(2,128)S(1)}, f32[2,768]{1,0:T(2,128)}, u32[]{:S(2)}) copy-start(f32[2,768]{1,0:T(2,128)} %param.31) | copy-start | bytes 18436
  15.1 14.3 %copy-start.4 = (f32[1,384,768]{2,1,0:T(8,128)S(1)}, f32[1,384,768]{2,1,0:T(8,128)}, u32[]{:S(2)}) copy-start(f32[1,384,768]{2,1,0:T(8,128)} %param.29) | copy-start | bytes 3538948
  15.1 40.3 %all-to-all-start = ((bf16[8,32,1152]{2,1,0:T(8,128)(2,1)}), bf16[8,32,1152]{2,1,0:T(8,128)(2,1)S(1)}, u32[]{:S(2)}, u32[]{:S(2)}) async-start(bf16[8,32,1152]{2,1,0:T(8,128)(2,1)} %fusion.47), calls=%async_computation | async-start | bytes 1179648 | tf_op jit(solution)/shard_map/all_to_all | solution.py:564
  23.4 6.8 %copy-start.6 = (bf16[256,768]{1,0:T(8,128)(2,1)}, bf16[256,768]{1,0:T(8,128)(2,1)S(1)}, u32[]{:S(2)}) copy-start(bf16[256,768]{1,0:T(8,128)(2,1)S(1)} %fusion.6.refs_0_) | copy-start | bytes 1179652
  23.5 16.2 %collective-permute-start = (bf16[256,768]{1,0:T(8,128)(2,1)S(1)}, bf16[256,768]{1,0:T(8,128)(2,1)S(1)}, u32[]{:S(2)}, u32[]{:S(2)}) collective-permute-start(bf16[256,768]{1,0:T(8,128)(2,1)S(1)} %fusion.6.refs_0_), channel_id=1, source_target_pairs={{0,4},{4,0},{8,12},{12,8},{16,20},{20,16},{24,28},{28,24},{1,5},{5... | collective-permute-start | bytes 1179656 | tf_op jit(solution)/shard_map/ppermute | solution.py:611
  25.5 23.6 %collective-permute-start.1 = (bf16[256,768]{1,0:T(8,128)(2,1)S(1)}, bf16[256,768]{1,0:T(8,128)(2,1)}, u32[]{:S(2)}, u32[]{:S(2)}) collective-permute-start(bf16[256,768]{1,0:T(8,128)(2,1)S(1)} %fusion.6.refs_0_), channel_id=1, source_target_pairs={{0,8},{4,12},{8,0},{12,4},{16,24},{20,28},{24,16},{28,20},{1,9},{5... | collective-permute-start | bytes 1179656 | tf_op jit(solution)/shard_map/ppermute | solution.py:611
  27.0 28.4 %collective-permute-start.2 = (bf16[256,768]{1,0:T(8,128)(2,1)S(1)}, bf16[256,768]{1,0:T(8,128)(2,1)}, u32[]{:S(2)}, u32[]{:S(2)}) collective-permute-start(bf16[256,768]{1,0:T(8,128)(2,1)S(1)} %fusion.6.refs_0_), channel_id=1, source_target_pairs={{0,16},{4,20},{8,24},{12,28},{16,0},{20,4},{24,8},{28,12},{1,17},{... | collective-permute-start | bytes 1179656 | tf_op jit(solution)/shard_map/ppermute | solution.py:611
  39.6 9.6 %copy-start.14 = (bf16[256,768]{1,0:T(8,128)(2,1)}, bf16[256,768]{1,0:T(8,128)(2,1)S(1)}, u32[]{:S(2)}) copy-start(bf16[256,768]{1,0:T(8,128)(2,1)S(1)} %collective-permute-done.refs_1_) | copy-start | bytes 1179652
  55.4 1.4 copy-start.9
  56.8 3.8 copy-start.34
  56.8 4.0 copy-start.7
  56.8 34.1 %all-to-all-start.1 = ((bf16[4,8,24,1152]{3,2,1,0:T(8,128)(2,1)}), bf16[4,8,24,1152]{3,2,1,0:T(8,128)(2,1)S(1)}, u32[]{:S(2)}, u32[]{:S(2)}) async-start(bf16[4,8,24,1152]{3,2,1,0:T(8,128)(2,1)} %broadcast_in_dim.24), calls=%async_computation.1 | async-start | bytes 3538944 | tf_op jit(solution)/shard_map/all_to_all | solution.py:564
  60.5 22.0 %copy-start.5 = (f32[1,384,768]{2,1,0:T(8,128)S(1)}, f32[1,384,768]{2,1,0:T(8,128)}, u32[]{:S(2)}) copy-start(f32[1,384,768]{2,1,0:T(8,128)} %param.30) | copy-start | bytes 3538948
  60.5 18.7 %collective-permute-start.5 = (bf16[256,768]{1,0:T(8,128)(2,1)}, bf16[256,768]{1,0:T(8,128)(2,1)S(1)}, u32[]{:S(2)}, u32[]{:S(2)}) collective-permute-start(bf16[256,768]{1,0:T(8,128)(2,1)} %collective-permute-done.2.refs_4_), channel_id=1, source_target_pairs={{0,8},{4,12},{8,0},{12,4},{16,24},{20,28},{24,16},{28,20},{1,9},{5... | collective-permute-start | bytes 1179656 | tf_op jit(solution)/shard_map/ppermute | solution.py:611
  60.8 29.3 %collective-permute-start.7 = (bf16[384,768]{1,0:T(8,128)(2,1)S(1)}, bf16[384,768]{1,0:T(8,128)(2,1)S(1)}, u32[]{:S(2)}, u32[]{:S(2)}) collective-permute-start(bf16[384,768]{1,0:T(8,128)(2,1)S(1)} %copy-done.7), channel_id=1, source_target_pairs={{16,0},{0,16},{17,1},{1,17},{18,2},{2,18},{19,3},{3,19},{20,4},{4,... | collective-permute-start | bytes 1769480 | tf_op jit(solution)/shard_map/ppermute | solution.py:617
  62.7 20.7 %collective-permute-start.4 = (bf16[256,768]{1,0:T(8,128)(2,1)}, bf16[256,768]{1,0:T(8,128)(2,1)S(1)}, u32[]{:S(2)}, u32[]{:S(2)}) collective-permute-start(bf16[256,768]{1,0:T(8,128)(2,1)} %collective-permute-done.2.refs_4_), channel_id=1, source_target_pairs={{0,4},{4,0},{8,12},{12,8},{16,20},{20,16},{24,28},{28,24},{1,5},{5... | collective-permute-start | bytes 1179656 | tf_op jit(solution)/shard_map/ppermute | solution.py:611
  64.5 19.0 %collective-permute-start.3 = (bf16[256,768]{1,0:T(8,128)(2,1)}, bf16[256,768]{1,0:T(8,128)(2,1)S(1)}, u32[]{:S(2)}, u32[]{:S(2)}) collective-permute-start(bf16[256,768]{1,0:T(8,128)(2,1)} %collective-permute-done.1.refs_2_), channel_id=1, source_target_pairs={{0,4},{4,0},{8,12},{12,8},{16,20},{20,16},{24,28},{28,24},{1,5},{5... | collective-permute-start | bytes 1179656 | tf_op jit(solution)/shard_map/ppermute | solution.py:611
  79.2 4.2 copy-start.15
  79.2 11.7 %collective-permute-start.6 = (bf16[256,768]{1,0:T(8,128)(2,1)S(1)}, bf16[256,768]{1,0:T(8,128)(2,1)}, u32[]{:S(2)}, u32[]{:S(2)}) collective-permute-start(bf16[256,768]{1,0:T(8,128)(2,1)S(1)} %collective-permute-done.5.refs_6_), channel_id=1, source_target_pairs={{0,4},{4,0},{8,12},{12,8},{16,20},{20,16},{24,28},{28,24},{1,5},{5... | collective-permute-start | bytes 1179656 | tf_op jit(solution)/shard_map/ppermute | solution.py:611
  83.4 6.7 %copy-start.17 = (bf16[256,768]{1,0:T(8,128)(2,1)}, bf16[256,768]{1,0:T(8,128)(2,1)S(1)}, u32[]{:S(2)}) copy-start(bf16[256,768]{1,0:T(8,128)(2,1)S(1)} %collective-permute-done.3.refs_3_) | copy-start | bytes 1179652
  83.4 6.7 %copy-start.16 = (bf16[256,768]{1,0:T(8,128)(2,1)}, bf16[256,768]{1,0:T(8,128)(2,1)S(1)}, u32[]{:S(2)}) copy-start(bf16[256,768]{1,0:T(8,128)(2,1)S(1)} %collective-permute-done.4.refs_5_) | copy-start | bytes 1179652
  92.2 44.8 %all-to-all-start.2 = ((bf16[8,128,768]{2,1,0:T(8,128)(2,1)}), bf16[8,128,768]{2,1,0:T(8,128)(2,1)S(1)}, u32[]{:S(2)}, u32[]{:S(2)}) async-start(bf16[8,128,768]{2,1,0:T(8,128)(2,1)} %bitcast.164), calls=%async_computation.2 | async-start | bytes 3145728 | tf_op jit(solution)/shard_map/all_to_all | solution.py:564
  95.8 35.4 %collective-permute-start.10 = (bf16[384,768]{1,0:T(8,128)(2,1)}, bf16[384,768]{1,0:T(8,128)(2,1)}, u32[]{:S(2)}, u32[]{:S(2)}) collective-permute-start(bf16[384,768]{1,0:T(8,128)(2,1)} %bitcast_convert_fusion.refs_4_), channel_id=1, source_target_pairs={{4,0},{0,4},{5,1},{1,5},{6,2},{2,6},{7,3},{3,7},{12,8},{8,12},{13,... | collective-permute-start | bytes 1769480 | tf_op jit(solution)/shard_map/ppermute | solution.py:617
  97.4 33.8 %collective-permute-start.8 = (bf16[384,768]{1,0:T(8,128)(2,1)}, bf16[384,768]{1,0:T(8,128)(2,1)}, u32[]{:S(2)}, u32[]{:S(2)}) collective-permute-start(bf16[384,768]{1,0:T(8,128)(2,1)} %bitcast_convert_fusion.refs_4_), channel_id=1, source_target_pairs={{16,0},{0,16},{17,1},{1,17},{18,2},{2,18},{19,3},{3,19},{20,4},{4,... | collective-permute-start | bytes 1769480 | tf_op jit(solution)/shard_map/ppermute | solution.py:617
  99.0 32.2 %collective-permute-start.11 = (bf16[384,768]{1,0:T(8,128)(2,1)}, bf16[384,768]{1,0:T(8,128)(2,1)}, u32[]{:S(2)}, u32[]{:S(2)}) collective-permute-start(bf16[384,768]{1,0:T(8,128)(2,1)} %copy-done.24), channel_id=1, source_target_pairs={{4,0},{0,4},{5,1},{1,5},{6,2},{2,6},{7,3},{3,7},{12,8},{8,12},{13,... | collective-permute-start | bytes 1769480 | tf_op jit(solution)/shard_map/ppermute | solution.py:617
  99.6 37.5 %collective-permute-start.9 = (bf16[384,768]{1,0:T(8,128)(2,1)}, bf16[384,768]{1,0:T(8,128)(2,1)}, u32[]{:S(2)}, u32[]{:S(2)}) collective-permute-start(bf16[384,768]{1,0:T(8,128)(2,1)} %bitcast_convert_fusion.1.refs_0_), channel_id=1, source_target_pairs={{4,0},{0,4},{5,1},{1,5},{6,2},{2,6},{7,3},{3,7},{12,8},{8,12},{13,... | collective-permute-start | bytes 1769480 | tf_op jit(solution)/shard_map/ppermute | solution.py:617
  137.0 27.7 %copy-start = (bf16[8,128,768]{2,1,0:T(8,128)(2,1)}, bf16[8,128,768]{2,1,0:T(8,128)(2,1)S(1)}, u32[]{:S(2)}) copy-start(bf16[8,128,768]{2,1,0:T(8,128)(2,1)S(1)} %all-to-all-done.2) | copy-start | bytes 4718596
  137.0 25.3 %all-to-all-start.3 = ((bf16[8,256,128]{2,1,0:T(8,128)(2,1)}), bf16[8,256,128]{2,1,0:T(8,128)(2,1)S(1)}, u32[]{:S(2)}, u32[]{:S(2)}) async-start(bf16[8,256,128]{2,1,0:T(8,128)(2,1)} %bitcast.185), calls=%async_computation.3 | async-start | bytes 1048576 | tf_op jit(solution)/shard_map/all_to_all | solution.py:564
  142.2 96.1 %all-gather.2.cloned.1.call-start = ((), (), s32[]{:S(2)}) async-start(), calls=%async_computation.11 | async-start | bytes 3649536 | tf_op jit(solution)/shard_map/all_gather | solution.py:790
  142.2 20.2 %collective-permute-start.12 = (bf16[384,768]{1,0:T(8,128)(2,1)}, bf16[384,768]{1,0:T(8,128)(2,1)}, u32[]{:S(2)}, u32[]{:S(2)}) collective-permute-start(bf16[384,768]{1,0:T(8,128)(2,1)} %collective-permute-done.8.refs_5_), channel_id=1, source_target_pairs={{4,0},{0,4},{5,1},{1,5},{6,2},{2,6},{7,3},{3,7},{12,8},{8,12},{13,... | collective-permute-start | bytes 1769480 | tf_op jit(solution)/shard_map/ppermute | solution.py:617
  163.2 1.5 copy-start.26
  163.2 1.9 copy-start.36
  210.6 27.7 %all-to-all-start.5 = ((bf16[8,128,768]{2,1,0:T(8,128)(2,1)}), bf16[8,128,768]{2,1,0:T(8,128)(2,1)}, u32[]{:S(2)}, u32[]{:S(2)}) async-start(bf16[8,128,768]{2,1,0:T(8,128)(2,1)} %bitcast.180), calls=%async_computation.5 | async-start | bytes 3145728 | tf_op jit(solution)/shard_map/all_to_all | solution.py:564
  221.7 15.8 %collective-permute-start.13 = (bf16[384,768]{1,0:T(8,128)(2,1)}, bf16[384,768]{1,0:T(8,128)(2,1)S(1)}, u32[]{:S(2)}, u32[]{:S(2)}) collective-permute-start(bf16[384,768]{1,0:T(8,128)(2,1)} %get-tuple-element.162), channel_id=1, source_target_pairs={{0,4},{4,0},{1,5},{5,1},{2,6},{6,2},{3,7},{7,3},{8,12},{12,8},{9,1... | collective-permute-start | bytes 1769480 | tf_op jit(solution)/shard_map/ppermute | solution.py:626
  241.2 16.9 %copy-start.1 = (f32[256,768]{1,0:T(8,128)}, f32[256,768]{1,0:T(8,128)S(1)}, u32[]{:S(2)}) copy-start(f32[256,768]{1,0:T(8,128)S(1)} %multiply_add_fusion.residual_ref) | copy-start | bytes 2359300
  241.7 10.6 %copy-start.19 = (f32[384,768]{1,0:T(8,128)S(1)}, f32[384,768]{1,0:T(8,128)}, u32[]{:S(2)}) copy-start(f32[384,768]{1,0:T(8,128)} %get-tuple-element.177) | copy-start | bytes 3538948
  247.1 45.5 %all-to-all-start.6 = ((bf16[8,256,128]{2,1,0:T(8,128)(2,1)}), bf16[8,256,128]{2,1,0:T(8,128)(2,1)S(1)}, u32[]{:S(2)}, u32[]{:S(2)}) async-start(bf16[8,256,128]{2,1,0:T(8,128)(2,1)} %fusion.48), calls=%async_computation.6 | async-start | bytes 1048576 | tf_op jit(solution)/shard_map/all_to_all | solution.py:564
  252.3 4.3 %copy-start.35 = (bf16[384,768]{1,0:T(8,128)(2,1)S(1)}, bf16[384,768]{1,0:T(8,128)(2,1)}, u32[]{:S(2)}) copy-start(bf16[384,768]{1,0:T(8,128)(2,1)} %get-tuple-element.176) | copy-start | bytes 1769476
  252.4 5.7 %copy-start.12 = (bf16[256,768]{1,0:T(8,128)(2,1)S(1)}, bf16[256,768]{1,0:T(8,128)(2,1)}, u32[]{:S(2)}) copy-start(bf16[256,768]{1,0:T(8,128)(2,1)} %copy-done.11) | copy-start | bytes 1179652
  253.6 38.2 %collective-permute-start.15 = (bf16[384,768]{1,0:T(8,128)(2,1)S(1)}, bf16[384,768]{1,0:T(8,128)(2,1)S(1)}, u32[]{:S(2)}, u32[]{:S(2)}) collective-permute-start(bf16[384,768]{1,0:T(8,128)(2,1)S(1)} %add_convert_fusion.1), channel_id=1, source_target_pairs={{0,16},{16,0},{1,17},{17,1},{2,18},{18,2},{3,19},{19,3},{4,20},{20... | collective-permute-start | bytes 1769480 | tf_op jit(solution)/shard_map/ppermute | solution.py:626
  256.6 36.0 %collective-permute-start.14 = (bf16[384,768]{1,0:T(8,128)(2,1)S(1)}, bf16[384,768]{1,0:T(8,128)(2,1)}, u32[]{:S(2)}, u32[]{:S(2)}) collective-permute-start(bf16[384,768]{1,0:T(8,128)(2,1)S(1)} %copy-done.35), channel_id=1, source_target_pairs={{0,4},{4,0},{1,5},{5,1},{2,6},{6,2},{3,7},{7,3},{8,12},{12,8},{9,1... | collective-permute-start | bytes 1769480 | tf_op jit(solution)/shard_map/ppermute | solution.py:626
  258.7 8.8 %collective-permute-start.16 = (bf16[8,24,768]{2,1,0:T(8,128)(2,1)S(1)}, bf16[8,24,768]{2,1,0:T(8,128)(2,1)S(1)}, u32[]{:S(2)}, u32[]{:S(2)}) collective-permute-start(bf16[8,24,768]{2,1,0:T(8,128)(2,1)S(1)} %get-tuple-element.236), channel_id=1, source_target_pairs={{0,1},{1,2},{2,3},{3,0},{4,5},{5,6},{6,7},{7,4},{8,9},{9,10},{10,1... | collective-permute-start | bytes 884744 | tf_op jit(solution)/shard_map/ppermute | solution.py:626
  258.8 9.9 %collective-permute-start.17 = (bf16[8,24,768]{2,1,0:T(8,128)(2,1)S(1)}, bf16[8,24,768]{2,1,0:T(8,128)(2,1)S(1)}, u32[]{:S(2)}, u32[]{:S(2)}) collective-permute-start(bf16[8,24,768]{2,1,0:T(8,128)(2,1)S(1)} %get-tuple-element.235), channel_id=1, source_target_pairs={{0,2},{1,3},{2,0},{3,1},{4,6},{5,7},{6,4},{7,5},{8,10},{9,11},{10,... | collective-permute-start | bytes 884744 | tf_op jit(solution)/shard_map/ppermute | solution.py:626
  260.3 13.1 %collective-permute-start.18 = (bf16[8,24,768]{2,1,0:T(8,128)(2,1)S(1)}, bf16[8,24,768]{2,1,0:T(8,128)(2,1)S(1)}, u32[]{:S(2)}, u32[]{:S(2)}) collective-permute-start(bf16[8,24,768]{2,1,0:T(8,128)(2,1)S(1)} %get-tuple-element.234), channel_id=1, source_target_pairs={{0,3},{1,0},{2,1},{3,2},{4,7},{5,4},{6,5},{7,6},{8,11},{9,8},{10,9... | collective-permute-start | bytes 884744 | tf_op jit(solution)/shard_map/ppermute | solution.py:626
  267.5 24.4 %copy-start.27 = (bf16[8,24,768]{2,1,0:T(8,128)(2,1)}, bf16[8,24,768]{2,1,0:T(8,128)(2,1)S(1)}, u32[]{:S(2)}) copy-start(bf16[8,24,768]{2,1,0:T(8,128)(2,1)S(1)} %collective-permute-done.16) | copy-start | bytes 884740
  268.7 23.1 %copy-start.28 = (bf16[8,24,768]{2,1,0:T(8,128)(2,1)}, bf16[8,24,768]{2,1,0:T(8,128)(2,1)S(1)}, u32[]{:S(2)}) copy-start(bf16[8,24,768]{2,1,0:T(8,128)(2,1)S(1)} %collective-permute-done.17) | copy-start | bytes 884740
  273.4 18.4 %copy-start.29 = (bf16[8,24,768]{2,1,0:T(8,128)(2,1)}, bf16[8,24,768]{2,1,0:T(8,128)(2,1)S(1)}, u32[]{:S(2)}) copy-start(bf16[8,24,768]{2,1,0:T(8,128)(2,1)S(1)} %collective-permute-done.18) | copy-start | bytes 884740
  293.4 36.2 %all-to-all-start.7 = ((bf16[8,128,768]{2,1,0:T(8,128)(2,1)}), bf16[8,128,768]{2,1,0:T(8,128)(2,1)S(1)}, u32[]{:S(2)}, u32[]{:S(2)}) async-start(bf16[8,128,768]{2,1,0:T(8,128)(2,1)} %bitcast.163), calls=%async_computation.7 | async-start | bytes 3145728 | tf_op jit(solution)/shard_map/all_to_all | solution.py:564
  299.4 28.3 %collective-permute-start.21 = (bf16[384,768]{1,0:T(8,128)(2,1)}, bf16[384,768]{1,0:T(8,128)(2,1)}, u32[]{:S(2)}, u32[]{:S(2)}) collective-permute-start(bf16[384,768]{1,0:T(8,128)(2,1)} %add_convert_fusion), channel_id=1, source_target_pairs={{0,16},{16,0},{1,17},{17,1},{2,18},{18,2},{3,19},{19,3},{4,20},{20... | collective-permute-start | bytes 1769480 | tf_op jit(solution)/shard_map/ppermute | solution.py:626
  299.7 28.0 %collective-permute-start.19 = (bf16[384,768]{1,0:T(8,128)(2,1)}, bf16[384,768]{1,0:T(8,128)(2,1)}, u32[]{:S(2)}, u32[]{:S(2)}) collective-permute-start(bf16[384,768]{1,0:T(8,128)(2,1)} %get-tuple-element.184), channel_id=1, source_target_pairs={{0,4},{4,0},{1,5},{5,1},{2,6},{6,2},{3,7},{7,3},{8,12},{12,8},{9,1... | collective-permute-start | bytes 1769480 | tf_op jit(solution)/shard_map/ppermute | solution.py:626
  301.4 26.7 %collective-permute-start.20 = (bf16[384,768]{1,0:T(8,128)(2,1)}, bf16[384,768]{1,0:T(8,128)(2,1)}, u32[]{:S(2)}, u32[]{:S(2)}) collective-permute-start(bf16[384,768]{1,0:T(8,128)(2,1)} %get-tuple-element.185), channel_id=1, source_target_pairs={{0,4},{4,0},{1,5},{5,1},{2,6},{6,2},{3,7},{7,3},{8,12},{12,8},{9,1... | collective-permute-start | bytes 1769480 | tf_op jit(solution)/shard_map/ppermute | solution.py:626
  329.7 41.4 %all-to-all-start.8 = ((bf16[8,256,384]{2,1,0:T(8,128)(2,1)}), bf16[8,256,384]{2,1,0:T(8,128)(2,1)}, u32[]{:S(2)}, u32[]{:S(2)}) async-start(bf16[8,256,384]{2,1,0:T(8,128)(2,1)} %bitcast.179), calls=%async_computation.8 | async-start | bytes 3145728 | tf_op jit(solution)/shard_map/all_to_all | solution.py:564
  341.7 4.2 copy-start.22
  342.9 9.0 %collective-permute-start.22 = (bf16[8,24,384]{2,1,0:T(8,128)(2,1)S(1)}, bf16[8,24,384]{2,1,0:T(8,128)(2,1)S(1)}, u32[]{:S(2)}, u32[]{:S(2)}) collective-permute-start(bf16[8,24,384]{2,1,0:T(8,128)(2,1)S(1)} %get-tuple-element.237), channel_id=1, source_target_pairs={{0,1},{1,2},{2,3},{3,0},{4,5},{5,6},{6,7},{7,4},{8,9},{9,10},{10,1... | collective-permute-start | bytes 442376 | tf_op jit(solution)/shard_map/ppermute | solution.py:626
  343.0 8.9 %collective-permute-start.23 = (bf16[8,24,384]{2,1,0:T(8,128)(2,1)S(1)}, bf16[8,24,384]{2,1,0:T(8,128)(2,1)S(1)}, u32[]{:S(2)}, u32[]{:S(2)}) collective-permute-start(bf16[8,24,384]{2,1,0:T(8,128)(2,1)S(1)} %get-tuple-element.239), channel_id=1, source_target_pairs={{0,2},{1,3},{2,0},{3,1},{4,6},{5,7},{6,4},{7,5},{8,10},{9,11},{10,... | collective-permute-start | bytes 442376 | tf_op jit(solution)/shard_map/ppermute | solution.py:626
  344.5 7.4 %collective-permute-start.24 = (bf16[8,24,384]{2,1,0:T(8,128)(2,1)S(1)}, bf16[8,24,384]{2,1,0:T(8,128)(2,1)S(1)}, u32[]{:S(2)}, u32[]{:S(2)}) collective-permute-start(bf16[8,24,384]{2,1,0:T(8,128)(2,1)S(1)} %get-tuple-element.238), channel_id=1, source_target_pairs={{0,3},{1,0},{2,1},{3,2},{4,7},{5,4},{6,5},{7,6},{8,11},{9,8},{10,9... | collective-permute-start | bytes 442376 | tf_op jit(solution)/shard_map/ppermute | solution.py:626
  345.9 7.0 %copy-start.20 = (bf16[8,24,768]{2,1,0:T(8,128)(2,1)S(1)}, bf16[8,24,768]{2,1,0:T(8,128)(2,1)}, u32[]{:S(2)}) copy-start(bf16[8,24,768]{2,1,0:T(8,128)(2,1)} %fusion.9) | copy-start | bytes 884740
  371.0 16.5 %all-to-all-start.9 = ((bf16[8,24,1152]{2,1,0:T(8,128)(2,1)}), bf16[8,24,1152]{2,1,0:T(8,128)(2,1)S(1)}, u32[]{:S(2)}, u32[]{:S(2)}) async-start(bf16[8,24,1152]{2,1,0:T(8,128)(2,1)} %pad_maximum_fusion), calls=%async_computation.9 | async-start | bytes 884736 | tf_op jit(solution)/shard_map/all_to_all | solution.py:564
  391.6 13.0 %all-to-all-start.10 = ((f32[32,1,1664]{2,1,0:T(1,128)}), f32[32,1,1664]{2,1,0:T(1,128)S(1)}, u32[]{:S(2)}, u32[]{:S(2)}) async-start(f32[32,1,1664]{2,1,0:T(1,128)} %broadcast_in_dim.62), calls=%async_computation.10 | async-start | bytes 425984 | tf_op jit(solution)/shard_map/all_to_all | solution.py:564
  395.5 11.8 %copy-start.32 = (f32[2,768]{1,0:T(2,128)S(1)}, f32[2,768]{1,0:T(2,128)}, u32[]{:S(2)}) copy-start(f32[2,768]{1,0:T(2,128)} %param.41) | copy-start | bytes 18436
  395.5 11.8 %copy-start.33 = (f32[2,768]{1,0:T(2,128)S(1)}, f32[2,768]{1,0:T(2,128)}, u32[]{:S(2)}) copy-start(f32[2,768]{1,0:T(2,128)} %param.40) | copy-start | bytes 18436
  405.9 11.3 %copy-start.30 = (f32[2,768]{1,0:T(2,128)}, f32[2,768]{1,0:T(2,128)S(1)}, u32[]{:S(2)}) copy-start(f32[2,768]{1,0:T(2,128)S(1)} %reshape.237) | copy-start | bytes 18436
  (9 other events, 7.8 us)
Sparse Core Ops, SparseCore 0:
  163.3 61.4 all-gather.1

commit v5 on v4

--- a/solution.py
+++ b/solution.py
@@ -749,13 +749,21 @@
     all_copies = swap(own_copies, EXP)
 
     peer_up = others(own_up, "hi")
-    *row_blocks, all_copies, peer_up, own_up, own_down, grad_slots_out = together(
-        *row_blocks, all_copies, peer_up, own_up, own_down, to_slots(cotangent[0])
-    )
-    all_copies = jnp.swapaxes(all_copies, 0, 1)
-    columns = all_copies[..., : 3 * LANES].reshape(width, 3 * LANES)
-    output_full = all_copies[..., 3 * LANES :].reshape(width, width)
-    grad_arrived = dispatch(grad_slots_out)
+    *row_blocks, all_copies, peer_up, own_up, own_down, slots_out, active, order, documents = (
+        together(
+            *row_blocks,
+            all_copies,
+            peer_up,
+            own_up,
+            own_down,
+            to_slots(cotangent[0]),
+            active,
+            order,
+            documents,
+        )
+    )
+    columns = jnp.swapaxes(all_copies[..., : 3 * LANES], 0, 1).reshape(width, 3 * LANES)
+    grad_arrived = dispatch(slots_out)
     peer_down = others(own_down, "hi")
     side_up = others(own_up, "in")
     side_down = others(own_down, "in")
@@ -780,9 +788,10 @@
     def to_tokens(values):
         return swap(values.reshape(count, row_count, values.shape[1]), SEQ)
 
-    mixed_low, grad_arrived, peer_down, side_up, side_down, far_up = together(
-        mixed_low, grad_arrived, peer_down, side_up, side_down, far_up
-    )
+    mixed_low, grad_arrived, peer_down, side_up, side_down, far_up, all_copies = together(
+        mixed_low, grad_arrived, peer_down, side_up, side_down, far_up, all_copies
+    )
+    output_full = jnp.swapaxes(all_copies[..., 3 * LANES :], 0, 1).reshape(width, width)
     far_down = others(peer_down, "in")
     mixed_pieces, projection_low, far_down = together(
         to_tokens(mixed_low), projection_low, far_down
@@ -910,7 +919,7 @@
             (expert_down, down_grad, down_first, down_second),
         ],
         (RATE_MATRIX, RATE_OUTPUT, RATE_MATRIX, RATE_MATRIX),
-        6,
+        3,
     )
     gains_moment, gains_square, gains_new = adam_update(
         norm_gains, gains_grad, gains_first, gains_second, factor, RATE_GAIN, 0.0

time: 427 us -> 431 us (level)
  waiting for transfers between devices: 138 us -> 144 us
    ppermute x6, waiting for transfers between devices: 30.7 us -> 35.7 us  [others(): lax.ppermute(value, axis, [((i + step) % size, i) for i in range(size)])]
    unnamed x82 -> x78, local copies, waits for them, and re-layouts: 10.2 us -> 10.7 us
  transfers between devices with their start and end apart: 36 -> 36, of which waited for: 19 -> 22; matrix products, arithmetic and copies ran while one was open for 7% -> 6% of each run, Pallas kernels for 22% -> 22%
where the time goes in v5:
time: 431 us; the launch traced here: 429 us
  waiting for transfers between devices  144 us (33%)
  Pallas kernels  105 us (24%)
  starting transfers between devices  77.1 us (18%)
  blocking collectives  27.6 us (6%)
  other arithmetic  27.3 us (6%)
  local copies, waits for them, and re-layouts  23 us (5%)
  between operations  18.4 us (4%)
  matrix products  7.19 us (2%)
    all_to_all x10, starting transfers between devices, swap(): return lax.all_to_all(value, axes, split_axis=0, concat_axis=0, tiled=True)  44.8 us
    ppermute x7, waiting for transfers between devices, flip(): lax.ppermute(value, SEQ, [(index, index ^ bits) for index in range(count)])  39.8 us
    ppermute x6, waiting for transfers between devices, others(): lax.ppermute(value, axis, [((i + step) % size, i) for i in range(size)])  35.7 us
    all_to_all x10, waiting for transfers between devices, swap(): return lax.all_to_all(value, axes, split_axis=0, concat_axis=0, tiled=True)  34.8 us
    ppermute x12, waiting for transfers between devices, to_owners(): lax.ppermute(block, axis, [(i, (i + step) % size) for i in range(size)])  33.6 us
    all_to_all x1, blocking collectives, swap(): return lax.all_to_all(value, axes, split_axis=0, concat_axis=0, tiled=True)  27.6 us
    pallas_call x1, Pallas kernels, attend_back(): pl.pallas_call(functools.partial(attend_back_kernel, block=block, chunk=2...  24.4 us
    pallas_call x1, Pallas kernels, attend(): pl.pallas_call(functools.partial(attend_kernel, block=block, chunk=2 * bl...  23.1 us
  transfers between devices with their start and end apart: 36, of which 22 were waited for; matrix products, arithmetic and copies ran while one was open for 6% of the time, Pallas kernels for 22%

profile of v5, /device:TPU:0, one launch (start us, length us, event | category | flops | bytes accessed | tf_op | source)
XLA Modules:
  0.0 429.5 jit_solution(13650409223090969343)
XLA Ops:
  15.1 7.4 %all-to-all-start = ((bf16[8,32,1152]{2,1,0:T(8,128)(2,1)}), bf16[8,32,1152]{2,1,0:T(8,128)(2,1)S(1)}, u32[]{:S(2)}, u32[]{:S(2)}) async-start(bf16[8,32,1152]{2,1,0:T(8,128)(2,1)} %fusion.47), calls=%async_computation | async-start | bytes 1179648 | tf_op jit(solution)/shard_map/all_to_all | solution.py:564
  23.5 2.1 collective-permute-start
  25.5 1.5 collective-permute-start.1
  27.0 2.4 collective-permute-start.2
  30.2 9.4 %collective-permute-done.refs_1_ = bf16[256,768]{1,0:T(8,128)(2,1)S(1)} collective-permute-done((bf16[256,768]{1,0:T(8,128)(2,1)S(1)}, bf16[256,768]{1,0:T(8,128)(2,1)S(1)}, u32[]{:S(2)}, u32[]{:S(2)}) %collective-permute-start) | collective-permute-done | bytes 393248 | tf_op jit(solution)/shard_map/ppermute | solution.py:611
  39.6 9.5 %collective-permute-done.1.refs_2_ = bf16[256,768]{1,0:T(8,128)(2,1)S(1)} collective-permute-done((bf16[256,768]{1,0:T(8,128)(2,1)S(1)}, bf16[256,768]{1,0:T(8,128)(2,1)S(1)}, u32[]{:S(2)}, u32[]{:S(2)}) %collective-permute-start.1) | collective-permute-done | bytes 393248 | tf_op jit(solution)/shard_map/ppermute | solution.py:611
  49.8 5.5 %collective-permute-done.2.refs_4_ = bf16[256,768]{1,0:T(8,128)(2,1)} collective-permute-done((bf16[256,768]{1,0:T(8,128)(2,1)S(1)}, bf16[256,768]{1,0:T(8,128)(2,1)}, u32[]{:S(2)}, u32[]{:S(2)}) %collective-permute-start.2) | collective-permute-done | bytes 393248 | tf_op jit(solution)/shard_map/ppermute | solution.py:611
  55.4 1.4 broadcast_in_dim.24
  56.8 3.7 all-to-all-start.1
  60.9 1.5 convolution_convert_fusion.2
  62.3 1.8 collective-permute-start.7
  65.3 1.7 collective-permute-start.4
  67.4 10.8 %collective-permute-done.5.refs_6_ = bf16[256,768]{1,0:T(8,128)(2,1)} collective-permute-done((bf16[256,768]{1,0:T(8,128)(2,1)}, bf16[256,768]{1,0:T(8,128)(2,1)}, u32[]{:S(2)}, u32[]{:S(2)}) %collective-permute-start.5) | collective-permute-done | bytes 393248 | tf_op jit(solution)/shard_map/ppermute | solution.py:611
  78.2 1.7 collective-permute-start.6
  82.1 3.8 collective-permute-done.3.refs_3_
  86.0 5.8 %collective-permute-done.7.refs_1_ = bf16[384,768]{1,0:T(8,128)(2,1)S(1)} collective-permute-done((bf16[384,768]{1,0:T(8,128)(2,1)}, bf16[384,768]{1,0:T(8,128)(2,1)S(1)}, u32[]{:S(2)}, u32[]{:S(2)}) %collective-permute-start.7) | collective-permute-done | bytes 589856 | tf_op jit(solution)/shard_map/ppermute | solution.py:617
  94.5 2.4 broadcast_in_dim.28
  97.0 3.6 all-to-all-start.2
  100.5 1.8 collective-permute-start.10
  102.3 1.6 collective-permute-start.8
  104.5 1.5 collective-permute-start.9
  106.9 23.1 %shard_map.380 = (bf16[2048,128]{1,0:T(8,128)(2,1)}, f32[2048,128]{1,0:T(8,128)}, bf16[2048,256]{1,0:T(8,128)(2,1)}, bf16[2048,256]{1,0:T(8,128)(2,1)}) custom-call(s32[2,8]{1,0:T(2,128)} %fusion.58.active_ref, s32[8]{0:T(128)} %iota_xor_fusion.order_ref, bf16[256,768]{1,0:T(8,128)(2,1)} %copy-done.6, bf16[256,768]{1,0:T(8,128)(2,1)} %copy-done.14, ...), custom_call_target="tpu_custom_call" | custom-call | flops 1 | bytes 1 | tf_op jit(solution)/shard_map/pallas_call | solution.py:278
  131.2 10.6 %collective-permute-done.9.refs_2_ = bf16[384,768]{1,0:T(8,128)(2,1)} collective-permute-done((bf16[384,768]{1,0:T(8,128)(2,1)}, bf16[384,768]{1,0:T(8,128)(2,1)}, u32[]{:S(2)}, u32[]{:S(2)}) %collective-permute-start.9) | collective-permute-done | bytes 589856 | tf_op jit(solution)/shard_map/ppermute | solution.py:617
  141.8 5.3 %all-to-all-start.3 = ((bf16[8,256,128]{2,1,0:T(8,128)(2,1)}), bf16[8,256,128]{2,1,0:T(8,128)(2,1)}, u32[]{:S(2)}, u32[]{:S(2)}) async-start(bf16[8,256,128]{2,1,0:T(8,128)(2,1)} %bitcast.186), calls=%async_computation.3 | async-start | bytes 1048576 | tf_op jit(solution)/shard_map/all_to_all | solution.py:564
  147.2 2.0 collective-permute-start.12
  149.1 18.2 %collective-permute-done.12.refs_7_ = bf16[384,768]{1,0:T(8,128)(2,1)} collective-permute-done((bf16[384,768]{1,0:T(8,128)(2,1)}, bf16[384,768]{1,0:T(8,128)(2,1)}, u32[]{:S(2)}, u32[]{:S(2)}) %collective-permute-start.12) | collective-permute-done | bytes 589856 | tf_op jit(solution)/shard_map/ppermute | solution.py:617
  167.6 1.3 copy-done.34
  168.9 1.7 fusion
  172.1 27.6 %all_to_all.55 = bf16[8,128,768]{2,1,0:T(8,128)(2,1)} all-to-all(bf16[8,128,768]{2,1,0:T(8,128)(2,1)S(1)} %bitcast.166), channel_id=1, replica_groups=mesh['hi'=2,'lo'=2,'in'=2,'exp'=4] {'lo','exp'}, dimensions={0} | all-to-all | bytes 3145728 | tf_op jit(solution)/shard_map/all_to_all | solution.py:564
  199.7 15.5 %shard_map.381 = (bf16[1024,768]{1,0:T(8,128)(2,1)}, bf16[1024,384]{1,0:T(8,128)(2,1)}, bf16[1024,384]{1,0:T(8,128)(2,1)}, bf16[1024,384]{1,0:T(8,128)(2,1)}, bf...) custom-call(bf16[1024,768]{1,0:T(8,128)(2,1)} %bitcast.158, ...), custom_call_target="tpu_custom_call" | custom-call | flops 1 | bytes 1 | tf_op jit(solution)/shard_map/pallas_call | solution.py:372
  215.2 4.3 %all-to-all-start.5 = ((bf16[8,128,768]{2,1,0:T(8,128)(2,1)}), bf16[8,128,768]{2,1,0:T(8,128)(2,1)}, u32[]{:S(2)}, u32[]{:S(2)}) async-start(bf16[8,128,768]{2,1,0:T(8,128)(2,1)} %bitcast.181), calls=%async_computation.5 | async-start | bytes 3145728 | tf_op jit(solution)/shard_map/all_to_all | solution.py:564
  219.5 6.7 %shard_map.382 = (bf16[384,768]{1,0:T(8,128)(2,1)}, bf16[384,768]{1,0:T(8,128)(2,1)}, f32[384,768]{1,0:T(8,128)}, f32[384,768]{1,0:T(8,128)}) custom-call(bf16[1024,768]{1,0:T(8,128)(2,1)} %bitcast.156, bf16[1024,768]{1,0:T(8,128)(2,1)} %bitcast.159, bf16[1024,384]{1,0:T(8,128)(2,1)} %get-tuple-element.166.refs_0_.refs_3_, ...), custom_call_target="tpu_custom_call" | custom-call | flops 1 | bytes 1 | tf_op jit(solution)/shard_map/pallas_call | solution.py:425
  226.8 7.1 %shard_map.383 = bf16[1024,768]{1,0:T(8,128)(2,1)} custom-call(bf16[1024,384]{1,0:T(8,128)(2,1)} %get-tuple-element.174.refs_0_.refs_2_, bf16[1024,384]{1,0:T(8,128)(2,1)} %get-tuple-element.168.refs_2_.refs_1_, bf16[1024,384]{1,0:T(8,128)(2,1)} %get-tuple-element.175.refs_2_.refs_0_, bf16[1024,384]{1,0:T(8,128)(2,1)} %get-tuple-element.166.refs_0_.refs_3_, ...), custom_call_target="tpu_custom_call" | custom-call | flops 1 | bytes 1 | tf_op jit(solution)/shard_map/pallas_call | solution.py:396
  234.0 6.7 %shard_map.384 = (bf16[384,768]{1,0:T(8,128)(2,1)}, bf16[384,768]{1,0:T(8,128)(2,1)}, f32[384,768]{1,0:T(8,128)}, f32[384,768]{1,0:T(8,128)}) custom-call(bf16[1024,768]{1,0:T(8,128)(2,1)} %bitcast.157, bf16[1024,768]{1,0:T(8,128)(2,1)} %bitcast.160, bf16[1024,384]{1,0:T(8,128)(2,1)} %get-tuple-element.175.refs_2_.refs_0_, ...), custom_call_target="tpu_custom_call" | custom-call | flops 1 | bytes 1 | tf_op jit(solution)/shard_map/pallas_call | solution.py:425
  240.7 1.4 collective-permute-done.13
  243.0 1.7 convert_reduce_fusion.1
  251.8 5.1 %all-to-all-start.6 = ((bf16[8,256,128]{2,1,0:T(8,128)(2,1)}), bf16[8,256,128]{2,1,0:T(8,128)(2,1)S(1)}, u32[]{:S(2)}, u32[]{:S(2)}) async-start(bf16[8,256,128]{2,1,0:T(8,128)(2,1)} %fusion.48), calls=%async_computation.6 | async-start | bytes 1048576 | tf_op jit(solution)/shard_map/all_to_all | solution.py:564
  258.2 3.0 collective-permute-start.15
  261.2 1.5 collective-permute-start.14
  263.4 1.5 collective-permute-start.17
  264.9 1.4 collective-permute-start.18
  266.3 5.8 %collective-permute-done.16 = bf16[8,24,768]{2,1,0:T(8,128)(2,1)S(1)} collective-permute-done((bf16[8,24,768]{2,1,0:T(8,128)(2,1)S(1)}, bf16[8,24,768]{2,1,0:T(8,128)(2,1)S(1)}, u32[]{:S(2)}, u32[]{:S(2)}) %collective-permute-start.16) | collective-permute-done | bytes 294944 | tf_op jit(solution)/shard_map/ppermute | solution.py:626
  273.3 4.7 %collective-permute-done.18 = bf16[8,24,768]{2,1,0:T(8,128)(2,1)S(1)} collective-permute-done((bf16[8,24,768]{2,1,0:T(8,128)(2,1)S(1)}, bf16[8,24,768]{2,1,0:T(8,128)(2,1)S(1)}, u32[]{:S(2)}, u32[]{:S(2)}) %collective-permute-start.18) | collective-permute-done | bytes 294944 | tf_op jit(solution)/shard_map/ppermute | solution.py:626
  278.0 18.5 %collective-permute-done.15 = bf16[384,768]{1,0:T(8,128)(2,1)S(1)} collective-permute-done((bf16[384,768]{1,0:T(8,128)(2,1)S(1)}, bf16[384,768]{1,0:T(8,128)(2,1)S(1)}, u32[]{:S(2)}, u32[]{:S(2)}) %collective-permute-start.15) | collective-permute-done | bytes 589856 | tf_op jit(solution)/shard_map/ppermute | solution.py:626
  298.1 3.6 all-to-all-start.7
  301.7 2.3 add_convert_fusion
  304.3 1.8 collective-permute-start.19
  306.3 24.4 %shard_map.385 = (bf16[2048,384]{1,0:T(8,128)(2,1)}, bf16[2048,384]{1,0:T(8,128)(2,1)}) custom-call(s32[2,8]{1,0:T(2,128)} %fusion.58.active_ref, s32[8]{0:T(128)} %iota_xor_fusion.order_ref, bf16[2048,256]{1,0:T(8,128)(2,1)} %get-tuple-element.158.pair_ref, bf16[2048,128]{1,0:T(8,128)(2,1)} %broadcast_in_dim.26.refs_9_.documents_ref, ...), custom_call_target="tpu_custom_call" | custom-call | flops 1 | bytes 1 | tf_op jit(solution)/shard_map/pallas_call | solution.py:309
  330.7 1.6 collective-permute-done.21
  332.8 1.5 all-to-all-done.7
  334.3 4.5 %all-to-all-start.8 = ((bf16[8,256,384]{2,1,0:T(8,128)(2,1)}), bf16[8,256,384]{2,1,0:T(8,128)(2,1)}, u32[]{:S(2)}, u32[]{:S(2)}) async-start(bf16[8,256,384]{2,1,0:T(8,128)(2,1)} %bitcast.180), calls=%async_computation.8 | async-start | bytes 3145728 | tf_op jit(solution)/shard_map/all_to_all | solution.py:564
  338.8 2.0 fusion.9
  340.8 5.5 %shard_map.386 = bf16[768,384]{1,0:T(8,128)(2,1)} custom-call(bf16[256,768]{1,0:T(8,128)(2,1)} %copy-done.6, bf16[256,768]{1,0:T(8,128)(2,1)} %copy-done.14, bf16[256,768]{1,0:T(8,128)(2,1)} %copy-done.15, bf16[256,768]{1,0:T(8,128)(2,1)} %copy-done.17, bf16[256,768]{1,0:T(8,128)(2,1)} %collective-permute-done.2.refs_4_, bf16[256,768]{1,0:T(8,128)(2,1)} %copy-done.16, ...), custom_call_target="tpu_custom_call" | custom-call | flops 1 | bytes 1 | tf_op jit(solution)/shard_map/pallas_call | solution.py:452
  347.6 1.5 collective-permute-start.23
  349.2 1.4 collective-permute-start.24
  350.6 4.7 %multiply_reduce_fusion = (f32[]{:T(128)}, f32[384,768]{1,0:T(8,128)}, f32[]{:T(128)}, f32[384,768]{1,0:T(8,128)}) fusion(bf16[384,768]{1,0:T(8,128)(2,1)S(1)} %copy-done.22, f32[384,768]{1,0:T(8,128)} %get-tuple-element.205, bf16[384,768]{1,0:T(8,128)(2,1)} %collective-permute-done.19, bf16[384,768]{1,0:T(8,128)(2,1)} %collective-permute-done.21, ...), kind=kLoop, calls=%fused_computation.14 | loop fusion | flops 3538942 | bytes 7077896 | tf_op jit(solution)/shard_map/reduce_sum | solution.py:891
  358.4 17.3 %all-to-all-done.8.pieces_ref = bf16[8,256,384]{2,1,0:T(8,128)(2,1)} async-done(((bf16[8,256,384]{2,1,0:T(8,128)(2,1)}), bf16[8,256,384]{2,1,0:T(8,128)(2,1)}, u32[]{:S(2)}, u32[]{:S(2)}) %all-to-all-start.8) | async-done | bytes 1572896 | tf_op jit(solution)/shard_map/all_to_all | solution.py:564
  375.7 3.6 all-to-all-start.9
  379.3 5.1 %shard_map.387 = (f32[256,768]{1,0:T(8,128)}, f32[1,768]{1,0:T(1,128)}) custom-call(bf16[8,256,384]{2,1,0:T(8,128)(2,1)} %all-to-all-done.8.pieces_ref, bf16[768,2304]{1,0:T(8,128)(2,1)} %all-gather.2.cloned.1.call-done.matrix_ref, bf16[256,768]{1,0:T(8,128)(2,1)} %bitcast.167, f32[1,768]{1,0:T(1,128)} %get-tuple-element.272.gain_ref, f32[256,768]{1,0:T(8,128)} %copy-done.1), custom_call_target="tpu_custom_call" | custom-call | flops 1 | bytes 1 | tf_op jit(solution)/shard_map/pallas_call | solution.py:499
  385.1 7.1 %all-to-all-done.9.terms_ref = bf16[8,24,1152]{2,1,0:T(8,128)(2,1)S(1)} async-done(((bf16[8,24,1152]{2,1,0:T(8,128)(2,1)}), bf16[8,24,1152]{2,1,0:T(8,128)(2,1)S(1)}, u32[]{:S(2)}, u32[]{:S(2)}) %all-to-all-start.9) | async-done | bytes 442400 | tf_op jit(solution)/shard_map/all_to_all | solution.py:564
  393.0 1.8 shard_map.388
  396.3 3.6 all-to-all-start.10
  401.3 7.9 %all-to-all-done.10 = f32[32,1,1664]{2,1,0:T(1,128)S(1)} async-done(((f32[32,1,1664]{2,1,0:T(1,128)}), f32[32,1,1664]{2,1,0:T(1,128)S(1)}, u32[]{:S(2)}, u32[]{:S(2)}) %all-to-all-start.10) | async-done | bytes 213024 | tf_op jit(solution)/shard_map/all_to_all | solution.py:564
  412.6 8.9 %shard_map.389 = (f32[24,2304]{1,0:T(8,128)}, f32[24,2304]{1,0:T(8,128)}, f32[24,2304]{1,0:T(8,128)}, f32[24,768]{1,0:T(8,128)}, f32[24,768]{1,0:T(8,128)}, /*in...) custom-call(f32[1]{0:T(128)} %bitcast.55.factor_ref, ...), custom_call_target="tpu_custom_call" | custom-call | flops 13271040 | bytes 18579456 | tf_op jit(solution)/shard_map/pallas_call | solution.py:590
  (163 shorter events, 45.2 us)
Async XLA Ops:
  8.1 7.0 %copy-start.18 = (bf16[24,2304]{1,0:T(8,128)(2,1)}, bf16[24,2304]{1,0:T(8,128)(2,1)S(1)}, u32[]{:S(2)}) copy-start(bf16[24,2304]{1,0:T(8,128)(2,1)S(1)} %convert_element_type.132) | copy-start | bytes 331780
  8.3 14.2 %copy-start.2 = (bf16[1,256,768]{2,1,0:T(8,128)(2,1)S(1)}, bf16[1,256,768]{2,1,0:T(8,128)(2,1)}, u32[]{:S(2)}) copy-start(bf16[1,256,768]{2,1,0:T(8,128)(2,1)} %param.23) | copy-start | bytes 1179652
  11.2 11.4 %copy-start.29 = (f32[2,768]{1,0:T(2,128)S(1)}, f32[2,768]{1,0:T(2,128)}, u32[]{:S(2)}) copy-start(f32[2,768]{1,0:T(2,128)} %param.31) | copy-start | bytes 18436
  15.1 14.3 %copy-start.4 = (f32[1,384,768]{2,1,0:T(8,128)S(1)}, f32[1,384,768]{2,1,0:T(8,128)}, u32[]{:S(2)}) copy-start(f32[1,384,768]{2,1,0:T(8,128)} %param.29) | copy-start | bytes 3538948
  15.1 40.3 %all-to-all-start = ((bf16[8,32,1152]{2,1,0:T(8,128)(2,1)}), bf16[8,32,1152]{2,1,0:T(8,128)(2,1)S(1)}, u32[]{:S(2)}, u32[]{:S(2)}) async-start(bf16[8,32,1152]{2,1,0:T(8,128)(2,1)} %fusion.47), calls=%async_computation | async-start | bytes 1179648 | tf_op jit(solution)/shard_map/all_to_all | solution.py:564
  23.4 6.8 %copy-start.6 = (bf16[256,768]{1,0:T(8,128)(2,1)}, bf16[256,768]{1,0:T(8,128)(2,1)S(1)}, u32[]{:S(2)}) copy-start(bf16[256,768]{1,0:T(8,128)(2,1)S(1)} %fusion.6.refs_0_) | copy-start | bytes 1179652
  23.5 16.2 %collective-permute-start = (bf16[256,768]{1,0:T(8,128)(2,1)S(1)}, bf16[256,768]{1,0:T(8,128)(2,1)S(1)}, u32[]{:S(2)}, u32[]{:S(2)}) collective-permute-start(bf16[256,768]{1,0:T(8,128)(2,1)S(1)} %fusion.6.refs_0_), channel_id=1, source_target_pairs={{0,4},{4,0},{8,12},{12,8},{16,20},{20,16},{24,28},{28,24},{1,5},{5... | collective-permute-start | bytes 1179656 | tf_op jit(solution)/shard_map/ppermute | solution.py:611
  25.5 23.5 %collective-permute-start.1 = (bf16[256,768]{1,0:T(8,128)(2,1)S(1)}, bf16[256,768]{1,0:T(8,128)(2,1)S(1)}, u32[]{:S(2)}, u32[]{:S(2)}) collective-permute-start(bf16[256,768]{1,0:T(8,128)(2,1)S(1)} %fusion.6.refs_0_), channel_id=1, source_target_pairs={{0,8},{4,12},{8,0},{12,4},{16,24},{20,28},{24,16},{28,20},{1,9},{5... | collective-permute-start | bytes 1179656 | tf_op jit(solution)/shard_map/ppermute | solution.py:611
  27.0 28.4 %collective-permute-start.2 = (bf16[256,768]{1,0:T(8,128)(2,1)S(1)}, bf16[256,768]{1,0:T(8,128)(2,1)}, u32[]{:S(2)}, u32[]{:S(2)}) collective-permute-start(bf16[256,768]{1,0:T(8,128)(2,1)S(1)} %fusion.6.refs_0_), channel_id=1, source_target_pairs={{0,16},{4,20},{8,24},{12,28},{16,0},{20,4},{24,8},{28,12},{1,17},{... | collective-permute-start | bytes 1179656 | tf_op jit(solution)/shard_map/ppermute | solution.py:611
  39.6 9.5 %copy-start.14 = (bf16[256,768]{1,0:T(8,128)(2,1)}, bf16[256,768]{1,0:T(8,128)(2,1)S(1)}, u32[]{:S(2)}) copy-start(bf16[256,768]{1,0:T(8,128)(2,1)S(1)} %collective-permute-done.refs_1_) | copy-start | bytes 1179652
  55.4 1.5 copy-start.8
  56.8 3.7 copy-start.32
  56.8 4.0 copy-start.12
  56.8 36.6 %all-to-all-start.1 = ((bf16[4,8,24,1152]{3,2,1,0:T(8,128)(2,1)}), bf16[4,8,24,1152]{3,2,1,0:T(8,128)(2,1)S(1)}, u32[]{:S(2)}, u32[]{:S(2)}) async-start(bf16[4,8,24,1152]{3,2,1,0:T(8,128)(2,1)} %broadcast_in_dim.24), calls=%async_computation.1 | async-start | bytes 3538944 | tf_op jit(solution)/shard_map/all_to_all | solution.py:564
  60.5 19.9 %copy-start.5 = (f32[1,384,768]{2,1,0:T(8,128)S(1)}, f32[1,384,768]{2,1,0:T(8,128)}, u32[]{:S(2)}) copy-start(f32[1,384,768]{2,1,0:T(8,128)} %param.30) | copy-start | bytes 3538948
  60.8 17.4 %collective-permute-start.5 = (bf16[256,768]{1,0:T(8,128)(2,1)}, bf16[256,768]{1,0:T(8,128)(2,1)}, u32[]{:S(2)}, u32[]{:S(2)}) collective-permute-start(bf16[256,768]{1,0:T(8,128)(2,1)} %collective-permute-done.2.refs_4_), channel_id=1, source_target_pairs={{0,8},{4,12},{8,0},{12,4},{16,24},{20,28},{24,16},{28,20},{1,9},{5... | collective-permute-start | bytes 1179656 | tf_op jit(solution)/shard_map/ppermute | solution.py:611
  62.3 29.5 %collective-permute-start.7 = (bf16[384,768]{1,0:T(8,128)(2,1)}, bf16[384,768]{1,0:T(8,128)(2,1)S(1)}, u32[]{:S(2)}, u32[]{:S(2)}) collective-permute-start(bf16[384,768]{1,0:T(8,128)(2,1)} %bitcast_convert_fusion.1.refs_0_), channel_id=1, source_target_pairs={{16,0},{0,16},{17,1},{1,17},{18,2},{2,18},{19,3},{3,19},{20,4},{4,... | collective-permute-start | bytes 1769480 | tf_op jit(solution)/shard_map/ppermute | solution.py:617
  65.3 20.6 %collective-permute-start.4 = (bf16[256,768]{1,0:T(8,128)(2,1)}, bf16[256,768]{1,0:T(8,128)(2,1)S(1)}, u32[]{:S(2)}, u32[]{:S(2)}) collective-permute-start(bf16[256,768]{1,0:T(8,128)(2,1)} %collective-permute-done.2.refs_4_), channel_id=1, source_target_pairs={{0,4},{4,0},{8,12},{12,8},{16,20},{20,16},{24,28},{28,24},{1,5},{5... | collective-permute-start | bytes 1179656 | tf_op jit(solution)/shard_map/ppermute | solution.py:611
  67.1 18.9 %collective-permute-start.3 = (bf16[256,768]{1,0:T(8,128)(2,1)}, bf16[256,768]{1,0:T(8,128)(2,1)S(1)}, u32[]{:S(2)}, u32[]{:S(2)}) collective-permute-start(bf16[256,768]{1,0:T(8,128)(2,1)} %copy-done.15), channel_id=1, source_target_pairs={{0,4},{4,0},{8,12},{12,8},{16,20},{20,16},{24,28},{28,24},{1,5},{5... | collective-permute-start | bytes 1179656 | tf_op jit(solution)/shard_map/ppermute | solution.py:611
  78.2 15.2 %collective-permute-start.6 = (bf16[256,768]{1,0:T(8,128)(2,1)}, bf16[256,768]{1,0:T(8,128)(2,1)}, u32[]{:S(2)}, u32[]{:S(2)}) collective-permute-start(bf16[256,768]{1,0:T(8,128)(2,1)} %collective-permute-done.5.refs_6_), channel_id=1, source_target_pairs={{0,4},{4,0},{8,12},{12,8},{16,20},{20,16},{24,28},{28,24},{1,5},{5... | collective-permute-start | bytes 1179656 | tf_op jit(solution)/shard_map/ppermute | solution.py:611
  86.0 5.9 %copy-start.17 = (bf16[256,768]{1,0:T(8,128)(2,1)}, bf16[256,768]{1,0:T(8,128)(2,1)S(1)}, u32[]{:S(2)}) copy-start(bf16[256,768]{1,0:T(8,128)(2,1)S(1)} %collective-permute-done.3.refs_3_) | copy-start | bytes 1179652
  86.0 11.0 %copy-start.16 = (bf16[256,768]{1,0:T(8,128)(2,1)}, bf16[256,768]{1,0:T(8,128)(2,1)S(1)}, u32[]{:S(2)}) copy-start(bf16[256,768]{1,0:T(8,128)(2,1)S(1)} %collective-permute-done.4.refs_5_) | copy-start | bytes 1179652
  97.0 44.8 %all-to-all-start.2 = ((bf16[8,128,768]{2,1,0:T(8,128)(2,1)}), bf16[8,128,768]{2,1,0:T(8,128)(2,1)S(1)}, u32[]{:S(2)}, u32[]{:S(2)}) async-start(bf16[8,128,768]{2,1,0:T(8,128)(2,1)} %bitcast.165), calls=%async_computation.2 | async-start | bytes 3145728 | tf_op jit(solution)/shard_map/all_to_all | solution.py:564
  100.5 29.5 %collective-permute-start.10 = (bf16[384,768]{1,0:T(8,128)(2,1)}, bf16[384,768]{1,0:T(8,128)(2,1)}, u32[]{:S(2)}, u32[]{:S(2)}) collective-permute-start(bf16[384,768]{1,0:T(8,128)(2,1)} %bitcast_convert_fusion.refs_4_), channel_id=1, source_target_pairs={{4,0},{0,4},{5,1},{1,5},{6,2},{2,6},{7,3},{3,7},{12,8},{8,12},{13,... | collective-permute-start | bytes 1769480 | tf_op jit(solution)/shard_map/ppermute | solution.py:617
  102.3 28.8 %collective-permute-start.8 = (bf16[384,768]{1,0:T(8,128)(2,1)}, bf16[384,768]{1,0:T(8,128)(2,1)}, u32[]{:S(2)}, u32[]{:S(2)}) collective-permute-start(bf16[384,768]{1,0:T(8,128)(2,1)} %bitcast_convert_fusion.refs_4_), channel_id=1, source_target_pairs={{16,0},{0,16},{17,1},{1,17},{18,2},{2,18},{19,3},{3,19},{20,4},{4,... | collective-permute-start | bytes 1769480 | tf_op jit(solution)/shard_map/ppermute | solution.py:617
  104.0 26.1 %collective-permute-start.11 = (bf16[384,768]{1,0:T(8,128)(2,1)}, bf16[384,768]{1,0:T(8,128)(2,1)}, u32[]{:S(2)}, u32[]{:S(2)}) collective-permute-start(bf16[384,768]{1,0:T(8,128)(2,1)} %copy-done.24), channel_id=1, source_target_pairs={{4,0},{0,4},{5,1},{1,5},{6,2},{2,6},{7,3},{3,7},{12,8},{8,12},{13,... | collective-permute-start | bytes 1769480 | tf_op jit(solution)/shard_map/ppermute | solution.py:617
  104.5 37.3 %collective-permute-start.9 = (bf16[384,768]{1,0:T(8,128)(2,1)}, bf16[384,768]{1,0:T(8,128)(2,1)}, u32[]{:S(2)}, u32[]{:S(2)}) collective-permute-start(bf16[384,768]{1,0:T(8,128)(2,1)} %bitcast_convert_fusion.1.refs_0_), channel_id=1, source_target_pairs={{4,0},{0,4},{5,1},{1,5},{6,2},{2,6},{7,3},{3,7},{12,8},{8,12},{13,... | collective-permute-start | bytes 1769480 | tf_op jit(solution)/shard_map/ppermute | solution.py:617
  141.8 25.7 %copy-start = (bf16[8,128,768]{2,1,0:T(8,128)(2,1)}, bf16[8,128,768]{2,1,0:T(8,128)(2,1)S(1)}, u32[]{:S(2)}) copy-start(bf16[8,128,768]{2,1,0:T(8,128)(2,1)S(1)} %all-to-all-done.2) | copy-start | bytes 4718596
  141.8 25.5 %all-to-all-start.3 = ((bf16[8,256,128]{2,1,0:T(8,128)(2,1)}), bf16[8,256,128]{2,1,0:T(8,128)(2,1)}, u32[]{:S(2)}, u32[]{:S(2)}) async-start(bf16[8,256,128]{2,1,0:T(8,128)(2,1)} %bitcast.186), calls=%async_computation.3 | async-start | bytes 1048576 | tf_op jit(solution)/shard_map/all_to_all | solution.py:564
  147.1 95.9 %all-gather.2.cloned.1.call-start = ((), (), s32[]{:S(2)}) async-start(), calls=%async_computation.11 | async-start | bytes 3649536 | tf_op jit(solution)/shard_map/all_gather | solution.py:799
  147.2 20.2 %collective-permute-start.12 = (bf16[384,768]{1,0:T(8,128)(2,1)}, bf16[384,768]{1,0:T(8,128)(2,1)}, u32[]{:S(2)}, u32[]{:S(2)}) collective-permute-start(bf16[384,768]{1,0:T(8,128)(2,1)} %collective-permute-done.8.refs_5_), channel_id=1, source_target_pairs={{4,0},{0,4},{5,1},{1,5},{6,2},{2,6},{7,3},{3,7},{12,8},{8,12},{13,... | collective-permute-start | bytes 1769480 | tf_op jit(solution)/shard_map/ppermute | solution.py:617
  167.5 1.4 copy-start.34
  168.9 1.7 copy-start.3
  215.2 27.7 %all-to-all-start.5 = ((bf16[8,128,768]{2,1,0:T(8,128)(2,1)}), bf16[8,128,768]{2,1,0:T(8,128)(2,1)}, u32[]{:S(2)}, u32[]{:S(2)}) async-start(bf16[8,128,768]{2,1,0:T(8,128)(2,1)} %bitcast.181), calls=%async_computation.5 | async-start | bytes 3145728 | tf_op jit(solution)/shard_map/all_to_all | solution.py:564
  226.3 15.8 %collective-permute-start.13 = (bf16[384,768]{1,0:T(8,128)(2,1)}, bf16[384,768]{1,0:T(8,128)(2,1)S(1)}, u32[]{:S(2)}, u32[]{:S(2)}) collective-permute-start(bf16[384,768]{1,0:T(8,128)(2,1)} %get-tuple-element.170), channel_id=1, source_target_pairs={{0,4},{4,0},{1,5},{5,1},{2,6},{6,2},{3,7},{7,3},{8,12},{12,8},{9,1... | collective-permute-start | bytes 1769480 | tf_op jit(solution)/shard_map/ppermute | solution.py:626
  244.6 1.0 copy-start.13
  245.9 16.8 %copy-start.1 = (f32[256,768]{1,0:T(8,128)}, f32[256,768]{1,0:T(8,128)S(1)}, u32[]{:S(2)}) copy-start(f32[256,768]{1,0:T(8,128)S(1)} %multiply_add_fusion.residual_ref) | copy-start | bytes 2359300
  246.4 10.5 %copy-start.19 = (f32[384,768]{1,0:T(8,128)S(1)}, f32[384,768]{1,0:T(8,128)}, u32[]{:S(2)}) copy-start(f32[384,768]{1,0:T(8,128)} %get-tuple-element.185) | copy-start | bytes 3538948
  251.8 45.5 %all-to-all-start.6 = ((bf16[8,256,128]{2,1,0:T(8,128)(2,1)}), bf16[8,256,128]{2,1,0:T(8,128)(2,1)S(1)}, u32[]{:S(2)}, u32[]{:S(2)}) async-start(bf16[8,256,128]{2,1,0:T(8,128)(2,1)} %fusion.48), calls=%async_computation.6 | async-start | bytes 1048576 | tf_op jit(solution)/shard_map/all_to_all | solution.py:564
  256.9 4.3 copy-start.33
  257.0 5.7 %copy-start.11 = (bf16[256,768]{1,0:T(8,128)(2,1)S(1)}, bf16[256,768]{1,0:T(8,128)(2,1)}, u32[]{:S(2)}) copy-start(bf16[256,768]{1,0:T(8,128)(2,1)} %copy-done.10) | copy-start | bytes 1179652
  258.2 38.2 %collective-permute-start.15 = (bf16[384,768]{1,0:T(8,128)(2,1)S(1)}, bf16[384,768]{1,0:T(8,128)(2,1)S(1)}, u32[]{:S(2)}, u32[]{:S(2)}) collective-permute-start(bf16[384,768]{1,0:T(8,128)(2,1)S(1)} %add_convert_fusion.1), channel_id=1, source_target_pairs={{0,16},{16,0},{1,17},{17,1},{2,18},{18,2},{3,19},{19,3},{4,20},{20... | collective-permute-start | bytes 1769480 | tf_op jit(solution)/shard_map/ppermute | solution.py:626
  261.2 36.1 %collective-permute-start.14 = (bf16[384,768]{1,0:T(8,128)(2,1)S(1)}, bf16[384,768]{1,0:T(8,128)(2,1)}, u32[]{:S(2)}, u32[]{:S(2)}) collective-permute-start(bf16[384,768]{1,0:T(8,128)(2,1)S(1)} %copy-done.33), channel_id=1, source_target_pairs={{0,4},{4,0},{1,5},{5,1},{2,6},{6,2},{3,7},{7,3},{8,12},{12,8},{9,1... | collective-permute-start | bytes 1769480 | tf_op jit(solution)/shard_map/ppermute | solution.py:626
  263.3 8.8 %collective-permute-start.16 = (bf16[8,24,768]{2,1,0:T(8,128)(2,1)S(1)}, bf16[8,24,768]{2,1,0:T(8,128)(2,1)S(1)}, u32[]{:S(2)}, u32[]{:S(2)}) collective-permute-start(bf16[8,24,768]{2,1,0:T(8,128)(2,1)S(1)} %get-tuple-element.244), channel_id=1, source_target_pairs={{0,1},{1,2},{2,3},{3,0},{4,5},{5,6},{6,7},{7,4},{8,9},{9,10},{10,1... | collective-permute-start | bytes 884744 | tf_op jit(solution)/shard_map/ppermute | solution.py:626
  263.4 9.9 %collective-permute-start.17 = (bf16[8,24,768]{2,1,0:T(8,128)(2,1)S(1)}, bf16[8,24,768]{2,1,0:T(8,128)(2,1)S(1)}, u32[]{:S(2)}, u32[]{:S(2)}) collective-permute-start(bf16[8,24,768]{2,1,0:T(8,128)(2,1)S(1)} %get-tuple-element.243), channel_id=1, source_target_pairs={{0,2},{1,3},{2,0},{3,1},{4,6},{5,7},{6,4},{7,5},{8,10},{9,11},{10,... | collective-permute-start | bytes 884744 | tf_op jit(solution)/shard_map/ppermute | solution.py:626
  264.9 13.1 %collective-permute-start.18 = (bf16[8,24,768]{2,1,0:T(8,128)(2,1)S(1)}, bf16[8,24,768]{2,1,0:T(8,128)(2,1)S(1)}, u32[]{:S(2)}, u32[]{:S(2)}) collective-permute-start(bf16[8,24,768]{2,1,0:T(8,128)(2,1)S(1)} %get-tuple-element.242), channel_id=1, source_target_pairs={{0,3},{1,0},{2,1},{3,2},{4,7},{5,4},{6,5},{7,6},{8,11},{9,8},{10,9... | collective-permute-start | bytes 884744 | tf_op jit(solution)/shard_map/ppermute | solution.py:626
  272.0 24.4 %copy-start.25 = (bf16[8,24,768]{2,1,0:T(8,128)(2,1)}, bf16[8,24,768]{2,1,0:T(8,128)(2,1)S(1)}, u32[]{:S(2)}) copy-start(bf16[8,24,768]{2,1,0:T(8,128)(2,1)S(1)} %collective-permute-done.16) | copy-start | bytes 884740
  273.3 23.2 %copy-start.26 = (bf16[8,24,768]{2,1,0:T(8,128)(2,1)}, bf16[8,24,768]{2,1,0:T(8,128)(2,1)S(1)}, u32[]{:S(2)}) copy-start(bf16[8,24,768]{2,1,0:T(8,128)(2,1)S(1)} %collective-permute-done.17) | copy-start | bytes 884740
  278.0 18.5 %copy-start.27 = (bf16[8,24,768]{2,1,0:T(8,128)(2,1)}, bf16[8,24,768]{2,1,0:T(8,128)(2,1)S(1)}, u32[]{:S(2)}) copy-start(bf16[8,24,768]{2,1,0:T(8,128)(2,1)S(1)} %collective-permute-done.18) | copy-start | bytes 884740
  298.1 36.2 %all-to-all-start.7 = ((bf16[8,128,768]{2,1,0:T(8,128)(2,1)}), bf16[8,128,768]{2,1,0:T(8,128)(2,1)S(1)}, u32[]{:S(2)}, u32[]{:S(2)}) async-start(bf16[8,128,768]{2,1,0:T(8,128)(2,1)} %bitcast.164), calls=%async_computation.7 | async-start | bytes 3145728 | tf_op jit(solution)/shard_map/all_to_all | solution.py:564
  304.0 28.3 %collective-permute-start.21 = (bf16[384,768]{1,0:T(8,128)(2,1)}, bf16[384,768]{1,0:T(8,128)(2,1)}, u32[]{:S(2)}, u32[]{:S(2)}) collective-permute-start(bf16[384,768]{1,0:T(8,128)(2,1)} %add_convert_fusion), channel_id=1, source_target_pairs={{0,16},{16,0},{1,17},{17,1},{2,18},{18,2},{3,19},{19,3},{4,20},{20... | collective-permute-start | bytes 1769480 | tf_op jit(solution)/shard_map/ppermute | solution.py:626
  304.3 28.0 %collective-permute-start.19 = (bf16[384,768]{1,0:T(8,128)(2,1)}, bf16[384,768]{1,0:T(8,128)(2,1)}, u32[]{:S(2)}, u32[]{:S(2)}) collective-permute-start(bf16[384,768]{1,0:T(8,128)(2,1)} %get-tuple-element.192), channel_id=1, source_target_pairs={{0,4},{4,0},{1,5},{5,1},{2,6},{6,2},{3,7},{7,3},{8,12},{12,8},{9,1... | collective-permute-start | bytes 1769480 | tf_op jit(solution)/shard_map/ppermute | solution.py:626
  306.1 26.7 %collective-permute-start.20 = (bf16[384,768]{1,0:T(8,128)(2,1)}, bf16[384,768]{1,0:T(8,128)(2,1)}, u32[]{:S(2)}, u32[]{:S(2)}) collective-permute-start(bf16[384,768]{1,0:T(8,128)(2,1)} %get-tuple-element.193), channel_id=1, source_target_pairs={{0,4},{4,0},{1,5},{5,1},{2,6},{6,2},{3,7},{7,3},{8,12},{12,8},{9,1... | collective-permute-start | bytes 1769480 | tf_op jit(solution)/shard_map/ppermute | solution.py:626
  334.3 41.4 %all-to-all-start.8 = ((bf16[8,256,384]{2,1,0:T(8,128)(2,1)}), bf16[8,256,384]{2,1,0:T(8,128)(2,1)}, u32[]{:S(2)}, u32[]{:S(2)}) async-start(bf16[8,256,384]{2,1,0:T(8,128)(2,1)} %bitcast.180), calls=%async_computation.8 | async-start | bytes 3145728 | tf_op jit(solution)/shard_map/all_to_all | solution.py:564
  346.4 4.2 copy-start.22
  347.6 9.0 %collective-permute-start.22 = (bf16[8,24,384]{2,1,0:T(8,128)(2,1)S(1)}, bf16[8,24,384]{2,1,0:T(8,128)(2,1)S(1)}, u32[]{:S(2)}, u32[]{:S(2)}) collective-permute-start(bf16[8,24,384]{2,1,0:T(8,128)(2,1)S(1)} %get-tuple-element.245), channel_id=1, source_target_pairs={{0,1},{1,2},{2,3},{3,0},{4,5},{5,6},{6,7},{7,4},{8,9},{9,10},{10,1... | collective-permute-start | bytes 442376 | tf_op jit(solution)/shard_map/ppermute | solution.py:626
  347.6 8.9 %collective-permute-start.23 = (bf16[8,24,384]{2,1,0:T(8,128)(2,1)S(1)}, bf16[8,24,384]{2,1,0:T(8,128)(2,1)S(1)}, u32[]{:S(2)}, u32[]{:S(2)}) collective-permute-start(bf16[8,24,384]{2,1,0:T(8,128)(2,1)S(1)} %get-tuple-element.247), channel_id=1, source_target_pairs={{0,2},{1,3},{2,0},{3,1},{4,6},{5,7},{6,4},{7,5},{8,10},{9,11},{10,... | collective-permute-start | bytes 442376 | tf_op jit(solution)/shard_map/ppermute | solution.py:626
  349.2 7.4 %collective-permute-start.24 = (bf16[8,24,384]{2,1,0:T(8,128)(2,1)S(1)}, bf16[8,24,384]{2,1,0:T(8,128)(2,1)S(1)}, u32[]{:S(2)}, u32[]{:S(2)}) collective-permute-start(bf16[8,24,384]{2,1,0:T(8,128)(2,1)S(1)} %get-tuple-element.246), channel_id=1, source_target_pairs={{0,3},{1,0},{2,1},{3,2},{4,7},{5,4},{6,5},{7,6},{8,11},{9,8},{10,9... | collective-permute-start | bytes 442376 | tf_op jit(solution)/shard_map/ppermute | solution.py:626
  350.6 7.0 %copy-start.20 = (bf16[8,24,768]{2,1,0:T(8,128)(2,1)S(1)}, bf16[8,24,768]{2,1,0:T(8,128)(2,1)}, u32[]{:S(2)}) copy-start(bf16[8,24,768]{2,1,0:T(8,128)(2,1)} %fusion.9) | copy-start | bytes 884740
  375.7 16.5 %all-to-all-start.9 = ((bf16[8,24,1152]{2,1,0:T(8,128)(2,1)}), bf16[8,24,1152]{2,1,0:T(8,128)(2,1)S(1)}, u32[]{:S(2)}, u32[]{:S(2)}) async-start(bf16[8,24,1152]{2,1,0:T(8,128)(2,1)} %pad_maximum_fusion), calls=%async_computation.9 | async-start | bytes 884736 | tf_op jit(solution)/shard_map/all_to_all | solution.py:564
  396.3 13.0 %all-to-all-start.10 = ((f32[32,1,1664]{2,1,0:T(1,128)}), f32[32,1,1664]{2,1,0:T(1,128)S(1)}, u32[]{:S(2)}, u32[]{:S(2)}) async-start(f32[32,1,1664]{2,1,0:T(1,128)} %broadcast_in_dim.62), calls=%async_computation.10 | async-start | bytes 425984 | tf_op jit(solution)/shard_map/all_to_all | solution.py:564
  400.1 11.8 %copy-start.30 = (f32[2,768]{1,0:T(2,128)S(1)}, f32[2,768]{1,0:T(2,128)}, u32[]{:S(2)}) copy-start(f32[2,768]{1,0:T(2,128)} %param.41) | copy-start | bytes 18436
  400.2 11.8 %copy-start.31 = (f32[2,768]{1,0:T(2,128)S(1)}, f32[2,768]{1,0:T(2,128)}, u32[]{:S(2)}) copy-start(f32[2,768]{1,0:T(2,128)} %param.40) | copy-start | bytes 18436
  410.6 10.9 %copy-start.28 = (f32[2,768]{1,0:T(2,128)}, f32[2,768]{1,0:T(2,128)S(1)}, u32[]{:S(2)}) copy-start(f32[2,768]{1,0:T(2,128)S(1)} %reshape.237) | copy-start | bytes 18436
  (7 other events, 5.6 us)
Sparse Core Ops, SparseCore 0:
  167.5 62.0 all-gather.1

commit v6 on v4

--- a/solution.py
+++ b/solution.py
@@ -752,9 +752,7 @@
     *row_blocks, all_copies, peer_up, own_up, own_down, grad_slots_out = together(
         *row_blocks, all_copies, peer_up, own_up, own_down, to_slots(cotangent[0])
     )
-    all_copies = jnp.swapaxes(all_copies, 0, 1)
-    columns = all_copies[..., : 3 * LANES].reshape(width, 3 * LANES)
-    output_full = all_copies[..., 3 * LANES :].reshape(width, width)
+    columns = jnp.swapaxes(all_copies[..., : 3 * LANES], 0, 1).reshape(width, 3 * LANES)
     grad_arrived = dispatch(grad_slots_out)
     peer_down = others(own_down, "hi")
     side_up = others(own_up, "in")
@@ -780,9 +778,10 @@
     def to_tokens(values):
         return swap(values.reshape(count, row_count, values.shape[1]), SEQ)
 
-    mixed_low, grad_arrived, peer_down, side_up, side_down, far_up = together(
-        mixed_low, grad_arrived, peer_down, side_up, side_down, far_up
-    )
+    mixed_low, grad_arrived, peer_down, side_up, side_down, far_up, all_copies = together(
+        mixed_low, grad_arrived, peer_down, side_up, side_down, far_up, all_copies
+    )
+    output_full = jnp.swapaxes(all_copies[..., 3 * LANES :], 0, 1).reshape(width, width)
     far_down = others(peer_down, "in")
     mixed_pieces, projection_low, far_down = together(
         to_tokens(mixed_low), projection_low, far_down

time: 427 us -> 427 us (level)
    unnamed x82 -> x78, local copies, waits for them, and re-layouts: 10.2 us -> 10 us
where the time goes in v6:
time: 427 us; the launch traced here: 425 us
  waiting for transfers between devices  141 us (33%)
  Pallas kernels  105 us (25%)
  starting transfers between devices  76.7 us (18%)
  blocking collectives  27.6 us (6%)
  other arithmetic  27.3 us (6%)
  local copies, waits for them, and re-layouts  21.1 us (5%)
  between operations  18.4 us (4%)
  matrix products  7.29 us (2%)
    all_to_all x10, starting transfers between devices, swap(): return lax.all_to_all(value, axes, split_axis=0, concat_axis=0, tiled=True)  44.6 us
    ppermute x7, waiting for transfers between devices, flip(): lax.ppermute(value, SEQ, [(index, index ^ bits) for index in range(count)])  39.6 us
    all_to_all x10, waiting for transfers between devices, swap(): return lax.all_to_all(value, axes, split_axis=0, concat_axis=0, tiled=True)  34.8 us
    ppermute x12, waiting for transfers between devices, to_owners(): lax.ppermute(block, axis, [(i, (i + step) % size) for i in range(size)])  33.6 us
    ppermute x6, waiting for transfers between devices, others(): lax.ppermute(value, axis, [((i + step) % size, i) for i in range(size)])  33 us
    all_to_all x1, blocking collectives, swap(): return lax.all_to_all(value, axes, split_axis=0, concat_axis=0, tiled=True)  27.6 us
    pallas_call x1, Pallas kernels, attend_back(): pl.pallas_call(functools.partial(attend_back_kernel, block=block, chunk=2...  24.4 us
    pallas_call x1, Pallas kernels, attend(): pl.pallas_call(functools.partial(attend_kernel, block=block, chunk=2 * bl...  23.1 us
  transfers between devices with their start and end apart: 36, of which 19 were waited for; matrix products, arithmetic and copies ran while one was open for 7% of the time, Pallas kernels for 22%

profile of v6, /device:TPU:0, one launch (start us, length us, event | category | flops | bytes accessed | tf_op | source)
XLA Modules:
  0.0 424.9 jit_solution(527090277481547070)
XLA Ops:
  15.1 7.4 %all-to-all-start = ((bf16[8,32,1152]{2,1,0:T(8,128)(2,1)}), bf16[8,32,1152]{2,1,0:T(8,128)(2,1)S(1)}, u32[]{:S(2)}, u32[]{:S(2)}) async-start(bf16[8,32,1152]{2,1,0:T(8,128)(2,1)} %fusion.47), calls=%async_computation | async-start | bytes 1179648 | tf_op jit(solution)/shard_map/all_to_all | solution.py:564
  23.5 2.1 collective-permute-start
  25.5 1.5 collective-permute-start.1
  27.0 2.4 collective-permute-start.2
  30.2 9.4 %collective-permute-done.refs_1_ = bf16[256,768]{1,0:T(8,128)(2,1)S(1)} collective-permute-done((bf16[256,768]{1,0:T(8,128)(2,1)S(1)}, bf16[256,768]{1,0:T(8,128)(2,1)S(1)}, u32[]{:S(2)}, u32[]{:S(2)}) %collective-permute-start) | collective-permute-done | bytes 393248 | tf_op jit(solution)/shard_map/ppermute | solution.py:611
  39.6 9.6 %collective-permute-done.1.refs_2_ = bf16[256,768]{1,0:T(8,128)(2,1)} collective-permute-done((bf16[256,768]{1,0:T(8,128)(2,1)S(1)}, bf16[256,768]{1,0:T(8,128)(2,1)}, u32[]{:S(2)}, u32[]{:S(2)}) %collective-permute-start.1) | collective-permute-done | bytes 393248 | tf_op jit(solution)/shard_map/ppermute | solution.py:611
  49.2 6.2 %collective-permute-done.2.refs_4_ = bf16[256,768]{1,0:T(8,128)(2,1)} collective-permute-done((bf16[256,768]{1,0:T(8,128)(2,1)S(1)}, bf16[256,768]{1,0:T(8,128)(2,1)}, u32[]{:S(2)}, u32[]{:S(2)}) %collective-permute-start.2) | collective-permute-done | bytes 393248 | tf_op jit(solution)/shard_map/ppermute | solution.py:611
  55.4 1.4 broadcast_in_dim.24
  56.8 3.7 all-to-all-start.1
  60.9 1.9 collective-permute-start.7
  62.7 1.7 collective-permute-start.4
  64.8 14.5 %collective-permute-done.5.refs_6_ = bf16[256,768]{1,0:T(8,128)(2,1)S(1)} collective-permute-done((bf16[256,768]{1,0:T(8,128)(2,1)}, bf16[256,768]{1,0:T(8,128)(2,1)S(1)}, u32[]{:S(2)}, u32[]{:S(2)}) %collective-permute-start.5) | collective-permute-done | bytes 393248 | tf_op jit(solution)/shard_map/ppermute | solution.py:611
  79.2 1.7 collective-permute-start.6
  81.0 1.6 convolution_convert_fusion.2
  83.5 6.6 %collective-permute-done.7.refs_1_ = bf16[384,768]{1,0:T(8,128)(2,1)S(1)} collective-permute-done((bf16[384,768]{1,0:T(8,128)(2,1)S(1)}, bf16[384,768]{1,0:T(8,128)(2,1)S(1)}, u32[]{:S(2)}, u32[]{:S(2)}) %collective-permute-start.7) | collective-permute-done | bytes 589856 | tf_op jit(solution)/shard_map/ppermute | solution.py:617
  90.9 1.3 broadcast_in_dim.28
  92.2 3.6 all-to-all-start.2
  95.8 1.6 collective-permute-start.10
  97.4 1.6 collective-permute-start.8
  99.6 1.5 collective-permute-start.9
  105.7 23.1 %shard_map.380 = (bf16[2048,128]{1,0:T(8,128)(2,1)}, f32[2048,128]{1,0:T(8,128)}, bf16[2048,256]{1,0:T(8,128)(2,1)}, bf16[2048,256]{1,0:T(8,128)(2,1)}) custom-call(s32[2,8]{1,0:T(2,128)} %fusion.58.active_ref, s32[8]{0:T(128)} %iota_xor_fusion.order_ref, bf16[256,768]{1,0:T(8,128)(2,1)} %copy-done.6, bf16[256,768]{1,0:T(8,128)(2,1)} %copy-done.14, ...), custom_call_target="tpu_custom_call" | custom-call | flops 1 | bytes 1 | tf_op jit(solution)/shard_map/pallas_call | solution.py:278
  128.8 8.2 %collective-permute-done.9.refs_2_ = bf16[384,768]{1,0:T(8,128)(2,1)} collective-permute-done((bf16[384,768]{1,0:T(8,128)(2,1)}, bf16[384,768]{1,0:T(8,128)(2,1)}, u32[]{:S(2)}, u32[]{:S(2)}) %collective-permute-start.9) | collective-permute-done | bytes 589856 | tf_op jit(solution)/shard_map/ppermute | solution.py:617
  137.0 5.1 %all-to-all-start.3 = ((bf16[8,256,128]{2,1,0:T(8,128)(2,1)}), bf16[8,256,128]{2,1,0:T(8,128)(2,1)}, u32[]{:S(2)}, u32[]{:S(2)}) async-start(bf16[8,256,128]{2,1,0:T(8,128)(2,1)} %bitcast.186), calls=%async_computation.3 | async-start | bytes 1048576 | tf_op jit(solution)/shard_map/all_to_all | solution.py:564
  142.2 2.0 collective-permute-start.12
  144.2 18.2 %collective-permute-done.12.refs_7_ = bf16[384,768]{1,0:T(8,128)(2,1)} collective-permute-done((bf16[384,768]{1,0:T(8,128)(2,1)}, bf16[384,768]{1,0:T(8,128)(2,1)}, u32[]{:S(2)}, u32[]{:S(2)}) %collective-permute-start.12) | collective-permute-done | bytes 589856 | tf_op jit(solution)/shard_map/ppermute | solution.py:617
  162.7 1.3 copy-done.34
  164.0 1.7 fusion
  167.1 27.6 %all_to_all.55 = bf16[8,128,768]{2,1,0:T(8,128)(2,1)} all-to-all(bf16[8,128,768]{2,1,0:T(8,128)(2,1)S(1)} %bitcast.166), channel_id=1, replica_groups=mesh['hi'=2,'lo'=2,'in'=2,'exp'=4] {'lo','exp'}, dimensions={0} | all-to-all | bytes 3145728 | tf_op jit(solution)/shard_map/all_to_all | solution.py:564
  194.7 15.5 %shard_map.381 = (bf16[1024,768]{1,0:T(8,128)(2,1)}, bf16[1024,384]{1,0:T(8,128)(2,1)}, bf16[1024,384]{1,0:T(8,128)(2,1)}, bf16[1024,384]{1,0:T(8,128)(2,1)}, bf...) custom-call(bf16[1024,768]{1,0:T(8,128)(2,1)} %bitcast.158, ...), custom_call_target="tpu_custom_call" | custom-call | flops 1 | bytes 1 | tf_op jit(solution)/shard_map/pallas_call | solution.py:372
  210.3 4.3 %all-to-all-start.5 = ((bf16[8,128,768]{2,1,0:T(8,128)(2,1)}), bf16[8,128,768]{2,1,0:T(8,128)(2,1)}, u32[]{:S(2)}, u32[]{:S(2)}) async-start(bf16[8,128,768]{2,1,0:T(8,128)(2,1)} %bitcast.181), calls=%async_computation.5 | async-start | bytes 3145728 | tf_op jit(solution)/shard_map/all_to_all | solution.py:564
  214.6 6.7 %shard_map.382 = (bf16[384,768]{1,0:T(8,128)(2,1)}, bf16[384,768]{1,0:T(8,128)(2,1)}, f32[384,768]{1,0:T(8,128)}, f32[384,768]{1,0:T(8,128)}) custom-call(bf16[1024,768]{1,0:T(8,128)(2,1)} %bitcast.156, bf16[1024,768]{1,0:T(8,128)(2,1)} %bitcast.159, bf16[1024,384]{1,0:T(8,128)(2,1)} %get-tuple-element.160.refs_0_.refs_3_, ...), custom_call_target="tpu_custom_call" | custom-call | flops 1 | bytes 1 | tf_op jit(solution)/shard_map/pallas_call | solution.py:425
  221.9 7.1 %shard_map.383 = bf16[1024,768]{1,0:T(8,128)(2,1)} custom-call(bf16[1024,384]{1,0:T(8,128)(2,1)} %get-tuple-element.168.refs_0_.refs_2_, bf16[1024,384]{1,0:T(8,128)(2,1)} %get-tuple-element.162.refs_2_.refs_1_, bf16[1024,384]{1,0:T(8,128)(2,1)} %get-tuple-element.169.refs_2_.refs_0_, bf16[1024,384]{1,0:T(8,128)(2,1)} %get-tuple-element.160.refs_0_.refs_3_, ...), custom_call_target="tpu_custom_call" | custom-call | flops 1 | bytes 1 | tf_op jit(solution)/shard_map/pallas_call | solution.py:396
  229.0 6.7 %shard_map.384 = (bf16[384,768]{1,0:T(8,128)(2,1)}, bf16[384,768]{1,0:T(8,128)(2,1)}, f32[384,768]{1,0:T(8,128)}, f32[384,768]{1,0:T(8,128)}) custom-call(bf16[1024,768]{1,0:T(8,128)(2,1)} %bitcast.157, bf16[1024,768]{1,0:T(8,128)(2,1)} %bitcast.160, bf16[1024,384]{1,0:T(8,128)(2,1)} %get-tuple-element.169.refs_2_.refs_0_, ...), custom_call_target="tpu_custom_call" | custom-call | flops 1 | bytes 1 | tf_op jit(solution)/shard_map/pallas_call | solution.py:425
  235.7 1.4 collective-permute-done.13
  238.0 1.7 convert_reduce_fusion.1
  246.9 5.1 %all-to-all-start.6 = ((bf16[8,256,128]{2,1,0:T(8,128)(2,1)}), bf16[8,256,128]{2,1,0:T(8,128)(2,1)S(1)}, u32[]{:S(2)}, u32[]{:S(2)}) async-start(bf16[8,256,128]{2,1,0:T(8,128)(2,1)} %fusion.48), calls=%async_computation.6 | async-start | bytes 1048576 | tf_op jit(solution)/shard_map/all_to_all | solution.py:564
  252.0 1.3 add_convert_fusion.1
  253.3 3.0 collective-permute-start.15
  256.2 1.5 collective-permute-start.14
  258.4 1.5 collective-permute-start.17
  259.9 1.4 collective-permute-start.18
  261.3 5.8 %collective-permute-done.16 = bf16[8,24,768]{2,1,0:T(8,128)(2,1)S(1)} collective-permute-done((bf16[8,24,768]{2,1,0:T(8,128)(2,1)S(1)}, bf16[8,24,768]{2,1,0:T(8,128)(2,1)S(1)}, u32[]{:S(2)}, u32[]{:S(2)}) %collective-permute-start.16) | collective-permute-done | bytes 294944 | tf_op jit(solution)/shard_map/ppermute | solution.py:626
  268.3 4.7 %collective-permute-done.18 = bf16[8,24,768]{2,1,0:T(8,128)(2,1)S(1)} collective-permute-done((bf16[8,24,768]{2,1,0:T(8,128)(2,1)S(1)}, bf16[8,24,768]{2,1,0:T(8,128)(2,1)S(1)}, u32[]{:S(2)}, u32[]{:S(2)}) %collective-permute-start.18) | collective-permute-done | bytes 294944 | tf_op jit(solution)/shard_map/ppermute | solution.py:626
  273.0 18.5 %collective-permute-done.15 = bf16[384,768]{1,0:T(8,128)(2,1)S(1)} collective-permute-done((bf16[384,768]{1,0:T(8,128)(2,1)S(1)}, bf16[384,768]{1,0:T(8,128)(2,1)S(1)}, u32[]{:S(2)}, u32[]{:S(2)}) %collective-permute-start.15) | collective-permute-done | bytes 589856 | tf_op jit(solution)/shard_map/ppermute | solution.py:626
  293.1 3.6 all-to-all-start.7
  296.7 2.3 add_convert_fusion
  299.4 1.8 collective-permute-start.19
  301.4 24.4 %shard_map.385 = (bf16[2048,384]{1,0:T(8,128)(2,1)}, bf16[2048,384]{1,0:T(8,128)(2,1)}) custom-call(s32[2,8]{1,0:T(2,128)} %fusion.58.active_ref, s32[8]{0:T(128)} %iota_xor_fusion.order_ref, bf16[2048,256]{1,0:T(8,128)(2,1)} %get-tuple-element.152.pair_ref, bf16[2048,128]{1,0:T(8,128)(2,1)} %broadcast_in_dim.26.refs_9_.documents_ref, ...), custom_call_target="tpu_custom_call" | custom-call | flops 1 | bytes 1 | tf_op jit(solution)/shard_map/pallas_call | solution.py:309
  325.8 1.6 collective-permute-done.21
  327.8 1.5 all-to-all-done.7
  329.3 4.5 %all-to-all-start.8 = ((bf16[8,256,384]{2,1,0:T(8,128)(2,1)}), bf16[8,256,384]{2,1,0:T(8,128)(2,1)}, u32[]{:S(2)}, u32[]{:S(2)}) async-start(bf16[8,256,384]{2,1,0:T(8,128)(2,1)} %bitcast.180), calls=%async_computation.8 | async-start | bytes 3145728 | tf_op jit(solution)/shard_map/all_to_all | solution.py:564
  333.9 2.0 fusion.9
  335.9 5.5 %shard_map.386 = bf16[768,384]{1,0:T(8,128)(2,1)} custom-call(bf16[256,768]{1,0:T(8,128)(2,1)} %copy-done.6, bf16[256,768]{1,0:T(8,128)(2,1)} %copy-done.14, bf16[256,768]{1,0:T(8,128)(2,1)} %collective-permute-done.1.refs_2_, bf16[256,768]{1,0:T(8,128)(2,1)} %copy-done.17, bf16[256,768]{1,0:T(8,128)(2,1)} %collective-permute-done.2.refs_4_, ...), custom_call_target="tpu_custom_call" | custom-call | flops 1 | bytes 1 | tf_op jit(solution)/shard_map/pallas_call | solution.py:452
  342.7 1.6 collective-permute-start.23
  344.2 1.4 collective-permute-start.24
  345.6 4.7 %multiply_reduce_fusion = (f32[]{:T(128)}, f32[384,768]{1,0:T(8,128)}, f32[]{:T(128)}, f32[384,768]{1,0:T(8,128)}) fusion(bf16[384,768]{1,0:T(8,128)(2,1)S(1)} %copy-done.22, f32[384,768]{1,0:T(8,128)} %get-tuple-element.199, bf16[384,768]{1,0:T(8,128)(2,1)} %collective-permute-done.19, bf16[384,768]{1,0:T(8,128)(2,1)} %collective-permute-done.21, ...), kind=kLoop, calls=%fused_computation.14 | loop fusion | flops 3538942 | bytes 7077896 | tf_op jit(solution)/shard_map/reduce_sum | solution.py:881
  353.4 17.3 %all-to-all-done.8.pieces_ref = bf16[8,256,384]{2,1,0:T(8,128)(2,1)} async-done(((bf16[8,256,384]{2,1,0:T(8,128)(2,1)}), bf16[8,256,384]{2,1,0:T(8,128)(2,1)}, u32[]{:S(2)}, u32[]{:S(2)}) %all-to-all-start.8) | async-done | bytes 1572896 | tf_op jit(solution)/shard_map/all_to_all | solution.py:564
  370.7 3.6 all-to-all-start.9
  374.4 5.1 %shard_map.387 = (f32[256,768]{1,0:T(8,128)}, f32[1,768]{1,0:T(1,128)}) custom-call(bf16[8,256,384]{2,1,0:T(8,128)(2,1)} %all-to-all-done.8.pieces_ref, bf16[768,2304]{1,0:T(8,128)(2,1)} %all-gather.2.cloned.1.call-done.matrix_ref, bf16[256,768]{1,0:T(8,128)(2,1)} %bitcast.167, f32[1,768]{1,0:T(1,128)} %get-tuple-element.266.gain_ref, f32[256,768]{1,0:T(8,128)} %copy-done.1), custom_call_target="tpu_custom_call" | custom-call | flops 1 | bytes 1 | tf_op jit(solution)/shard_map/pallas_call | solution.py:499
  380.1 7.1 %all-to-all-done.9.terms_ref = bf16[8,24,1152]{2,1,0:T(8,128)(2,1)S(1)} async-done(((bf16[8,24,1152]{2,1,0:T(8,128)(2,1)}), bf16[8,24,1152]{2,1,0:T(8,128)(2,1)S(1)}, u32[]{:S(2)}, u32[]{:S(2)}) %all-to-all-start.9) | async-done | bytes 442400 | tf_op jit(solution)/shard_map/all_to_all | solution.py:564
  388.0 1.8 shard_map.388
  391.3 3.6 all-to-all-start.10
  396.4 7.9 %all-to-all-done.10 = f32[32,1,1664]{2,1,0:T(1,128)S(1)} async-done(((f32[32,1,1664]{2,1,0:T(1,128)}), f32[32,1,1664]{2,1,0:T(1,128)S(1)}, u32[]{:S(2)}, u32[]{:S(2)}) %all-to-all-start.10) | async-done | bytes 213024 | tf_op jit(solution)/shard_map/all_to_all | solution.py:564
  407.6 9.2 %shard_map.389 = (f32[24,2304]{1,0:T(8,128)}, f32[24,2304]{1,0:T(8,128)}, f32[24,2304]{1,0:T(8,128)}, f32[24,768]{1,0:T(8,128)}, f32[24,768]{1,0:T(8,128)}, /*in...) custom-call(f32[1]{0:T(128)} %bitcast.55.factor_ref, ...), custom_call_target="tpu_custom_call" | custom-call | flops 13271040 | bytes 18579456 | tf_op jit(solution)/shard_map/pallas_call | solution.py:590
  (163 shorter events, 41.3 us)
Async XLA Ops:
  8.1 7.0 %copy-start.18 = (bf16[24,2304]{1,0:T(8,128)(2,1)}, bf16[24,2304]{1,0:T(8,128)(2,1)S(1)}, u32[]{:S(2)}) copy-start(bf16[24,2304]{1,0:T(8,128)(2,1)S(1)} %convert_element_type.132) | copy-start | bytes 331780
  8.3 14.2 %copy-start.2 = (bf16[1,256,768]{2,1,0:T(8,128)(2,1)S(1)}, bf16[1,256,768]{2,1,0:T(8,128)(2,1)}, u32[]{:S(2)}) copy-start(bf16[1,256,768]{2,1,0:T(8,128)(2,1)} %param.23) | copy-start | bytes 1179652
  11.2 11.4 %copy-start.29 = (f32[2,768]{1,0:T(2,128)S(1)}, f32[2,768]{1,0:T(2,128)}, u32[]{:S(2)}) copy-start(f32[2,768]{1,0:T(2,128)} %param.31) | copy-start | bytes 18436
  15.1 14.3 %copy-start.4 = (f32[1,384,768]{2,1,0:T(8,128)S(1)}, f32[1,384,768]{2,1,0:T(8,128)}, u32[]{:S(2)}) copy-start(f32[1,384,768]{2,1,0:T(8,128)} %param.29) | copy-start | bytes 3538948
  15.1 40.3 %all-to-all-start = ((bf16[8,32,1152]{2,1,0:T(8,128)(2,1)}), bf16[8,32,1152]{2,1,0:T(8,128)(2,1)S(1)}, u32[]{:S(2)}, u32[]{:S(2)}) async-start(bf16[8,32,1152]{2,1,0:T(8,128)(2,1)} %fusion.47), calls=%async_computation | async-start | bytes 1179648 | tf_op jit(solution)/shard_map/all_to_all | solution.py:564
  23.4 6.8 %copy-start.6 = (bf16[256,768]{1,0:T(8,128)(2,1)}, bf16[256,768]{1,0:T(8,128)(2,1)S(1)}, u32[]{:S(2)}) copy-start(bf16[256,768]{1,0:T(8,128)(2,1)S(1)} %fusion.6.refs_0_) | copy-start | bytes 1179652
  23.5 16.2 %collective-permute-start = (bf16[256,768]{1,0:T(8,128)(2,1)S(1)}, bf16[256,768]{1,0:T(8,128)(2,1)S(1)}, u32[]{:S(2)}, u32[]{:S(2)}) collective-permute-start(bf16[256,768]{1,0:T(8,128)(2,1)S(1)} %fusion.6.refs_0_), channel_id=1, source_target_pairs={{0,4},{4,0},{8,12},{12,8},{16,20},{20,16},{24,28},{28,24},{1,5},{5... | collective-permute-start | bytes 1179656 | tf_op jit(solution)/shard_map/ppermute | solution.py:611
  25.5 23.6 %collective-permute-start.1 = (bf16[256,768]{1,0:T(8,128)(2,1)S(1)}, bf16[256,768]{1,0:T(8,128)(2,1)}, u32[]{:S(2)}, u32[]{:S(2)}) collective-permute-start(bf16[256,768]{1,0:T(8,128)(2,1)S(1)} %fusion.6.refs_0_), channel_id=1, source_target_pairs={{0,8},{4,12},{8,0},{12,4},{16,24},{20,28},{24,16},{28,20},{1,9},{5... | collective-permute-start | bytes 1179656 | tf_op jit(solution)/shard_map/ppermute | solution.py:611
  27.0 28.4 %collective-permute-start.2 = (bf16[256,768]{1,0:T(8,128)(2,1)S(1)}, bf16[256,768]{1,0:T(8,128)(2,1)}, u32[]{:S(2)}, u32[]{:S(2)}) collective-permute-start(bf16[256,768]{1,0:T(8,128)(2,1)S(1)} %fusion.6.refs_0_), channel_id=1, source_target_pairs={{0,16},{4,20},{8,24},{12,28},{16,0},{20,4},{24,8},{28,12},{1,17},{... | collective-permute-start | bytes 1179656 | tf_op jit(solution)/shard_map/ppermute | solution.py:611
  39.6 9.6 %copy-start.14 = (bf16[256,768]{1,0:T(8,128)(2,1)}, bf16[256,768]{1,0:T(8,128)(2,1)S(1)}, u32[]{:S(2)}) copy-start(bf16[256,768]{1,0:T(8,128)(2,1)S(1)} %collective-permute-done.refs_1_) | copy-start | bytes 1179652
  55.4 1.5 copy-start.9
  56.8 3.8 copy-start.32
  56.8 4.0 copy-start.7
  56.8 34.1 %all-to-all-start.1 = ((bf16[4,8,24,1152]{3,2,1,0:T(8,128)(2,1)}), bf16[4,8,24,1152]{3,2,1,0:T(8,128)(2,1)S(1)}, u32[]{:S(2)}, u32[]{:S(2)}) async-start(bf16[4,8,24,1152]{3,2,1,0:T(8,128)(2,1)} %broadcast_in_dim.24), calls=%async_computation.1 | async-start | bytes 3538944 | tf_op jit(solution)/shard_map/all_to_all | solution.py:564
  60.5 22.0 %copy-start.5 = (f32[1,384,768]{2,1,0:T(8,128)S(1)}, f32[1,384,768]{2,1,0:T(8,128)}, u32[]{:S(2)}) copy-start(f32[1,384,768]{2,1,0:T(8,128)} %param.30) | copy-start | bytes 3538948
  60.6 18.7 %collective-permute-start.5 = (bf16[256,768]{1,0:T(8,128)(2,1)}, bf16[256,768]{1,0:T(8,128)(2,1)S(1)}, u32[]{:S(2)}, u32[]{:S(2)}) collective-permute-start(bf16[256,768]{1,0:T(8,128)(2,1)} %collective-permute-done.2.refs_4_), channel_id=1, source_target_pairs={{0,8},{4,12},{8,0},{12,4},{16,24},{20,28},{24,16},{28,20},{1,9},{5... | collective-permute-start | bytes 1179656 | tf_op jit(solution)/shard_map/ppermute | solution.py:611
  60.9 29.3 %collective-permute-start.7 = (bf16[384,768]{1,0:T(8,128)(2,1)S(1)}, bf16[384,768]{1,0:T(8,128)(2,1)S(1)}, u32[]{:S(2)}, u32[]{:S(2)}) collective-permute-start(bf16[384,768]{1,0:T(8,128)(2,1)S(1)} %copy-done.7), channel_id=1, source_target_pairs={{16,0},{0,16},{17,1},{1,17},{18,2},{2,18},{19,3},{3,19},{20,4},{4,... | collective-permute-start | bytes 1769480 | tf_op jit(solution)/shard_map/ppermute | solution.py:617
  62.7 20.7 %collective-permute-start.4 = (bf16[256,768]{1,0:T(8,128)(2,1)}, bf16[256,768]{1,0:T(8,128)(2,1)S(1)}, u32[]{:S(2)}, u32[]{:S(2)}) collective-permute-start(bf16[256,768]{1,0:T(8,128)(2,1)} %collective-permute-done.2.refs_4_), channel_id=1, source_target_pairs={{0,4},{4,0},{8,12},{12,8},{16,20},{20,16},{24,28},{28,24},{1,5},{5... | collective-permute-start | bytes 1179656 | tf_op jit(solution)/shard_map/ppermute | solution.py:611
  64.5 19.0 %collective-permute-start.3 = (bf16[256,768]{1,0:T(8,128)(2,1)}, bf16[256,768]{1,0:T(8,128)(2,1)S(1)}, u32[]{:S(2)}, u32[]{:S(2)}) collective-permute-start(bf16[256,768]{1,0:T(8,128)(2,1)} %collective-permute-done.1.refs_2_), channel_id=1, source_target_pairs={{0,4},{4,0},{8,12},{12,8},{16,20},{20,16},{24,28},{28,24},{1,5},{5... | collective-permute-start | bytes 1179656 | tf_op jit(solution)/shard_map/ppermute | solution.py:611
  79.2 4.2 copy-start.15
  79.2 11.7 %collective-permute-start.6 = (bf16[256,768]{1,0:T(8,128)(2,1)S(1)}, bf16[256,768]{1,0:T(8,128)(2,1)}, u32[]{:S(2)}, u32[]{:S(2)}) collective-permute-start(bf16[256,768]{1,0:T(8,128)(2,1)S(1)} %collective-permute-done.5.refs_6_), channel_id=1, source_target_pairs={{0,4},{4,0},{8,12},{12,8},{16,20},{20,16},{24,28},{28,24},{1,5},{5... | collective-permute-start | bytes 1179656 | tf_op jit(solution)/shard_map/ppermute | solution.py:611
  83.5 6.7 %copy-start.17 = (bf16[256,768]{1,0:T(8,128)(2,1)}, bf16[256,768]{1,0:T(8,128)(2,1)S(1)}, u32[]{:S(2)}) copy-start(bf16[256,768]{1,0:T(8,128)(2,1)S(1)} %collective-permute-done.3.refs_3_) | copy-start | bytes 1179652
  83.5 6.7 %copy-start.16 = (bf16[256,768]{1,0:T(8,128)(2,1)}, bf16[256,768]{1,0:T(8,128)(2,1)S(1)}, u32[]{:S(2)}) copy-start(bf16[256,768]{1,0:T(8,128)(2,1)S(1)} %collective-permute-done.4.refs_5_) | copy-start | bytes 1179652
  92.2 44.8 %all-to-all-start.2 = ((bf16[8,128,768]{2,1,0:T(8,128)(2,1)}), bf16[8,128,768]{2,1,0:T(8,128)(2,1)S(1)}, u32[]{:S(2)}, u32[]{:S(2)}) async-start(bf16[8,128,768]{2,1,0:T(8,128)(2,1)} %bitcast.165), calls=%async_computation.2 | async-start | bytes 3145728 | tf_op jit(solution)/shard_map/all_to_all | solution.py:564
  95.8 33.0 %collective-permute-start.10 = (bf16[384,768]{1,0:T(8,128)(2,1)}, bf16[384,768]{1,0:T(8,128)(2,1)}, u32[]{:S(2)}, u32[]{:S(2)}) collective-permute-start(bf16[384,768]{1,0:T(8,128)(2,1)} %bitcast_convert_fusion.refs_4_), channel_id=1, source_target_pairs={{4,0},{0,4},{5,1},{1,5},{6,2},{2,6},{7,3},{3,7},{12,8},{8,12},{13,... | collective-permute-start | bytes 1769480 | tf_op jit(solution)/shard_map/ppermute | solution.py:617
  97.4 31.4 %collective-permute-start.8 = (bf16[384,768]{1,0:T(8,128)(2,1)}, bf16[384,768]{1,0:T(8,128)(2,1)}, u32[]{:S(2)}, u32[]{:S(2)}) collective-permute-start(bf16[384,768]{1,0:T(8,128)(2,1)} %bitcast_convert_fusion.refs_4_), channel_id=1, source_target_pairs={{16,0},{0,16},{17,1},{1,17},{18,2},{2,18},{19,3},{3,19},{20,4},{4,... | collective-permute-start | bytes 1769480 | tf_op jit(solution)/shard_map/ppermute | solution.py:617
  99.0 29.8 %collective-permute-start.11 = (bf16[384,768]{1,0:T(8,128)(2,1)}, bf16[384,768]{1,0:T(8,128)(2,1)}, u32[]{:S(2)}, u32[]{:S(2)}) collective-permute-start(bf16[384,768]{1,0:T(8,128)(2,1)} %copy-done.24), channel_id=1, source_target_pairs={{4,0},{0,4},{5,1},{1,5},{6,2},{2,6},{7,3},{3,7},{12,8},{8,12},{13,... | collective-permute-start | bytes 1769480 | tf_op jit(solution)/shard_map/ppermute | solution.py:617
  99.6 37.5 %collective-permute-start.9 = (bf16[384,768]{1,0:T(8,128)(2,1)}, bf16[384,768]{1,0:T(8,128)(2,1)}, u32[]{:S(2)}, u32[]{:S(2)}) collective-permute-start(bf16[384,768]{1,0:T(8,128)(2,1)} %bitcast_convert_fusion.1.refs_0_), channel_id=1, source_target_pairs={{4,0},{0,4},{5,1},{1,5},{6,2},{2,6},{7,3},{3,7},{12,8},{8,12},{13,... | collective-permute-start | bytes 1769480 | tf_op jit(solution)/shard_map/ppermute | solution.py:617
  137.0 25.5 %copy-start = (bf16[8,128,768]{2,1,0:T(8,128)(2,1)}, bf16[8,128,768]{2,1,0:T(8,128)(2,1)S(1)}, u32[]{:S(2)}) copy-start(bf16[8,128,768]{2,1,0:T(8,128)(2,1)S(1)} %all-to-all-done.2) | copy-start | bytes 4718596
  137.0 25.3 %all-to-all-start.3 = ((bf16[8,256,128]{2,1,0:T(8,128)(2,1)}), bf16[8,256,128]{2,1,0:T(8,128)(2,1)}, u32[]{:S(2)}, u32[]{:S(2)}) async-start(bf16[8,256,128]{2,1,0:T(8,128)(2,1)} %bitcast.186), calls=%async_computation.3 | async-start | bytes 1048576 | tf_op jit(solution)/shard_map/all_to_all | solution.py:564
  142.2 95.9 %all-gather.2.cloned.1.call-start = ((), (), s32[]{:S(2)}) async-start(), calls=%async_computation.11 | async-start | bytes 3649536 | tf_op jit(solution)/shard_map/all_gather | solution.py:789
  142.2 20.2 %collective-permute-start.12 = (bf16[384,768]{1,0:T(8,128)(2,1)}, bf16[384,768]{1,0:T(8,128)(2,1)}, u32[]{:S(2)}, u32[]{:S(2)}) collective-permute-start(bf16[384,768]{1,0:T(8,128)(2,1)} %collective-permute-done.8.refs_5_), channel_id=1, source_target_pairs={{4,0},{0,4},{5,1},{1,5},{6,2},{2,6},{7,3},{3,7},{12,8},{8,12},{13,... | collective-permute-start | bytes 1769480 | tf_op jit(solution)/shard_map/ppermute | solution.py:617
  162.5 1.4 copy-start.34
  164.0 1.7 copy-start.3
  210.3 27.7 %all-to-all-start.5 = ((bf16[8,128,768]{2,1,0:T(8,128)(2,1)}), bf16[8,128,768]{2,1,0:T(8,128)(2,1)}, u32[]{:S(2)}, u32[]{:S(2)}) async-start(bf16[8,128,768]{2,1,0:T(8,128)(2,1)} %bitcast.181), calls=%async_computation.5 | async-start | bytes 3145728 | tf_op jit(solution)/shard_map/all_to_all | solution.py:564
  221.3 15.8 %collective-permute-start.13 = (bf16[384,768]{1,0:T(8,128)(2,1)}, bf16[384,768]{1,0:T(8,128)(2,1)S(1)}, u32[]{:S(2)}, u32[]{:S(2)}) collective-permute-start(bf16[384,768]{1,0:T(8,128)(2,1)} %get-tuple-element.164), channel_id=1, source_target_pairs={{0,4},{4,0},{1,5},{5,1},{2,6},{6,2},{3,7},{7,3},{8,12},{12,8},{9,1... | collective-permute-start | bytes 1769480 | tf_op jit(solution)/shard_map/ppermute | solution.py:626
  240.9 16.8 %copy-start.1 = (f32[256,768]{1,0:T(8,128)}, f32[256,768]{1,0:T(8,128)S(1)}, u32[]{:S(2)}) copy-start(f32[256,768]{1,0:T(8,128)S(1)} %multiply_add_fusion.residual_ref) | copy-start | bytes 2359300
  241.4 10.5 %copy-start.19 = (f32[384,768]{1,0:T(8,128)S(1)}, f32[384,768]{1,0:T(8,128)}, u32[]{:S(2)}) copy-start(f32[384,768]{1,0:T(8,128)} %get-tuple-element.179) | copy-start | bytes 3538948
  246.9 45.5 %all-to-all-start.6 = ((bf16[8,256,128]{2,1,0:T(8,128)(2,1)}), bf16[8,256,128]{2,1,0:T(8,128)(2,1)S(1)}, u32[]{:S(2)}, u32[]{:S(2)}) async-start(bf16[8,256,128]{2,1,0:T(8,128)(2,1)} %fusion.48), calls=%async_computation.6 | async-start | bytes 1048576 | tf_op jit(solution)/shard_map/all_to_all | solution.py:564
  252.0 4.3 %copy-start.33 = (bf16[384,768]{1,0:T(8,128)(2,1)S(1)}, bf16[384,768]{1,0:T(8,128)(2,1)}, u32[]{:S(2)}) copy-start(bf16[384,768]{1,0:T(8,128)(2,1)} %get-tuple-element.178) | copy-start | bytes 1769476
  252.0 5.7 %copy-start.12 = (bf16[256,768]{1,0:T(8,128)(2,1)S(1)}, bf16[256,768]{1,0:T(8,128)(2,1)}, u32[]{:S(2)}) copy-start(bf16[256,768]{1,0:T(8,128)(2,1)} %copy-done.11) | copy-start | bytes 1179652
  253.3 38.2 %collective-permute-start.15 = (bf16[384,768]{1,0:T(8,128)(2,1)S(1)}, bf16[384,768]{1,0:T(8,128)(2,1)S(1)}, u32[]{:S(2)}, u32[]{:S(2)}) collective-permute-start(bf16[384,768]{1,0:T(8,128)(2,1)S(1)} %add_convert_fusion.1), channel_id=1, source_target_pairs={{0,16},{16,0},{1,17},{17,1},{2,18},{18,2},{3,19},{19,3},{4,20},{20... | collective-permute-start | bytes 1769480 | tf_op jit(solution)/shard_map/ppermute | solution.py:626
  256.2 36.1 %collective-permute-start.14 = (bf16[384,768]{1,0:T(8,128)(2,1)S(1)}, bf16[384,768]{1,0:T(8,128)(2,1)}, u32[]{:S(2)}, u32[]{:S(2)}) collective-permute-start(bf16[384,768]{1,0:T(8,128)(2,1)S(1)} %copy-done.33), channel_id=1, source_target_pairs={{0,4},{4,0},{1,5},{5,1},{2,6},{6,2},{3,7},{7,3},{8,12},{12,8},{9,1... | collective-permute-start | bytes 1769480 | tf_op jit(solution)/shard_map/ppermute | solution.py:626
  258.3 8.8 %collective-permute-start.16 = (bf16[8,24,768]{2,1,0:T(8,128)(2,1)S(1)}, bf16[8,24,768]{2,1,0:T(8,128)(2,1)S(1)}, u32[]{:S(2)}, u32[]{:S(2)}) collective-permute-start(bf16[8,24,768]{2,1,0:T(8,128)(2,1)S(1)} %get-tuple-element.238), channel_id=1, source_target_pairs={{0,1},{1,2},{2,3},{3,0},{4,5},{5,6},{6,7},{7,4},{8,9},{9,10},{10,1... | collective-permute-start | bytes 884744 | tf_op jit(solution)/shard_map/ppermute | solution.py:626
  258.4 9.9 %collective-permute-start.17 = (bf16[8,24,768]{2,1,0:T(8,128)(2,1)S(1)}, bf16[8,24,768]{2,1,0:T(8,128)(2,1)S(1)}, u32[]{:S(2)}, u32[]{:S(2)}) collective-permute-start(bf16[8,24,768]{2,1,0:T(8,128)(2,1)S(1)} %get-tuple-element.237), channel_id=1, source_target_pairs={{0,2},{1,3},{2,0},{3,1},{4,6},{5,7},{6,4},{7,5},{8,10},{9,11},{10,... | collective-permute-start | bytes 884744 | tf_op jit(solution)/shard_map/ppermute | solution.py:626
  259.9 13.1 %collective-permute-start.18 = (bf16[8,24,768]{2,1,0:T(8,128)(2,1)S(1)}, bf16[8,24,768]{2,1,0:T(8,128)(2,1)S(1)}, u32[]{:S(2)}, u32[]{:S(2)}) collective-permute-start(bf16[8,24,768]{2,1,0:T(8,128)(2,1)S(1)} %get-tuple-element.236), channel_id=1, source_target_pairs={{0,3},{1,0},{2,1},{3,2},{4,7},{5,4},{6,5},{7,6},{8,11},{9,8},{10,9... | collective-permute-start | bytes 884744 | tf_op jit(solution)/shard_map/ppermute | solution.py:626
  267.1 24.4 %copy-start.25 = (bf16[8,24,768]{2,1,0:T(8,128)(2,1)}, bf16[8,24,768]{2,1,0:T(8,128)(2,1)S(1)}, u32[]{:S(2)}) copy-start(bf16[8,24,768]{2,1,0:T(8,128)(2,1)S(1)} %collective-permute-done.16) | copy-start | bytes 884740
  268.3 23.2 %copy-start.26 = (bf16[8,24,768]{2,1,0:T(8,128)(2,1)}, bf16[8,24,768]{2,1,0:T(8,128)(2,1)S(1)}, u32[]{:S(2)}) copy-start(bf16[8,24,768]{2,1,0:T(8,128)(2,1)S(1)} %collective-permute-done.17) | copy-start | bytes 884740
  273.0 18.5 %copy-start.27 = (bf16[8,24,768]{2,1,0:T(8,128)(2,1)}, bf16[8,24,768]{2,1,0:T(8,128)(2,1)S(1)}, u32[]{:S(2)}) copy-start(bf16[8,24,768]{2,1,0:T(8,128)(2,1)S(1)} %collective-permute-done.18) | copy-start | bytes 884740
  293.1 36.2 %all-to-all-start.7 = ((bf16[8,128,768]{2,1,0:T(8,128)(2,1)}), bf16[8,128,768]{2,1,0:T(8,128)(2,1)S(1)}, u32[]{:S(2)}, u32[]{:S(2)}) async-start(bf16[8,128,768]{2,1,0:T(8,128)(2,1)} %bitcast.164), calls=%async_computation.7 | async-start | bytes 3145728 | tf_op jit(solution)/shard_map/all_to_all | solution.py:564
  299.1 28.3 %collective-permute-start.21 = (bf16[384,768]{1,0:T(8,128)(2,1)}, bf16[384,768]{1,0:T(8,128)(2,1)}, u32[]{:S(2)}, u32[]{:S(2)}) collective-permute-start(bf16[384,768]{1,0:T(8,128)(2,1)} %add_convert_fusion), channel_id=1, source_target_pairs={{0,16},{16,0},{1,17},{17,1},{2,18},{18,2},{3,19},{19,3},{4,20},{20... | collective-permute-start | bytes 1769480 | tf_op jit(solution)/shard_map/ppermute | solution.py:626
  299.4 28.0 %collective-permute-start.19 = (bf16[384,768]{1,0:T(8,128)(2,1)}, bf16[384,768]{1,0:T(8,128)(2,1)}, u32[]{:S(2)}, u32[]{:S(2)}) collective-permute-start(bf16[384,768]{1,0:T(8,128)(2,1)} %get-tuple-element.186), channel_id=1, source_target_pairs={{0,4},{4,0},{1,5},{5,1},{2,6},{6,2},{3,7},{7,3},{8,12},{12,8},{9,1... | collective-permute-start | bytes 1769480 | tf_op jit(solution)/shard_map/ppermute | solution.py:626
  301.1 26.7 %collective-permute-start.20 = (bf16[384,768]{1,0:T(8,128)(2,1)}, bf16[384,768]{1,0:T(8,128)(2,1)}, u32[]{:S(2)}, u32[]{:S(2)}) collective-permute-start(bf16[384,768]{1,0:T(8,128)(2,1)} %get-tuple-element.187), channel_id=1, source_target_pairs={{0,4},{4,0},{1,5},{5,1},{2,6},{6,2},{3,7},{7,3},{8,12},{12,8},{9,1... | collective-permute-start | bytes 1769480 | tf_op jit(solution)/shard_map/ppermute | solution.py:626
  329.3 41.4 %all-to-all-start.8 = ((bf16[8,256,384]{2,1,0:T(8,128)(2,1)}), bf16[8,256,384]{2,1,0:T(8,128)(2,1)}, u32[]{:S(2)}, u32[]{:S(2)}) async-start(bf16[8,256,384]{2,1,0:T(8,128)(2,1)} %bitcast.180), calls=%async_computation.8 | async-start | bytes 3145728 | tf_op jit(solution)/shard_map/all_to_all | solution.py:564
  341.4 4.2 copy-start.22
  342.6 9.0 %collective-permute-start.22 = (bf16[8,24,384]{2,1,0:T(8,128)(2,1)S(1)}, bf16[8,24,384]{2,1,0:T(8,128)(2,1)S(1)}, u32[]{:S(2)}, u32[]{:S(2)}) collective-permute-start(bf16[8,24,384]{2,1,0:T(8,128)(2,1)S(1)} %get-tuple-element.239), channel_id=1, source_target_pairs={{0,1},{1,2},{2,3},{3,0},{4,5},{5,6},{6,7},{7,4},{8,9},{9,10},{10,1... | collective-permute-start | bytes 442376 | tf_op jit(solution)/shard_map/ppermute | solution.py:626
  342.7 8.9 %collective-permute-start.23 = (bf16[8,24,384]{2,1,0:T(8,128)(2,1)S(1)}, bf16[8,24,384]{2,1,0:T(8,128)(2,1)S(1)}, u32[]{:S(2)}, u32[]{:S(2)}) collective-permute-start(bf16[8,24,384]{2,1,0:T(8,128)(2,1)S(1)} %get-tuple-element.241), channel_id=1, source_target_pairs={{0,2},{1,3},{2,0},{3,1},{4,6},{5,7},{6,4},{7,5},{8,10},{9,11},{10,... | collective-permute-start | bytes 442376 | tf_op jit(solution)/shard_map/ppermute | solution.py:626
  344.2 7.4 %collective-permute-start.24 = (bf16[8,24,384]{2,1,0:T(8,128)(2,1)S(1)}, bf16[8,24,384]{2,1,0:T(8,128)(2,1)S(1)}, u32[]{:S(2)}, u32[]{:S(2)}) collective-permute-start(bf16[8,24,384]{2,1,0:T(8,128)(2,1)S(1)} %get-tuple-element.240), channel_id=1, source_target_pairs={{0,3},{1,0},{2,1},{3,2},{4,7},{5,4},{6,5},{7,6},{8,11},{9,8},{10,9... | collective-permute-start | bytes 442376 | tf_op jit(solution)/shard_map/ppermute | solution.py:626
  345.6 7.0 %copy-start.20 = (bf16[8,24,768]{2,1,0:T(8,128)(2,1)S(1)}, bf16[8,24,768]{2,1,0:T(8,128)(2,1)}, u32[]{:S(2)}) copy-start(bf16[8,24,768]{2,1,0:T(8,128)(2,1)} %fusion.9) | copy-start | bytes 884740
  370.7 16.5 %all-to-all-start.9 = ((bf16[8,24,1152]{2,1,0:T(8,128)(2,1)}), bf16[8,24,1152]{2,1,0:T(8,128)(2,1)S(1)}, u32[]{:S(2)}, u32[]{:S(2)}) async-start(bf16[8,24,1152]{2,1,0:T(8,128)(2,1)} %pad_maximum_fusion), calls=%async_computation.9 | async-start | bytes 884736 | tf_op jit(solution)/shard_map/all_to_all | solution.py:564
  391.3 13.0 %all-to-all-start.10 = ((f32[32,1,1664]{2,1,0:T(1,128)}), f32[32,1,1664]{2,1,0:T(1,128)S(1)}, u32[]{:S(2)}, u32[]{:S(2)}) async-start(f32[32,1,1664]{2,1,0:T(1,128)} %broadcast_in_dim.62), calls=%async_computation.10 | async-start | bytes 425984 | tf_op jit(solution)/shard_map/all_to_all | solution.py:564
  395.2 11.8 %copy-start.30 = (f32[2,768]{1,0:T(2,128)S(1)}, f32[2,768]{1,0:T(2,128)}, u32[]{:S(2)}) copy-start(f32[2,768]{1,0:T(2,128)} %param.41) | copy-start | bytes 18436
  395.2 11.8 %copy-start.31 = (f32[2,768]{1,0:T(2,128)S(1)}, f32[2,768]{1,0:T(2,128)}, u32[]{:S(2)}) copy-start(f32[2,768]{1,0:T(2,128)} %param.40) | copy-start | bytes 18436
  405.6 11.3 %copy-start.28 = (f32[2,768]{1,0:T(2,128)}, f32[2,768]{1,0:T(2,128)S(1)}, u32[]{:S(2)}) copy-start(f32[2,768]{1,0:T(2,128)S(1)} %reshape.237) | copy-start | bytes 18436
  (7 other events, 5.8 us)
Sparse Core Ops, SparseCore 0:
  162.5 62.0 all-gather.1
